TPU v7x, 32 devices: a whole 2x2x4 slice. The times are simulated.
32 devices in a mesh: dp: 4 (over z), seq: 8 (over y, x, core).
Axes of the slice: x: 2, y: 2, z: 4, core: 2. Of those that a mesh axis runs over, the one named last changes fastest.
Arguments:
- tokens: bfloat16 [4096, 2048], P(('dp', 'seq')), may hold values from -6 to 6
- cotangent: bfloat16 [4096, 2048], P(('dp', 'seq')), may hold values from -6 to 6
- lengths: int32 [8], P('dp'), may hold values from 16 to 1008, as said below
- lower_bound: float32 [2048], replicated, may hold values from 0.5 to 1
- mixer_w: float32 [2048, 4, 2048], P(('dp', 'seq')), may hold values from -0.125 to 0.125
- mlp_in: float32 [2048, 2, 5632], P(('dp', 'seq')), may hold values from -0.125 to 0.125
- mlp_down: float32 [5632, 2048], P(('dp', 'seq')), may hold values from -0.078125 to 0.078125
- gains: float32 [3, 2048], P(None, ('dp', 'seq')), may hold values from 0.3 to 2.5
- mixer_m: float32 [2048, 4, 2048], P(('dp', 'seq')), may hold values from -9.1552734e-05 to 9.1552734e-05
- mixer_v: float32 [2048, 4, 2048], P(('dp', 'seq')), may hold values from 1.9460414e-11 to 7.784166e-11
- in_m: float32 [2048, 2, 5632], P(('dp', 'seq')), may hold values from -9.1552734e-05 to 9.1552734e-05
- in_v: float32 [2048, 2, 5632], P(('dp', 'seq')), may hold values from 1.9460414e-11 to 7.784166e-11
- down_m: float32 [5632, 2048], P(('dp', 'seq')), may hold values from -9.1552734e-05 to 9.1552734e-05
- down_v: float32 [5632, 2048], P(('dp', 'seq')), may hold values from 1.9460414e-11 to 7.784166e-11
- gain_m: float32 [3, 2048], P(None, ('dp', 'seq')), may hold values from -0.00036621094 to 0.00036621094
- gain_v: float32 [3, 2048], P(None, ('dp', 'seq')), may hold values from 3.1136663e-10 to 1.2454665e-09
Outputs:
- block_out: bfloat16 [4096, 2048], P(('dp', 'seq'))
- input_grad: float32 [4096, 2048], P(('dp', 'seq'))
- grad_norm: float32 [], replicated
- new_mixer: float32 [2048, 4, 2048], P(('dp', 'seq'))
- new_mixer_m: float32 [2048, 4, 2048], P(('dp', 'seq'))
- new_mixer_v: float32 [2048, 4, 2048], P(('dp', 'seq'))
- new_in: float32 [2048, 2, 5632], P(('dp', 'seq'))
- new_in_m: float32 [2048, 2, 5632], P(('dp', 'seq'))
- new_in_v: float32 [2048, 2, 5632], P(('dp', 'seq'))
- new_down: float32 [5632, 2048], P(('dp', 'seq'))
- new_down_m: float32 [5632, 2048], P(('dp', 'seq'))
- new_down_v: float32 [5632, 2048], P(('dp', 'seq'))
- new_gains: float32 [3, 2048], P(None, ('dp', 'seq'))
- new_gain_m: float32 [3, 2048], P(None, ('dp', 'seq'))
- new_gain_v: float32 [3, 2048], P(None, ('dp', 'seq'))
Inputs may be any that keep to these rules, and one draw needn't show every extreme that they name: Positions beyond the sum of a group's lengths are padding at the group's end, fewer than 128 of them; one sequence of each group starts on the group's first device and ends on its last.
All inputs are finite; a program needn't handle non-finite values.
Results may differ from a plain program's by a relative error of at most 0.0098.
Values may be sent and summed in bfloat16 or wider, within the bound.
No kernel may reach another device: no remote copies, remote signals or barrier semaphores. Data moves between devices by JAX's collectives and lax.ppermute only.
A program may use at most 640 MiB of HBM per device.

v0:
```python
import jax
import jax.numpy as jnp
from jax import lax
from jax.sharding import PartitionSpec as P

STEP = 10


EPS_NORM = 1e-06
BETA_ONE = 0.9
BETA_TWO = 0.999
ADAM_EPS = 1e-08
RATE_MATRIX = 0.03
RATE_GAIN = 0.5
DECAY_WEIGHT = 0.1
CLIP_NORM = 1.0


def prefix(value, axis, join, neutral, backward):
    count, mine = (lax.axis_size(axis), lax.axis_index(axis))
    pieces = jax.tree.map(lambda part: lax.all_gather(part, axis), value)
    if backward:
        pieces = jax.tree.map(lambda part: part[::-1], pieces)
        mine = count - 1 - mine
    subtotal = jax.tree.map(
        lambda part, zero: jnp.full_like(part, 0) + jnp.asarray(zero, part.dtype), value, neutral
    )

    def hop(position, subtotal):
        longer = join(subtotal, jax.tree.map(lambda part: part[position], pieces))
        return jax.tree.map(lambda new, old: jnp.where(position < mine, new, old), longer, subtotal)

    return lax.fori_loop(0, count - 1, hop, subtotal)


def combine_pairs(earlier, later):
    return (earlier[0] * later[0], later[0] * earlier[1] + later[1])


def normalize(value):
    factor = lax.rsqrt(jnp.mean(value * value, axis=-1, keepdims=True) + EPS_NORM)
    return (value * factor, factor)


def norm_back(grad_normed, normed, factor):
    return factor * (grad_normed - normed * jnp.mean(grad_normed * normed, axis=-1, keepdims=True))


def silu(value):
    return value * jax.nn.sigmoid(value)


def silu_grad(value):
    sig = jax.nn.sigmoid(value)
    return sig * (1.0 + value * (1.0 - sig))


def adam_step(weight, first, second, grad, rate, decay_w):
    first_new = BETA_ONE * first + (1.0 - BETA_ONE) * grad
    second_new = BETA_TWO * second + (1.0 - BETA_TWO) * grad * grad
    step_size = (
        first_new
        / (1.0 - BETA_ONE**STEP)
        / (jnp.sqrt(second_new / (1.0 - BETA_TWO**STEP)) + ADAM_EPS)
    )
    return (weight - rate * (step_size + decay_w * weight), first_new, second_new)


def shards(
    tokens,
    cotangent,
    lengths,
    lower_bound,
    mixer_w,
    mlp_in,
    mlp_down,
    gains,
    mixer_m,
    mixer_v,
    in_m,
    in_v,
    down_m,
    down_v,
    gain_m,
    gain_v,
):
    rows = tokens.shape[0]
    width = tokens.shape[1]
    hidden_width = mlp_in.shape[2]
    full_mixer, full_in, full_down = (
        lax.all_gather(mixer_w.astype(jnp.bfloat16), ("dp", "seq"), axis=0, tiled=True),
        lax.all_gather(mlp_in.astype(jnp.bfloat16), ("dp", "seq"), axis=0, tiled=True),
        lax.all_gather(mlp_down.astype(jnp.bfloat16), ("dp", "seq"), axis=0, tiled=True),
    )
    full_gains = lax.all_gather(gains, ("dp", "seq"), axis=1, tiled=True)
    places = lax.axis_index("seq") * rows + jnp.arange(rows, dtype=jnp.int32)
    ends = jnp.cumsum(lengths)
    starts = ends - lengths
    is_start = jnp.any(places[:, None] == starts[None, :], axis=-1)
    valid = (places < ends[-1]).astype(jnp.float32)
    x = tokens.astype(jnp.float32)
    x_normed, x_factor = normalize(x)
    n1 = (x_normed * full_gains[0]).astype(jnp.bfloat16)
    proj = jnp.einsum("td,dkc->tkc", n1, full_mixer[:, :3, :], preferred_element_type=jnp.float32)
    in_proj = proj[:, 0, :]
    forget_proj = proj[:, 1, :]
    gate_proj = proj[:, 2, :]
    gap = 1.0 - lower_bound
    keep = gap * jax.nn.sigmoid(-forget_proj)
    decay = jnp.where(is_start[:, None], jnp.zeros_like(keep), 1.0 - keep)
    silu_in = silu(in_proj)
    inputs = silu_in * keep
    cum_decay, local_state = lax.associative_scan(combine_pairs, (decay, inputs), axis=0)
    ones_row = jnp.ones((width,), jnp.float32)
    zeros_row = jnp.zeros((width,), jnp.float32)
    carry_decay, carry_state = prefix(
        (cum_decay[-1], local_state[-1]), "seq", combine_pairs, (ones_row, zeros_row), False
    )
    state = local_state + cum_decay * carry_state[None, :]
    state_normed, state_factor = normalize(state)
    gate_act = silu(gate_proj)
    mixed_in = (state_normed * full_gains[1] * gate_act).astype(jnp.bfloat16)
    mix = jnp.dot(mixed_in, full_mixer[:, 3, :], preferred_element_type=jnp.float32)
    after_mix = x + mix
    mid_normed, mid_factor = normalize(after_mix)
    n2 = (mid_normed * full_gains[2]).astype(jnp.bfloat16)
    gate_up = jnp.einsum("td,dkf->tkf", n2, full_in, preferred_element_type=jnp.float32)
    gate = gate_up[:, 0, :]
    up_value = gate_up[:, 1, :]
    silu_gate = silu(gate)
    hidden = (silu_gate * up_value).astype(jnp.bfloat16)
    down = jnp.dot(hidden, full_down, preferred_element_type=jnp.float32)
    block_out = (after_mix + down).astype(jnp.bfloat16)
    full_mixer, full_in, full_down = (
        lax.all_gather(mixer_w.astype(jnp.bfloat16), ("dp", "seq"), axis=0, tiled=True),
        lax.all_gather(mlp_in.astype(jnp.bfloat16), ("dp", "seq"), axis=0, tiled=True),
        lax.all_gather(mlp_down.astype(jnp.bfloat16), ("dp", "seq"), axis=0, tiled=True),
    )
    cot = cotangent.astype(jnp.float32) * valid[:, None]
    cot_low = cot.astype(jnp.bfloat16)
    shard_down = lax.psum_scatter(
        jnp.einsum("tf,td->fd", hidden, cot_low, preferred_element_type=jnp.float32),
        ("dp", "seq"),
        scatter_dimension=0,
        tiled=True,
    )
    d_hidden = jnp.einsum("td,fd->tf", cot_low, full_down, preferred_element_type=jnp.float32)
    d_gate = d_hidden * up_value * silu_grad(gate)
    d_up = d_hidden * silu_gate
    d_gate_up = jnp.stack([d_gate, d_up], axis=1).astype(jnp.bfloat16)
    d_n2 = jnp.einsum("tkf,dkf->td", d_gate_up, full_in, preferred_element_type=jnp.float32)
    grad_gain_mlp = jnp.sum(d_n2 * mid_normed, axis=0)
    d_mid = cot + norm_back(d_n2 * full_gains[2], mid_normed, mid_factor)
    d_mix = d_mid.astype(jnp.bfloat16)
    d_mixed = jnp.einsum(
        "tc,dc->td", d_mix, full_mixer[:, 3, :], preferred_element_type=jnp.float32
    )
    grad_gain_inner = jnp.sum(d_mixed * state_normed * gate_act, axis=0)
    d_gate_proj = d_mixed * state_normed * full_gains[1] * silu_grad(gate_proj)
    d_state = norm_back(d_mixed * full_gains[1] * gate_act, state_normed, state_factor)
    next_decay = jnp.concatenate([decay[1:], jnp.ones((1, width), jnp.float32)], axis=0)
    back_cum, back_local = lax.associative_scan(
        combine_pairs, (next_decay[::-1], d_state[::-1]), axis=0
    )
    back_cum = back_cum[::-1]
    back_local = back_local[::-1]
    carry_decay_back, carry_grad = prefix(
        (cum_decay[-1], decay[0] * back_local[0]), "seq", combine_pairs, (ones_row, zeros_row), True
    )
    d_total = back_local + back_cum * carry_grad[None, :]
    previous = jnp.concatenate([carry_state[None, :], state[:-1]], axis=0)
    d_decay = jnp.where(is_start[:, None], jnp.zeros_like(d_total), d_total * previous)
    d_in_proj = d_total * keep * silu_grad(in_proj)
    d_keep = d_total * silu_in - d_decay
    sig_neg = jax.nn.sigmoid(-forget_proj)
    d_forget_proj = -d_keep * gap * sig_neg * (1.0 - sig_neg)
    d_proj = jnp.stack([d_in_proj, d_forget_proj, d_gate_proj], axis=1).astype(jnp.bfloat16)
    d_n1 = jnp.einsum(
        "tkc,dkc->td", d_proj, full_mixer[:, :3, :], preferred_element_type=jnp.float32
    )
    grad_gain_first = jnp.sum(d_n1 * x_normed, axis=0)
    input_grad = d_mid + norm_back(d_n1 * full_gains[0], x_normed, x_factor)
    gain_columns = jnp.stack([grad_gain_first, grad_gain_inner, grad_gain_mlp], axis=1)
    count = mixer_w.shape[0] * lax.axis_size(("dp", "seq"))
    proj_grad = jnp.einsum("td,tkc->dkc", n1, d_proj, preferred_element_type=jnp.float32).reshape(
        count, 3 * width
    )
    out_grad = jnp.einsum("td,tc->dc", mixed_in, d_mix, preferred_element_type=jnp.float32)
    in_grad = jnp.einsum("td,tkf->dkf", n2, d_gate_up, preferred_element_type=jnp.float32).reshape(
        count, 2 * hidden_width
    )
    shard_rows = lax.psum_scatter(
        jnp.concatenate([proj_grad, out_grad, in_grad, gain_columns], axis=1),
        ("dp", "seq"),
        scatter_dimension=0,
        tiled=True,
    )
    shard_mixer = shard_rows[:, : 4 * width].reshape(-1, 4, width)
    shard_in = shard_rows[:, 4 * width : 4 * width + 2 * hidden_width].reshape(-1, 2, hidden_width)
    shard_gains = shard_rows[:, 4 * width + 2 * hidden_width :].T
    local_total = (
        jnp.sum(shard_mixer * shard_mixer)
        + jnp.sum(shard_in * shard_in)
        + jnp.sum(shard_down * shard_down)
        + jnp.sum(shard_gains * shard_gains)
    )
    total = lax.psum(local_total, ("dp", "seq"))
    grad_norm = jnp.sqrt(total)
    clip = jnp.minimum(1.0, CLIP_NORM / (grad_norm + 1e-06))
    new_mixer, new_mixer_m, new_mixer_v = adam_step(
        mixer_w, mixer_m, mixer_v, clip * shard_mixer, RATE_MATRIX, DECAY_WEIGHT
    )
    new_in, new_in_m, new_in_v = adam_step(
        mlp_in, in_m, in_v, clip * shard_in, RATE_MATRIX, DECAY_WEIGHT
    )
    new_down, new_down_m, new_down_v = adam_step(
        mlp_down, down_m, down_v, clip * shard_down, RATE_MATRIX, DECAY_WEIGHT
    )
    new_gains, new_gain_m, new_gain_v = adam_step(
        gains, gain_m, gain_v, clip * shard_gains, RATE_GAIN, 0.0
    )
    return (
        block_out,
        input_grad,
        grad_norm,
        new_mixer,
        new_mixer_m,
        new_mixer_v,
        new_in,
        new_in_m,
        new_in_v,
        new_down,
        new_down_m,
        new_down_v,
        new_gains,
        new_gain_m,
        new_gain_v,
    )


def solution(mesh):
    placed = (
        P(("dp", "seq"), None),
        P(("dp", "seq"), None),
        P("dp"),
        P(),
        P(("dp", "seq"), None, None),
        P(("dp", "seq"), None, None),
        P(("dp", "seq"), None),
        P(None, ("dp", "seq")),
        P(("dp", "seq"), None, None),
        P(("dp", "seq"), None, None),
        P(("dp", "seq"), None, None),
        P(("dp", "seq"), None, None),
        P(("dp", "seq"), None),
        P(("dp", "seq"), None),
        P(None, ("dp", "seq")),
        P(None, ("dp", "seq")),
    )
    return jax.shard_map(
        shards,
        mesh=mesh,
        in_specs=placed,
        out_specs=(
            P(("dp", "seq"), None),
            P(("dp", "seq"), None),
            P(),
            P(("dp", "seq"), None, None),
            P(("dp", "seq"), None, None),
            P(("dp", "seq"), None, None),
            P(("dp", "seq"), None, None),
            P(("dp", "seq"), None, None),
            P(("dp", "seq"), None, None),
            P(("dp", "seq"), None),
            P(("dp", "seq"), None),
            P(("dp", "seq"), None),
            P(None, ("dp", "seq")),
            P(None, ("dp", "seq")),
            P(None, ("dp", "seq")),
        ),
        check_vma=False,
    )
```

profile of v0, /device:TPU:0, one launch (start us, length us, event | category | flops | bytes accessed | tf_op | source)
XLA Modules:
  0.0 2922.2 jit_solution(9472219985054979527)
XLA Ops:
  16.0 44.4 %all-gather = f32[32,64,3]{1,2,0:T(4,128)S(1)} all-gather(f32[1,64,3]{1,2,0:T(4,128)S(1)} %bitcast.183), channel_id=1, replica_groups=mesh['dp'=4,'seq'=8] {'dp','seq'}, dimensions={0}, use_global_device_ids=true | all-gather | bytes 25344 | tf_op jit(solution)/shard_map/all_gather | solution.py:95
  62.7 146.4 %all-gather.8.cloned.1.call-done = bf16[2048,4,2048]{2,0,1:T(8,128)(2,1)} async-done(((bf16[64,4,2048]{2,0,1:T(8,128)(2,1)}), bf16[2048,4,2048]{2,0,1:T(8,128)(2,1)}) %all-gather.8.cloned.1.call-update) | async-done | bytes 33554448 | tf_op jit(solution)/shard_map/all_gather | solution.py:91
  209.1 10.1 fusion.2
  237.6 4.6 pad.201
  243.0 4.6 pad.187
  253.7 9.2 all-gather.1
  264.8 4.6 pad.186
  270.3 8.3 all-gather.2
  283.2 5.1 multiply_reduce_fusion.7
  288.4 177.9 %all-gather.10.cloned.1.call-done = bf16[2048,2,5632]{2,0,1:T(8,128)(2,1)} async-done(((bf16[64,2,5632]{2,0,1:T(8,128)(2,1)}), bf16[2048,2,5632]{2,0,1:T(8,128)(2,1)}) %all-gather.10.cloned.1.call-update) | async-done | bytes 46137360 | tf_op jit(solution)/shard_map/all_gather | solution.py:92
  466.4 20.7 fusion.68
  487.0 125.6 %all-gather.12.cloned.1.call-done = bf16[5632,2048]{1,0:T(8,128)(2,1)} async-done(((bf16[176,2048]{1,0:T(8,128)(2,1)}), bf16[5632,2048]{1,0:T(8,128)(2,1)}) %all-gather.12.cloned.1.call-update) | async-done | bytes 23068688 | tf_op jit(solution)/shard_map/all_gather | solution.py:93
  612.6 15.3 fusion.21
  627.9 19.3 fusion.57
  647.3 5.2 rev.16
  663.5 8.3 slice.574
  671.7 8.3 slice.565
  680.0 8.3 slice.567
  688.3 22.7 multiply_reduce_fusion.3
  713.4 6.6 multiply_reduce_fusion.4
  732.9 8.3 slice.569
  741.1 8.3 slice.571
  780.4 8.3 slice.619
  834.9 4.6 pad.214
  839.5 4.6 pad.215
  846.8 8.9 rev.14
  856.6 12.2 all-gather.3
  869.2 4.6 pad.228
  873.8 4.6 pad.229
  881.2 8.9 rev.15
  890.1 6.3 while.29
  896.4 4.0 fusion.49
  900.5 8.2 fusion.54
  908.8 14.7 fusion.27
  923.4 21.2 fusion.42
  944.7 34.2 %fusion.14 = f32[2048,2,5632]{0,2,1:T(8,128)} fusion(bf16[128,1,5632]{2,0,1:T(8,128)(2,1)} %get-tuple-element.286, bf16[128,1,5632]{2,0,1:T(8,128)(2,1)S(1)} %copy-done.14, f32[128,2048]{1,0:T(8,128)S(1)} %get-tuple-element.358, f32[2048]{0:T(1024)S(1)} %bitcast.163, f32[128]{0:T(128)} %copy-done.51), kind=kOutput, calls=%fused_computation.41 | convolution fusion | flops 5912133632 | bytes 96215552 | tf_op jit(solution)/shard_map/td,tkf->dkf/dot_general | solution.py:189
  978.9 347.0 %concatenate.107 = f32[2048,19459]{0,1:T(8,128)} concatenate(f32[2048,6144]{0,1:T(8,128)} %bitcast.156, f32[2048,2048]{0,1:T(8,128)} %fusion.54, f32[2048,11264]{0,1:T(8,128)} %bitcast.30, f32[2048,1]{0,1:T(1,128)S(1)} %bitcast.182, f32[2048,1]{0,1:T(1,128)S(1)} %bitcast.181, f32[2048,1]{0,1:T(1,128)S(1)} %bitcast.180), dimensions={1} | concatenate | bytes 318816256 | tf_op jit(solution)/shard_map/concatenate | solution.py:193
  1325.9 154.3 %copy.81 = f32[2048,19459]{1,0:T(8,128)} copy(f32[2048,19459]{0,1:T(8,128)} %concatenate.107) | data formatting | bytes 318816256
  1481.9 15.2 fusion.12
  1499.7 1310.4 %reduce-scatter.7.cloned.1.call-done = f32[64,19459]{1,0:T(8,128)} async-done(((f32[2048,19459]{1,0:T(8,128)}), f32[64,19459]{1,0:T(8,128)}) %reduce-scatter.7.cloned.1.call-update) | async-done | bytes 4981520
  2820.3 3.9 copy.87
  2824.2 4.2 multiply_reduce_fusion
  2832.4 39.5 %psum.7 = f32[]{:T(128)} all-reduce(f32[]{:T(128)S(6)} %add.569), channel_id=1, replica_groups=mesh['dp'=4,'seq'=8] {'dp','seq'}, use_global_device_ids=true, to_apply=%region_21.22 | all-reduce | flops 1 | bytes 8 | tf_op jit(solution)/shard_map/psum | solution.py:207
  2872.7 5.0 broadcast_multiply_fusion
  2880.9 5.3 copy.74
  2886.2 4.9 copy.71
  2891.8 7.9 multiply_subtract_fusion.1
  2899.7 11.5 multiply_subtract_fusion
  (442 shorter events, 181.9 us)
Async XLA Ops:
  7.2 201.9 %all-gather.8.cloned.1.call-start = ((), (), s32[]{:S(2)}) async-start(), calls=%async_computation.2 | async-start | bytes 34603008 | tf_op jit(solution)/shard_map/all_gather | solution.py:91
  11.1 455.3 %all-gather.10.cloned.1.call-start = ((), (), s32[]{:S(2)}) async-start(), calls=%async_computation.3 | async-start | bytes 47579136 | tf_op jit(solution)/shard_map/all_gather | solution.py:92
  12.7 49.1 %copy-start.15 = (bf16[128,2048]{1,0:T(8,128)(2,1)S(1)}, bf16[128,2048]{1,0:T(8,128)(2,1)}, u32[]{:S(2)}) copy-start(bf16[128,2048]{1,0:T(8,128)(2,1)} %param.20) | copy-start | bytes 1572868
  12.7 49.3 %copy-start.62 = (f32[2048]{0:T(1024)S(1)}, f32[2048]{0:T(1024)}, u32[]{:S(2)}) copy-start(f32[2048]{0:T(1024)} %param.23) | copy-start | bytes 24580
  12.7 599.9 %all-gather.12.cloned.1.call-start = ((), (), s32[]{:S(2)}) async-start(), calls=%async_computation.4 | async-start | bytes 23789568 | tf_op jit(solution)/shard_map/all_gather | solution.py:93
  15.2 1482.0 %reduce-scatter.5.cloned.1.call-start = ((), (), s32[]{:S(2)}) async-start(), calls=%async_computation.5 | async-start | bytes 47579136 | tf_op jit(solution)/shard_map/reduce_scatter | solution.py:141
  61.8 157.4 %copy-start.68 = (pred[128]{0:T(512)(128)(4,1)}, pred[128]{0:T(512)(128)(4,1)S(1)}, u32[]{:S(2)}) copy-start(pred[128]{0:T(512)(128)(4,1)S(1)} %compare_reduce_fusion) | copy-start | bytes 388
  62.0 157.2 %copy-start.65 = (f32[128]{0:T(128)}, f32[128]{0:T(128)S(1)}, u32[]{:S(2)}) copy-start(f32[128]{0:T(128)S(1)} %add_rsqrt_fusion.2) | copy-start | bytes 1540
  62.0 157.2 %copy-start.45 = (f32[2048]{0:T(1024)}, f32[2048]{0:T(1024)S(1)}, u32[]{:S(2)}) copy-start(f32[2048]{0:T(1024)S(1)} %broadcast_subtract_fusion) | copy-start | bytes 24580
  62.7 156.6 %copy-start.47 = (f32[1,2048]{1,0:T(1,128)}, f32[1,2048]{1,0:T(1,128)S(1)}, u32[]{:S(2)}) copy-start(f32[1,2048]{1,0:T(1,128)S(1)} %get-tuple-element.336) | copy-start | bytes 24580
  247.6 15.3 copy-start.53
  249.8 29.5 %copy-start.23 = (f32[128,2048]{1,0:T(8,128)S(1)}, f32[128,2048]{1,0:T(8,128)}, u32[]{:S(2)}) copy-start(f32[128,2048]{1,0:T(8,128)} %pad.201) | copy-start | bytes 3145732
  252.7 26.6 copy-start.24
  288.4 656.3 %copy-start.1 = (f32[128,2048]{1,0:T(8,128)}, f32[128,2048]{1,0:T(8,128)S(1)}, u32[]{:S(2)}) copy-start(f32[128,2048]{1,0:T(8,128)S(1)} %get-tuple-element.358) | copy-start | bytes 3145732
  288.4 422.6 %copy-start.51 = (f32[128]{0:T(128)}, f32[128]{0:T(128)S(1)}, u32[]{:S(2)}) copy-start(f32[128]{0:T(128)S(1)} %add_rsqrt_fusion) | copy-start | bytes 1540
  466.4 146.2 %copy-start.72 = (f32[128]{0:T(128)S(1)}, f32[128]{0:T(128)}, u32[]{:S(2)}) copy-start(f32[128]{0:T(128)} %compare_convert_fusion) | copy-start | bytes 1540
  647.3 2162.9 %reduce-scatter.7.cloned.1.call-start = ((), (), s32[]{:S(2)}) async-start(), calls=%async_computation.6 | async-start | bytes 165445632
  778.2 15.8 copy-start.43
  778.2 15.8 copy-start.44
  806.5 10.2 copy-start.59
  806.5 13.6 copy-start.57
  816.7 10.3 copy-start.39
  878.4 11.7 copy-start.42
  878.4 18.0 copy-start.25
  878.4 18.0 copy-start.46
  878.4 18.0 copy-start.69
  900.4 8.3 copy-start.17
  900.4 8.3 copy-start.29
  900.5 8.3 copy-start.30
  900.5 8.3 copy-start.31
  900.5 8.3 copy-start.48
  900.5 8.3 copy-start.66
  923.4 21.2 copy-start.14
  944.7 34.2 %copy-start.52 = (f32[2048]{0:T(1024)S(1)}, f32[2048]{0:T(1024)}, u32[]{:S(2)}) copy-start(f32[2048]{0:T(1024)} %get-tuple-element.243) | copy-start | bytes 24580
  944.7 34.2 %copy-start.60 = (f32[2048]{0:T(1024)S(1)}, f32[2048]{0:T(1024)}, u32[]{:S(2)}) copy-start(f32[2048]{0:T(1024)} %get-tuple-element.241) | copy-start | bytes 24580
  944.7 34.2 %copy-start.61 = (f32[2048]{0:T(1024)S(1)}, f32[2048]{0:T(1024)}, u32[]{:S(2)}) copy-start(f32[2048]{0:T(1024)} %get-tuple-element.245) | copy-start | bytes 24580
  2824.2 6.8 copy-start.9
  2824.2 6.8 copy-start.18
  2824.2 6.8 copy-start.40
  2824.2 6.8 copy-start.49
  2824.2 6.8 copy-start.67
  2891.8 7.9 copy-start.6
  2891.8 7.9 copy-start.27
  2891.8 7.9 copy-start.28
  2899.7 11.5 copy-start.12
  2899.7 11.5 copy-start.13
  2899.7 11.5 copy-start.37
  2899.7 11.5 copy-start.38
  (34 other events, 107.7 us)
Sparse Core Ops, SparseCore 0:
  11.5 197.5 all-gather.7
  212.5 253.7 all-gather.9
  469.8 142.7 all-gather.11
  647.4 483.4 reduce-scatter.4
  1480.4 1329.7 reduce-scatter.6
where the time goes:
time: 2950 us; the launch traced here: 2920 us
  waiting for transfers between devices  1760 us (60%)
  local copies, waits for them, and re-layouts  728 us (25%)
  matrix products  194 us (7%)
  blocking collectives  114 us (4%)
  other arithmetic  106 us (4%)
    unnamed x6, waiting for transfers between devices  1310 us
    concatenate x1, local copies, waits for them, and re-layouts, shards(): jnp.concatenate([proj_grad, out_grad, in_grad, gain_columns], axis=1)  347 us
    all_gather x1, waiting for transfers between devices, shards(): lax.all_gather(mlp_in.astype(jnp.bfloat16), ('dp', 'seq'), axis=0, tiled=...  178 us
    unnamed x160, local copies, waits for them, and re-layouts  175 us
    all_gather x1, waiting for transfers between devices, shards(): lax.all_gather(mixer_w.astype(jnp.bfloat16), ('dp', 'seq'), axis=0, tiled...  146 us
    all_gather x1, waiting for transfers between devices, shards(): lax.all_gather(mlp_down.astype(jnp.bfloat16), ('dp', 'seq'), axis=0, tile...  126 us
    slice x49, local copies, waits for them, and re-layouts, shards(): lax.associative_scan(combine_pairs, (next_decay[::-1], d_state[::-1]), ax...  94.4 us
  transfers between devices with their start and end apart: 5, of which 4 were waited for; matrix products, arithmetic and copies ran while one was open for 32% of the time, Pallas kernels for 0%

commit v1 on v0

v1 whole, which is shorter than its diff:
```python
import functools
import math

import jax
import jax.numpy as jnp
from jax import lax
from jax.experimental import pallas as pl
from jax.experimental.pallas import tpu as pltpu
from jax.sharding import Mesh, PartitionSpec as P

STEP = 10


EPS_NORM = 1e-06
BETA_ONE = 0.9
BETA_TWO = 0.999
ADAM_EPS = 1e-08
RATE_MATRIX = 0.03
RATE_GAIN = 0.5
DECAY_WEIGHT = 0.1
CLIP_NORM = 1.0

ALL = ("z", "y", "x", "c")
PLANE = ("y", "x", "c")
LINE = ("z", "c")
QUAD = ("y", "x")
TILE = 8
BF = jnp.bfloat16
F32 = jnp.float32


def gather(value, axes):
    return lax.all_gather(value, axes, axis=0, tiled=True)


def scatter(value, axes):
    return lax.psum_scatter(value, axes, scatter_dimension=0, tiled=True)


def exchange(value, axes):
    return lax.all_to_all(value, axes, 0, 0, tiled=True)


def total_of(value):
    for axis in ("c", "x", "y", "z"):
        count = lax.axis_size(axis)
        hop = 1
        while hop < count:
            value = value + lax.ppermute(value, axis, [(i, i ^ hop) for i in range(count)])
            hop *= 2
    return value


def normalize(value):
    factor = lax.rsqrt(jnp.mean(value * value, axis=-1, keepdims=True) + EPS_NORM)
    return (value * factor, factor)


def norm_back(grad_normed, normed, factor):
    return factor * (grad_normed - normed * jnp.mean(grad_normed * normed, axis=-1, keepdims=True))


def silu(value):
    return value * jax.nn.sigmoid(value)


def silu_grad(value):
    sig = jax.nn.sigmoid(value)
    return sig * (1.0 + value * (1.0 - sig))


def adam_step(weight, first, second, grad, rate, decay_w):
    first_new = BETA_ONE * first + (1.0 - BETA_ONE) * grad
    second_new = BETA_TWO * second + (1.0 - BETA_TWO) * grad * grad
    step_size = (
        first_new
        / (1.0 - BETA_ONE**STEP)
        / (jnp.sqrt(second_new / (1.0 - BETA_TWO**STEP)) + ADAM_EPS)
    )
    return (weight - rate * (step_size + decay_w * weight), first_new, second_new)


def shifted(value, hop, fill, row, later):
    size = value.shape[0]
    moved = pltpu.roll(value, size - hop if later else hop, 0)
    inside = row < size - hop if later else row >= hop
    return jnp.where(inside, moved, fill)


def tile_scan(coeff, value, row, later):
    hop = 1
    while hop < value.shape[0]:
        value = coeff * shifted(value, hop, 0.0, row, later) + value
        coeff = coeff * shifted(coeff, hop, 1.0, row, later)
        hop *= 2
    return coeff, value


def gates(forget_proj, gap, started):
    sig_neg = jax.nn.sigmoid(-forget_proj)
    keep = gap * sig_neg
    return sig_neg, keep, jnp.where(started > 0.0, 0.0, 1.0 - keep)


def scan_forward(proj_ref, started_ref, gap_ref, state_ref):
    rows, width = state_ref.shape
    row = lax.broadcasted_iota(jnp.int32, (TILE, width), 0)
    gap = gap_ref[...]

    def step(index, carry):
        place = pl.ds(pl.multiple_of(index * TILE, TILE), TILE)
        in_proj = proj_ref[place, pl.ds(0, width)]
        forget_proj = proj_ref[place, pl.ds(width, width)]
        _, keep, decay = gates(forget_proj, gap, started_ref[place, :])
        coeff, value = tile_scan(decay, silu(in_proj) * keep, row, False)
        state = value + coeff * carry
        state_ref[place, :] = state
        return state[TILE - 1 :, :]

    lax.fori_loop(0, rows // TILE, step, jnp.zeros((1, width), F32), unroll=4)


def scan_backward(proj_ref, state_ref, d_state_ref, started_ref, gap_ref, d_in_ref, d_forget_ref):
    rows, width = state_ref.shape
    row = lax.broadcasted_iota(jnp.int32, (TILE, width), 0)
    gap = gap_ref[...]
    tiles = rows // TILE

    def step(count, carry):
        index = tiles - 1 - count
        place = pl.ds(pl.multiple_of(index * TILE, TILE), TILE)
        before = pl.ds(pl.multiple_of(jnp.maximum(index - 1, 0) * TILE, TILE), TILE)
        in_proj = proj_ref[place, pl.ds(0, width)]
        forget_proj = proj_ref[place, pl.ds(width, width)]
        started = started_ref[place, :]
        sig_neg, keep, decay = gates(forget_proj, gap, started)
        d_state = d_state_ref[place, :]
        coeff, value = tile_scan(decay, decay * d_state, row, True)
        passed = value + coeff * carry
        moved = jnp.where(row < TILE - 1, pltpu.roll(passed, TILE - 1, 0), carry)
        d_total = d_state + moved
        last = state_ref[before, :][TILE - 1 :, :]
        previous = jnp.where(row >= 1, pltpu.roll(state_ref[place, :], 1, 0), last)
        previous = jnp.where(started > 0.0, 0.0, previous)
        sig = jax.nn.sigmoid(in_proj)
        d_in_ref[place, :] = d_total * keep * (sig * (1.0 + in_proj * (1.0 - sig)))
        d_keep = d_total * (in_proj * sig) - d_total * previous
        d_forget_ref[place, :] = -d_keep * gap * sig_neg * (1.0 - sig_neg)
        return passed[:1, :]

    lax.fori_loop(0, tiles, step, jnp.zeros((1, width), F32), unroll=4)


def run_forward(proj, started, gap):
    rows, width = proj.shape[0], gap.shape[1]
    return pl.pallas_call(
        scan_forward,
        out_shape=jax.ShapeDtypeStruct((rows, width), F32),
        compiler_params=pltpu.CompilerParams(vmem_limit_bytes=48 * 2**20),
    )(proj, started, gap)


def run_backward(proj, state, d_state, started, gap):
    rows, width = state.shape
    return pl.pallas_call(
        scan_backward,
        out_shape=[jax.ShapeDtypeStruct((rows, width), F32)] * 2,
        compiler_params=pltpu.CompilerParams(vmem_limit_bytes=48 * 2**20),
    )(proj, state, d_state, started, gap)


def shards(
    tokens,
    cotangent,
    lengths,
    lower_bound,
    mixer_w,
    mlp_in,
    mlp_down,
    gains,
    mixer_m,
    mixer_v,
    in_m,
    in_v,
    down_m,
    down_v,
    gain_m,
    gain_v,
):
    rows, width = tokens.shape
    own, _, hidden_width = mlp_in.shape
    down_rows = mlp_down.shape[0]
    planes = lax.axis_size("z")
    spots = lax.axis_size(PLANE)
    quads = lax.axis_size(QUAD)
    pairs = lax.axis_size("c")
    group = spots * rows
    spot = lax.axis_index(PLANE)
    chans = planes * own

    low_mixer = mixer_w.astype(BF)
    sent = low_mixer[:, :3, :].reshape(own, 3, planes, spots, own).transpose(3, 0, 1, 2, 4)
    part = exchange(sent.reshape(spots, own, 3 * chans), PLANE)
    w_proj = gather(part.reshape(spots * own, 3 * chans), "z")
    w_out = gather(low_mixer[:, 3, :], "z")
    low_in = mlp_in.astype(BF)
    sent = low_in.reshape(own, 2, planes, quads, pairs, down_rows).transpose(2, 4, 0, 1, 3, 5)
    inner = quads * down_rows
    part = exchange(sent.reshape(planes * pairs, own, 2 * inner), LINE)
    w_in = gather(part.reshape(planes * pairs * own, 2 * inner), QUAD)
    w_down = gather(mlp_down.astype(BF), QUAD)

    full_gains = gather(gather(gains.T, PLANE), "z").T
    bound = lower_bound.reshape(planes, spots, own)
    gap = (1.0 - lax.dynamic_index_in_dim(bound, spot, 1, False)).reshape(1, chans)
    gain_mid = full_gains[1].reshape(planes, spots, own)
    gain_mid = lax.dynamic_index_in_dim(gain_mid, spot, 1, False).reshape(1, chans)

    ends = jnp.cumsum(lengths)
    starts = ends - lengths
    places = jnp.arange(group, dtype=jnp.int32)
    started = jnp.any(places[:, None] == starts[None, :], axis=-1, keepdims=True).astype(F32)
    home = spot * rows + jnp.arange(rows, dtype=jnp.int32)
    valid = (home < ends[-1]).astype(F32)

    def swapped(value, first, second):
        return value.reshape(rows, first, second, -1).swapaxes(1, 2).reshape(rows, width)

    x = tokens.astype(F32)
    x_normed, x_factor = normalize(x)
    n1 = gather((x_normed * full_gains[0]).astype(BF), PLANE)
    cot = cotangent.astype(F32) * valid[:, None]
    cot_all = gather(cot.astype(BF), LINE)
    proj = jnp.dot(n1, w_proj, preferred_element_type=F32)
    state = run_forward(proj[:, : 2 * chans], started, gap)
    gate_proj = proj[:, 2 * chans :]
    gate_act = silu(gate_proj)
    raw = (state * gain_mid * gate_act).astype(BF)
    squares = lax.psum(jnp.sum(state * state, axis=-1), PLANE)
    state_factor = lax.rsqrt(squares / width + EPS_NORM)
    mix_raw = scatter(jnp.dot(raw, w_out, preferred_element_type=F32).astype(BF), PLANE)
    home_factor = lax.dynamic_slice_in_dim(state_factor, spot * rows, rows)
    mix = mix_raw.astype(F32) * home_factor[:, None]
    after_mix = x + mix

    mid_normed, mid_factor = normalize(after_mix)
    n2 = gather(swapped((mid_normed * full_gains[2]).astype(BF), planes, quads), LINE)
    gate_up = jnp.dot(n2, w_in, preferred_element_type=F32)
    gate, up_value = gate_up[:, :inner], gate_up[:, inner:]
    silu_gate = silu(gate)
    hidden = (silu_gate * up_value).astype(BF)
    down = scatter(jnp.dot(hidden, w_down, preferred_element_type=F32).astype(BF), LINE)
    block_out = (after_mix + down.astype(F32)).astype(BF)

    grad_down = lax.dot_general(hidden, cot_all, (((0,), (0,)), ((), ())), preferred_element_type=F32)
    shard_down = scatter(grad_down.astype(BF), QUAD).astype(F32)
    d_hidden = lax.dot_general(cot_all, w_down, (((1,), (1,)), ((), ())), preferred_element_type=F32)
    d_gate = d_hidden * up_value * silu_grad(gate)
    d_up = d_hidden * silu_gate
    d_gate_up = jnp.concatenate([d_gate.astype(BF), d_up.astype(BF)], axis=1)
    d_n2 = lax.dot_general(d_gate_up, w_in, (((1,), (1,)), ((), ())), preferred_element_type=F32)
    d_n2 = swapped(scatter(d_n2.astype(BF), LINE), quads, planes).astype(F32)
    grad_in = lax.dot_general(n2, d_gate_up, (((0,), (0,)), ((), ())), preferred_element_type=F32)
    shard_in = scatter(grad_in.astype(BF), QUAD)
    shard_in = exchange(shard_in.reshape(planes * pairs, own, 2 * inner), LINE)
    shard_in = shard_in.reshape(planes, pairs, own, 2, quads, down_rows).transpose(2, 3, 0, 4, 1, 5)
    shard_in = shard_in.reshape(own, 2, hidden_width).astype(F32)
    d_mid = cot + norm_back(d_n2 * full_gains[2], mid_normed, mid_factor)

    d_mix_home = d_mid.astype(BF)
    d_mix = gather(d_mix_home, PLANE)
    mean = gather(jnp.sum(d_mix_home.astype(F32) * mix, axis=-1) / width, PLANE)
    d_mixed = lax.dot_general(d_mix, w_out, (((1,), (1,)), ((), ())), preferred_element_type=F32)
    factor = state_factor[:, None]
    state_normed = state * factor
    mixed_in = (state_normed * gain_mid * gate_act).astype(BF)
    grad_out = lax.dot_general(mixed_in, d_mix, (((0,), (0,)), ((), ())), preferred_element_type=F32)
    shard_out = scatter(grad_out.astype(BF), "z").astype(F32)
    d_gate_proj = d_mixed * state_normed * gain_mid * silu_grad(gate_proj)
    d_state = factor * (d_mixed * gain_mid * gate_act - state_normed * mean[:, None])
    d_in_proj, d_forget_proj = run_backward(proj[:, : 2 * chans], state, d_state, started, gap)
    d_proj = jnp.concatenate(
        [d_in_proj.astype(BF), d_forget_proj.astype(BF), d_gate_proj.astype(BF)], axis=1
    )
    grad_proj = lax.dot_general(n1, d_proj, (((0,), (0,)), ((), ())), preferred_element_type=F32)
    shard_proj = scatter(grad_proj.astype(BF), "z")
    shard_proj = exchange(shard_proj.reshape(spots, own, 3 * chans), PLANE)
    shard_proj = shard_proj.reshape(spots, own, 3, planes, own).transpose(1, 2, 3, 0, 4)
    shard_proj = shard_proj.reshape(own, 3, width).astype(F32)
    d_n1 = lax.dot_general(d_proj, w_proj, (((1,), (1,)), ((), ())), preferred_element_type=F32)
    d_n1 = scatter(d_n1.astype(BF), PLANE).astype(F32)
    input_grad = d_mid + norm_back(d_n1 * full_gains[0], x_normed, x_factor)

    low_rows = low_mixer.astype(F32)
    shard_gains = jnp.stack(
        [
            jnp.sum(shard_proj * low_rows[:, :3, :], axis=(1, 2)),
            jnp.sum(shard_out * low_rows[:, 3, :], axis=1),
            jnp.sum(shard_in * low_in.astype(F32), axis=(1, 2)),
        ],
        axis=0,
    ) / gains
    shard_mixer = jnp.concatenate([shard_proj, shard_out[:, None, :]], axis=1)

    local_total = (
        jnp.sum(shard_mixer * shard_mixer)
        + jnp.sum(shard_in * shard_in)
        + jnp.sum(shard_down * shard_down)
        + jnp.sum(shard_gains * shard_gains)
    )
    grad_norm = jnp.sqrt(total_of(local_total.reshape(1, 1))[0, 0])
    clip = jnp.minimum(1.0, CLIP_NORM / (grad_norm + 1e-06))
    new_mixer, new_mixer_m, new_mixer_v = adam_step(
        mixer_w, mixer_m, mixer_v, clip * shard_mixer, RATE_MATRIX, DECAY_WEIGHT
    )
    new_in, new_in_m, new_in_v = adam_step(
        mlp_in, in_m, in_v, clip * shard_in, RATE_MATRIX, DECAY_WEIGHT
    )
    new_down, new_down_m, new_down_v = adam_step(
        mlp_down, down_m, down_v, clip * shard_down, RATE_MATRIX, DECAY_WEIGHT
    )
    new_gains, new_gain_m, new_gain_v = adam_step(
        gains, gain_m, gain_v, clip * shard_gains, RATE_GAIN, 0.0
    )
    return (
        block_out,
        input_grad,
        grad_norm,
        new_mixer,
        new_mixer_m,
        new_mixer_v,
        new_in,
        new_in_m,
        new_in_v,
        new_down,
        new_down_m,
        new_down_v,
        new_gains,
        new_gain_m,
        new_gain_v,
    )


def solution(mesh):
    planes, spots = mesh.shape["dp"], mesh.shape["seq"]
    side = math.isqrt(spots // 2)
    split = Mesh(mesh.devices.reshape(planes, spots // (2 * side), side, 2), ALL)
    rows2, rows3, cols = P(ALL, None), P(ALL, None, None), P(None, ALL)
    return jax.shard_map(
        shards,
        mesh=split,
        in_specs=(rows2, rows2, P("z"), P(), rows3, rows3, rows2, cols)
        + (rows3,) * 4
        + (rows2,) * 2
        + (cols,) * 2,
        out_specs=(rows2, rows2, P()) + (rows3,) * 6 + (rows2,) * 3 + (cols,) * 3,
        check_vma=False,
    )
```

time: 2950 us -> 926 us (0.31)
  waiting for transfers between devices: 1760 us -> 526 us
  local copies, waits for them, and re-layouts: 728 us -> 84.3 us
  matrix products: 194 us -> 88.9 us
  other arithmetic: 106 us -> 62.5 us
    unnamed x6 -> x16, waiting for transfers between devices: 1310 us -> 0.27 us
    concatenate x3 -> x0, local copies, waits for them, and re-layouts: 349 us -> none  [the longest x1 347 us: shards(): jnp.concatenate([proj_grad, out_grad, in_grad, gain_columns], axis=1)]
    reduce_scatter x1 -> x8, waiting for transfers between devices: 0.01 us -> 236 us  [scatter(): return lax.psum_scatter(value, axes, scatter_dimension=0, tiled=True)]
    all_gather x3 -> x8, waiting for transfers between devices: 450 us -> 287 us  [gather(): return lax.all_gather(value, axes, axis=0, tiled=True)]
    unnamed x160 -> x66, local copies, waits for them, and re-layouts: 175 us -> 14.7 us
    slice x101 -> x5, local copies, waits for them, and re-layouts: 110 us -> 2.65 us  [the longest x1 1.68 us: shards(): w_out = gather(low_mixer[:, 3, :], 'z')]
    dot_general x12, matrix products: 194 us -> 88.9 us  [the longest x1 11.8 us: shards(): gate_up = jnp.dot(n2, w_in, preferred_element_type=F32)]
    all_to_all x0 -> x2, blocking collectives: none -> 55.9 us  [exchange(): return lax.all_to_all(value, axes, 0, 0, tiled=True)]
  transfers between devices with their start and end apart: 5 -> 23, of which waited for: 4 -> 19; matrix products, arithmetic and copies ran while one was open for 32% -> 16% of each run, Pallas kernels for 0% -> 1%
where the time goes in v1:
time: 926 us; the launch traced here: 918 us
  waiting for transfers between devices  526 us (57%)
  blocking collectives  99.7 us (11%)
  matrix products  88.9 us (10%)
  local copies, waits for them, and re-layouts  84.3 us (9%)
  other arithmetic  62.5 us (7%)
  starting transfers between devices  24.2 us (3%)
  between operations  23.5 us (3%)
    all_gather x8, waiting for transfers between devices, gather(): return lax.all_gather(value, axes, axis=0, tiled=True)  287 us
    reduce_scatter x8, waiting for transfers between devices, scatter(): return lax.psum_scatter(value, axes, scatter_dimension=0, tiled=True)  236 us
    all_to_all x2, blocking collectives, exchange(): return lax.all_to_all(value, axes, 0, 0, tiled=True)  55.9 us
    all_gather x3, blocking collectives, gather(): return lax.all_gather(value, axes, axis=0, tiled=True)  30.1 us
    convert_element_type x3, local copies, waits for them, and re-layouts, shards(): shard_in = shard_in.reshape(own, 2, hidden_width).astype(F32)  24.5 us
    sub x4, other arithmetic, adam_step(): weight - rate * (step_size + decay_w * weight)  22.1 us
  transfers between devices with their start and end apart: 23, of which 19 were waited for; matrix products, arithmetic and copies ran while one was open for 16% of the time, Pallas kernels for 1%

profile of v1, /device:TPU:0, one launch (start us, length us, event | category | flops | bytes accessed | tf_op | source)
XLA Modules:
  0.0 918.4 jit_solution(17988862480769245983)
XLA Ops:
  8.1 4.2 fusion.40
  16.5 17.6 %all_to_all.20 = bf16[8,64,768]{2,1,0:T(8,128)(2,1)} all-to-all(bf16[8,64,768]{2,1,0:T(8,128)(2,1)S(1)} %reshape.156), channel_id=1, replica_groups=mesh['z'=4,'y'=2,'x'=2,'c'=2] {'y','x','c'}, dimensions={0} | all-to-all | bytes 1572864 | tf_op jit(solution)/shard_map/all_to_all | solution.py:41
  34.3 8.0 all-gather.1
  42.3 13.5 %all_gather.34 = f32[2048,3]{0,1:T(4,128)S(1)} all-gather(f32[512,3]{0,1:T(4,128)S(1)} %reshape.178), channel_id=1, replica_groups=mesh['z'=4,'y'=2,'x'=2,'c'=2] {'z'}, dimensions={0}, use_global_device_ids=true | all-gather | bytes 30720 | tf_op jit(solution)/shard_map/all_gather | solution.py:33
  60.5 37.2 %all-gather.14.cloned.1.call-done = bf16[2048,768]{1,0:T(8,128)(2,1)} async-done(((bf16[512,768]{1,0:T(8,128)(2,1)}), bf16[2048,768]{1,0:T(8,128)(2,1)}) %all-gather.14.cloned.1.call-update) | async-done | bytes 3145744 | tf_op jit(solution)/shard_map/all_gather | solution.py:33
  97.7 37.8 %all-gather.12.cloned.1.call-done = bf16[1024,2048]{1,0:T(8,128)(2,1)} async-done(((bf16[128,2048]{1,0:T(8,128)(2,1)}), bf16[1024,2048]{1,0:T(8,128)(2,1)}) %all-gather.12.cloned.1.call-update) | async-done | bytes 4194320 | tf_op jit(solution)/shard_map/all_gather | solution.py:33
  135.5 6.1 fusion.42
  147.6 18.0 %all-gather.26.cloned.1.call-done = bf16[256,1,2048]{2,0,1:T(8,128)(2,1)} async-done(((bf16[64,1,2048]{2,0,1:T(8,128)(2,1)}), bf16[256,1,2048]{2,0,1:T(8,128)(2,1)}) %all-gather.26.cloned.1.call-update) | async-done | bytes 1048592 | tf_op jit(solution)/shard_map/all_gather | solution.py:33
  165.6 4.9 convolution_convert_fusion.3
  170.9 3.9 convert_element_type.164
  174.8 9.0 reshape.163
  185.9 4.6 reshape.164
  190.5 38.3 %all_to_all.21 = bf16[8,64,1408]{2,1,0:T(8,128)(2,1)} all-to-all(bf16[8,64,1408]{2,1,0:T(8,128)(2,1)S(1)} %reshape.164), channel_id=1, replica_groups=mesh['z'=4,'y'=2,'x'=2,'c'=2] {'z','c'}, dimensions={0} | all-to-all | bytes 2883584 | tf_op jit(solution)/shard_map/all_to_all | solution.py:41
  229.1 13.6 %psum.7 = f32[1024]{0:T(1024)S(1)} all-reduce(f32[1024]{0:T(1024)S(1)} %multiply_reduce_fusion.6), channel_id=1, replica_groups=mesh['z'=4,'y'=2,'x'=2,'c'=2] {'y','x','c'}, use_global_device_ids=true, to_apply=%region_5.6 | all-reduce | flops 1024 | bytes 8192 | tf_op jit(solution)/shard_map/psum | solution.py:239
  255.8 37.4 %all-gather.18.cloned.1.call-done = bf16[2048,1408]{1,0:T(8,128)(2,1)} async-done(((bf16[512,1408]{1,0:T(8,128)(2,1)}), bf16[2048,1408]{1,0:T(8,128)(2,1)}) %all-gather.18.cloned.1.call-update) | async-done | bytes 5767184 | tf_op jit(solution)/shard_map/all_gather | solution.py:33
  293.2 49.8 %all-gather.16.cloned.1.call-done = bf16[1024,2048]{0,1:T(8,128)(2,1)} async-done(((bf16[128,2048]{0,1:T(8,128)(2,1)}), bf16[1024,2048]{0,1:T(8,128)(2,1)}) %all-gather.16.cloned.1.call-update) | async-done | bytes 4194320 | tf_op jit(solution)/shard_map/all_gather | solution.py:33
  343.0 11.8 %fusion.43 = f32[1024,1408]{1,0:T(8,128)} fusion(bf16[1024,2048]{0,1:T(8,128)(2,1)} %all-gather.16.cloned.1.call-done, bf16[2048,1408]{1,0:T(8,128)(2,1)} %all-gather.18.cloned.1.call-done), kind=kOutput, calls=%fused_computation.109 | convolution fusion | flops 5905580032 | bytes 15728640 | tf_op jit(solution)/shard_map/dot_general | solution.py:248
  354.9 30.5 %all-gather.20.cloned.1.call-done = bf16[704,2048]{1,0:T(8,128)(2,1)} async-done(((bf16[176,2048]{1,0:T(8,128)(2,1)}), bf16[704,2048]{1,0:T(8,128)(2,1)}) %all-gather.20.cloned.1.call-update) | async-done | bytes 2883600 | tf_op jit(solution)/shard_map/all_gather | solution.py:33
  385.4 49.1 %all-gather.22.cloned.1.call-done = bf16[1024,2048]{1,0:T(8,128)(2,1)} async-done(((bf16[128,2048]{1,0:T(8,128)(2,1)}), bf16[1024,2048]{1,0:T(8,128)(2,1)}) %all-gather.22.cloned.1.call-update) | async-done | bytes 4194320 | tf_op jit(solution)/shard_map/all_gather | solution.py:33
  434.5 9.0 multiply_convert_fusion.1
  445.2 11.0 %convolution_convert_fusion.1 = bf16[1024,2048]{1,0:T(8,128)(2,1)} fusion(bf16[2048,1408]{1,0:T(8,128)(2,1)} %all-gather.18.cloned.1.call-done, bf16[1024,704]{1,0:T(8,128)(2,1)S(1)} %get-tuple-element.99, bf16[1024,704]{1,0:T(8,128)(2,1)S(1)} %get-tuple-element.98), kind=kOutput, calls=%fused_computation.3 | convolution fusion | flops 5913444352 | bytes 12845056 | tf_op jit(solution)/shard_map/dot_general | solution.py:261
  456.3 6.8 convolution_convert_fusion.2
  463.3 41.6 %reduce-scatter.13.cloned.1.call-done = bf16[128,2048]{1,0:T(8,128)(2,1)} async-done(((bf16[1024,2048]{1,0:T(8,128)(2,1)}), bf16[128,2048]{1,0:T(8,128)(2,1)}) %reduce-scatter.13.cloned.1.call-update) | async-done | bytes 524304 | tf_op jit(solution)/shard_map/reduce_scatter | solution.py:37
  510.2 45.2 %reduce-scatter.11.cloned.1.call-done = bf16[128,2048]{1,0:T(8,128)(2,1)} async-done(((bf16[1024,2048]{1,0:T(8,128)(2,1)}), bf16[128,2048]{1,0:T(8,128)(2,1)}) %reduce-scatter.11.cloned.1.call-update) | async-done | bytes 524304 | tf_op jit(solution)/shard_map/reduce_scatter | solution.py:37
  558.6 11.2 %convolution_convert_fusion = bf16[2048,1408]{1,0:T(8,128)(2,1)} fusion(bf16[1024,2048]{0,1:T(8,128)(2,1)} %all-gather.16.cloned.1.call-done, bf16[1024,704]{1,0:T(8,128)(2,1)} %copy-done.30, bf16[1024,704]{1,0:T(8,128)(2,1)} %copy-done.29), kind=kOutput, calls=%fused_computation | convolution fusion | flops 5914230784 | bytes 12845056 | tf_op jit(solution)/shard_map/dot_general | solution.py:263
  571.2 7.0 convolution_convert_fusion.6
  578.2 27.2 %all-gather.24.cloned.1.call-done = bf16[1024,2048]{1,0:T(8,128)(2,1)} async-done(((bf16[128,2048]{1,0:T(8,128)(2,1)}), bf16[1024,2048]{1,0:T(8,128)(2,1)}) %all-gather.24.cloned.1.call-update) | async-done | bytes 4194320 | tf_op jit(solution)/shard_map/all_gather | solution.py:33
  605.4 4.9 convolution_convert_fusion.7
  610.4 8.7 all-gather.2
  619.1 4.3 subtract_multiply_fusion
  623.4 5.7 shard_map.272
  629.3 4.9 convolution_convert_fusion.5
  634.3 7.0 convolution_convert_fusion.4
  641.3 3.8 reduce-scatter.21.cloned.1.call-done
  645.1 4.8 all-to-all-start.3
  649.9 40.6 %reduce-scatter.23.cloned.1.call-done = bf16[176,2048]{1,0:T(8,128)(2,1)} async-done(((bf16[704,2048]{1,0:T(8,128)(2,1)}), bf16[176,2048]{1,0:T(8,128)(2,1)}) %reduce-scatter.23.cloned.1.call-update) | async-done | bytes 720912 | tf_op jit(solution)/shard_map/reduce_scatter | solution.py:37
  692.6 7.5 reshape.175
  700.1 7.5 copy.137
  707.6 9.5 %reshape.172 = f32[64,2,5632]{2,1,0:T(2,128)} reshape(f32[64,2,4,4,2,176]{5,4,3,2,1,0:T(2,128)} %bitcast.78) | data formatting | bytes 5767168 | tf_op jit(solution)/shard_map/convert_element_type | solution.py:267
  719.8 3.7 multiply_reduce_fusion
  726.6 55.0 %reduce-scatter.17.cloned.1.call-done = bf16[512,768]{1,0:T(8,128)(2,1)} async-done(((bf16[2048,768]{1,0:T(8,128)(2,1)}), bf16[512,768]{1,0:T(8,128)(2,1)}) %reduce-scatter.17.cloned.1.call-update) | async-done | bytes 786448 | tf_op jit(solution)/shard_map/reduce_scatter | solution.py:37
  781.7 4.6 all-to-all-start.2
  786.3 49.7 %reduce-scatter.15.cloned.1.call-done = bf16[128,2048]{1,0:T(8,128)(2,1)} async-done(((bf16[1024,2048]{1,0:T(8,128)(2,1)}), bf16[128,2048]{1,0:T(8,128)(2,1)}) %reduce-scatter.15.cloned.1.call-update) | async-done | bytes 524304 | tf_op jit(solution)/shard_map/reduce_scatter | solution.py:37
  843.8 5.4 copy.138
  849.2 3.8 reshape.171
  874.3 3.8 collective-permute-start.4
  879.6 7.5 multiply_subtract_fusion.1
  895.2 11.1 %multiply_subtract_fusion = (f32[64,2,5632]{2,1,0:T(2,128)}, f32[64,2,5632]{2,1,0:T(2,128)}, f32[64,2,5632]{2,1,0:T(2,128)}) fusion(f32[64,2,5632]{2,1,0:T(2,128)S(1)} %copy-done.5, f32[64,2,5632]{2,1,0:T(2,128)S(1)} %copy-done.6, f32[]{:T(128)S(6)} %min.3, f32[64,2,5632]{2,1,0:T(2,128)S(1)} %copy-done.15, f32[64,2,5632]{2,1,0:T(2,128)S(1)} %copy-done.16), kind=kLoop, calls=%fused_computation.18 | loop fusion | flops 11534336 | bytes 20185092 | tf_op jit(solution)/shard_map/sub | solution.py:80
  (169 shorter events, 86.7 us)
Async XLA Ops:
  8.0 89.7 %all-gather.14.cloned.1.call-start = ((), (), s32[]{:S(2)}) async-start(), calls=%async_computation.13 | async-start | bytes 3932160 | tf_op jit(solution)/shard_map/all_gather | solution.py:33
  15.5 18.7 %copy-start.20 = (f32[3,64]{1,0:T(4,128)S(1)}, f32[3,64]{1,0:T(4,128)}, u32[]{:S(2)}) copy-start(f32[3,64]{1,0:T(4,128)} %param.23) | copy-start | bytes 2308
  15.5 40.2 %copy-start.3 = (bf16[128,2048]{1,0:T(8,128)(2,1)S(1)}, bf16[128,2048]{1,0:T(8,128)(2,1)}, u32[]{:S(2)}) copy-start(bf16[128,2048]{1,0:T(8,128)(2,1)} %param.16) | copy-start | bytes 1572868
  16.5 42.3 %copy-start.26 = (s32[2]{0:T(128)S(1)}, s32[2]{0:T(128)}, u32[]{:S(2)}) copy-start(s32[2]{0:T(128)} %param.18) | copy-start | bytes 28
  16.5 42.6 %copy-start.21 = (f32[2048]{0:T(1024)S(1)}, f32[2048]{0:T(1024)}, u32[]{:S(2)}) copy-start(f32[2048]{0:T(1024)} %param.19) | copy-start | bytes 24580
  34.2 101.3 %all-gather.12.cloned.1.call-start = ((), (), s32[]{:S(2)}) async-start(), calls=%async_computation.12 | async-start | bytes 4718592 | tf_op jit(solution)/shard_map/all_gather | solution.py:33
  57.0 108.6 %all-gather.26.cloned.1.call-start = ((), (), s32[]{:S(2)}) async-start(), calls=%async_computation.27 | async-start | bytes 1310720 | tf_op jit(solution)/shard_map/all_gather | solution.py:33
  58.7 184.1 %reduce-scatter.9.cloned.1.call-start = ((), (), s32[]{:S(2)}) async-start(), calls=%async_computation.14 | async-start | bytes 4718592 | tf_op jit(solution)/shard_map/reduce_scatter | solution.py:37
  144.4 26.1 %copy-start = (f32[1024,512]{1,0:T(8,128)}, f32[1024,512]{1,0:T(8,128)S(1)}, u32[]{:S(2)}) copy-start(f32[1024,512]{1,0:T(8,128)S(1)} %slice.54.proj_ref) | copy-start | bytes 6291460
  170.5 122.7 %all-gather.18.cloned.1.call-start = ((), (), s32[]{:S(2)}) async-start(), calls=%async_computation.16 | async-start | bytes 7208960 | tf_op jit(solution)/shard_map/all_gather | solution.py:33
  190.5 52.3 %copy-start.4 = (bf16[128,2048]{1,0:T(8,128)(2,1)S(1)}, bf16[128,2048]{1,0:T(8,128)(2,1)}, u32[]{:S(2)}) copy-start(bf16[128,2048]{1,0:T(8,128)(2,1)} %param.16) | copy-start | bytes 1572868
  228.8 114.2 %all-gather.16.cloned.1.call-start = ((), (), s32[]{:S(2)}) async-start(), calls=%async_computation.15 | async-start | bytes 4718592 | tf_op jit(solution)/shard_map/all_gather | solution.py:33
  229.1 21.9 %copy-start.10 = (f32[176,2048]{1,0:T(8,128)S(1)}, f32[176,2048]{1,0:T(8,128)}, u32[]{:S(2)}) copy-start(f32[176,2048]{1,0:T(8,128)} %param.22) | copy-start | bytes 4325380
  250.9 134.5 %all-gather.20.cloned.1.call-start = ((), (), s32[]{:S(2)}) async-start(), calls=%async_computation.17 | async-start | bytes 3604480 | tf_op jit(solution)/shard_map/all_gather | solution.py:33
  251.9 182.5 %all-gather.22.cloned.1.call-start = ((), (), s32[]{:S(2)}) async-start(), calls=%async_computation.19 | async-start | bytes 4718592 | tf_op jit(solution)/shard_map/all_gather | solution.py:33
  255.2 249.7 %reduce-scatter.13.cloned.1.call-start = ((), (), s32[]{:S(2)}) async-start(), calls=%async_computation.20 | async-start | bytes 4718592 | tf_op jit(solution)/shard_map/reduce_scatter | solution.py:37
  443.5 12.7 %copy-start.27 = (bf16[1024,704]{1,0:T(8,128)(2,1)}, bf16[1024,704]{1,0:T(8,128)(2,1)S(1)}, u32[]{:S(2)}) copy-start(bf16[1024,704]{1,0:T(8,128)(2,1)S(1)} %get-tuple-element.100) | copy-start | bytes 4325380
  456.2 99.1 %reduce-scatter.11.cloned.1.call-start = ((), (), s32[]{:S(2)}) async-start(), calls=%async_computation.18 | async-start | bytes 4718592 | tf_op jit(solution)/shard_map/reduce_scatter | solution.py:37
  463.0 46.7 %copy-start.9 = (bf16[128,2048]{1,0:T(8,128)(2,1)S(1)}, bf16[128,2048]{1,0:T(8,128)(2,1)}, u32[]{:S(2)}) copy-start(bf16[128,2048]{1,0:T(8,128)(2,1)} %reduce-scatter.9.cloned.1.call-done) | copy-start | bytes 1572868
  463.1 142.3 %all-gather.24.cloned.1.call-start = ((), (), s32[]{:S(2)}) async-start(), calls=%async_computation.21 | async-start | bytes 4718592 | tf_op jit(solution)/shard_map/all_gather | solution.py:33
  558.5 86.6 %reduce-scatter.21.cloned.1.call-start = ((), (), s32[]{:S(2)}) async-start(), calls=%async_computation.25 | async-start | bytes 7208960 | tf_op jit(solution)/shard_map/reduce_scatter | solution.py:37
  569.8 120.7 %reduce-scatter.23.cloned.1.call-start = ((), (), s32[]{:S(2)}) async-start(), calls=%async_computation.26 | async-start | bytes 3604480 | tf_op jit(solution)/shard_map/reduce_scatter | solution.py:37
  578.2 40.9 %copy-start.25 = (bf16[256,1,2048]{2,0,1:T(8,128)(2,1)S(1)}, bf16[256,1,2048]{2,0,1:T(8,128)(2,1)}, u32[]{:S(2)}) copy-start(bf16[256,1,2048]{2,0,1:T(8,128)(2,1)} %all-gather.26.cloned.1.call-done) | copy-start | bytes 3145732
  578.2 145.4 %reduce-scatter.19.cloned.1.call-start = ((), (), s32[]{:S(2)}) async-start(), calls=%async_computation.24 | async-start | bytes 1310720 | tf_op jit(solution)/shard_map/reduce_scatter | solution.py:37
  610.3 171.4 %reduce-scatter.17.cloned.1.call-start = ((), (), s32[]{:S(2)}) async-start(), calls=%async_computation.23 | async-start | bytes 3932160 | tf_op jit(solution)/shard_map/reduce_scatter | solution.py:37
  619.1 4.3 copy-start.2
  623.4 5.8 copy-start.24
  634.2 201.8 %reduce-scatter.15.cloned.1.call-start = ((), (), s32[]{:S(2)}) async-start(), calls=%async_computation.22 | async-start | bytes 4718592 | tf_op jit(solution)/shard_map/reduce_scatter | solution.py:37
  645.1 47.5 %all-to-all-start.3 = ((bf16[8,64,1408]{2,1,0:T(8,128)(2,1)}), bf16[8,64,1408]{2,1,0:T(8,128)(2,1)S(1)}, u32[]{:S(2)}, u32[]{:S(2)}) async-start(bf16[8,64,1408]{2,1,0:T(8,128)(2,1)} %bitcast.86), calls=%async_computation.10 | async-start | bytes 2883584 | tf_op jit(solution)/shard_map/all_to_all | solution.py:41
  692.6 15.0 %copy-start.8 = (bf16[8,64,1408]{2,1,0:T(8,128)(2,1)}, bf16[8,64,1408]{2,1,0:T(8,128)(2,1)S(1)}, u32[]{:S(2)}) copy-start(bf16[8,64,1408]{2,1,0:T(8,128)(2,1)S(1)} %all-to-all-done.3) | copy-start | bytes 4325380
  707.6 12.2 %copy-start.5 = (f32[64,2,5632]{2,1,0:T(2,128)S(1)}, f32[64,2,5632]{2,1,0:T(2,128)}, u32[]{:S(2)}) copy-start(f32[64,2,5632]{2,1,0:T(2,128)} %param.21) | copy-start | bytes 8650756
  781.7 58.5 %all-to-all-start.2 = ((bf16[8,64,768]{2,1,0:T(8,128)(2,1)}), bf16[8,64,768]{2,1,0:T(8,128)(2,1)}, u32[]{:S(2)}, u32[]{:S(2)}) async-start(bf16[8,64,768]{2,1,0:T(8,128)(2,1)} %bitcast.87), calls=%async_computation.7 | async-start | bytes 1572864 | tf_op jit(solution)/shard_map/all_to_all | solution.py:41
  849.2 6.1 copy-start.12
  853.0 2.4 copy-start.7
  859.7 1.2 collective-permute-start
  861.6 3.6 collective-permute-start.1
  865.8 3.6 collective-permute-start.2
  870.1 3.6 collective-permute-start.3
  874.3 4.5 collective-permute-start.4
  887.1 8.0 copy-start.16
  889.8 5.3 copy-start.15
  892.5 2.7 copy-start.6
  895.1 11.2 %copy-start.22 = (f32[3,64]{1,0:T(4,128)S(1)}, f32[3,64]{1,0:T(4,128)}, u32[]{:S(2)}) copy-start(f32[3,64]{1,0:T(4,128)} %param.30) | copy-start | bytes 2308
  895.1 11.2 %copy-start.23 = (f32[3,64]{1,0:T(4,128)S(1)}, f32[3,64]{1,0:T(4,128)}, u32[]{:S(2)}) copy-start(f32[3,64]{1,0:T(4,128)} %param.31) | copy-start | bytes 2308
  895.2 11.8 %copy-start.11 = (f32[176,2048]{1,0:T(8,128)S(1)}, f32[176,2048]{1,0:T(8,128)}, u32[]{:S(2)}) copy-start(f32[176,2048]{1,0:T(8,128)} %param.22) | copy-start | bytes 4325380
  895.2 11.7 %copy-start.14 = (bf16[176,2048]{1,0:T(8,128)(2,1)S(1)}, bf16[176,2048]{1,0:T(8,128)(2,1)}, u32[]{:S(2)}) copy-start(bf16[176,2048]{1,0:T(8,128)(2,1)} %reduce-scatter.23.cloned.1.call-done) | copy-start | bytes 2162692
  895.2 11.7 %copy-start.17 = (f32[176,2048]{1,0:T(8,128)S(1)}, f32[176,2048]{1,0:T(8,128)}, u32[]{:S(2)}) copy-start(f32[176,2048]{1,0:T(8,128)} %param.28) | copy-start | bytes 4325380
  895.2 11.7 %copy-start.18 = (f32[176,2048]{1,0:T(8,128)S(1)}, f32[176,2048]{1,0:T(8,128)}, u32[]{:S(2)}) copy-start(f32[176,2048]{1,0:T(8,128)} %param.29) | copy-start | bytes 4325380
  (6 other events, 8.0 us)
Sparse Core Ops, SparseCore 0:
  34.3 63.3 all-gather.13
  100.1 35.3 all-gather.11
  137.6 27.9 all-gather.25
  170.6 50.8 reduce-scatter.8
  558.6 46.7 all-gather.23
Sparse Core Ops, SparseCore 1:
  228.9 64.3 all-gather.17
  295.4 47.6 all-gather.15
  345.5 39.8 all-gather.19
  387.7 46.7 all-gather.21
  456.3 48.6 reduce-scatter.12
  507.3 47.9 reduce-scatter.10
  569.9 75.1 reduce-scatter.20
  648.8 41.6 reduce-scatter.22
  693.3 27.1 reduce-scatter.18
  722.8 58.8 reduce-scatter.16
  784.9 51.1 reduce-scatter.14

commit v2 on v1

--- a/solution.py
+++ b/solution.py
@@ -5,6 +5,7 @@
 import jax.numpy as jnp
 from jax import lax
 from jax.experimental import pallas as pl
+from jax.experimental.layout import Layout, with_layout_constraint
 from jax.experimental.pallas import tpu as pltpu
 from jax.sharding import Mesh, PartitionSpec as P
 
@@ -41,6 +42,124 @@
     return lax.all_to_all(value, axes, 0, 0, tiled=True)
 
 
+def ring_gather(value, axis):
+    count, mine = lax.axis_size(axis), lax.axis_index(axis)
+    if count == 2:
+        other = lax.ppermute(value, axis, [(0, 1), (1, 0)])
+        return jnp.stack([jnp.where(mine == 0, value, other), jnp.where(mine == 0, other, value)])
+    up, down, ups, downs = value, value, [], []
+    for hop in range(1, count):
+        up = lax.ppermute(up, axis, [(i, i + 1) for i in range(hop - 1, count - 1)])
+        down = lax.ppermute(down, axis, [(i, i - 1) for i in range(1, count - hop + 1)])
+        ups.append(up)
+        downs.append(down)
+    places = []
+    for place in range(count):
+        found = value
+        for back in range(1, count):
+            if place + back < count:
+                found = jnp.where(mine == place + back, ups[back - 1], found)
+            if place >= back:
+                found = jnp.where(mine == place - back, downs[back - 1], found)
+        places.append(found)
+    return jnp.stack(places)
+
+
+def ring_scatter(value, axis):
+    count, mine = lax.axis_size(axis), lax.axis_index(axis)
+
+    def block(back):
+        return lax.dynamic_index_in_dim(value, (mine - back) % count, 0, False)
+
+    if count == 2:
+        return block(0).astype(F32) + lax.ppermute(block(1), axis, [(0, 1), (1, 0)]).astype(F32)
+    up = down = None
+    for hop in range(1, count):
+        up_sum, down_sum = block(hop), block(count - hop)
+        if up is not None:
+            up_sum = (up_sum.astype(F32) + up.astype(F32)).astype(BF)
+            down_sum = (down_sum.astype(F32) + down.astype(F32)).astype(BF)
+        up = lax.ppermute(up_sum, axis, [(i, i + 1) for i in range(hop)])
+        down = lax.ppermute(down_sum, axis, [(i, i - 1) for i in range(count - hop, count)])
+    return block(0).astype(F32) + up.astype(F32) + down.astype(F32)
+
+
+def double_gather(value):
+    value = value[None]
+    for axis in ("c", "x", "y", "z"):
+        count, mine = lax.axis_size(axis), lax.axis_index(axis)
+        hop = 1
+        while hop < count:
+            other = lax.ppermute(value, axis, [(i, i ^ hop) for i in range(count)])
+            low = (mine // hop) % 2 == 0
+            value = jnp.concatenate([jnp.where(low, value, other), jnp.where(low, other, value)])
+            hop *= 2
+    return value
+
+
+def tied(*values):
+    return lax.optimization_barrier(values)
+
+
+def in_parts_of(value):
+    upper = value.astype(BF)
+    rest = value - upper.astype(F32)
+    middle = rest.astype(BF)
+    lower = (rest - middle.astype(F32)).astype(BF)
+    return [upper[:, None], middle[:, None], lower[:, None]]
+
+
+def as_stored(value):
+    return with_layout_constraint(value, Layout(tuple(range(value.ndim))))
+
+
+def direct_scatter(value, axis):
+    count, mine = lax.axis_size(axis), lax.axis_index(axis)
+    total = lax.dynamic_index_in_dim(value, mine, 0, False).astype(F32)
+    for back in range(1, count):
+        block = lax.dynamic_index_in_dim(value, (mine - back) % count, 0, False)
+        total += lax.ppermute(block, axis, [(i, (i - back) % count) for i in range(count)])
+    return total
+
+
+def quad_parts(value, axis):
+    half = value.shape[axis] // 2
+    first = ring_gather(ring_gather(lax.slice_in_dim(value, 0, half, axis=axis), "x"), "y")
+    second = lax.slice_in_dim(value, half, 2 * half, axis=axis)
+    second = ring_gather(ring_gather(second, "y"), "x").swapaxes(0, 1)
+    return [first, second]
+
+
+def quad_whole(parts):
+    return jnp.concatenate(parts, axis=2).reshape(-1, parts[0].shape[-1])
+
+
+def quad_sums(value):
+    value = value.reshape(lax.axis_size("y"), lax.axis_size("x"), -1, value.shape[1])
+    half = value.shape[2] // 2
+    first = ring_scatter(value[:, :, :half], "y").astype(BF)
+    return first, ring_scatter(value[:, :, half:].swapaxes(0, 1), "x").astype(BF)
+
+
+def quad_rest(first, second):
+    return jnp.concatenate([ring_scatter(first, "x"), ring_scatter(second, "y")], axis=0)
+
+
+def core_gather(parts):
+    both = ring_gather(jnp.concatenate(parts, axis=3), "c")
+    return jnp.moveaxis(both, 0, 2).reshape(-1, both.shape[-1])
+
+
+def line_gather(value):
+    both = ring_gather(ring_gather(value, "z"), "c")
+    return both.swapaxes(0, 1).reshape(-1, value.shape[1])
+
+
+def line_scatter(value):
+    value = value.reshape(lax.axis_size("z"), 2, -1, value.shape[1]).swapaxes(0, 1)
+    return direct_scatter(ring_scatter(value, "c").astype(BF), "z")
+
+
 def total_of(value):
     for axis in ("c", "x", "y", "z"):
         count = lax.axis_size(axis)
@@ -102,7 +221,7 @@
     return sig_neg, keep, jnp.where(started > 0.0, 0.0, 1.0 - keep)
 
 
-def scan_forward(proj_ref, started_ref, gap_ref, state_ref):
+def scan_forward(proj_ref, started_ref, gap_ref, state_ref, squares_ref):
     rows, width = state_ref.shape
     row = lax.broadcasted_iota(jnp.int32, (TILE, width), 0)
     gap = gap_ref[...]
@@ -115,6 +234,7 @@
         coeff, value = tile_scan(decay, silu(in_proj) * keep, row, False)
         state = value + coeff * carry
         state_ref[place, :] = state
+        squares_ref[place, :] = jnp.sum(state * state, axis=-1, keepdims=True)
         return state[TILE - 1 :, :]
 
     lax.fori_loop(0, rows // TILE, step, jnp.zeros((1, width), F32), unroll=4)
@@ -124,12 +244,14 @@
     rows, width = state_ref.shape
     row = lax.broadcasted_iota(jnp.int32, (TILE, width), 0)
     gap = gap_ref[...]
-    tiles = rows // TILE
+
+    def located(index):
+        return pl.ds(pl.multiple_of(index * TILE, TILE), TILE)
 
     def step(count, carry):
-        index = tiles - 1 - count
-        place = pl.ds(pl.multiple_of(index * TILE, TILE), TILE)
-        before = pl.ds(pl.multiple_of(jnp.maximum(index - 1, 0) * TILE, TILE), TILE)
+        index = rows // TILE - 1 - count
+        place = located(index)
+        before = located(jnp.maximum(index - 1, 0))
         in_proj = proj_ref[place, pl.ds(0, width)]
         forget_proj = proj_ref[place, pl.ds(width, width)]
         started = started_ref[place, :]
@@ -148,14 +270,17 @@
         d_forget_ref[place, :] = -d_keep * gap * sig_neg * (1.0 - sig_neg)
         return passed[:1, :]
 
-    lax.fori_loop(0, tiles, step, jnp.zeros((1, width), F32), unroll=4)
+    lax.fori_loop(0, rows // TILE, step, jnp.zeros((1, width), F32), unroll=4)
 
 
 def run_forward(proj, started, gap):
     rows, width = proj.shape[0], gap.shape[1]
     return pl.pallas_call(
         scan_forward,
-        out_shape=jax.ShapeDtypeStruct((rows, width), F32),
+        out_shape=[
+            jax.ShapeDtypeStruct((rows, width), F32),
+            jax.ShapeDtypeStruct((rows, 1), F32),
+        ],
         compiler_params=pltpu.CompilerParams(vmem_limit_bytes=48 * 2**20),
     )(proj, started, gap)
 
@@ -200,17 +325,23 @@
 
     low_mixer = mixer_w.astype(BF)
     sent = low_mixer[:, :3, :].reshape(own, 3, planes, spots, own).transpose(3, 0, 1, 2, 4)
-    part = exchange(sent.reshape(spots, own, 3 * chans), PLANE)
-    w_proj = gather(part.reshape(spots * own, 3 * chans), "z")
-    w_out = gather(low_mixer[:, 3, :], "z")
+    x_low, sent, low_gains = tied(tokens, sent.reshape(spots, own, 3 * chans), gains)
+    part = exchange(sent, PLANE)
+    part = jnp.concatenate(
+        [part.reshape(spots * own, 3 * chans), low_mixer[:, 3, :].reshape(spots * own, chans)], axis=1
+    )
+    x_parts = quad_parts(x_low, 1)
+    full_gains = double_gather(low_gains).swapaxes(0, 1).reshape(3, width)
     low_in = mlp_in.astype(BF)
-    sent = low_in.reshape(own, 2, planes, quads, pairs, down_rows).transpose(2, 4, 0, 1, 3, 5)
     inner = quads * down_rows
-    part = exchange(sent.reshape(planes * pairs, own, 2 * inner), LINE)
-    w_in = gather(part.reshape(planes * pairs * own, 2 * inner), QUAD)
-    w_down = gather(mlp_down.astype(BF), QUAD)
-
-    full_gains = gather(gather(gains.T, PLANE), "z").T
+    sent_in = low_in.reshape(own, 2, planes, quads, pairs, down_rows).transpose(2, 4, 0, 1, 3, 5)
+    sent_in = sent_in.reshape(planes * pairs, own, 2 * inner)
+    part, sent_in = tied(part, sent_in)
+    w_all = gather(part, "z")
+    w_proj = w_all[:, : 3 * chans]
+    w_out = w_all[:, 3 * chans :].reshape(chans, width)
+    x_all = core_gather(x_parts)
+
     bound = lower_bound.reshape(planes, spots, own)
     gap = (1.0 - lax.dynamic_index_in_dim(bound, spot, 1, False)).reshape(1, chans)
     gain_mid = full_gains[1].reshape(planes, spots, own)
@@ -228,62 +359,99 @@
 
     x = tokens.astype(F32)
     x_normed, x_factor = normalize(x)
-    n1 = gather((x_normed * full_gains[0]).astype(BF), PLANE)
+    n1 = (normalize(x_all.astype(F32))[0] * full_gains[0]).astype(BF)
     cot = cotangent.astype(F32) * valid[:, None]
-    cot_all = gather(cot.astype(BF), LINE)
+    cot_low = cot.astype(BF)
     proj = jnp.dot(n1, w_proj, preferred_element_type=F32)
-    state = run_forward(proj[:, : 2 * chans], started, gap)
+    proj, sent_in = tied(proj, sent_in)
+    part_in = exchange(sent_in, LINE)
+    cot_low, part_in = tied(cot_low, part_in)
+    cot_all = gather(cot_low, LINE)
+    state, squares = run_forward(proj[:, : 2 * chans], started, gap)
     gate_proj = proj[:, 2 * chans :]
     gate_act = silu(gate_proj)
     raw = (state * gain_mid * gate_act).astype(BF)
-    squares = lax.psum(jnp.sum(state * state, axis=-1), PLANE)
-    state_factor = lax.rsqrt(squares / width + EPS_NORM)
-    mix_raw = scatter(jnp.dot(raw, w_out, preferred_element_type=F32).astype(BF), PLANE)
-    home_factor = lax.dynamic_slice_in_dim(state_factor, spot * rows, rows)
-    mix = mix_raw.astype(F32) * home_factor[:, None]
+    lane = jnp.arange(128, dtype=jnp.int32)[None, :]
+    upper = squares.astype(BF).astype(F32)
+    riders = jnp.where(lane == spot, upper, jnp.where(lane == spots + spot, squares - upper, 0.0))
+    raw = jnp.concatenate([raw, riders.astype(BF)], axis=1)
+    ride = jnp.pad(jnp.eye(128, dtype=BF), ((chans, 0), (width, 0)))
+    w_ride = ride + jnp.pad(w_out, ((0, 128), (0, 128)))
+    mix_part = jnp.dot(raw, w_ride, preferred_element_type=F32).astype(BF)
+    in_parts = quad_parts(part_in.reshape(planes * pairs * own, 2 * inner), 0)
+    mix_raw = scatter(mix_part, PLANE)
+    mix_raw, cot_all, *in_parts = tied(mix_raw, cot_all, *in_parts)
+    w_in = quad_whole(in_parts)
+    squares = jnp.sum(mix_raw[:, width : width + 2 * spots].astype(F32), axis=1)
+    home_factor = lax.rsqrt(squares / width + EPS_NORM)
+    mix = mix_raw[:, :width].astype(F32) * home_factor[:, None]
     after_mix = x + mix
 
     mid_normed, mid_factor = normalize(after_mix)
-    n2 = gather(swapped((mid_normed * full_gains[2]).astype(BF), planes, quads), LINE)
+    n2_home = swapped((mid_normed * full_gains[2]).astype(BF), planes, quads)
+    low_down, n2_home = tied(mlp_down.astype(BF), n2_home)
+    w_down = quad_whole(quad_parts(low_down, 0))
+    n2, w_down = tied(gather(n2_home, LINE), w_down)
     gate_up = jnp.dot(n2, w_in, preferred_element_type=F32)
     gate, up_value = gate_up[:, :inner], gate_up[:, inner:]
     silu_gate = silu(gate)
     hidden = (silu_gate * up_value).astype(BF)
-    down = scatter(jnp.dot(hidden, w_down, preferred_element_type=F32).astype(BF), LINE)
-    block_out = (after_mix + down.astype(F32)).astype(BF)
 
     grad_down = lax.dot_general(hidden, cot_all, (((0,), (0,)), ((), ())), preferred_element_type=F32)
-    shard_down = scatter(grad_down.astype(BF), QUAD).astype(F32)
+    grad_down = grad_down.astype(BF)
     d_hidden = lax.dot_general(cot_all, w_down, (((1,), (1,)), ((), ())), preferred_element_type=F32)
     d_gate = d_hidden * up_value * silu_grad(gate)
     d_up = d_hidden * silu_gate
     d_gate_up = jnp.concatenate([d_gate.astype(BF), d_up.astype(BF)], axis=1)
     d_n2 = lax.dot_general(d_gate_up, w_in, (((1,), (1,)), ((), ())), preferred_element_type=F32)
-    d_n2 = swapped(scatter(d_n2.astype(BF), LINE), quads, planes).astype(F32)
+    d_n2 = swapped(scatter(d_n2.astype(BF), LINE).astype(F32), quads, planes)
     grad_in = lax.dot_general(n2, d_gate_up, (((0,), (0,)), ((), ())), preferred_element_type=F32)
-    shard_in = scatter(grad_in.astype(BF), QUAD)
-    shard_in = exchange(shard_in.reshape(planes * pairs, own, 2 * inner), LINE)
-    shard_in = shard_in.reshape(planes, pairs, own, 2, quads, down_rows).transpose(2, 3, 0, 4, 1, 5)
-    shard_in = shard_in.reshape(own, 2, hidden_width).astype(F32)
+    grad_in = grad_in.astype(BF)
+    down = jnp.dot(hidden, w_down, preferred_element_type=F32).astype(BF)
+    sums_in = quad_sums(grad_in)
+    d_n2, grad_down, down, *sums_in = tied(d_n2, grad_down, down, *sums_in)
     d_mid = cot + norm_back(d_n2 * full_gains[2], mid_normed, mid_factor)
-
     d_mix_home = d_mid.astype(BF)
-    d_mix = gather(d_mix_home, PLANE)
-    mean = gather(jnp.sum(d_mix_home.astype(F32) * mix, axis=-1) / width, PLANE)
-    d_mixed = lax.dot_general(d_mix, w_out, (((1,), (1,)), ((), ())), preferred_element_type=F32)
-    factor = state_factor[:, None]
+    down, d_mix_home = tied(down, d_mix_home)
+    down = line_scatter(down)
+    shard_in = quad_rest(*sums_in).astype(BF)
+    mean = jnp.sum(d_mix_home.astype(F32) * mix, axis=-1) / width
+    riders = jnp.concatenate(in_parts_of(mean) + in_parts_of(home_factor), axis=1)
+    riders = jnp.pad(riders, ((0, 0), (0, 128 - riders.shape[1])))
+    d_mix = gather(jnp.concatenate([d_mix_home, riders], axis=1), PLANE)
+    d_mix, shard_in, grad_down = tied(d_mix, shard_in, grad_down)
+    riders = d_mix[:, width : width + 6].astype(F32)
+    mean = jnp.sum(riders[:, :3], axis=1, keepdims=True)
+    factor = jnp.sum(riders[:, 3:], axis=1, keepdims=True)
+    shard_down = scatter(grad_down, QUAD).astype(F32)
+    got_in = exchange(shard_in.reshape(planes * pairs, own, 2 * inner), LINE)
+
+    d_mixed = lax.dot_general(
+        d_mix, w_ride[:chans], (((1,), (1,)), ((), ())), preferred_element_type=F32
+    )
     state_normed = state * factor
     mixed_in = (state_normed * gain_mid * gate_act).astype(BF)
     grad_out = lax.dot_general(mixed_in, d_mix, (((0,), (0,)), ((), ())), preferred_element_type=F32)
-    shard_out = scatter(grad_out.astype(BF), "z").astype(F32)
     d_gate_proj = d_mixed * state_normed * gain_mid * silu_grad(gate_proj)
-    d_state = factor * (d_mixed * gain_mid * gate_act - state_normed * mean[:, None])
+    d_state = factor * (d_mixed * gain_mid * gate_act - state_normed * mean)
+    d_gate_proj = d_gate_proj.astype(BF)
     d_in_proj, d_forget_proj = run_backward(proj[:, : 2 * chans], state, d_state, started, gap)
     d_proj = jnp.concatenate(
-        [d_in_proj.astype(BF), d_forget_proj.astype(BF), d_gate_proj.astype(BF)], axis=1
+        [d_in_proj.astype(BF), d_forget_proj.astype(BF), d_gate_proj], axis=1
     )
     grad_proj = lax.dot_general(n1, d_proj, (((0,), (0,)), ((), ())), preferred_element_type=F32)
-    shard_proj = scatter(grad_proj.astype(BF), "z")
+    grad_out = grad_out[:, :width].astype(BF).reshape(planes, spots * own, chans)
+    grad_all = jnp.concatenate(
+        [grad_proj.astype(BF).reshape(planes, spots * own, 3 * chans), grad_out], axis=2
+    )
+    grad_all, down, got_in = tied(grad_all, down, got_in)
+    block_out = (after_mix + down).astype(BF)
+    shard_all = scatter(grad_all.reshape(planes * spots * own, 4 * chans), "z")
+    shard_in = got_in.reshape(planes, pairs, own, 2, quads, down_rows).transpose(2, 3, 0, 4, 1, 5)
+    shard_in = as_stored(shard_in.reshape(own, 2, hidden_width).astype(F32))
+    shard_all, shard_in, shard_down = tied(shard_all, shard_in, shard_down)
+    shard_proj = shard_all[:, : 3 * chans]
+    shard_out = shard_all[:, 3 * chans :].reshape(own, width).astype(F32)
     shard_proj = exchange(shard_proj.reshape(spots, own, 3 * chans), PLANE)
     shard_proj = shard_proj.reshape(spots, own, 3, planes, own).transpose(1, 2, 3, 0, 4)
     shard_proj = shard_proj.reshape(own, 3, width).astype(F32)
@@ -300,7 +468,7 @@
         ],
         axis=0,
     ) / gains
-    shard_mixer = jnp.concatenate([shard_proj, shard_out[:, None, :]], axis=1)
+    shard_mixer = as_stored(jnp.concatenate([shard_proj, shard_out[:, None, :]], axis=1))
 
     local_total = (
         jnp.sum(shard_mixer * shard_mixer)

time: 926 us -> 736 us (0.79)
  waiting for transfers between devices: 526 us -> 342 us
  blocking collectives: 99.7 us -> 0 us
  other arithmetic: 62.5 us -> 107 us
  starting transfers between devices: 24.2 us -> 68.4 us
  local copies, waits for them, and re-layouts: 84.3 us -> 101 us
  matrix products: 88.9 us -> 75.5 us
    all_gather x8 -> x4, waiting for transfers between devices: 287 us -> 69 us  [gather(): return lax.all_gather(value, axes, axis=0, tiled=True)]
    reduce_scatter x8 -> x5, waiting for transfers between devices: 236 us -> 44.7 us  [scatter(): return lax.psum_scatter(value, axes, scatter_dimension=0, tiled=True)]
    ppermute x0 -> x26, waiting for transfers between devices: none -> 169 us  [the longest x13 82.7 us: ring_gather(): other = lax.ppermute(value, axis, [(0, 1), (1, 0)])]
    all_to_all x2 -> x4, waiting for transfers between devices: 0.01 us -> 56.5 us  [exchange(): return lax.all_to_all(value, axes, 0, 0, tiled=True)]
    all_to_all x2 -> x0, blocking collectives: 55.9 us -> none  [exchange(): return lax.all_to_all(value, axes, 0, 0, tiled=True)]
    ppermute x0 -> x26, starting transfers between devices: none -> 34.2 us  [the longest x13 15.4 us: ring_gather(): other = lax.ppermute(value, axis, [(0, 1), (1, 0)])]
    all_gather x3 -> x0, blocking collectives: 30.1 us -> none  [gather(): return lax.all_gather(value, axes, axis=0, tiled=True)]
    convert_element_type x4 -> x19, other arithmetic: 6.15 us -> 22.2 us  [the longest x2 3.39 us: shards(): n1 = (normalize(x_all.astype(F32))[0] * full_gains[0]).astype(BF)]
  transfers between devices with their start and end apart: 23 -> 44, of which waited for: 19 -> 29; matrix products, arithmetic and copies ran while one was open for 16% -> 23% of each run, Pallas kernels for 1% -> 1%
where the time goes in v2:
time: 736 us; the launch traced here: 727 us
  waiting for transfers between devices  342 us (46%)
  other arithmetic  107 us (15%)
  local copies, waits for them, and re-layouts  101 us (14%)
  matrix products  75.5 us (10%)
  starting transfers between devices  68.4 us (9%)
  between operations  21.8 us (3%)
  Pallas kernels  11.4 us (2%)
    ppermute x13, waiting for transfers between devices, ring_gather(): other = lax.ppermute(value, axis, [(0, 1), (1, 0)])  82.7 us
    all_gather x4, waiting for transfers between devices, gather(): return lax.all_gather(value, axes, axis=0, tiled=True)  69 us
    all_to_all x4, waiting for transfers between devices, exchange(): return lax.all_to_all(value, axes, 0, 0, tiled=True)  56.5 us
    ppermute x5, waiting for transfers between devices, ring_scatter(): lax.ppermute(block(1), axis, [(0, 1), (1, 0)]).astype(F32)  45.6 us
    reduce_scatter x5, waiting for transfers between devices, scatter(): return lax.psum_scatter(value, axes, scatter_dimension=0, tiled=True)  44.7 us
    ppermute x3, waiting for transfers between devices, direct_scatter(): lax.ppermute(block, axis, [(i, (i - back) % count) for i in range(count)])  29.9 us
    convert_element_type x3, local copies, waits for them, and re-layouts, shards(): shard_in = as_stored(shard_in.reshape(own, 2, hidden_width).astype(F32))  25.5 us
    sub x4, other arithmetic, adam_step(): weight - rate * (step_size + decay_w * weight)  22.9 us
  transfers between devices with their start and end apart: 44, of which 29 were waited for; matrix products, arithmetic and copies ran while one was open for 23% of the time, Pallas kernels for 1%

profile of v2, /device:TPU:0, one launch (start us, length us, event | category | flops | bytes accessed | tf_op | source)
XLA Modules:
  0.0 727.0 jit_solution(5268228813660024519)
XLA Ops:
  7.2 4.2 fusion.64
  15.8 3.7 reshape.340
  19.5 5.2 all-to-all-start
  34.6 8.9 %reshape.342 = bf16[64,2,4,4,2,176]{5,4,3,2,1,0:T(2,128)(2,1)S(1)} reshape(bf16[64,2,5632]{2,1,0:T(2,128)(2,1)} %convert_element_type.393) | data formatting | bytes 2883584 | tf_op jit(solution)/shard_map/reshape | solution.py:337
  45.6 5.4 reshape.343
  58.4 10.2 %collective-permute-done.3 = bf16[2,128,1024]{2,1,0:T(8,128)(2,1)S(1)} collective-permute-done((bf16[2,128,1024]{2,1,0:T(8,128)(2,1)S(1)}, bf16[2,128,1024]{2,1,0:T(8,128)(2,1)S(1)}, u32[]{:S(2)}, u32[]{:S(2)}) %collective-permute-start.3) | collective-permute-done | bytes 524320 | tf_op jit(solution)/shard_map/ppermute | solution.py:48
  83.3 5.1 collective-permute-done.9
  95.8 39.5 %all-gather.5.cloned.1.call-done = bf16[2048,1024]{1,0:T(8,128)(2,1)} async-done(((bf16[512,1024]{1,0:T(8,128)(2,1)}), bf16[2048,1024]{1,0:T(8,128)(2,1)}) %all-gather.5.cloned.1.call-update) | async-done | bytes 4194320 | tf_op jit(solution)/shard_map/all_gather | solution.py:34
  137.2 6.5 fusion.8
  144.1 5.7 shard_map.271
  154.7 3.7 all-to-all-start.1
  160.7 32.7 %all-to-all-done.1 = bf16[8,64,1408]{2,1,0:T(8,128)(2,1)S(1)} async-done(((bf16[8,64,1408]{2,1,0:T(8,128)(2,1)}), bf16[8,64,1408]{2,1,0:T(8,128)(2,1)S(1)}, u32[]{:S(2)}, u32[]{:S(2)}) %all-to-all-start.1) | async-done | bytes 1441824 | tf_op jit(solution)/shard_map/all_to_all | solution.py:42
  196.6 20.7 %collective-permute-done.10 = bf16[256,1408]{1,0:T(8,128)(2,1)S(1)} collective-permute-done((bf16[256,1408]{1,0:T(8,128)(2,1)S(1)}, bf16[256,1408]{1,0:T(8,128)(2,1)S(1)}, u32[]{:S(2)}, u32[]{:S(2)}) %collective-permute-start.10) | collective-permute-done | bytes 720928 | tf_op jit(solution)/shard_map/ppermute | solution.py:48
  225.1 26.2 %collective-permute-done.11 = bf16[2,256,1408]{2,1,0:T(8,128)(2,1)} collective-permute-done((bf16[2,256,1408]{2,1,0:T(8,128)(2,1)}, bf16[2,256,1408]{2,1,0:T(8,128)(2,1)}, u32[]{:S(2)}, u32[]{:S(2)}) %collective-permute-start.11) | collective-permute-done | bytes 1441824 | tf_op jit(solution)/shard_map/ppermute | solution.py:48
  270.2 7.6 %collective-permute-done.14 = bf16[88,2048]{1,0:T(8,128)(2,1)S(1)} collective-permute-done((bf16[88,2048]{1,0:T(8,128)(2,1)S(1)}, bf16[88,2048]{1,0:T(8,128)(2,1)S(1)}, u32[]{:S(2)}, u32[]{:S(2)}) %collective-permute-start.14) | collective-permute-done | bytes 360480 | tf_op jit(solution)/shard_map/ppermute | solution.py:48
  284.4 12.1 %collective-permute-done.17 = bf16[2,88,2048]{2,1,0:T(8,128)(2,1)S(1)} collective-permute-done((bf16[2,88,2048]{2,1,0:T(8,128)(2,1)S(1)}, bf16[2,88,2048]{2,1,0:T(8,128)(2,1)S(1)}, u32[]{:S(2)}, u32[]{:S(2)}) %collective-permute-start.17) | collective-permute-done | bytes 720928 | tf_op jit(solution)/shard_map/ppermute | solution.py:48
  301.8 11.8 %all-gather.9.cloned.1.call-done = bf16[1024,2048]{0,1:T(8,128)(2,1)} async-done(((bf16[128,2048]{0,1:T(8,128)(2,1)}), bf16[1024,2048]{0,1:T(8,128)(2,1)}) %all-gather.9.cloned.1.call-update) | async-done | bytes 4194320 | tf_op jit(solution)/shard_map/all_gather | solution.py:34
  313.5 10.7 %fusion.70 = f32[1024,1408]{0,1:T(8,128)S(1)} fusion(bf16[1024,2048]{0,1:T(8,128)(2,1)} %all-gather.9.cloned.1.call-done, bf16[2048,1408]{1,0:T(8,128)(2,1)} %bitcast.211), kind=kOutput, calls=%fused_computation.225 | convolution fusion | flops 5905580032 | bytes 15728640 | tf_op jit(solution)/shard_map/dot_general | solution.py:395
  324.3 5.3 multiply_convert_fusion.2
  330.7 11.0 %convolution_convert_fusion.3 = bf16[1024,2048]{1,0:T(8,128)(2,1)} fusion(bf16[2048,1408]{1,0:T(8,128)(2,1)} %bitcast.212, bf16[1024,704]{0,1:T(8,128)(2,1)S(1)} %get-tuple-element.118, bf16[1024,704]{0,1:T(8,128)(2,1)S(1)} %get-tuple-element.117), kind=kOutput, calls=%fused_computation.13 | convolution fusion | flops 5913444352 | bytes 12845056 | tf_op jit(solution)/shard_map/dot_general | solution.py:406
  342.2 9.0 %convolution_convert_fusion = bf16[2048,1408]{1,0:T(8,128)(2,1)S(1)} fusion(bf16[1024,2048]{0,1:T(8,128)(2,1)} %all-gather.9.cloned.1.call-done, bf16[1024,704]{0,1:T(8,128)(2,1)} %copy-done.53, bf16[1024,704]{0,1:T(8,128)(2,1)S(1)} %get-tuple-element.117), kind=kOutput, calls=%fused_computation.4 | convolution fusion | flops 5914230784 | bytes 12845056 | tf_op jit(solution)/shard_map/dot_general | solution.py:408
  357.6 5.1 convolution_convert_fusion.2
  362.7 4.5 convolution_convert_fusion.6
  367.1 19.9 %collective-permute-done.18 = bf16[2,256,1408]{2,1,0:T(8,128)(2,1)} collective-permute-done((bf16[2,256,1408]{2,1,0:T(8,128)(2,1)}, bf16[2,256,1408]{2,1,0:T(8,128)(2,1)}, u32[]{:S(2)}, u32[]{:S(2)}) %collective-permute-start.18) | collective-permute-done | bytes 1441824 | tf_op jit(solution)/shard_map/ppermute | solution.py:75
  406.5 20.4 %collective-permute-done.21 = bf16[256,1408]{1,0:T(8,128)(2,1)S(1)} collective-permute-done((bf16[256,1408]{1,0:T(8,128)(2,1)S(1)}, bf16[256,1408]{1,0:T(8,128)(2,1)S(1)}, u32[]{:S(2)}, u32[]{:S(2)}) %collective-permute-start.21) | collective-permute-done | bytes 720928 | tf_op jit(solution)/shard_map/ppermute | solution.py:75
  429.6 14.6 %all-gather.11.cloned.1.call-done = bf16[1024,2176]{1,0:T(8,128)(2,1)} async-done(((bf16[128,2176]{1,0:T(8,128)(2,1)}), bf16[1024,2176]{1,0:T(8,128)(2,1)}) %all-gather.11.cloned.1.call-update) | async-done | bytes 4456464 | tf_op jit(solution)/shard_map/all_gather | solution.py:34
  446.0 4.7 subtract_multiply_fusion
  450.7 5.7 shard_map.272
  456.6 5.0 convolution_convert_fusion.4
  465.2 4.2 collective-permute-done.22
  480.3 4.3 all-to-all-start.2
  484.6 7.3 %collective-permute-done.25 = bf16[128,2048]{1,0:T(8,128)(2,1)} collective-permute-done((bf16[128,2048]{1,0:T(8,128)(2,1)}, bf16[128,2048]{1,0:T(8,128)(2,1)}, u32[]{:S(2)}, u32[]{:S(2)}) %collective-permute-start.25) | collective-permute-done | bytes 524320 | tf_op jit(solution)/shard_map/ppermute | solution.py:121
  491.9 22.6 %collective-permute-done.24 = bf16[128,2048]{1,0:T(8,128)(2,1)} collective-permute-done((bf16[128,2048]{1,0:T(8,128)(2,1)}, bf16[128,2048]{1,0:T(8,128)(2,1)}, u32[]{:S(2)}, u32[]{:S(2)}) %collective-permute-start.24) | collective-permute-done | bytes 524320 | tf_op jit(solution)/shard_map/ppermute | solution.py:121
  517.9 4.1 fusion.39
  523.5 6.0 convolution_convert_fusion.5
  532.1 23.8 %all-to-all-done.2 = bf16[8,64,1408]{2,1,0:T(8,128)(2,1)} async-done(((bf16[8,64,1408]{2,1,0:T(8,128)(2,1)}), bf16[8,64,1408]{2,1,0:T(8,128)(2,1)}, u32[]{:S(2)}, u32[]{:S(2)}) %all-to-all-start.2) | async-done | bytes 1441824 | tf_op jit(solution)/shard_map/all_to_all | solution.py:42
  555.9 8.4 %reshape.380 = f32[4,2,64,2,4,176]{5,4,3,2,1,0:T(4,128)} reshape(bf16[8,64,1408]{2,1,0:T(8,128)(2,1)} %all-to-all-done.2) | data formatting | bytes 4325376 | tf_op jit(solution)/shard_map/convert_element_type | solution.py:451
  564.4 7.4 %copy.103 = f32[64,2,4,4,2,176]{5,4,3,2,1,0:T(2,128)} copy(f32[64,2,4,4,2,176]{5,3,1,0,4,2:T(4,128)} %bitcast.207) | data formatting | bytes 5767168 | tf_op jit(solution)/shard_map/convert_element_type | solution.py:451
  571.8 9.7 %reshape.373 = f32[64,2,5632]{2,1,0:T(2,128)} reshape(f32[64,2,4,4,2,176]{5,4,3,2,1,0:T(2,128)} %copy.103) | data formatting | bytes 5767168 | tf_op jit(solution)/shard_map/convert_element_type | solution.py:451
  588.3 44.7 %reduce-scatter.12.cloned.1.call-done = bf16[512,1024]{1,0:T(8,128)(2,1)} async-done(((bf16[2048,1024]{1,0:T(8,128)(2,1)}), bf16[512,1024]{1,0:T(8,128)(2,1)}) %reduce-scatter.12.cloned.1.call-update) | async-done | bytes 1048592 | tf_op jit(solution)/shard_map/reduce_scatter | solution.py:38
  636.9 4.5 all-to-all-start.3
  648.5 6.8 multiply_reduce_fusion.1
  655.4 3.7 reshape.381
  659.0 5.4 copy.104
  664.4 3.8 reshape.374
  690.9 4.3 collective-permute-start.30
  696.2 8.2 %multiply_subtract_fusion.1 = (f32[64,4,2048]{2,1,0:T(4,128)}, f32[64,4,2048]{2,1,0:T(4,128)}, f32[64,4,2048]{2,1,0:T(4,128)}) fusion(f32[64,4,2048]{2,1,0:T(4,128)} %param.20, f32[64,1,2048]{2,1,0:T(1,128)S(1)} %reshape.375, f32[64,3,2048]{2,1,0:T(4,128)} %copy-done.7, f32[]{:T(128)S(6)} %min.3, f32[64,4,2048]{2,1,0:T(4,128)} %param.24, ...), kind=kLoop, calls=%fused_computation.48 | loop fusion | flops 8912896 | bytes 14680068 | tf_op jit(solution)/shard_map/sub | solution.py:199
  704.5 11.1 %multiply_subtract_fusion = (f32[64,2,5632]{2,1,0:T(2,128)}, f32[64,2,5632]{2,1,0:T(2,128)}, f32[64,2,5632]{2,1,0:T(2,128)}) fusion(f32[64,2,5632]{2,1,0:T(2,128)S(1)} %copy-done.5, f32[64,2,5632]{2,1,0:T(2,128)S(1)} %copy-done.6, f32[]{:T(128)S(6)} %min.3, f32[64,2,5632]{2,1,0:T(2,128)S(1)} %copy-done.32, f32[64,2,5632]{2,1,0:T(2,128)S(1)} %copy-done.33), kind=kLoop, calls=%fused_computation.28 | loop fusion | flops 11534336 | bytes 20185092 | tf_op jit(solution)/shard_map/sub | solution.py:199
  (316 shorter events, 189.9 us)
Async XLA Ops:
  15.8 16.7 %copy-start.4 = (f32[64,2,5632]{2,1,0:T(2,128)S(1)}, f32[64,2,5632]{2,1,0:T(2,128)}, u32[]{:S(2)}) copy-start(f32[64,2,5632]{2,1,0:T(2,128)} %param.21) | copy-start | bytes 8650756
  19.5 31.5 %all-to-all-start = ((bf16[8,64,768]{2,1,0:T(8,128)(2,1)}), bf16[8,64,768]{2,1,0:T(8,128)(2,1)}, u32[]{:S(2)}, u32[]{:S(2)}) async-start(bf16[8,64,768]{2,1,0:T(8,128)(2,1)} %reshape.340), calls=%async_computation | async-start | bytes 1572864 | tf_op jit(solution)/shard_map/all_to_all | solution.py:42
  24.7 110.6 %all-gather.5.cloned.1.call-start = ((), (), s32[]{:S(2)}) async-start(), calls=%async_computation.9 | async-start | bytes 5242880 | tf_op jit(solution)/shard_map/all_gather | solution.py:34
  25.6 28.2 %collective-permute-start = (bf16[128,1024]{1,0:T(8,128)(2,1)}, bf16[128,1024]{1,0:T(8,128)(2,1)}, u32[]{:S(2)}, u32[]{:S(2)}) collective-permute-start(bf16[128,1024]{1,0:T(8,128)(2,1)} %get-tuple-element.163), channel_id=1, source_target_pairs={{0,2},{2,0},{1,3},{3,1},{4,6},{6,4},{5,7},{7,5},{8,10},{10,8},{9,1... | collective-permute-start | bytes 786440 | tf_op jit(solution)/shard_map/ppermute | solution.py:48
  27.6 26.3 %collective-permute-start.2 = (bf16[128,1024]{1,0:T(8,128)(2,1)}, bf16[128,1024]{1,0:T(8,128)(2,1)}, u32[]{:S(2)}, u32[]{:S(2)}) collective-permute-start(bf16[128,1024]{1,0:T(8,128)(2,1)} %get-tuple-element.164), channel_id=1, source_target_pairs={{0,4},{4,0},{1,5},{5,1},{2,6},{6,2},{3,7},{7,3},{8,12},{12,8},{9,1... | collective-permute-start | bytes 786440 | tf_op jit(solution)/shard_map/ppermute | solution.py:48
  53.3 205.1 %reduce-scatter.6.cloned.1.call-start = ((), (), s32[]{:S(2)}) async-start(), calls=%async_computation.10 | async-start | bytes 5013504 | tf_op jit(solution)/shard_map/reduce_scatter | solution.py:38
  55.0 13.5 %collective-permute-start.3 = (bf16[2,128,1024]{2,1,0:T(8,128)(2,1)S(1)}, bf16[2,128,1024]{2,1,0:T(8,128)(2,1)S(1)}, u32[]{:S(2)}, u32[]{:S(2)}) collective-permute-start(bf16[2,128,1024]{2,1,0:T(8,128)(2,1)S(1)} %pad_maximum_fusion.19), channel_id=1, source_target_pairs={{0,2},{2,0},{1,3},{3,1},{4,6},{6,4},{5,7},{7,5},{8,10},{10,8},{9,1... | collective-permute-start | bytes 1572872 | tf_op jit(solution)/shard_map/ppermute | solution.py:48
  55.6 1.2 collective-permute-start.5
  55.9 14.4 %collective-permute-start.1 = (bf16[2,128,1024]{2,1,0:T(8,128)(2,1)S(1)}, bf16[2,128,1024]{2,1,0:T(8,128)(2,1)S(1)}, u32[]{:S(2)}, u32[]{:S(2)}) collective-permute-start(bf16[2,128,1024]{2,1,0:T(8,128)(2,1)S(1)} %pad_maximum_fusion.18), channel_id=1, source_target_pairs={{0,4},{4,0},{1,5},{5,1},{2,6},{6,2},{3,7},{7,3},{8,12},{12,8},{9,1... | collective-permute-start | bytes 1572872 | tf_op jit(solution)/shard_map/ppermute | solution.py:48
  56.8 15.1 %collective-permute-start.6 = (f32[2,3,64]{2,1,0:T(4,128)S(1)}, f32[2,3,64]{2,1,0:T(4,128)S(1)}, u32[]{:S(2)}, u32[]{:S(2)}) collective-permute-start(f32[2,3,64]{2,1,0:T(4,128)S(1)} %pad_maximum_fusion.23), channel_id=1, source_target_pairs={{0,2},{2,0},{1,3},{3,1},{4,6},{6,4},{5,7},{7,5},{8,10},{10,8},{9,1... | collective-permute-start | bytes 4616 | tf_op jit(solution)/shard_map/ppermute | solution.py:93
  71.9 16.8 %collective-permute-start.4 = (bf16[2,2,128,2048]{3,2,1,0:T(8,128)(2,1)}, bf16[2,2,128,2048]{3,2,1,0:T(8,128)(2,1)}, u32[]{:S(2)}, u32[]{:S(2)}) collective-permute-start(bf16[2,2,128,2048]{3,2,1,0:T(8,128)(2,1)} %pad_maximum_fusion.5), channel_id=1, source_target_pairs={{0,1},{1,0},{2,3},{3,2},{4,5},{5,4},{6,7},{7,6},{8,9},{9,8},{10,11... | collective-permute-start | bytes 6291464 | tf_op jit(solution)/shard_map/ppermute | solution.py:48
  71.9 3.7 collective-permute-start.7
  75.7 4.1 collective-permute-start.8
  79.8 8.6 %collective-permute-start.9 = (f32[16,3,64]{2,1,0:T(4,128)S(1)}, f32[16,3,64]{2,1,0:T(4,128)S(1)}, u32[]{:S(2)}, u32[]{:S(2)}) collective-permute-start(f32[16,3,64]{2,1,0:T(4,128)S(1)} %pad_maximum_fusion.20), channel_id=1, source_target_pairs={{0,16},{8,24},{16,0},{24,8},{1,17},{9,25},{17,1},{25,9},{2,18},{10... | collective-permute-start | bytes 36872 | tf_op jit(solution)/shard_map/ppermute | solution.py:93
  154.7 38.7 %all-to-all-start.1 = ((bf16[8,64,1408]{2,1,0:T(8,128)(2,1)}), bf16[8,64,1408]{2,1,0:T(8,128)(2,1)S(1)}, u32[]{:S(2)}, u32[]{:S(2)}) async-start(bf16[8,64,1408]{2,1,0:T(8,128)(2,1)} %reshape.343), calls=%async_computation.2 | async-start | bytes 2883584 | tf_op jit(solution)/shard_map/all_to_all | solution.py:42
  158.4 103.1 %all-gather.7.cloned.1.call-start = ((), (), s32[]{:S(2)}) async-start(), calls=%async_computation.11 | async-start | bytes 4718592 | tf_op jit(solution)/shard_map/all_gather | solution.py:34
  193.4 120.1 %all-gather.9.cloned.1.call-start = ((), (), s32[]{:S(2)}) async-start(), calls=%async_computation.12 | async-start | bytes 4718592 | tf_op jit(solution)/shard_map/all_gather | solution.py:34
  193.6 23.7 %collective-permute-start.10 = (bf16[256,1408]{1,0:T(8,128)(2,1)S(1)}, bf16[256,1408]{1,0:T(8,128)(2,1)S(1)}, u32[]{:S(2)}, u32[]{:S(2)}) collective-permute-start(bf16[256,1408]{1,0:T(8,128)(2,1)S(1)} %bitcast.223), channel_id=1, source_target_pairs={{0,2},{2,0},{1,3},{3,1},{4,6},{6,4},{5,7},{7,5},{8,10},{10,8},{9,1... | collective-permute-start | bytes 2162696 | tf_op jit(solution)/shard_map/ppermute | solution.py:48
  195.2 25.1 %collective-permute-start.12 = (bf16[256,1408]{1,0:T(8,128)(2,1)S(1)}, bf16[256,1408]{1,0:T(8,128)(2,1)S(1)}, u32[]{:S(2)}, u32[]{:S(2)}) collective-permute-start(bf16[256,1408]{1,0:T(8,128)(2,1)S(1)} %bitcast.222), channel_id=1, source_target_pairs={{0,4},{4,0},{1,5},{5,1},{2,6},{6,2},{3,7},{7,3},{8,12},{12,8},{9,1... | collective-permute-start | bytes 2162696 | tf_op jit(solution)/shard_map/ppermute | solution.py:48
  218.7 32.5 %collective-permute-start.11 = (bf16[2,256,1408]{2,1,0:T(8,128)(2,1)}, bf16[2,256,1408]{2,1,0:T(8,128)(2,1)}, u32[]{:S(2)}, u32[]{:S(2)}) collective-permute-start(bf16[2,256,1408]{2,1,0:T(8,128)(2,1)} %pad_maximum_fusion.10), channel_id=1, source_target_pairs={{0,4},{4,0},{1,5},{5,1},{2,6},{6,2},{3,7},{7,3},{8,12},{12,8},{9,1... | collective-permute-start | bytes 4325384 | tf_op jit(solution)/shard_map/ppermute | solution.py:48
  222.5 32.3 %collective-permute-start.13 = (bf16[2,256,1408]{2,1,0:T(8,128)(2,1)}, bf16[2,256,1408]{2,1,0:T(8,128)(2,1)}, u32[]{:S(2)}, u32[]{:S(2)}) collective-permute-start(bf16[2,256,1408]{2,1,0:T(8,128)(2,1)} %pad_maximum_fusion.11), channel_id=1, source_target_pairs={{0,2},{2,0},{1,3},{3,1},{4,6},{6,4},{5,7},{7,5},{8,10},{10,8},{9,1... | collective-permute-start | bytes 4325384 | tf_op jit(solution)/shard_map/ppermute | solution.py:48
  266.9 124.9 %reduce-scatter.8.cloned.1.call-start = ((), (), s32[]{:S(2)}) async-start(), calls=%async_computation.13 | async-start | bytes 4718592 | tf_op jit(solution)/shard_map/reduce_scatter | solution.py:38
  267.2 10.6 %collective-permute-start.14 = (bf16[88,2048]{1,0:T(8,128)(2,1)S(1)}, bf16[88,2048]{1,0:T(8,128)(2,1)S(1)}, u32[]{:S(2)}, u32[]{:S(2)}) collective-permute-start(bf16[88,2048]{1,0:T(8,128)(2,1)S(1)} %get-tuple-element.157), channel_id=1, source_target_pairs={{0,2},{2,0},{1,3},{3,1},{4,6},{6,4},{5,7},{7,5},{8,10},{10,8},{9,1... | collective-permute-start | bytes 1081352 | tf_op jit(solution)/shard_map/ppermute | solution.py:48
  268.7 10.3 %collective-permute-start.16 = (bf16[88,2048]{1,0:T(8,128)(2,1)S(1)}, bf16[88,2048]{1,0:T(8,128)(2,1)S(1)}, u32[]{:S(2)}, u32[]{:S(2)}) collective-permute-start(bf16[88,2048]{1,0:T(8,128)(2,1)S(1)} %get-tuple-element.158), channel_id=1, source_target_pairs={{0,4},{4,0},{1,5},{5,1},{2,6},{6,2},{3,7},{7,3},{8,12},{12,8},{9,1... | collective-permute-start | bytes 1081352 | tf_op jit(solution)/shard_map/ppermute | solution.py:48
  279.2 17.3 %collective-permute-start.17 = (bf16[2,88,2048]{2,1,0:T(8,128)(2,1)S(1)}, bf16[2,88,2048]{2,1,0:T(8,128)(2,1)S(1)}, u32[]{:S(2)}, u32[]{:S(2)}) collective-permute-start(bf16[2,88,2048]{2,1,0:T(8,128)(2,1)S(1)} %pad_maximum_fusion.15), channel_id=1, source_target_pairs={{0,2},{2,0},{1,3},{3,1},{4,6},{6,4},{5,7},{7,5},{8,10},{10,8},{9,1... | collective-permute-start | bytes 2162696 | tf_op jit(solution)/shard_map/ppermute | solution.py:48
  282.8 17.1 %collective-permute-start.15 = (bf16[2,88,2048]{2,1,0:T(8,128)(2,1)S(1)}, bf16[2,88,2048]{2,1,0:T(8,128)(2,1)S(1)}, u32[]{:S(2)}, u32[]{:S(2)}) collective-permute-start(bf16[2,88,2048]{2,1,0:T(8,128)(2,1)S(1)} %pad_maximum_fusion.14), channel_id=1, source_target_pairs={{0,4},{4,0},{1,5},{5,1},{2,6},{6,2},{3,7},{7,3},{8,12},{12,8},{9,1... | collective-permute-start | bytes 2162696 | tf_op jit(solution)/shard_map/ppermute | solution.py:48
  341.7 102.6 %all-gather.11.cloned.1.call-start = ((), (), s32[]{:S(2)}) async-start(), calls=%async_computation.14 | async-start | bytes 5013504 | tf_op jit(solution)/shard_map/all_gather | solution.py:34
  353.0 34.1 %collective-permute-start.18 = (bf16[2,256,1408]{2,1,0:T(8,128)(2,1)}, bf16[2,256,1408]{2,1,0:T(8,128)(2,1)}, u32[]{:S(2)}, u32[]{:S(2)}) collective-permute-start(bf16[2,256,1408]{2,1,0:T(8,128)(2,1)} %dynamic-slice_bitcast_fusion.2), channel_id=1, source_target_pairs={{0,4},{4,0},{1,5},{5,1},{2,6},{6,2},{3,7},{7,3},{8,12},{12,8},{9,1... | collective-permute-start | bytes 4325384 | tf_op jit(solution)/shard_map/ppermute | solution.py:75
  356.0 34.2 %collective-permute-start.19 = (bf16[2,256,1408]{2,1,0:T(8,128)(2,1)}, bf16[2,256,1408]{2,1,0:T(8,128)(2,1)S(1)}, u32[]{:S(2)}, u32[]{:S(2)}) collective-permute-start(bf16[2,256,1408]{2,1,0:T(8,128)(2,1)} %dynamic-slice_bitcast_fusion.1), channel_id=1, source_target_pairs={{0,2},{2,0},{1,3},{3,1},{4,6},{6,4},{5,7},{7,5},{8,10},{10,8},{9,1... | collective-permute-start | bytes 4325384 | tf_op jit(solution)/shard_map/ppermute | solution.py:75
  367.1 23.1 %copy-start.14 = (bf16[2,2,256,1408]{3,2,1,0:T(8,128)(2,1)S(1)}, bf16[2,2,256,1408]{3,2,1,0:T(8,128)(2,1)}, u32[]{:S(2)}) copy-start(bf16[2,2,256,1408]{3,2,1,0:T(8,128)(2,1)} %copy-done.13) | copy-start | bytes 8650756
  401.9 179.5 %reduce-scatter.14.cloned.1.call-start = ((), (), s32[]{:S(2)}) async-start(), calls=%async_computation.17 | async-start | bytes 3604480 | tf_op jit(solution)/shard_map/reduce_scatter | solution.py:38
  402.0 24.8 %copy-start.24 = (bf16[2,256,1408]{2,1,0:T(8,128)(2,1)S(1)}, bf16[2,256,1408]{2,1,0:T(8,128)(2,1)}, u32[]{:S(2)}) copy-start(bf16[2,256,1408]{2,1,0:T(8,128)(2,1)} %fusion.4) | copy-start | bytes 4325380
  403.3 23.5 %collective-permute-start.21 = (bf16[256,1408]{1,0:T(8,128)(2,1)S(1)}, bf16[256,1408]{1,0:T(8,128)(2,1)S(1)}, u32[]{:S(2)}, u32[]{:S(2)}) collective-permute-start(bf16[256,1408]{1,0:T(8,128)(2,1)S(1)} %dynamic-slice_bitcast_fusion.3), channel_id=1, source_target_pairs={{0,4},{4,0},{1,5},{5,1},{2,6},{6,2},{3,7},{7,3},{8,12},{12,8},{9,1... | collective-permute-start | bytes 2162696 | tf_op jit(solution)/shard_map/ppermute | solution.py:75
  404.9 23.3 %collective-permute-start.20 = (bf16[256,1408]{1,0:T(8,128)(2,1)S(1)}, bf16[256,1408]{1,0:T(8,128)(2,1)S(1)}, u32[]{:S(2)}, u32[]{:S(2)}) collective-permute-start(bf16[256,1408]{1,0:T(8,128)(2,1)S(1)} %dynamic-slice_bitcast_fusion.4), channel_id=1, source_target_pairs={{0,2},{2,0},{1,3},{3,1},{4,6},{6,4},{5,7},{7,5},{8,10},{10,8},{9,1... | collective-permute-start | bytes 2162696 | tf_op jit(solution)/shard_map/ppermute | solution.py:75
  429.6 16.4 %copy-start.2 = (f32[1024,256]{1,0:T(8,128)S(1)}, f32[1024,256]{1,0:T(8,128)}, u32[]{:S(2)}) copy-start(f32[1024,256]{1,0:T(8,128)} %copy-done.1) | copy-start | bytes 3145732
  444.3 139.7 %reduce-scatter.10.cloned.1.call-start = ((), (), s32[]{:S(2)}) async-start(), calls=%async_computation.15 | async-start | bytes 4718592 | tf_op jit(solution)/shard_map/reduce_scatter | solution.py:38
  464.9 4.5 collective-permute-start.22
  474.9 17.0 %collective-permute-start.25 = (bf16[128,2048]{1,0:T(8,128)(2,1)}, bf16[128,2048]{1,0:T(8,128)(2,1)}, u32[]{:S(2)}, u32[]{:S(2)}) collective-permute-start(bf16[128,2048]{1,0:T(8,128)(2,1)} %get-tuple-element.131), channel_id=1, source_target_pairs={{0,8},{8,16},{16,24},{24,0},{1,9},{9,17},{17,25},{25,1},{2,10},{10... | collective-permute-start | bytes 1572872 | tf_op jit(solution)/shard_map/ppermute | solution.py:121
  476.4 38.1 %collective-permute-start.24 = (bf16[128,2048]{1,0:T(8,128)(2,1)}, bf16[128,2048]{1,0:T(8,128)(2,1)}, u32[]{:S(2)}, u32[]{:S(2)}) collective-permute-start(bf16[128,2048]{1,0:T(8,128)(2,1)} %get-tuple-element.132), channel_id=1, source_target_pairs={{0,16},{8,24},{16,0},{24,8},{1,17},{9,25},{17,1},{25,9},{2,18},{10... | collective-permute-start | bytes 1572872 | tf_op jit(solution)/shard_map/ppermute | solution.py:121
  478.8 35.7 %collective-permute-start.23 = (bf16[128,2048]{1,0:T(8,128)(2,1)}, bf16[128,2048]{1,0:T(8,128)(2,1)}, u32[]{:S(2)}, u32[]{:S(2)}) collective-permute-start(bf16[128,2048]{1,0:T(8,128)(2,1)} %get-tuple-element.130), channel_id=1, source_target_pairs={{0,24},{8,0},{16,8},{24,16},{1,25},{9,1},{17,9},{25,17},{2,26},{10... | collective-permute-start | bytes 1572872 | tf_op jit(solution)/shard_map/ppermute | solution.py:121
  480.3 75.7 %all-to-all-start.2 = ((bf16[8,64,1408]{2,1,0:T(8,128)(2,1)}), bf16[8,64,1408]{2,1,0:T(8,128)(2,1)}, u32[]{:S(2)}, u32[]{:S(2)}) async-start(bf16[8,64,1408]{2,1,0:T(8,128)(2,1)} %bitcast.214), calls=%async_computation.4 | async-start | bytes 2883584 | tf_op jit(solution)/shard_map/all_to_all | solution.py:42
  484.5 148.5 %reduce-scatter.12.cloned.1.call-start = ((), (), s32[]{:S(2)}) async-start(), calls=%async_computation.16 | async-start | bytes 5242880 | tf_op jit(solution)/shard_map/reduce_scatter | solution.py:38
  636.9 18.5 %all-to-all-start.3 = ((bf16[8,64,768]{2,1,0:T(8,128)(2,1)}), bf16[8,64,768]{2,1,0:T(8,128)(2,1)}, u32[]{:S(2)}, u32[]{:S(2)}) async-start(bf16[8,64,768]{2,1,0:T(8,128)(2,1)} %bitcast.218), calls=%async_computation.8 | async-start | bytes 1572864 | tf_op jit(solution)/shard_map/all_to_all | solution.py:42
  676.1 1.4 collective-permute-start.26
  678.1 3.7 collective-permute-start.27
  682.3 3.7 collective-permute-start.28
  686.6 3.7 collective-permute-start.29
  690.9 4.6 collective-permute-start.30
  (50 other events, 316.5 us)
Sparse Core Ops, SparseCore 0:
  53.4 81.8 all-gather.4
  154.8 57.1 reduce-scatter.5
  214.3 47.1 all-gather.6
  267.0 46.5 all-gather.8
  341.8 48.2 reduce-scatter.7
  402.1 42.1 all-gather.10
  447.6 41.7 reduce-scatter.13
  493.1 51.3 reduce-scatter.9
  556.0 76.9 reduce-scatter.11

commit v3 on v2

--- a/solution.py
+++ b/solution.py
@@ -65,14 +65,22 @@
     return jnp.stack(places)
 
 
-def ring_scatter(value, axis):
+def added(terms):
+    return sum(term.astype(F32) for term in terms)
+
+
+def ring_scatter(value, axis, dim=0):
+    return added(ring_terms(value, axis, dim))
+
+
+def ring_terms(value, axis, dim=0):
     count, mine = lax.axis_size(axis), lax.axis_index(axis)
 
     def block(back):
-        return lax.dynamic_index_in_dim(value, (mine - back) % count, 0, False)
+        return lax.dynamic_index_in_dim(value, (mine - back) % count, dim, False)
 
     if count == 2:
-        return block(0).astype(F32) + lax.ppermute(block(1), axis, [(0, 1), (1, 0)]).astype(F32)
+        return [block(0), lax.ppermute(block(1), axis, [(0, 1), (1, 0)])]
     up = down = None
     for hop in range(1, count):
         up_sum, down_sum = block(hop), block(count - hop)
@@ -81,7 +89,7 @@
             down_sum = (down_sum.astype(F32) + down.astype(F32)).astype(BF)
         up = lax.ppermute(up_sum, axis, [(i, i + 1) for i in range(hop)])
         down = lax.ppermute(down_sum, axis, [(i, i - 1) for i in range(count - hop, count)])
-    return block(0).astype(F32) + up.astype(F32) + down.astype(F32)
+    return [block(0), up, down]
 
 
 def double_gather(value):
@@ -106,7 +114,7 @@
     rest = value - upper.astype(F32)
     middle = rest.astype(BF)
     lower = (rest - middle.astype(F32)).astype(BF)
-    return [upper[:, None], middle[:, None], lower[:, None]]
+    return [upper, middle, lower]
 
 
 def as_stored(value):
@@ -122,12 +130,18 @@
     return total
 
 
+def quad_halves(value, axis):
+    half = value.shape[axis] // 2
+    first = ring_gather(lax.slice_in_dim(value, 0, half, axis=axis), "x")
+    return [first, ring_gather(lax.slice_in_dim(value, half, 2 * half, axis=axis), "y")]
+
+
+def quad_others(first, second):
+    return [ring_gather(first, "y"), ring_gather(second, "x").swapaxes(0, 1)]
+
+
 def quad_parts(value, axis):
-    half = value.shape[axis] // 2
-    first = ring_gather(ring_gather(lax.slice_in_dim(value, 0, half, axis=axis), "x"), "y")
-    second = lax.slice_in_dim(value, half, 2 * half, axis=axis)
-    second = ring_gather(ring_gather(second, "y"), "x").swapaxes(0, 1)
-    return [first, second]
+    return quad_others(*quad_halves(value, axis))
 
 
 def quad_whole(parts):
@@ -137,11 +151,13 @@
 def quad_sums(value):
     value = value.reshape(lax.axis_size("y"), lax.axis_size("x"), -1, value.shape[1])
     half = value.shape[2] // 2
-    first = ring_scatter(value[:, :, :half], "y").astype(BF)
-    return first, ring_scatter(value[:, :, half:].swapaxes(0, 1), "x").astype(BF)
-
-
-def quad_rest(first, second):
+    first = ring_terms(value[:, :, :half], "y")
+    return first + ring_terms(value[:, :, half:].swapaxes(0, 1), "x")
+
+
+def quad_rest(*terms):
+    half = len(terms) // 2
+    first, second = added(terms[:half]).astype(BF), added(terms[half:]).astype(BF)
     return jnp.concatenate([ring_scatter(first, "x"), ring_scatter(second, "y")], axis=0)
 
 
@@ -155,9 +171,60 @@
     return both.swapaxes(0, 1).reshape(-1, value.shape[1])
 
 
-def line_scatter(value):
+def plane_scatter(value):
+    value = value.reshape(lax.axis_size("y"), lax.axis_size("x"), 2, -1, value.shape[1])
+    value = ring_scatter(value, "c", 2).astype(BF)
+    half = value.shape[3] // 2
+    first = ring_scatter(ring_scatter(value[..., :half], "y").astype(BF), "x")
+    second = ring_scatter(ring_scatter(value[..., half:], "x", 1).astype(BF), "y")
+    return jnp.concatenate([first, second], axis=1)
+
+
+def direct_gather(value, axis):
+    count = lax.axis_size(axis)
+    hops = [[(i, (i + back) % count) for i in range(count)] for back in range(1, count)]
+    return [value] + [lax.ppermute(value, axis, hop) for hop in hops]
+
+
+def in_order(values, axis):
+    count, mine = lax.axis_size(axis), lax.axis_index(axis)
+    places = []
+    for place in range(count):
+        found = values[0]
+        for back in range(1, count):
+            found = jnp.where((mine - back) % count == place, values[back], found)
+        places.append(found)
+    return jnp.stack(places)
+
+
+def core_exchange(value):
+    count, core = lax.axis_size("z"), lax.axis_index("c")
+    value = value.reshape((count, 2) + value.shape[1:])
+    kept = lax.dynamic_index_in_dim(value, core, 1, False)
+    other = lax.dynamic_index_in_dim(value, 1 - core, 1, False)
+    other = lax.ppermute(other, "c", [(0, 1), (1, 0)])
+    first, second = jnp.where(core == 0, kept, other), jnp.where(core == 0, other, kept)
+    return jnp.stack([first, second], axis=1)
+
+
+def line_exchange(value):
+    count, mine = lax.axis_size("z"), lax.axis_index("z")
+    blocks = [lax.dynamic_index_in_dim(value, (mine - back) % count, 0, False) for back in range(count)]
+    got = [blocks[0]]
+    for back in range(1, count):
+        got.append(lax.ppermute(blocks[back], "z", [(i, (i - back) % count) for i in range(count)]))
+    places = []
+    for place in range(count):
+        found = got[0]
+        for back in range(1, count):
+            found = jnp.where((mine + back) % count == place, got[back], found)
+        places.append(found)
+    return jnp.concatenate(places)
+
+
+def core_terms(value):
     value = value.reshape(lax.axis_size("z"), 2, -1, value.shape[1]).swapaxes(0, 1)
-    return direct_scatter(ring_scatter(value, "c").astype(BF), "z")
+    return ring_terms(value, "c")
 
 
 def total_of(value):
@@ -191,11 +258,8 @@
 def adam_step(weight, first, second, grad, rate, decay_w):
     first_new = BETA_ONE * first + (1.0 - BETA_ONE) * grad
     second_new = BETA_TWO * second + (1.0 - BETA_TWO) * grad * grad
-    step_size = (
-        first_new
-        / (1.0 - BETA_ONE**STEP)
-        / (jnp.sqrt(second_new / (1.0 - BETA_TWO**STEP)) + ADAM_EPS)
-    )
+    scale_one, scale_two = 1.0 / (1.0 - BETA_ONE**STEP), 1.0 / (1.0 - BETA_TWO**STEP)
+    step_size = (first_new * scale_one) / (jnp.sqrt(second_new * scale_two) + ADAM_EPS)
     return (weight - rate * (step_size + decay_w * weight), first_new, second_new)
 
 
@@ -271,6 +335,146 @@
         return passed[:1, :]
 
     lax.fori_loop(0, rows // TILE, step, jnp.zeros((1, width), F32), unroll=4)
+
+
+def settle(got_ref, out_ref, low_ref, grad_ref, first_ref, inner_ref, total_ref):
+    spots, own, packed = got_ref.shape
+    width = out_ref.shape[1]
+    planes = packed // (3 * own)
+    low_half = lax.broadcasted_iota(jnp.int32, (own, 2 * own), 1) < own
+    total = jnp.zeros((own, 2 * own), F32)
+    first, inner = total, total
+    for pair in range(0, spots, 2):
+        for kind in range(3):
+            for plane in range(0, planes, 2):
+                at = pl.ds((kind * planes + plane) * own, 2 * own)
+                even = got_ref[pair, :, at].astype(F32)
+                odd = got_ref[pair + 1, :, at].astype(F32)
+                near = jnp.where(low_half, even, pltpu.roll(odd, own, 1))
+                far = jnp.where(low_half, pltpu.roll(even, own, 1), odd)
+                for step, grad in enumerate((near, far)):
+                    place = pl.ds(((plane + step) * spots + pair) * own, 2 * own)
+                    grad_ref[kind, :, place] = grad
+                    total += grad * grad
+                    first += grad * low_ref[kind, :, place].astype(F32)
+    for start in range(0, width, 2 * own):
+        place = pl.ds(start, 2 * own)
+        grad = out_ref[:, place].astype(F32)
+        grad_ref[3, :, place] = grad
+        total += grad * grad
+        inner += grad * low_ref[3, :, place].astype(F32)
+    first_ref[...] = jnp.sum(first, axis=1, keepdims=True)
+    inner_ref[...] = jnp.sum(inner, axis=1, keepdims=True)
+    total_ref[...] = jnp.sum(total, axis=1, keepdims=True)
+
+
+def run_settle(got, shard_out, low_mixer):
+    spots, own, packed = got.shape
+    width = shard_out.shape[1]
+    planes = packed // (3 * own)
+    if 2 * own != 128 or planes % 2 != 0:
+        grad = got.reshape(spots, own, 3, planes, own).transpose(1, 2, 3, 0, 4)
+        grad = jnp.concatenate([grad.reshape(own, 3, width), shard_out[:, None, :]], axis=1)
+        grad = grad.astype(F32)
+        product = jnp.sum(grad * low_mixer.astype(F32), axis=2)
+        return grad, jnp.sum(product[:, :3], axis=1), product[:, 3], jnp.sum(grad * grad, axis=(1, 2))
+    column = jax.ShapeDtypeStruct((own, 1), F32)
+    grad, *sums = pl.pallas_call(
+        settle,
+        out_shape=[jax.ShapeDtypeStruct((4, own, width), F32)] + [column] * 3,
+        compiler_params=pltpu.CompilerParams(vmem_limit_bytes=48 * 2**20),
+    )(got, shard_out, low_mixer.swapaxes(0, 1))
+    return [grad.swapaxes(0, 1)] + [column[:, 0] for column in sums]
+
+
+def column_blocks(width, first, second):
+    size = width // (first * second)
+    for i in range(first):
+        for j in range(second):
+            yield pl.ds((i * second + j) * size, size), pl.ds((j * first + i) * size, size)
+
+
+def enter_glu(order, mix_ref, x_ref, gain_ref, after_ref, n2_ref, mid_ref, home_ref):
+    width = x_ref.shape[1]
+    squares = jnp.sum(mix_ref[:, width:].astype(F32), axis=1, keepdims=True)
+    home = lax.rsqrt(squares / width + EPS_NORM)
+    after = x_ref[...].astype(F32) + mix_ref[:, :width].astype(F32) * home
+    mid = lax.rsqrt(jnp.mean(after * after, axis=1, keepdims=True) + EPS_NORM)
+    after_ref[...] = after
+    mid_ref[...] = mid
+    home_ref[...] = home
+    n2 = (after * mid * gain_ref[...]).astype(BF)
+    for source, target in column_blocks(width, *order):
+        n2_ref[:, target] = n2[:, source.start : source.start + source.size]
+
+
+def leave_glu(
+    order, d_n2_ref, cot_ref, after_ref, mid_ref, mix_ref, home_ref, gain_ref, d_mid_ref, out_ref, held_ref
+):
+    width = cot_ref.shape[1]
+    mid, home = mid_ref[...], home_ref[...]
+    for target, source in column_blocks(width, *order):
+        held_ref[:, target] = d_n2_ref[:, source].astype(F32) * gain_ref[:, target]
+    normed = after_ref[...] * mid
+    grad = held_ref[...]
+    inner = jnp.mean(grad * normed, axis=1, keepdims=True)
+    d_mid = cot_ref[...].astype(F32) + mid * (grad - normed * inner)
+    d_mid_ref[...] = d_mid
+    low = d_mid.astype(BF)
+    out_ref[:, :width] = low
+    mean = jnp.sum(low.astype(F32) * (mix_ref[:, :width].astype(F32) * home), axis=1, keepdims=True) / width
+    lane = lax.broadcasted_iota(jnp.int32, (mid.shape[0], 128), 1)
+    riders = jnp.zeros((mid.shape[0], 128), F32)
+    for at, value in ((0, mean), (3, home)):
+        for part in range(3):
+            upper = value.astype(BF).astype(F32)
+            riders = jnp.where(lane == at + part, upper, riders)
+            value = value - upper
+    out_ref[:, width:] = riders.astype(BF)
+
+
+def run_enter(mix_raw, tokens, gain, order):
+    rows, width = tokens.shape
+    if width // (order[0] * order[1]) % 128 != 0:
+        squares = jnp.sum(mix_raw[:, width:].astype(F32), axis=1, keepdims=True)
+        home = lax.rsqrt(squares / width + EPS_NORM)
+        after = tokens.astype(F32) + mix_raw[:, :width].astype(F32) * home
+        normed, mid = normalize(after)
+        n2 = (normed * gain).astype(BF).reshape(rows, *order, -1).swapaxes(1, 2)
+        return after, n2.reshape(rows, width), mid, home
+    column = jax.ShapeDtypeStruct((rows, 1), F32)
+    return pl.pallas_call(
+        functools.partial(enter_glu, order),
+        out_shape=[
+            jax.ShapeDtypeStruct((rows, width), F32),
+            jax.ShapeDtypeStruct((rows, width), BF),
+            column,
+            column,
+        ],
+        compiler_params=pltpu.CompilerParams(vmem_limit_bytes=48 * 2**20),
+    )(mix_raw, tokens, gain)
+
+
+def run_leave(d_n2, cot, after, mid, mix_raw, home, gain, order):
+    rows, width = cot.shape
+    if width // (order[0] * order[1]) % 128 != 0:
+        grad = d_n2.reshape(rows, order[1], order[0], -1).swapaxes(1, 2).reshape(rows, width)
+        d_mid = cot.astype(F32) + norm_back(grad.astype(F32) * gain, after * mid, mid)
+        low = d_mid.astype(BF)
+        mix = mix_raw[:, :width].astype(F32) * home
+        mean = jnp.sum(low.astype(F32) * mix, axis=1, keepdims=True) / width
+        riders = jnp.concatenate(in_parts_of(mean) + in_parts_of(home), axis=1)
+        riders = jnp.pad(riders, ((0, 0), (0, 128 - riders.shape[1])))
+        return d_mid, jnp.concatenate([low, riders], axis=1)
+    return pl.pallas_call(
+        functools.partial(leave_glu, order),
+        out_shape=[
+            jax.ShapeDtypeStruct((rows, width), F32),
+            jax.ShapeDtypeStruct((rows, width + 128), BF),
+        ],
+        scratch_shapes=[pltpu.VMEM((rows, width), F32)],
+        compiler_params=pltpu.CompilerParams(vmem_limit_bytes=48 * 2**20),
+    )(d_n2, cot, after, mid, mix_raw, home, gain)
 
 
 def run_forward(proj, started, gap):
@@ -323,30 +527,6 @@
     spot = lax.axis_index(PLANE)
     chans = planes * own
 
-    low_mixer = mixer_w.astype(BF)
-    sent = low_mixer[:, :3, :].reshape(own, 3, planes, spots, own).transpose(3, 0, 1, 2, 4)
-    x_low, sent, low_gains = tied(tokens, sent.reshape(spots, own, 3 * chans), gains)
-    part = exchange(sent, PLANE)
-    part = jnp.concatenate(
-        [part.reshape(spots * own, 3 * chans), low_mixer[:, 3, :].reshape(spots * own, chans)], axis=1
-    )
-    x_parts = quad_parts(x_low, 1)
-    full_gains = double_gather(low_gains).swapaxes(0, 1).reshape(3, width)
-    low_in = mlp_in.astype(BF)
-    inner = quads * down_rows
-    sent_in = low_in.reshape(own, 2, planes, quads, pairs, down_rows).transpose(2, 4, 0, 1, 3, 5)
-    sent_in = sent_in.reshape(planes * pairs, own, 2 * inner)
-    part, sent_in = tied(part, sent_in)
-    w_all = gather(part, "z")
-    w_proj = w_all[:, : 3 * chans]
-    w_out = w_all[:, 3 * chans :].reshape(chans, width)
-    x_all = core_gather(x_parts)
-
-    bound = lower_bound.reshape(planes, spots, own)
-    gap = (1.0 - lax.dynamic_index_in_dim(bound, spot, 1, False)).reshape(1, chans)
-    gain_mid = full_gains[1].reshape(planes, spots, own)
-    gain_mid = lax.dynamic_index_in_dim(gain_mid, spot, 1, False).reshape(1, chans)
-
     ends = jnp.cumsum(lengths)
     starts = ends - lengths
     places = jnp.arange(group, dtype=jnp.int32)
@@ -354,20 +534,43 @@
     home = spot * rows + jnp.arange(rows, dtype=jnp.int32)
     valid = (home < ends[-1]).astype(F32)
 
-    def swapped(value, first, second):
-        return value.reshape(rows, first, second, -1).swapaxes(1, 2).reshape(rows, width)
+    cot_low = (cotangent.astype(F32) * valid[:, None]).astype(BF)
+
+    low_mixer = mixer_w.astype(BF)
+    sent = low_mixer[:, :3, :].reshape(own, 3, planes, spots, own).transpose(3, 0, 1, 2, 4)
+    part = exchange(sent.reshape(spots, own, 3 * chans), PLANE)
+    part = jnp.concatenate(
+        [part.reshape(spots * own, 3 * chans), low_mixer[:, 3, :].reshape(spots * own, chans)], axis=1
+    )
+    x_low, part, low_gains, low_down, low_in = tied(tokens, part, gains, mlp_down, mlp_in)
+    x_parts = quad_parts(x_low, 1)
+    full_gains = double_gather(low_gains).swapaxes(0, 1).reshape(3, width)
+    low_in = low_in.astype(BF)
+    inner = quads * down_rows
+    sent_in = low_in.reshape(own, 2, planes, quads, pairs, down_rows).transpose(2, 4, 0, 1, 3, 5)
+    sent_in = sent_in.reshape(planes * pairs, own, 2 * inner)
+    w_down = quad_whole(quad_parts(low_down.astype(BF), 0))
+    w_all = gather(part, "z")
+    x_all = core_gather(x_parts)
+
+    bound = lower_bound.reshape(planes, spots, own)
+    gap = (1.0 - lax.dynamic_index_in_dim(bound, spot, 1, False)).reshape(1, chans)
+    gain_mid = full_gains[1].reshape(planes, spots, own)
+    gain_mid = lax.dynamic_index_in_dim(gain_mid, spot, 1, False).reshape(1, chans)
 
     x = tokens.astype(F32)
     x_normed, x_factor = normalize(x)
     n1 = (normalize(x_all.astype(F32))[0] * full_gains[0]).astype(BF)
-    cot = cotangent.astype(F32) * valid[:, None]
-    cot_low = cot.astype(BF)
+    blocks_in = core_exchange(sent_in)
+    w_all, w_down, n1, blocks_in = tied(w_all, w_down, n1, blocks_in)
+    w_proj = w_all[:, : 3 * chans]
+    w_out = w_all[:, 3 * chans :].reshape(chans, width)
     proj = jnp.dot(n1, w_proj, preferred_element_type=F32)
-    proj, sent_in = tied(proj, sent_in)
-    part_in = exchange(sent_in, LINE)
-    cot_low, part_in = tied(cot_low, part_in)
-    cot_all = gather(cot_low, LINE)
+    proj, blocks_in = tied(proj, blocks_in)
+    part_in = line_exchange(blocks_in)
     state, squares = run_forward(proj[:, : 2 * chans], started, gap)
+    state, held_cot = tied(state, cot_low)
+    cots = direct_gather(held_cot, "z")
     gate_proj = proj[:, 2 * chans :]
     gate_act = silu(gate_proj)
     raw = (state * gain_mid * gate_act).astype(BF)
@@ -378,20 +581,14 @@
     ride = jnp.pad(jnp.eye(128, dtype=BF), ((chans, 0), (width, 0)))
     w_ride = ride + jnp.pad(w_out, ((0, 128), (0, 128)))
     mix_part = jnp.dot(raw, w_ride, preferred_element_type=F32).astype(BF)
-    in_parts = quad_parts(part_in.reshape(planes * pairs * own, 2 * inner), 0)
-    mix_raw = scatter(mix_part, PLANE)
-    mix_raw, cot_all, *in_parts = tied(mix_raw, cot_all, *in_parts)
-    w_in = quad_whole(in_parts)
-    squares = jnp.sum(mix_raw[:, width : width + 2 * spots].astype(F32), axis=1)
-    home_factor = lax.rsqrt(squares / width + EPS_NORM)
-    mix = mix_raw[:, :width].astype(F32) * home_factor[:, None]
-    after_mix = x + mix
-
-    mid_normed, mid_factor = normalize(after_mix)
-    n2_home = swapped((mid_normed * full_gains[2]).astype(BF), planes, quads)
-    low_down, n2_home = tied(mlp_down.astype(BF), n2_home)
-    w_down = quad_whole(quad_parts(low_down, 0))
-    n2, w_down = tied(gather(n2_home, LINE), w_down)
+    mix_raw, part_in, *cots = tied(scatter(mix_part, PLANE), part_in, *cots)
+    cot_all = ring_gather(in_order(cots, "z"), "c").swapaxes(0, 1)
+    cot_all = cot_all.reshape(planes * pairs * rows, width)
+    w_in = quad_whole(quad_parts(part_in.reshape(planes * pairs * own, 2 * inner), 0))
+
+    order, gain_glu = (planes, quads), full_gains[2].reshape(1, width)
+    after_mix, n2_home, mid_factor, home_factor = run_enter(mix_raw, tokens, gain_glu, order)
+    n2 = gather(n2_home, LINE)
     gate_up = jnp.dot(n2, w_in, preferred_element_type=F32)
     gate, up_value = gate_up[:, :inner], gate_up[:, inner:]
     silu_gate = silu(gate)
@@ -404,22 +601,23 @@
     d_up = d_hidden * silu_gate
     d_gate_up = jnp.concatenate([d_gate.astype(BF), d_up.astype(BF)], axis=1)
     d_n2 = lax.dot_general(d_gate_up, w_in, (((1,), (1,)), ((), ())), preferred_element_type=F32)
-    d_n2 = swapped(scatter(d_n2.astype(BF), LINE).astype(F32), quads, planes)
+    d_n2 = scatter(d_n2.astype(BF), LINE)
     grad_in = lax.dot_general(n2, d_gate_up, (((0,), (0,)), ((), ())), preferred_element_type=F32)
     grad_in = grad_in.astype(BF)
     down = jnp.dot(hidden, w_down, preferred_element_type=F32).astype(BF)
     sums_in = quad_sums(grad_in)
-    d_n2, grad_down, down, *sums_in = tied(d_n2, grad_down, down, *sums_in)
-    d_mid = cot + norm_back(d_n2 * full_gains[2], mid_normed, mid_factor)
-    d_mix_home = d_mid.astype(BF)
-    down, d_mix_home = tied(down, d_mix_home)
-    down = line_scatter(down)
+    downs = core_terms(down)
+    d_n2, grad_down, *held_terms = tied(d_n2, grad_down, *downs, *sums_in)
+    downs, sums_in = held_terms[: len(downs)], held_terms[len(downs) :]
+    d_mid, d_mix_home = run_leave(
+        d_n2, cot_low, after_mix, mid_factor, mix_raw, home_factor, gain_glu, order
+    )
+    *downs, d_mix_home = tied(*downs, d_mix_home)
+    down = direct_scatter(added(downs).astype(BF), "z")
     shard_in = quad_rest(*sums_in).astype(BF)
-    mean = jnp.sum(d_mix_home.astype(F32) * mix, axis=-1) / width
-    riders = jnp.concatenate(in_parts_of(mean) + in_parts_of(home_factor), axis=1)
-    riders = jnp.pad(riders, ((0, 0), (0, 128 - riders.shape[1])))
-    d_mix = gather(jnp.concatenate([d_mix_home, riders], axis=1), PLANE)
-    d_mix, shard_in, grad_down = tied(d_mix, shard_in, grad_down)
+    d_mix = gather(d_mix_home, PLANE)
+    d_mix, shard_in, grad_down, down = tied(d_mix, shard_in, grad_down, down)
+    block_out = (after_mix + down).astype(BF)
     riders = d_mix[:, width : width + 6].astype(F32)
     mean = jnp.sum(riders[:, :3], axis=1, keepdims=True)
     factor = jnp.sum(riders[:, 3:], axis=1, keepdims=True)
@@ -444,38 +642,25 @@
     grad_all = jnp.concatenate(
         [grad_proj.astype(BF).reshape(planes, spots * own, 3 * chans), grad_out], axis=2
     )
-    grad_all, down, got_in = tied(grad_all, down, got_in)
-    block_out = (after_mix + down).astype(BF)
+    grad_all, got_in, held_proj = tied(grad_all, got_in, d_proj)
     shard_all = scatter(grad_all.reshape(planes * spots * own, 4 * chans), "z")
     shard_in = got_in.reshape(planes, pairs, own, 2, quads, down_rows).transpose(2, 3, 0, 4, 1, 5)
     shard_in = as_stored(shard_in.reshape(own, 2, hidden_width).astype(F32))
-    shard_all, shard_in, shard_down = tied(shard_all, shard_in, shard_down)
-    shard_proj = shard_all[:, : 3 * chans]
-    shard_out = shard_all[:, 3 * chans :].reshape(own, width).astype(F32)
-    shard_proj = exchange(shard_proj.reshape(spots, own, 3 * chans), PLANE)
-    shard_proj = shard_proj.reshape(spots, own, 3, planes, own).transpose(1, 2, 3, 0, 4)
-    shard_proj = shard_proj.reshape(own, 3, width).astype(F32)
-    d_n1 = lax.dot_general(d_proj, w_proj, (((1,), (1,)), ((), ())), preferred_element_type=F32)
-    d_n1 = scatter(d_n1.astype(BF), PLANE).astype(F32)
+    gain_in = jnp.sum(shard_in * low_in.astype(F32), axis=(1, 2))
+    total_early = jnp.sum(shard_in * shard_in) + jnp.sum(shard_down * shard_down)
+    d_n1 = lax.dot_general(held_proj, w_proj, (((1,), (1,)), ((), ())), preferred_element_type=F32)
+    d_n1 = plane_scatter(d_n1.astype(BF))
     input_grad = d_mid + norm_back(d_n1 * full_gains[0], x_normed, x_factor)
-
-    low_rows = low_mixer.astype(F32)
-    shard_gains = jnp.stack(
-        [
-            jnp.sum(shard_proj * low_rows[:, :3, :], axis=(1, 2)),
-            jnp.sum(shard_out * low_rows[:, 3, :], axis=1),
-            jnp.sum(shard_in * low_in.astype(F32), axis=(1, 2)),
-        ],
-        axis=0,
-    ) / gains
-    shard_mixer = as_stored(jnp.concatenate([shard_proj, shard_out[:, None, :]], axis=1))
-
-    local_total = (
-        jnp.sum(shard_mixer * shard_mixer)
-        + jnp.sum(shard_in * shard_in)
-        + jnp.sum(shard_down * shard_down)
-        + jnp.sum(shard_gains * shard_gains)
-    )
+    shard_all, shard_in, shard_down, gain_in, total_early, input_grad = tied(
+        shard_all, shard_in, shard_down, gain_in, total_early, input_grad
+    )
+    got_proj = exchange(shard_all[:, : 3 * chans].reshape(spots, own, 3 * chans), PLANE)
+    shard_out = shard_all[:, 3 * chans :].reshape(own, width)
+
+    shard_mixer, gain_first, gain_inner, total_mixer = run_settle(got_proj, shard_out, low_mixer)
+    shard_mixer = as_stored(shard_mixer)
+    shard_gains = jnp.stack([gain_first, gain_inner, gain_in]) / gains
+    local_total = jnp.sum(total_mixer) + total_early + jnp.sum(shard_gains * shard_gains)
     grad_norm = jnp.sqrt(total_of(local_total.reshape(1, 1))[0, 0])
     clip = jnp.minimum(1.0, CLIP_NORM / (grad_norm + 1e-06))
     new_mixer, new_mixer_m, new_mixer_v = adam_step(

time: 736 us -> 626 us (0.85)
  waiting for transfers between devices: 342 us -> 247 us
  other arithmetic: 107 us -> 89.2 us
  starting transfers between devices: 68.4 us -> 78.8 us
    all_gather x4 -> x3, waiting for transfers between devices: 69 us -> 8.96 us  [gather(): return lax.all_gather(value, axes, axis=0, tiled=True)]
    ppermute x5 -> x17, waiting for transfers between devices: 45.6 us -> 90.2 us  [the longest x3 37.3 us: direct_gather(): return [value] + [lax.ppermute(value, axis, hop) for hop in hops]]
    all_to_all x4 -> x3, waiting for transfers between devices: 56.5 us -> 21.1 us  [exchange(): return lax.all_to_all(value, axes, 0, 0, tiled=True)]
    reduce_scatter x5 -> x4, waiting for transfers between devices: 44.7 us -> 22.1 us  [scatter(): return lax.psum_scatter(value, axes, scatter_dimension=0, tiled=True)]
    convert_element_type x6 -> x0, local copies, waits for them, and re-layouts: 18.9 us -> none  [the longest x4 15.5 us: shards(): shard_proj = shard_proj.reshape(own, 3, width).astype(F32)]
    ppermute x13 -> x14, waiting for transfers between devices: 82.7 us -> 66.1 us  [ring_gather(): other = lax.ppermute(value, axis, [(0, 1), (1, 0)])]
    unnamed x108 -> x115, local copies, waits for them, and re-layouts: 5.95 us -> 18.1 us
    reshape x7 -> x2, local copies, waits for them, and re-layouts: 15.6 us -> 3.73 us  [the longest x1 3.6 us: shards(): part = exchange(sent.reshape(spots, own, 3 * chans), PLANE)]
  transfers between devices with their start and end apart: 44 -> 54, of which waited for: 29 -> 33; matrix products, arithmetic and copies ran while one was open for 23% -> 27% of each run, Pallas kernels for 1% -> 1%
where the time goes in v3:
time: 626 us; the launch traced here: 619 us
  waiting for transfers between devices  247 us (39%)
  local copies, waits for them, and re-layouts  97.1 us (16%)
  other arithmetic  89.2 us (14%)
  starting transfers between devices  78.8 us (13%)
  matrix products  70.6 us (11%)
  between operations  22.6 us (4%)
  Pallas kernels  14 us (2%)
    ppermute x14, waiting for transfers between devices, ring_gather(): other = lax.ppermute(value, axis, [(0, 1), (1, 0)])  66.1 us
    ppermute x3, waiting for transfers between devices, direct_gather(): return [value] + [lax.ppermute(value, axis, hop) for hop in hops]  37.3 us
    ppermute x10, waiting for transfers between devices, ring_terms(): return [block(0), lax.ppermute(block(1), axis, [(0, 1), (1, 0)])]  30 us
    ppermute x3, waiting for transfers between devices, direct_scatter(): lax.ppermute(block, axis, [(i, (i - back) % count) for i in range(count)])  26.3 us
    convert_element_type x3, local copies, waits for them, and re-layouts, shards(): shard_in = as_stored(shard_in.reshape(own, 2, hidden_width).astype(F32))  25.6 us
    sub x4, other arithmetic, adam_step(): weight - rate * (step_size + decay_w * weight)  23.7 us
    ppermute x3, waiting for transfers between devices, line_exchange(): lax.ppermute(blocks[back], 'z', [(i, (i - back) % count) for i in range(c...  22.9 us
    reduce_scatter x4, waiting for transfers between devices, scatter(): return lax.psum_scatter(value, axes, scatter_dimension=0, tiled=True)  22.1 us
  transfers between devices with their start and end apart: 54, of which 33 were waited for; matrix products, arithmetic and copies ran while one was open for 27% of the time, Pallas kernels for 1%

profile of v3, /device:TPU:0, one launch (start us, length us, event | category | flops | bytes accessed | tf_op | source)
XLA Modules:
  0.0 619.2 jit_solution(3799181881990367498)
XLA Ops:
  13.2 3.6 reshape.213
  16.8 5.3 all-to-all-start
  28.3 6.4 %all-to-all-done = bf16[8,64,768]{2,1,0:T(8,128)(2,1)S(1)} async-done(((bf16[8,64,768]{2,1,0:T(8,128)(2,1)}), bf16[8,64,768]{2,1,0:T(8,128)(2,1)S(1)}, u32[]{:S(2)}, u32[]{:S(2)}) %all-to-all-start) | async-done | bytes 786464 | tf_op jit(solution)/shard_map/all_to_all | solution.py:42
  50.8 9.2 %reshape.216 = bf16[64,2,4,4,2,176]{5,4,3,2,1,0:T(2,128)(2,1)S(1)} reshape(bf16[64,2,5632]{2,1,0:T(2,128)(2,1)} %convert_element_type.252) | data formatting | bytes 2883584 | tf_op jit(solution)/shard_map/reshape | solution.py:550
  62.1 4.6 reshape_reshape.3
  69.4 3.5 collective-permute-done.13
  80.3 9.1 %collective-permute-done.7 = bf16[2,128,1024]{2,1,0:T(8,128)(2,1)S(1)} collective-permute-done((bf16[2,128,1024]{2,1,0:T(8,128)(2,1)S(1)}, bf16[2,128,1024]{2,1,0:T(8,128)(2,1)S(1)}, u32[]{:S(2)}, u32[]{:S(2)}) %collective-permute-start.7) | collective-permute-done | bytes 524320 | tf_op jit(solution)/shard_map/ppermute | solution.py:48
  93.9 10.6 %collective-permute-done.3 = bf16[2,88,2048]{2,1,0:T(8,128)(2,1)S(1)} collective-permute-done((bf16[2,88,2048]{2,1,0:T(8,128)(2,1)S(1)}, bf16[2,88,2048]{2,1,0:T(8,128)(2,1)S(1)}, u32[]{:S(2)}, u32[]{:S(2)}) %collective-permute-start.3) | collective-permute-done | bytes 720928 | tf_op jit(solution)/shard_map/ppermute | solution.py:48
  113.3 7.2 %all-gather.4.cloned.1.call-done = bf16[2048,1024]{1,0:T(8,128)(2,1)} async-done(((bf16[512,1024]{1,0:T(8,128)(2,1)}), bf16[2048,1024]{1,0:T(8,128)(2,1)}) %all-gather.4.cloned.1.call-update) | async-done | bytes 4194320 | tf_op jit(solution)/shard_map/all_gather | solution.py:34
  122.3 6.7 %fusion.6 = f32[1024,768]{1,0:T(8,128)S(1)} fusion(bf16[1024,2048]{1,0:T(8,128)(2,1)} %fusion.1, bf16[2048,1024]{1,0:T(8,128)(2,1)} %all-gather.4.cloned.1.call-done), kind=kOutput, calls=%fused_computation.37 | convolution fusion | flops 3221225472 | bytes 10485760 | tf_op jit(solution)/shard_map/dot_general | solution.py:568
  129.3 5.7 shard_map.271
  136.3 3.6 convolution_convert_fusion.1
  148.2 7.5 %collective-permute-done.15 = bf16[2,64,1408]{2,1,0:T(8,128)(2,1)} collective-permute-done((bf16[2,64,1408]{2,1,0:T(8,128)(2,1)}, bf16[2,64,1408]{2,1,0:T(8,128)(2,1)}, u32[]{:S(2)}, u32[]{:S(2)}) %collective-permute-start.15) | collective-permute-done | bytes 360480 | tf_op jit(solution)/shard_map/ppermute | solution.py:215
  155.7 15.5 %collective-permute-done.16 = bf16[2,64,1408]{2,1,0:T(8,128)(2,1)} collective-permute-done((bf16[2,64,1408]{2,1,0:T(8,128)(2,1)S(1)}, bf16[2,64,1408]{2,1,0:T(8,128)(2,1)}, u32[]{:S(2)}, u32[]{:S(2)}) %collective-permute-start.16) | collective-permute-done | bytes 360480 | tf_op jit(solution)/shard_map/ppermute | solution.py:215
  174.0 8.3 %collective-permute-done.18 = bf16[128,2048]{1,0:T(8,128)(2,1)S(1)} collective-permute-done((bf16[128,2048]{1,0:T(8,128)(2,1)S(1)}, bf16[128,2048]{1,0:T(8,128)(2,1)S(1)}, u32[]{:S(2)}, u32[]{:S(2)}) %collective-permute-start.18) | collective-permute-done | bytes 524320 | tf_op jit(solution)/shard_map/ppermute | solution.py:186
  182.3 29.0 %collective-permute-done.19 = bf16[128,2048]{1,0:T(8,128)(2,1)S(1)} collective-permute-done((bf16[128,2048]{1,0:T(8,128)(2,1)S(1)}, bf16[128,2048]{1,0:T(8,128)(2,1)S(1)}, u32[]{:S(2)}, u32[]{:S(2)}) %collective-permute-start.19) | collective-permute-done | bytes 524320 | tf_op jit(solution)/shard_map/ppermute | solution.py:186
  220.8 11.1 %collective-permute-done.24 = bf16[256,1408]{1,0:T(8,128)(2,1)S(1)} collective-permute-done((bf16[256,1408]{1,0:T(8,128)(2,1)S(1)}, bf16[256,1408]{1,0:T(8,128)(2,1)S(1)}, u32[]{:S(2)}, u32[]{:S(2)}) %collective-permute-start.24) | collective-permute-done | bytes 720928 | tf_op jit(solution)/shard_map/ppermute | solution.py:48
  233.8 4.5 collective-permute-done.22
  242.5 26.2 %collective-permute-done.25 = bf16[2,256,1408]{2,1,0:T(8,128)(2,1)S(1)} collective-permute-done((bf16[2,256,1408]{2,1,0:T(8,128)(2,1)S(1)}, bf16[2,256,1408]{2,1,0:T(8,128)(2,1)S(1)}, u32[]{:S(2)}, u32[]{:S(2)}) %collective-permute-start.25) | collective-permute-done | bytes 1441824 | tf_op jit(solution)/shard_map/ppermute | solution.py:48
  271.8 4.7 pad_maximum_fusion
  276.5 10.7 %fusion.69 = f32[1024,1408]{0,1:T(8,128)S(1)} fusion(bf16[1024,2048]{1,0:T(8,128)(2,1)} %all-gather.6.cloned.1.call-done, bf16[2048,1408]{1,0:T(8,128)(2,1)} %bitcast.269), kind=kOutput, calls=%fused_computation.237 | convolution fusion | flops 5905580032 | bytes 15728640 | tf_op jit(solution)/shard_map/dot_general | solution.py:592
  287.3 5.3 multiply_convert_fusion.2
  294.1 8.3 %convolution_convert_fusion.3 = bf16[1024,2048]{1,0:T(8,128)(2,1)} fusion(bf16[2048,1408]{1,0:T(8,128)(2,1)S(1)} %bitcast.270, bf16[1024,704]{0,1:T(8,128)(2,1)S(1)} %get-tuple-element.152, bf16[1024,704]{0,1:T(8,128)(2,1)S(1)} %get-tuple-element.151), kind=kOutput, calls=%fused_computation.15 | convolution fusion | flops 5913444352 | bytes 12845056 | tf_op jit(solution)/shard_map/dot_general | solution.py:603
  303.0 5.7 convolution_convert_fusion.2
  313.3 7.0 %convolution_convert_fusion = bf16[2048,1408]{1,0:T(8,128)(2,1)S(1)} fusion(bf16[1024,2048]{1,0:T(8,128)(2,1)S(1)} %copy-done.49, bf16[1024,704]{0,1:T(8,128)(2,1)S(1)} %copy-done.55, bf16[1024,704]{0,1:T(8,128)(2,1)S(1)} %copy-done.53), kind=kOutput, calls=%fused_computation.4 | convolution fusion | flops 5914230784 | bytes 12845056 | tf_op jit(solution)/shard_map/dot_general | solution.py:605
  326.9 4.4 convolution_convert_fusion.6
  331.3 23.7 %collective-permute-done.27 = bf16[2,256,1408]{2,1,0:T(8,128)(2,1)} collective-permute-done((bf16[2,256,1408]{2,1,0:T(8,128)(2,1)}, bf16[2,256,1408]{2,1,0:T(8,128)(2,1)}, u32[]{:S(2)}, u32[]{:S(2)}) %collective-permute-start.27) | collective-permute-done | bytes 1441824 | tf_op jit(solution)/shard_map/ppermute | solution.py:83
  370.9 7.4 %collective-permute-start.33 = (bf16[128,2048]{1,0:T(8,128)(2,1)S(1)}, bf16[128,2048]{1,0:T(8,128)(2,1)S(1)}, u32[]{:S(2)}, u32[]{:S(2)}) collective-permute-start(bf16[128,2048]{1,0:T(8,128)(2,1)S(1)} %get-tuple-element.183), channel_id=1, source_target_pairs={{0,8},{8,16},{16,24},{24,0},{1,9},{9,17},{17,25},{25,1},{2,10},{10... | collective-permute-start | bytes 1572872 | tf_op jit(solution)/shard_map/ppermute | solution.py:129
  384.2 7.5 %collective-permute-done.33 = bf16[128,2048]{1,0:T(8,128)(2,1)S(1)} collective-permute-done((bf16[128,2048]{1,0:T(8,128)(2,1)S(1)}, bf16[128,2048]{1,0:T(8,128)(2,1)S(1)}, u32[]{:S(2)}, u32[]{:S(2)}) %collective-permute-start.33) | collective-permute-done | bytes 524320 | tf_op jit(solution)/shard_map/ppermute | solution.py:129
  391.8 18.8 %collective-permute-done.32 = bf16[128,2048]{1,0:T(8,128)(2,1)S(1)} collective-permute-done((bf16[128,2048]{1,0:T(8,128)(2,1)S(1)}, bf16[128,2048]{1,0:T(8,128)(2,1)S(1)}, u32[]{:S(2)}, u32[]{:S(2)}) %collective-permute-start.32) | collective-permute-done | bytes 524320 | tf_op jit(solution)/shard_map/ppermute | solution.py:129
  415.2 12.7 %all-to-all-start.1 = ((bf16[8,64,1408]{2,1,0:T(8,128)(2,1)}), bf16[8,64,1408]{2,1,0:T(8,128)(2,1)}, u32[]{:S(2)}, u32[]{:S(2)}) async-start(bf16[8,64,1408]{2,1,0:T(8,128)(2,1)} %bitcast.272), calls=%async_computation.3 | async-start | bytes 2883584 | tf_op jit(solution)/shard_map/all_to_all | solution.py:42
  429.5 4.3 fusion.37
  437.3 4.9 subtract_multiply_fusion
  442.2 5.6 shard_map.274
  450.7 3.8 convolution_convert_fusion.5
  457.1 6.0 all-to-all-done.1
  463.1 5.9 convolution_convert_fusion.4
  469.8 4.1 collective-permute-done.34
  479.7 8.8 %reshape.244 = f32[4,2,64,2,4,176]{5,4,3,2,1,0:T(4,128)} reshape(bf16[8,64,1408]{2,1,0:T(8,128)(2,1)} %all-to-all-done.1) | data formatting | bytes 4325376 | tf_op jit(solution)/shard_map/convert_element_type | solution.py:648
  488.5 7.5 %copy.78 = f32[64,2,4,4,2,176]{5,4,3,2,1,0:T(2,128)} copy(f32[64,2,4,4,2,176]{5,3,1,0,4,2:T(4,128)} %bitcast.266) | data formatting | bytes 5767168 | tf_op jit(solution)/shard_map/convert_element_type | solution.py:648
  496.0 9.3 %reshape.238 = f32[64,2,5632]{2,1,0:T(2,128)} reshape(f32[64,2,4,4,2,176]{5,4,3,2,1,0:T(2,128)} %copy.78) | data formatting | bytes 5767168 | tf_op jit(solution)/shard_map/convert_element_type | solution.py:648
  509.4 7.0 %multiply_reduce_fusion.1 = (f32[]{:T(128)}, f32[64]{0:T(128)S(1)}) fusion(f32[64,2,5632]{2,1,0:T(2,128)} %reshape.238, f32[64,2,5632]{2,1,0:T(2,128)S(1)} %copy-done.13), kind=kLoop, calls=%fused_computation.27 | loop fusion | flops 4325311 | bytes 5767428 | tf_op jit(solution)/shard_map/reduce_sum | solution.py:650
  524.8 19.5 %reduce-scatter.9.cloned.1.call-done = bf16[512,1024]{1,0:T(8,128)(2,1)} async-done(((bf16[2048,1024]{1,0:T(8,128)(2,1)}), bf16[512,1024]{1,0:T(8,128)(2,1)}) %reduce-scatter.9.cloned.1.call-update) | async-done | bytes 1048592 | tf_op jit(solution)/shard_map/reduce_scatter | solution.py:38
  546.4 3.9 all-to-all-start.2
  554.2 8.7 %all-to-all-done.2.got_ref = bf16[8,64,768]{2,1,0:T(8,128)(2,1)S(1)} async-done(((bf16[8,64,768]{2,1,0:T(8,128)(2,1)}), bf16[8,64,768]{2,1,0:T(8,128)(2,1)S(1)}, u32[]{:S(2)}, u32[]{:S(2)}) %all-to-all-start.2) | async-done | bytes 786464 | tf_op jit(solution)/shard_map/all_to_all | solution.py:42
  582.0 4.3 collective-permute-start.43
  587.2 9.0 %multiply_subtract_fusion.1 = (f32[64,4,2048]{2,1,0:T(4,128)}, f32[64,4,2048]{2,1,0:T(4,128)}, f32[64,4,2048]{2,1,0:T(4,128)}) fusion(f32[64,4,2048]{2,1,0:T(4,128)} %param.20, f32[4,64,2048]{2,1,0:T(8,128)} %copy-done.7, f32[]{:T(128)S(6)} %min.3, f32[64,4,2048]{2,1,0:T(4,128)} %param.24, f32[64,4,2048]{2,1,0:T(4,128)} %param.25), kind=kLoop, calls=%fused_computation.50 | loop fusion | flops 8388608 | bytes 14680068 | tf_op jit(solution)/shard_map/sub | solution.py:263
  596.3 11.1 %multiply_subtract_fusion = (f32[64,2,5632]{2,1,0:T(2,128)}, f32[64,2,5632]{2,1,0:T(2,128)}, f32[64,2,5632]{2,1,0:T(2,128)}) fusion(f32[64,2,5632]{2,1,0:T(2,128)S(1)} %copy-done.14, f32[64,2,5632]{2,1,0:T(2,128)S(1)} %copy-done.15, f32[]{:T(128)S(6)} %min.3, f32[64,2,5632]{2,1,0:T(2,128)S(1)} %copy-done.32, f32[64,2,5632]{2,1,0:T(2,128)S(1)} %copy-done.33), kind=kLoop, calls=%fused_computation.25 | loop fusion | flops 11534336 | bytes 20185092 | tf_op jit(solution)/shard_map/sub | solution.py:263
  (344 shorter events, 179.2 us)
Async XLA Ops:
  16.8 17.9 %all-to-all-start = ((bf16[8,64,768]{2,1,0:T(8,128)(2,1)}), bf16[8,64,768]{2,1,0:T(8,128)(2,1)S(1)}, u32[]{:S(2)}, u32[]{:S(2)}) async-start(bf16[8,64,768]{2,1,0:T(8,128)(2,1)} %reshape.213), calls=%async_computation | async-start | bytes 1572864 | tf_op jit(solution)/shard_map/all_to_all | solution.py:42
  22.1 98.4 %all-gather.4.cloned.1.call-start = ((), (), s32[]{:S(2)}) async-start(), calls=%async_computation.7 | async-start | bytes 5242880 | tf_op jit(solution)/shard_map/all_gather | solution.py:34
  37.9 174.2 %reduce-scatter.5.cloned.1.call-start = ((), (), s32[]{:S(2)}) async-start(), calls=%async_computation.8 | async-start | bytes 5013504 | tf_op jit(solution)/shard_map/reduce_scatter | solution.py:38
  40.7 3.8 collective-permute-start.11
  42.2 35.5 %collective-permute-start = (bf16[88,2048]{1,0:T(8,128)(2,1)}, bf16[88,2048]{1,0:T(8,128)(2,1)}, u32[]{:S(2)}, u32[]{:S(2)}) collective-permute-start(bf16[88,2048]{1,0:T(8,128)(2,1)} %get-tuple-element.216), channel_id=1, source_target_pairs={{0,2},{2,0},{1,3},{3,1},{4,6},{6,4},{5,7},{7,5},{8,10},{10,8},{9,1... | collective-permute-start | bytes 1081352 | tf_op jit(solution)/shard_map/ppermute | solution.py:48
  42.8 35.0 %collective-permute-start.2 = (bf16[88,2048]{1,0:T(8,128)(2,1)}, bf16[88,2048]{1,0:T(8,128)(2,1)}, u32[]{:S(2)}, u32[]{:S(2)}) collective-permute-start(bf16[88,2048]{1,0:T(8,128)(2,1)} %get-tuple-element.217), channel_id=1, source_target_pairs={{0,4},{4,0},{1,5},{5,1},{2,6},{6,2},{3,7},{7,3},{8,12},{12,8},{9,1... | collective-permute-start | bytes 1081352 | tf_op jit(solution)/shard_map/ppermute | solution.py:48
  44.5 22.1 %collective-permute-start.12 = (f32[8,3,64]{2,1,0:T(4,128)S(1)}, f32[8,3,64]{2,1,0:T(4,128)S(1)}, u32[]{:S(2)}, u32[]{:S(2)}) collective-permute-start(f32[8,3,64]{2,1,0:T(4,128)S(1)} %pad_maximum_fusion.20), channel_id=1, source_target_pairs={{0,8},{8,0},{16,24},{24,16},{1,9},{9,1},{17,25},{25,17},{2,10},{10... | collective-permute-start | bytes 18440 | tf_op jit(solution)/shard_map/ppermute | solution.py:101
  46.9 26.5 %collective-permute-start.4 = (bf16[128,1024]{1,0:T(8,128)(2,1)}, bf16[128,1024]{1,0:T(8,128)(2,1)}, u32[]{:S(2)}, u32[]{:S(2)}) collective-permute-start(bf16[128,1024]{1,0:T(8,128)(2,1)} %get-tuple-element.220), channel_id=1, source_target_pairs={{0,2},{2,0},{1,3},{3,1},{4,6},{6,4},{5,7},{7,5},{8,10},{10,8},{9,1... | collective-permute-start | bytes 786440 | tf_op jit(solution)/shard_map/ppermute | solution.py:48
  48.1 25.2 %collective-permute-start.6 = (bf16[128,1024]{1,0:T(8,128)(2,1)S(1)}, bf16[128,1024]{1,0:T(8,128)(2,1)}, u32[]{:S(2)}, u32[]{:S(2)}) collective-permute-start(bf16[128,1024]{1,0:T(8,128)(2,1)S(1)} %get-tuple-element.221), channel_id=1, source_target_pairs={{0,4},{4,0},{1,5},{5,1},{2,6},{6,2},{3,7},{7,3},{8,12},{12,8},{9,1... | collective-permute-start | bytes 786440 | tf_op jit(solution)/shard_map/ppermute | solution.py:48
  66.7 6.2 %collective-permute-start.13 = (f32[16,3,64]{2,1,0:T(4,128)S(1)}, f32[16,3,64]{2,1,0:T(4,128)S(1)}, u32[]{:S(2)}, u32[]{:S(2)}) collective-permute-start(f32[16,3,64]{2,1,0:T(4,128)S(1)} %pad_maximum_fusion.19), channel_id=1, source_target_pairs={{0,16},{8,24},{16,0},{24,8},{1,17},{9,25},{17,1},{25,9},{2,18},{10... | collective-permute-start | bytes 36872 | tf_op jit(solution)/shard_map/ppermute | solution.py:101
  72.9 18.4 %collective-permute-start.14 = (bf16[4,64,1408]{2,1,0:T(8,128)(2,1)S(1)}, bf16[4,64,1408]{2,1,0:T(8,128)(2,1)}, u32[]{:S(2)}, u32[]{:S(2)}) collective-permute-start(bf16[4,64,1408]{2,1,0:T(8,128)(2,1)S(1)} %dynamic-slice_bitcast_fusion.8), channel_id=1, source_target_pairs={{0,1},{1,0},{2,3},{3,2},{4,5},{5,4},{6,7},{7,6},{8,9},{9,8},{10,11... | collective-permute-start | bytes 2162696 | tf_op jit(solution)/shard_map/ppermute | solution.py:205
  74.6 14.8 %collective-permute-start.7 = (bf16[2,128,1024]{2,1,0:T(8,128)(2,1)S(1)}, bf16[2,128,1024]{2,1,0:T(8,128)(2,1)S(1)}, u32[]{:S(2)}, u32[]{:S(2)}) collective-permute-start(bf16[2,128,1024]{2,1,0:T(8,128)(2,1)S(1)} %pad_maximum_fusion.18), channel_id=1, source_target_pairs={{0,2},{2,0},{1,3},{3,1},{4,6},{6,4},{5,7},{7,5},{8,10},{10,8},{9,1... | collective-permute-start | bytes 1572872 | tf_op jit(solution)/shard_map/ppermute | solution.py:48
  76.2 14.8 %collective-permute-start.5 = (bf16[2,128,1024]{2,1,0:T(8,128)(2,1)S(1)}, bf16[2,128,1024]{2,1,0:T(8,128)(2,1)S(1)}, u32[]{:S(2)}, u32[]{:S(2)}) collective-permute-start(bf16[2,128,1024]{2,1,0:T(8,128)(2,1)S(1)} %pad_maximum_fusion.17), channel_id=1, source_target_pairs={{0,4},{4,0},{1,5},{5,1},{2,6},{6,2},{3,7},{7,3},{8,12},{12,8},{9,1... | collective-permute-start | bytes 1572872 | tf_op jit(solution)/shard_map/ppermute | solution.py:48
  79.0 25.4 %collective-permute-start.3 = (bf16[2,88,2048]{2,1,0:T(8,128)(2,1)S(1)}, bf16[2,88,2048]{2,1,0:T(8,128)(2,1)S(1)}, u32[]{:S(2)}, u32[]{:S(2)}) collective-permute-start(bf16[2,88,2048]{2,1,0:T(8,128)(2,1)S(1)} %pad_maximum_fusion.16), channel_id=1, source_target_pairs={{0,2},{2,0},{1,3},{3,1},{4,6},{6,4},{5,7},{7,5},{8,10},{10,8},{9,1... | collective-permute-start | bytes 2162696 | tf_op jit(solution)/shard_map/ppermute | solution.py:48
  79.7 26.0 %collective-permute-start.1 = (bf16[2,88,2048]{2,1,0:T(8,128)(2,1)S(1)}, bf16[2,88,2048]{2,1,0:T(8,128)(2,1)S(1)}, u32[]{:S(2)}, u32[]{:S(2)}) collective-permute-start(bf16[2,88,2048]{2,1,0:T(8,128)(2,1)S(1)} %pad_maximum_fusion.15), channel_id=1, source_target_pairs={{0,4},{4,0},{1,5},{5,1},{2,6},{6,2},{3,7},{7,3},{8,12},{12,8},{9,1... | collective-permute-start | bytes 2162696 | tf_op jit(solution)/shard_map/ppermute | solution.py:48
  91.3 16.4 %collective-permute-start.8 = (bf16[2,2,128,2048]{3,2,1,0:T(8,128)(2,1)S(1)}, bf16[2,2,128,2048]{3,2,1,0:T(8,128)(2,1)S(1)}, u32[]{:S(2)}, u32[]{:S(2)}) collective-permute-start(bf16[2,2,128,2048]{3,2,1,0:T(8,128)(2,1)S(1)} %pad_maximum_fusion.4), channel_id=1, source_target_pairs={{0,1},{1,0},{2,3},{3,2},{4,5},{5,4},{6,7},{7,6},{8,9},{9,8},{10,11... | collective-permute-start | bytes 6291464 | tf_op jit(solution)/shard_map/ppermute | solution.py:48
  140.0 136.5 %all-gather.6.cloned.1.call-start = ((), (), s32[]{:S(2)}) async-start(), calls=%async_computation.9 | async-start | bytes 4718592 | tf_op jit(solution)/shard_map/all_gather | solution.py:34
  142.1 13.5 %collective-permute-start.15 = (bf16[2,64,1408]{2,1,0:T(8,128)(2,1)}, bf16[2,64,1408]{2,1,0:T(8,128)(2,1)}, u32[]{:S(2)}, u32[]{:S(2)}) collective-permute-start(bf16[2,64,1408]{2,1,0:T(8,128)(2,1)} %get-tuple-element.197), channel_id=1, source_target_pairs={{0,8},{8,16},{16,24},{24,0},{1,9},{9,17},{17,25},{25,1},{2,10},{10... | collective-permute-start | bytes 1081352 | tf_op jit(solution)/shard_map/ppermute | solution.py:215
  142.1 29.0 %collective-permute-start.16 = (bf16[2,64,1408]{2,1,0:T(8,128)(2,1)S(1)}, bf16[2,64,1408]{2,1,0:T(8,128)(2,1)}, u32[]{:S(2)}, u32[]{:S(2)}) collective-permute-start(bf16[2,64,1408]{2,1,0:T(8,128)(2,1)S(1)} %get-tuple-element.196), channel_id=1, source_target_pairs={{0,16},{8,24},{16,0},{24,8},{1,17},{9,25},{17,1},{25,9},{2,18},{10... | collective-permute-start | bytes 1081352 | tf_op jit(solution)/shard_map/ppermute | solution.py:215
  143.4 27.7 %collective-permute-start.17 = (bf16[2,64,1408]{2,1,0:T(8,128)(2,1)S(1)}, bf16[2,64,1408]{2,1,0:T(8,128)(2,1)}, u32[]{:S(2)}, u32[]{:S(2)}) collective-permute-start(bf16[2,64,1408]{2,1,0:T(8,128)(2,1)S(1)} %get-tuple-element.195), channel_id=1, source_target_pairs={{0,24},{8,0},{16,8},{24,16},{1,25},{9,1},{17,9},{25,17},{2,26},{10... | collective-permute-start | bytes 1081352 | tf_op jit(solution)/shard_map/ppermute | solution.py:215
  146.0 36.2 %collective-permute-start.18 = (bf16[128,2048]{1,0:T(8,128)(2,1)S(1)}, bf16[128,2048]{1,0:T(8,128)(2,1)S(1)}, u32[]{:S(2)}, u32[]{:S(2)}) collective-permute-start(bf16[128,2048]{1,0:T(8,128)(2,1)S(1)} %copy-done.2), channel_id=1, source_target_pairs={{0,8},{8,16},{16,24},{24,0},{1,9},{9,17},{17,25},{25,1},{2,10},{10... | collective-permute-start | bytes 1572872 | tf_op jit(solution)/shard_map/ppermute | solution.py:186
  146.7 64.6 %collective-permute-start.19 = (bf16[128,2048]{1,0:T(8,128)(2,1)S(1)}, bf16[128,2048]{1,0:T(8,128)(2,1)S(1)}, u32[]{:S(2)}, u32[]{:S(2)}) collective-permute-start(bf16[128,2048]{1,0:T(8,128)(2,1)S(1)} %copy-done.2), channel_id=1, source_target_pairs={{0,16},{8,24},{16,0},{24,8},{1,17},{9,25},{17,1},{25,9},{2,18},{10... | collective-permute-start | bytes 1572872 | tf_op jit(solution)/shard_map/ppermute | solution.py:186
  155.7 56.4 %collective-permute-start.20 = (bf16[128,2048]{1,0:T(8,128)(2,1)S(1)}, bf16[128,2048]{1,0:T(8,128)(2,1)}, u32[]{:S(2)}, u32[]{:S(2)}) collective-permute-start(bf16[128,2048]{1,0:T(8,128)(2,1)S(1)} %copy-done.2), channel_id=1, source_target_pairs={{0,24},{8,0},{16,8},{24,16},{1,25},{9,1},{17,9},{25,17},{2,26},{10... | collective-permute-start | bytes 1572872 | tf_op jit(solution)/shard_map/ppermute | solution.py:186
  214.4 145.4 %reduce-scatter.7.cloned.1.call-start = ((), (), s32[]{:S(2)}) async-start(), calls=%async_computation.10 | async-start | bytes 4718592 | tf_op jit(solution)/shard_map/reduce_scatter | solution.py:38
  216.0 15.9 %collective-permute-start.24 = (bf16[256,1408]{1,0:T(8,128)(2,1)S(1)}, bf16[256,1408]{1,0:T(8,128)(2,1)S(1)}, u32[]{:S(2)}, u32[]{:S(2)}) collective-permute-start(bf16[256,1408]{1,0:T(8,128)(2,1)S(1)} %bitcast.282), channel_id=1, source_target_pairs={{0,4},{4,0},{1,5},{5,1},{2,6},{6,2},{3,7},{7,3},{8,12},{12,8},{9,1... | collective-permute-start | bytes 2162696 | tf_op jit(solution)/shard_map/ppermute | solution.py:48
  219.2 20.1 %collective-permute-start.21 = (bf16[4,128,2048]{2,1,0:T(8,128)(2,1)S(1)}, bf16[4,128,2048]{2,1,0:T(8,128)(2,1)S(1)}, u32[]{:S(2)}, u32[]{:S(2)}) collective-permute-start(bf16[4,128,2048]{2,1,0:T(8,128)(2,1)S(1)} %pad_maximum_fusion.5), channel_id=1, source_target_pairs={{0,1},{1,0},{2,3},{3,2},{4,5},{5,4},{6,7},{7,6},{8,9},{9,8},{10,11... | collective-permute-start | bytes 6291464 | tf_op jit(solution)/shard_map/ppermute | solution.py:48
  219.2 19.0 %collective-permute-start.22 = (bf16[256,1408]{1,0:T(8,128)(2,1)S(1)}, bf16[256,1408]{1,0:T(8,128)(2,1)S(1)}, u32[]{:S(2)}, u32[]{:S(2)}) collective-permute-start(bf16[256,1408]{1,0:T(8,128)(2,1)S(1)} %bitcast.281), channel_id=1, source_target_pairs={{0,2},{2,0},{1,3},{3,1},{4,6},{6,4},{5,7},{7,5},{8,10},{10,8},{9,1... | collective-permute-start | bytes 2162696 | tf_op jit(solution)/shard_map/ppermute | solution.py:48
  232.2 36.5 %collective-permute-start.25 = (bf16[2,256,1408]{2,1,0:T(8,128)(2,1)S(1)}, bf16[2,256,1408]{2,1,0:T(8,128)(2,1)S(1)}, u32[]{:S(2)}, u32[]{:S(2)}) collective-permute-start(bf16[2,256,1408]{2,1,0:T(8,128)(2,1)S(1)} %pad_maximum_fusion.12), channel_id=1, source_target_pairs={{0,2},{2,0},{1,3},{3,1},{4,6},{6,4},{5,7},{7,5},{8,10},{10,8},{9,1... | collective-permute-start | bytes 4325384 | tf_op jit(solution)/shard_map/ppermute | solution.py:48
  238.6 32.9 %collective-permute-start.23 = (bf16[2,256,1408]{2,1,0:T(8,128)(2,1)S(1)}, bf16[2,256,1408]{2,1,0:T(8,128)(2,1)S(1)}, u32[]{:S(2)}, u32[]{:S(2)}) collective-permute-start(bf16[2,256,1408]{2,1,0:T(8,128)(2,1)S(1)} %pad_maximum_fusion.11), channel_id=1, source_target_pairs={{0,4},{4,0},{1,5},{5,1},{2,6},{6,2},{3,7},{7,3},{8,12},{12,8},{9,1... | collective-permute-start | bytes 4325384 | tf_op jit(solution)/shard_map/ppermute | solution.py:48
  302.5 112.7 %all-gather.8.cloned.1.call-start = ((), (), s32[]{:S(2)}) async-start(), calls=%async_computation.11 | async-start | bytes 5013504 | tf_op jit(solution)/shard_map/all_gather | solution.py:34
  311.4 45.7 %collective-permute-start.26 = (bf16[4,128,2048]{2,1,0:T(8,128)(2,1)}, bf16[4,128,2048]{2,1,0:T(8,128)(2,1)}, u32[]{:S(2)}, u32[]{:S(2)}) collective-permute-start(bf16[4,128,2048]{2,1,0:T(8,128)(2,1)} %get-tuple-element.160), channel_id=1, source_target_pairs={{0,1},{1,0},{2,3},{3,2},{4,5},{5,4},{6,7},{7,6},{8,9},{9,8},{10,11... | collective-permute-start | bytes 6291464 | tf_op jit(solution)/shard_map/ppermute | solution.py:83
  322.6 32.5 %collective-permute-start.27 = (bf16[2,256,1408]{2,1,0:T(8,128)(2,1)}, bf16[2,256,1408]{2,1,0:T(8,128)(2,1)}, u32[]{:S(2)}, u32[]{:S(2)}) collective-permute-start(bf16[2,256,1408]{2,1,0:T(8,128)(2,1)} %get-tuple-element.168), channel_id=1, source_target_pairs={{0,4},{4,0},{1,5},{5,1},{2,6},{6,2},{3,7},{7,3},{8,12},{12,8},{9,1... | collective-permute-start | bytes 4325384 | tf_op jit(solution)/shard_map/ppermute | solution.py:83
  325.0 32.2 %collective-permute-start.28 = (bf16[2,256,1408]{2,1,0:T(8,128)(2,1)}, bf16[2,256,1408]{2,1,0:T(8,128)(2,1)}, u32[]{:S(2)}, u32[]{:S(2)}) collective-permute-start(bf16[2,256,1408]{2,1,0:T(8,128)(2,1)} %get-tuple-element.166), channel_id=1, source_target_pairs={{0,2},{2,0},{1,3},{3,1},{4,6},{6,4},{5,7},{7,5},{8,10},{10,8},{9,1... | collective-permute-start | bytes 4325384 | tf_op jit(solution)/shard_map/ppermute | solution.py:83
  364.4 154.6 %reduce-scatter.11.cloned.1.call-start = ((), (), s32[]{:S(2)}) async-start(), calls=%async_computation.13 | async-start | bytes 3604480 | tf_op jit(solution)/shard_map/reduce_scatter | solution.py:38
  366.9 45.0 %collective-permute-start.30 = (bf16[256,1408]{1,0:T(8,128)(2,1)S(1)}, bf16[256,1408]{1,0:T(8,128)(2,1)S(1)}, u32[]{:S(2)}, u32[]{:S(2)}) collective-permute-start(bf16[256,1408]{1,0:T(8,128)(2,1)S(1)} %dynamic-slice_bitcast_fusion.6), channel_id=1, source_target_pairs={{0,4},{4,0},{1,5},{5,1},{2,6},{6,2},{3,7},{7,3},{8,12},{12,8},{9,1... | collective-permute-start | bytes 2162696 | tf_op jit(solution)/shard_map/ppermute | solution.py:83
  370.9 20.8 %collective-permute-start.33 = (bf16[128,2048]{1,0:T(8,128)(2,1)S(1)}, bf16[128,2048]{1,0:T(8,128)(2,1)S(1)}, u32[]{:S(2)}, u32[]{:S(2)}) collective-permute-start(bf16[128,2048]{1,0:T(8,128)(2,1)S(1)} %get-tuple-element.183), channel_id=1, source_target_pairs={{0,8},{8,16},{16,24},{24,0},{1,9},{9,17},{17,25},{25,1},{2,10},{10... | collective-permute-start | bytes 1572872 | tf_op jit(solution)/shard_map/ppermute | solution.py:129
  378.3 32.2 %collective-permute-start.32 = (bf16[128,2048]{1,0:T(8,128)(2,1)S(1)}, bf16[128,2048]{1,0:T(8,128)(2,1)S(1)}, u32[]{:S(2)}, u32[]{:S(2)}) collective-permute-start(bf16[128,2048]{1,0:T(8,128)(2,1)S(1)} %get-tuple-element.184), channel_id=1, source_target_pairs={{0,16},{8,24},{16,0},{24,8},{1,17},{9,25},{17,1},{25,9},{2,18},{10... | collective-permute-start | bytes 1572872 | tf_op jit(solution)/shard_map/ppermute | solution.py:129
  379.4 31.2 %collective-permute-start.31 = (bf16[128,2048]{1,0:T(8,128)(2,1)S(1)}, bf16[128,2048]{1,0:T(8,128)(2,1)S(1)}, u32[]{:S(2)}, u32[]{:S(2)}) collective-permute-start(bf16[128,2048]{1,0:T(8,128)(2,1)S(1)} %get-tuple-element.182), channel_id=1, source_target_pairs={{0,24},{8,0},{16,8},{24,16},{1,25},{9,1},{17,9},{25,17},{2,26},{10... | collective-permute-start | bytes 1572872 | tf_op jit(solution)/shard_map/ppermute | solution.py:129
  382.7 29.4 %collective-permute-start.29 = (bf16[256,1408]{1,0:T(8,128)(2,1)S(1)}, bf16[256,1408]{1,0:T(8,128)(2,1)S(1)}, u32[]{:S(2)}, u32[]{:S(2)}) collective-permute-start(bf16[256,1408]{1,0:T(8,128)(2,1)S(1)} %dynamic-slice_bitcast_fusion.7), channel_id=1, source_target_pairs={{0,2},{2,0},{1,3},{3,1},{4,6},{6,4},{5,7},{7,5},{8,10},{10,8},{9,1... | collective-permute-start | bytes 2162696 | tf_op jit(solution)/shard_map/ppermute | solution.py:83
  415.2 47.9 %all-to-all-start.1 = ((bf16[8,64,1408]{2,1,0:T(8,128)(2,1)}), bf16[8,64,1408]{2,1,0:T(8,128)(2,1)}, u32[]{:S(2)}, u32[]{:S(2)}) async-start(bf16[8,64,1408]{2,1,0:T(8,128)(2,1)} %bitcast.272), calls=%async_computation.3 | async-start | bytes 2883584 | tf_op jit(solution)/shard_map/all_to_all | solution.py:42
  428.0 116.4 %reduce-scatter.9.cloned.1.call-start = ((), (), s32[]{:S(2)}) async-start(), calls=%async_computation.12 | async-start | bytes 5242880 | tf_op jit(solution)/shard_map/reduce_scatter | solution.py:38
  469.7 4.2 collective-permute-start.34
  476.7 28.6 %collective-permute-start.37 = (bf16[2,128,1024]{2,1,0:T(8,128)(2,1)}, bf16[2,128,1024]{2,1,0:T(8,128)(2,1)}, u32[]{:S(2)}, u32[]{:S(2)}) collective-permute-start(bf16[2,128,1024]{2,1,0:T(8,128)(2,1)} %dynamic-slice_bitcast_fusion.9), channel_id=1, source_target_pairs={{0,2},{2,0},{1,3},{3,1},{4,6},{6,4},{5,7},{7,5},{8,10},{10,8},{9,1... | collective-permute-start | bytes 1572872 | tf_op jit(solution)/shard_map/ppermute | solution.py:83
  479.2 29.3 %collective-permute-start.35 = (bf16[2,128,1024]{2,1,0:T(8,128)(2,1)}, bf16[2,128,1024]{2,1,0:T(8,128)(2,1)S(1)}, u32[]{:S(2)}, u32[]{:S(2)}) collective-permute-start(bf16[2,128,1024]{2,1,0:T(8,128)(2,1)} %dynamic-slice_bitcast_fusion.10), channel_id=1, source_target_pairs={{0,4},{4,0},{1,5},{5,1},{2,6},{6,2},{3,7},{7,3},{8,12},{12,8},{9,1... | collective-permute-start | bytes 1572872 | tf_op jit(solution)/shard_map/ppermute | solution.py:83
  506.9 9.6 %collective-permute-start.38 = (bf16[128,1024]{1,0:T(8,128)(2,1)S(1)}, bf16[128,1024]{1,0:T(8,128)(2,1)S(1)}, u32[]{:S(2)}, u32[]{:S(2)}) collective-permute-start(bf16[128,1024]{1,0:T(8,128)(2,1)S(1)} %dynamic-slice_bitcast_fusion.17), channel_id=1, source_target_pairs={{0,4},{4,0},{1,5},{5,1},{2,6},{6,2},{3,7},{7,3},{8,12},{12,8},{9,1... | collective-permute-start | bytes 786440 | tf_op jit(solution)/shard_map/ppermute | solution.py:83
  508.8 7.8 %collective-permute-start.36 = (bf16[128,1024]{1,0:T(8,128)(2,1)S(1)}, bf16[128,1024]{1,0:T(8,128)(2,1)S(1)}, u32[]{:S(2)}, u32[]{:S(2)}) collective-permute-start(bf16[128,1024]{1,0:T(8,128)(2,1)S(1)} %dynamic-slice_bitcast_fusion.18), channel_id=1, source_target_pairs={{0,2},{2,0},{1,3},{3,1},{4,6},{6,4},{5,7},{7,5},{8,10},{10,8},{9,1... | collective-permute-start | bytes 786440 | tf_op jit(solution)/shard_map/ppermute | solution.py:83
  546.4 16.4 %all-to-all-start.2 = ((bf16[8,64,768]{2,1,0:T(8,128)(2,1)}), bf16[8,64,768]{2,1,0:T(8,128)(2,1)S(1)}, u32[]{:S(2)}, u32[]{:S(2)}) async-start(bf16[8,64,768]{2,1,0:T(8,128)(2,1)} %bitcast.98), calls=%async_computation.6 | async-start | bytes 1572864 | tf_op jit(solution)/shard_map/all_to_all | solution.py:42
  582.0 4.5 collective-permute-start.43
  (64 other events, 377.2 us)
Sparse Core Ops, SparseCore 0:
  38.1 82.4 all-gather.3
  140.1 51.0 reduce-scatter.4
  214.5 55.1 all-gather.5
  302.6 57.1 reduce-scatter.6
  364.6 50.5 all-gather.7
  419.0 46.1 reduce-scatter.10
  467.6 76.7 reduce-scatter.8

commit v4 on v3

--- a/solution.py
+++ b/solution.py
@@ -5,7 +5,6 @@
 import jax.numpy as jnp
 from jax import lax
 from jax.experimental import pallas as pl
-from jax.experimental.layout import Layout, with_layout_constraint
 from jax.experimental.pallas import tpu as pltpu
 from jax.sharding import Mesh, PartitionSpec as P
 
@@ -117,10 +116,6 @@
     return [upper, middle, lower]
 
 
-def as_stored(value):
-    return with_layout_constraint(value, Layout(tuple(range(value.ndim))))
-
-
 def direct_scatter(value, axis):
     count, mine = lax.axis_size(axis), lax.axis_index(axis)
     total = lax.dynamic_index_in_dim(value, mine, 0, False).astype(F32)
@@ -304,37 +299,148 @@
     lax.fori_loop(0, rows // TILE, step, jnp.zeros((1, width), F32), unroll=4)
 
 
-def scan_backward(proj_ref, state_ref, d_state_ref, started_ref, gap_ref, d_in_ref, d_forget_ref):
+def scan_backward(
+    proj_ref, state_ref, d_mixed_ref, riders_ref, started_ref, gap_ref, gain_ref, d_proj_ref, mixed_ref
+):
     rows, width = state_ref.shape
     row = lax.broadcasted_iota(jnp.int32, (TILE, width), 0)
-    gap = gap_ref[...]
+    lane = lax.broadcasted_iota(jnp.int32, (2 * TILE, 128), 1)
+    gap, gain = gap_ref[...], gain_ref[...]
 
     def located(index):
         return pl.ds(pl.multiple_of(index * TILE, TILE), TILE)
 
-    def step(count, carry):
-        index = rows // TILE - 1 - count
+    def one(index, mean, factor, carry):
         place = located(index)
         before = located(jnp.maximum(index - 1, 0))
         in_proj = proj_ref[place, pl.ds(0, width)]
         forget_proj = proj_ref[place, pl.ds(width, width)]
+        gate_proj = proj_ref[place, pl.ds(2 * width, width)]
         started = started_ref[place, :]
         sig_neg, keep, decay = gates(forget_proj, gap, started)
-        d_state = d_state_ref[place, :]
+        state, d_mixed = state_ref[place, :], d_mixed_ref[place, :]
+        normed = state * factor
+        sig_gate = jax.nn.sigmoid(gate_proj)
+        gain_act = gain * (gate_proj * sig_gate)
+        d_gate = d_mixed * normed * gain * (sig_gate * (1.0 + gate_proj * (1.0 - sig_gate)))
+        d_state = factor * (d_mixed * gain_act - normed * mean)
         coeff, value = tile_scan(decay, decay * d_state, row, True)
         passed = value + coeff * carry
         moved = jnp.where(row < TILE - 1, pltpu.roll(passed, TILE - 1, 0), carry)
         d_total = d_state + moved
         last = state_ref[before, :][TILE - 1 :, :]
-        previous = jnp.where(row >= 1, pltpu.roll(state_ref[place, :], 1, 0), last)
+        previous = jnp.where(row >= 1, pltpu.roll(state, 1, 0), last)
         previous = jnp.where(started > 0.0, 0.0, previous)
         sig = jax.nn.sigmoid(in_proj)
-        d_in_ref[place, :] = d_total * keep * (sig * (1.0 + in_proj * (1.0 - sig)))
+        d_in = d_total * keep * (sig * (1.0 + in_proj * (1.0 - sig)))
         d_keep = d_total * (in_proj * sig) - d_total * previous
-        d_forget_ref[place, :] = -d_keep * gap * sig_neg * (1.0 - sig_neg)
-        return passed[:1, :]
-
-    lax.fori_loop(0, rows // TILE, step, jnp.zeros((1, width), F32), unroll=4)
+        d_forget = -d_keep * gap * sig_neg * (1.0 - sig_neg)
+        return [d_in, d_forget, d_gate, normed * gain_act], passed[:1, :]
+
+    def step(count, carry):
+        pair = rows // (2 * TILE) - 1 - count
+        place = pl.ds(pl.multiple_of(pair * 2 * TILE, 2 * TILE), 2 * TILE)
+        riders = riders_ref[place, :].astype(F32)
+        mean = jnp.sum(jnp.where(lane < 3, riders, 0.0), axis=1, keepdims=True)
+        factor = jnp.sum(jnp.where(lane < 3, 0.0, riders), axis=1, keepdims=True)
+        late, carry = one(2 * pair + 1, mean[TILE:], factor[TILE:], carry)
+        early, carry = one(2 * pair, mean[:TILE], factor[:TILE], carry)
+        both = [jnp.concatenate(parts, axis=0).astype(BF) for parts in zip(early, late)]
+        for kind in range(3):
+            d_proj_ref[place, pl.ds(kind * width, width)] = both[kind]
+        mixed_ref[place, :] = both[3]
+        return carry
+
+    lax.fori_loop(0, rows // (2 * TILE), step, jnp.zeros((1, width), F32), unroll=2)
+
+
+def run_forward(proj, started, gap):
+    rows, width = proj.shape[0], gap.shape[1]
+    return pl.pallas_call(
+        scan_forward,
+        out_shape=[
+            jax.ShapeDtypeStruct((rows, width), F32),
+            jax.ShapeDtypeStruct((rows, 1), F32),
+        ],
+        compiler_params=pltpu.CompilerParams(vmem_limit_bytes=48 * 2**20),
+    )(proj, started, gap)
+
+
+def run_backward(proj, state, d_mixed, riders, started, gap, gain):
+    rows, width = state.shape
+    return pl.pallas_call(
+        scan_backward,
+        out_shape=[
+            jax.ShapeDtypeStruct((rows, 3 * width), BF),
+            jax.ShapeDtypeStruct((rows, width), BF),
+        ],
+        compiler_params=pltpu.CompilerParams(vmem_limit_bytes=48 * 2**20),
+    )(proj, state, d_mixed, riders, started, gap, gain)
+
+
+def adam_rows(clip_ref, weight_ref, first_ref, second_ref, grad_ref, *new_refs):
+    clip = clip_ref[0, 0]
+    for kind in range(weight_ref.shape[1]):
+        moved = adam_step(
+            weight_ref[:, kind, :],
+            first_ref[:, kind, :],
+            second_ref[:, kind, :],
+            clip * grad_ref[kind].astype(F32),
+            RATE_MATRIX,
+            DECAY_WEIGHT,
+        )
+        for new_ref, value in zip(new_refs, moved):
+            new_ref[:, kind, :] = value
+
+
+def run_adam(weight, first, second, grad, clip):
+    own, kinds, width = weight.shape
+    rows = min(own, 16)
+    rest = pl.BlockSpec((rows, kinds, width), lambda i: (i, 0, 0))
+    return pl.pallas_call(
+        adam_rows,
+        grid=(own // rows,),
+        in_specs=[pl.BlockSpec(memory_space=pltpu.SMEM), rest, rest, rest]
+        + [pl.BlockSpec((kinds, rows, width), lambda i: (0, i, 0))],
+        out_specs=[rest] * 3,
+        out_shape=[jax.ShapeDtypeStruct(weight.shape, F32)] * 3,
+        compiler_params=pltpu.CompilerParams(vmem_limit_bytes=48 * 2**20),
+    )(clip.reshape(1, 1), weight, first, second, grad)
+
+
+def pack(weight_ref, sent_ref, low_ref):
+    spots, own, packed = sent_ref.shape
+    planes = packed // (3 * own)
+    low_half = lax.broadcasted_iota(jnp.int32, (own, 2 * own), 1) < own
+    for kind in range(3):
+        for pair in range(0, spots, 2):
+            for plane in range(0, planes, 2):
+                places = [pl.ds(((plane + i) * spots + pair) * own, 2 * own) for i in range(2)]
+                near, far = [weight_ref[:, kind, place] for place in places]
+                low_ref[kind, :, places[0]] = near.astype(BF)
+                low_ref[kind, :, places[1]] = far.astype(BF)
+                at = pl.ds((kind * planes + plane) * own, 2 * own)
+                even = jnp.where(low_half, near, pltpu.roll(far, own, 1))
+                odd = jnp.where(low_half, pltpu.roll(near, own, 1), far)
+                sent_ref[pair, :, at] = even.astype(BF)
+                sent_ref[pair + 1, :, at] = odd.astype(BF)
+    low_ref[3, :, :] = weight_ref[:, 3, :].astype(BF)
+
+
+def run_pack(weight, planes, spots):
+    own, _, width = weight.shape
+    if 2 * own != 128 or planes % 2 != 0:
+        low = weight.astype(BF)
+        sent = low[:, :3, :].reshape(own, 3, planes, spots, own).transpose(3, 0, 1, 2, 4)
+        return sent.reshape(spots, own, 3 * planes * own), low.swapaxes(0, 1)
+    return pl.pallas_call(
+        pack,
+        out_shape=[
+            jax.ShapeDtypeStruct((spots, own, 3 * planes * own), BF),
+            jax.ShapeDtypeStruct((4, own, width), BF),
+        ],
+        compiler_params=pltpu.CompilerParams(vmem_limit_bytes=48 * 2**20),
+    )(weight)
 
 
 def settle(got_ref, out_ref, low_ref, grad_ref, first_ref, inner_ref, total_ref):
@@ -376,15 +482,16 @@
         grad = got.reshape(spots, own, 3, planes, own).transpose(1, 2, 3, 0, 4)
         grad = jnp.concatenate([grad.reshape(own, 3, width), shard_out[:, None, :]], axis=1)
         grad = grad.astype(F32)
-        product = jnp.sum(grad * low_mixer.astype(F32), axis=2)
-        return grad, jnp.sum(product[:, :3], axis=1), product[:, 3], jnp.sum(grad * grad, axis=(1, 2))
+        product = jnp.sum(grad * low_mixer.swapaxes(0, 1).astype(F32), axis=2)
+        squares = jnp.sum(grad * grad, axis=(1, 2))
+        return grad.swapaxes(0, 1), jnp.sum(product[:, :3], axis=1), product[:, 3], squares
     column = jax.ShapeDtypeStruct((own, 1), F32)
     grad, *sums = pl.pallas_call(
         settle,
         out_shape=[jax.ShapeDtypeStruct((4, own, width), F32)] + [column] * 3,
         compiler_params=pltpu.CompilerParams(vmem_limit_bytes=48 * 2**20),
-    )(got, shard_out, low_mixer.swapaxes(0, 1))
-    return [grad.swapaxes(0, 1)] + [column[:, 0] for column in sums]
+    )(got, shard_out, low_mixer)
+    return [grad] + [column[:, 0] for column in sums]
 
 
 def column_blocks(width, first, second):
@@ -475,27 +582,6 @@
         scratch_shapes=[pltpu.VMEM((rows, width), F32)],
         compiler_params=pltpu.CompilerParams(vmem_limit_bytes=48 * 2**20),
     )(d_n2, cot, after, mid, mix_raw, home, gain)
-
-
-def run_forward(proj, started, gap):
-    rows, width = proj.shape[0], gap.shape[1]
-    return pl.pallas_call(
-        scan_forward,
-        out_shape=[
-            jax.ShapeDtypeStruct((rows, width), F32),
-            jax.ShapeDtypeStruct((rows, 1), F32),
-        ],
-        compiler_params=pltpu.CompilerParams(vmem_limit_bytes=48 * 2**20),
-    )(proj, started, gap)
-
-
-def run_backward(proj, state, d_state, started, gap):
-    rows, width = state.shape
-    return pl.pallas_call(
-        scan_backward,
-        out_shape=[jax.ShapeDtypeStruct((rows, width), F32)] * 2,
-        compiler_params=pltpu.CompilerParams(vmem_limit_bytes=48 * 2**20),
-    )(proj, state, d_state, started, gap)
 
 
 def shards(
@@ -536,21 +622,20 @@
 
     cot_low = (cotangent.astype(F32) * valid[:, None]).astype(BF)
 
-    low_mixer = mixer_w.astype(BF)
-    sent = low_mixer[:, :3, :].reshape(own, 3, planes, spots, own).transpose(3, 0, 1, 2, 4)
-    part = exchange(sent.reshape(spots, own, 3 * chans), PLANE)
-    part = jnp.concatenate(
-        [part.reshape(spots * own, 3 * chans), low_mixer[:, 3, :].reshape(spots * own, chans)], axis=1
-    )
-    x_low, part, low_gains, low_down, low_in = tied(tokens, part, gains, mlp_down, mlp_in)
-    x_parts = quad_parts(x_low, 1)
-    full_gains = double_gather(low_gains).swapaxes(0, 1).reshape(3, width)
-    low_in = low_in.astype(BF)
+    w_out = gather(mixer_w[:, 3, :].astype(BF), "z")
+    sent, low_mixer = run_pack(mixer_w, planes, spots)
+    part = exchange(sent, PLANE).reshape(spots * own, 3 * chans)
+    low_in = mlp_in.astype(BF)
     inner = quads * down_rows
     sent_in = low_in.reshape(own, 2, planes, quads, pairs, down_rows).transpose(2, 4, 0, 1, 3, 5)
     sent_in = sent_in.reshape(planes * pairs, own, 2 * inner)
+    part, w_out, x_low, low_gains, low_down, sent_in = tied(
+        part, w_out, tokens, gains, mlp_down, sent_in
+    )
+    x_parts = quad_parts(x_low, 1)
+    full_gains = double_gather(low_gains).swapaxes(0, 1).reshape(3, width)
     w_down = quad_whole(quad_parts(low_down.astype(BF), 0))
-    w_all = gather(part, "z")
+    w_proj = gather(part, "z")
     x_all = core_gather(x_parts)
 
     bound = lower_bound.reshape(planes, spots, own)
@@ -562,15 +647,12 @@
     x_normed, x_factor = normalize(x)
     n1 = (normalize(x_all.astype(F32))[0] * full_gains[0]).astype(BF)
     blocks_in = core_exchange(sent_in)
-    w_all, w_down, n1, blocks_in = tied(w_all, w_down, n1, blocks_in)
-    w_proj = w_all[:, : 3 * chans]
-    w_out = w_all[:, 3 * chans :].reshape(chans, width)
+    w_proj, w_down, n1, blocks_in, held_cot = tied(w_proj, w_down, n1, blocks_in, cot_low)
+    cots = direct_gather(held_cot, "z")
     proj = jnp.dot(n1, w_proj, preferred_element_type=F32)
     proj, blocks_in = tied(proj, blocks_in)
     part_in = line_exchange(blocks_in)
-    state, squares = run_forward(proj[:, : 2 * chans], started, gap)
-    state, held_cot = tied(state, cot_low)
-    cots = direct_gather(held_cot, "z")
+    state, squares = run_forward(proj, started, gap)
     gate_proj = proj[:, 2 * chans :]
     gate_act = silu(gate_proj)
     raw = (state * gain_mid * gate_act).astype(BF)
@@ -581,6 +663,7 @@
     ride = jnp.pad(jnp.eye(128, dtype=BF), ((chans, 0), (width, 0)))
     w_ride = ride + jnp.pad(w_out, ((0, 128), (0, 128)))
     mix_part = jnp.dot(raw, w_ride, preferred_element_type=F32).astype(BF)
+    mix_part, cots[1], cots[-1] = tied(mix_part, cots[1], cots[-1])
     mix_raw, part_in, *cots = tied(scatter(mix_part, PLANE), part_in, *cots)
     cot_all = ring_gather(in_order(cots, "z"), "c").swapaxes(0, 1)
     cot_all = cot_all.reshape(planes * pairs * rows, width)
@@ -618,25 +701,14 @@
     d_mix = gather(d_mix_home, PLANE)
     d_mix, shard_in, grad_down, down = tied(d_mix, shard_in, grad_down, down)
     block_out = (after_mix + down).astype(BF)
-    riders = d_mix[:, width : width + 6].astype(F32)
-    mean = jnp.sum(riders[:, :3], axis=1, keepdims=True)
-    factor = jnp.sum(riders[:, 3:], axis=1, keepdims=True)
     shard_down = scatter(grad_down, QUAD).astype(F32)
     got_in = exchange(shard_in.reshape(planes * pairs, own, 2 * inner), LINE)
 
     d_mixed = lax.dot_general(
         d_mix, w_ride[:chans], (((1,), (1,)), ((), ())), preferred_element_type=F32
     )
-    state_normed = state * factor
-    mixed_in = (state_normed * gain_mid * gate_act).astype(BF)
+    d_proj, mixed_in = run_backward(proj, state, d_mixed, d_mix[:, width:], started, gap, gain_mid)
     grad_out = lax.dot_general(mixed_in, d_mix, (((0,), (0,)), ((), ())), preferred_element_type=F32)
-    d_gate_proj = d_mixed * state_normed * gain_mid * silu_grad(gate_proj)
-    d_state = factor * (d_mixed * gain_mid * gate_act - state_normed * mean)
-    d_gate_proj = d_gate_proj.astype(BF)
-    d_in_proj, d_forget_proj = run_backward(proj[:, : 2 * chans], state, d_state, started, gap)
-    d_proj = jnp.concatenate(
-        [d_in_proj.astype(BF), d_forget_proj.astype(BF), d_gate_proj], axis=1
-    )
     grad_proj = lax.dot_general(n1, d_proj, (((0,), (0,)), ((), ())), preferred_element_type=F32)
     grad_out = grad_out[:, :width].astype(BF).reshape(planes, spots * own, chans)
     grad_all = jnp.concatenate(
@@ -644,10 +716,11 @@
     )
     grad_all, got_in, held_proj = tied(grad_all, got_in, d_proj)
     shard_all = scatter(grad_all.reshape(planes * spots * own, 4 * chans), "z")
-    shard_in = got_in.reshape(planes, pairs, own, 2, quads, down_rows).transpose(2, 3, 0, 4, 1, 5)
-    shard_in = as_stored(shard_in.reshape(own, 2, hidden_width).astype(F32))
-    gain_in = jnp.sum(shard_in * low_in.astype(F32), axis=(1, 2))
-    total_early = jnp.sum(shard_in * shard_in) + jnp.sum(shard_down * shard_down)
+    shard_in = got_in.reshape(planes, pairs, own, 2, quads, down_rows).transpose(3, 2, 0, 4, 1, 5)
+    shard_in = shard_in.reshape(2, own, hidden_width)
+    wide_in = shard_in.astype(F32)
+    gain_in = jnp.sum(wide_in * low_in.swapaxes(0, 1).astype(F32), axis=(0, 2))
+    total_early = jnp.sum(wide_in * wide_in) + jnp.sum(shard_down * shard_down)
     d_n1 = lax.dot_general(held_proj, w_proj, (((1,), (1,)), ((), ())), preferred_element_type=F32)
     d_n1 = plane_scatter(d_n1.astype(BF))
     input_grad = d_mid + norm_back(d_n1 * full_gains[0], x_normed, x_factor)
@@ -658,17 +731,12 @@
     shard_out = shard_all[:, 3 * chans :].reshape(own, width)
 
     shard_mixer, gain_first, gain_inner, total_mixer = run_settle(got_proj, shard_out, low_mixer)
-    shard_mixer = as_stored(shard_mixer)
     shard_gains = jnp.stack([gain_first, gain_inner, gain_in]) / gains
     local_total = jnp.sum(total_mixer) + total_early + jnp.sum(shard_gains * shard_gains)
     grad_norm = jnp.sqrt(total_of(local_total.reshape(1, 1))[0, 0])
     clip = jnp.minimum(1.0, CLIP_NORM / (grad_norm + 1e-06))
-    new_mixer, new_mixer_m, new_mixer_v = adam_step(
-        mixer_w, mixer_m, mixer_v, clip * shard_mixer, RATE_MATRIX, DECAY_WEIGHT
-    )
-    new_in, new_in_m, new_in_v = adam_step(
-        mlp_in, in_m, in_v, clip * shard_in, RATE_MATRIX, DECAY_WEIGHT
-    )
+    new_mixer, new_mixer_m, new_mixer_v = run_adam(mixer_w, mixer_m, mixer_v, shard_mixer, clip)
+    new_in, new_in_m, new_in_v = run_adam(mlp_in, in_m, in_v, shard_in, clip)
     new_down, new_down_m, new_down_v = adam_step(
         mlp_down, down_m, down_v, clip * shard_down, RATE_MATRIX, DECAY_WEIGHT
     )

time: 626 us -> 606 us (0.968)
  Pallas kernels: 14 us -> 38.3 us
  other arithmetic: 89.2 us -> 66.1 us
  local copies, waits for them, and re-layouts: 97.1 us -> 85 us
  starting transfers between devices: 78.8 us -> 69.4 us
    convert_element_type x3 -> x0, local copies, waits for them, and re-layouts: 25.6 us -> none  [shards(): shard_in = as_stored(shard_in.reshape(own, 2, hidden_width).astype(F32))]
    ppermute x3, waiting for transfers between devices: 37.3 us -> 13 us  [direct_gather(): return [value] + [lax.ppermute(value, axis, hop) for hop in hops]]
    pallas_call x1 -> x4, Pallas kernels: 5.59 us -> 28.8 us  [the longest x2 16.4 us: run_adam(): pl.pallas_call(adam_rows, grid=(own // rows,), in_specs=[pl.BlockSpec(mem...]
    ppermute x3, waiting for transfers between devices: 22.9 us -> 40.7 us  [line_exchange(): lax.ppermute(blocks[back], 'z', [(i, (i - back) % count) for i in range(c...]
    sub x4 -> x2, other arithmetic: 23.7 us -> 6.33 us  [adam_step(): weight - rate * (step_size + decay_w * weight)]
    reshape x4, local copies, waits for them, and re-layouts: 7.51 us -> 19.9 us  [the longest x1 7.83 us: shards(): got_in.reshape(planes, pairs, own, 2, quads, down_rows)]
    ppermute x3, waiting for transfers between devices: 26.3 us -> 37.3 us  [direct_scatter(): lax.ppermute(block, axis, [(i, (i - back) % count) for i in range(count)])]
    all_to_all x3, starting transfers between devices: 21.9 us -> 14.4 us  [exchange(): return lax.all_to_all(value, axes, 0, 0, tiled=True)]
  transfers between devices with their start and end apart: 54 -> 55, of which waited for: 33 -> 32; matrix products, arithmetic and copies ran while one was open for 27% -> 27% of each run, Pallas kernels for 1% -> 3%
where the time goes in v4:
time: 606 us; the launch traced here: 599 us
  waiting for transfers between devices  250 us (41%)
  local copies, waits for them, and re-layouts  85 us (14%)
  starting transfers between devices  69.4 us (11%)
  matrix products  68.1 us (11%)
  other arithmetic  66.1 us (11%)
  Pallas kernels  38.3 us (6%)
  between operations  22.5 us (4%)
    ppermute x14, waiting for transfers between devices, ring_gather(): other = lax.ppermute(value, axis, [(0, 1), (1, 0)])  64.8 us
    ppermute x3, waiting for transfers between devices, line_exchange(): lax.ppermute(blocks[back], 'z', [(i, (i - back) % count) for i in range(c...  40.7 us
    ppermute x3, waiting for transfers between devices, direct_scatter(): lax.ppermute(block, axis, [(i, (i - back) % count) for i in range(count)])  37.3 us
    ppermute x10, waiting for transfers between devices, ring_terms(): return [block(0), lax.ppermute(block(1), axis, [(0, 1), (1, 0)])]  34.7 us
    reduce_scatter x4, waiting for transfers between devices, scatter(): return lax.psum_scatter(value, axes, scatter_dimension=0, tiled=True)  22.8 us
    unnamed x106, local copies, waits for them, and re-layouts  22.5 us
    all_to_all x3, waiting for transfers between devices, exchange(): return lax.all_to_all(value, axes, 0, 0, tiled=True)  20.3 us
    pallas_call x2, Pallas kernels, run_adam(): pl.pallas_call(adam_rows, grid=(own // rows,), in_specs=[pl.BlockSpec(mem...  16.4 us
  transfers between devices with their start and end apart: 55, of which 32 were waited for; matrix products, arithmetic and copies ran while one was open for 27% of the time, Pallas kernels for 3%

profile of v4, /device:TPU:0, one launch (start us, length us, event | category | flops | bytes accessed | tf_op | source)
XLA Modules:
  0.0 599.1 jit_solution(14689719436925237968)
XLA Ops:
  12.0 5.4 shard_map.271
  19.3 5.2 all-to-all-start
  27.1 8.3 %reshape.215 = bf16[64,2,4,4,2,176]{5,4,3,2,0,1:T(2,128)(2,1)S(1)} reshape(bf16[64,2,5632]{2,0,1:T(8,128)(2,1)} %copy.89) | data formatting | bytes 2883584 | tf_op jit(solution)/shard_map/reshape | solution.py:630
  37.6 5.4 reshape.216
  73.7 9.1 %collective-permute-done.7 = bf16[2,128,1024]{2,1,0:T(8,128)(2,1)S(1)} collective-permute-done((bf16[2,128,1024]{2,1,0:T(8,128)(2,1)S(1)}, bf16[2,128,1024]{2,1,0:T(8,128)(2,1)S(1)}, u32[]{:S(2)}, u32[]{:S(2)}) %collective-permute-start.7) | collective-permute-done | bytes 524320 | tf_op jit(solution)/shard_map/ppermute | solution.py:47
  88.2 9.6 %collective-permute-done.3 = bf16[2,88,2048]{2,1,0:T(8,128)(2,1)S(1)} collective-permute-done((bf16[2,88,2048]{2,1,0:T(8,128)(2,1)S(1)}, bf16[2,88,2048]{2,1,0:T(8,128)(2,1)S(1)}, u32[]{:S(2)}, u32[]{:S(2)}) %collective-permute-start.3) | collective-permute-done | bytes 720928 | tf_op jit(solution)/shard_map/ppermute | solution.py:47
  103.8 2.8 fusion.1
  106.6 6.8 %all-gather.6.cloned.1.call-done = bf16[2048,768]{1,0:T(8,128)(2,1)} async-done(((bf16[512,768]{1,0:T(8,128)(2,1)}), bf16[2048,768]{1,0:T(8,128)(2,1)}) %all-gather.6.cloned.1.call-update) | async-done | bytes 3145744 | tf_op jit(solution)/shard_map/all_gather | solution.py:33
  115.9 6.1 %fusion.57.proj_ref = f32[1024,768]{1,0:T(8,128)S(1)} fusion(bf16[1024,2048]{1,0:T(8,128)(2,1)} %fusion.1, bf16[2048,768]{1,0:T(8,128)(2,1)} %all-gather.6.cloned.1.call-done), kind=kOutput, calls=%fused_computation.212 | convolution fusion | flops 3221225472 | bytes 10485760 | tf_op jit(solution)/shard_map/dot_general | solution.py:652
  122.1 5.7 shard_map.272
  129.0 3.5 convolution_convert_fusion.1
  132.5 6.0 %collective-permute-done.16 = bf16[128,2048]{1,0:T(8,128)(2,1)S(1)} collective-permute-done((bf16[128,2048]{1,0:T(8,128)(2,1)S(1)}, bf16[128,2048]{1,0:T(8,128)(2,1)S(1)}, u32[]{:S(2)}, u32[]{:S(2)}) %collective-permute-start.16) | collective-permute-done | bytes 524320 | tf_op jit(solution)/shard_map/ppermute | solution.py:181
  146.4 5.6 collective-permute-done.19
  152.1 35.1 %collective-permute-done.18 = bf16[2,64,1408]{2,1,0:T(8,128)(2,1)} collective-permute-done((bf16[2,64,1408]{2,1,0:T(8,128)(2,1)}, bf16[2,64,1408]{2,1,0:T(8,128)(2,1)}, u32[]{:S(2)}, u32[]{:S(2)}) %collective-permute-start.18) | collective-permute-done | bytes 360480 | tf_op jit(solution)/shard_map/ppermute | solution.py:210
  190.0 7.0 %collective-permute-done.20 = bf16[128,2048]{1,0:T(8,128)(2,1)} collective-permute-done((bf16[128,2048]{1,0:T(8,128)(2,1)S(1)}, bf16[128,2048]{1,0:T(8,128)(2,1)}, u32[]{:S(2)}, u32[]{:S(2)}) %collective-permute-start.20) | collective-permute-done | bytes 524320 | tf_op jit(solution)/shard_map/ppermute | solution.py:181
  206.7 12.0 %collective-permute-done.24 = bf16[256,1408]{1,0:T(8,128)(2,1)S(1)} collective-permute-done((bf16[256,1408]{1,0:T(8,128)(2,1)S(1)}, bf16[256,1408]{1,0:T(8,128)(2,1)S(1)}, u32[]{:S(2)}, u32[]{:S(2)}) %collective-permute-start.24) | collective-permute-done | bytes 720928 | tf_op jit(solution)/shard_map/ppermute | solution.py:47
  220.6 3.6 collective-permute-done.22
  228.6 26.0 %collective-permute-done.25 = bf16[2,256,1408]{2,1,0:T(8,128)(2,1)S(1)} collective-permute-done((bf16[2,256,1408]{2,1,0:T(8,128)(2,1)S(1)}, bf16[2,256,1408]{2,1,0:T(8,128)(2,1)S(1)}, u32[]{:S(2)}, u32[]{:S(2)}) %collective-permute-start.25) | collective-permute-done | bytes 1441824 | tf_op jit(solution)/shard_map/ppermute | solution.py:47
  257.7 4.7 pad_maximum_fusion
  262.5 10.3 %fusion.58 = f32[1024,1408]{0,1:T(8,128)S(1)} fusion(bf16[1024,2048]{1,0:T(8,128)(2,1)} %all-gather.8.cloned.1.call-done, bf16[2048,1408]{1,0:T(8,128)(2,1)} %bitcast.268), kind=kOutput, calls=%fused_computation.213 | convolution fusion | flops 5905580032 | bytes 15728640 | tf_op jit(solution)/shard_map/dot_general | solution.py:675
  272.8 5.2 multiply_convert_fusion.2
  279.5 8.3 %convolution_convert_fusion.3 = bf16[1024,2048]{1,0:T(8,128)(2,1)} fusion(bf16[2048,1408]{1,0:T(8,128)(2,1)S(1)} %bitcast.269, bf16[1024,704]{0,1:T(8,128)(2,1)S(1)} %get-tuple-element.164, bf16[1024,704]{0,1:T(8,128)(2,1)S(1)} %get-tuple-element.163), kind=kOutput, calls=%fused_computation.15 | convolution fusion | flops 5913444352 | bytes 12845056 | tf_op jit(solution)/shard_map/dot_general | solution.py:686
  288.5 5.7 convolution_convert_fusion.2
  298.8 7.0 %convolution_convert_fusion = bf16[2048,1408]{1,0:T(8,128)(2,1)S(1)} fusion(bf16[1024,2048]{1,0:T(8,128)(2,1)S(1)} %copy-done.42, bf16[1024,704]{0,1:T(8,128)(2,1)S(1)} %copy-done.49, bf16[1024,704]{0,1:T(8,128)(2,1)S(1)} %copy-done.47), kind=kOutput, calls=%fused_computation.4 | convolution fusion | flops 5914230784 | bytes 12845056 | tf_op jit(solution)/shard_map/dot_general | solution.py:688
  313.3 4.5 convolution_convert_fusion.6
  317.7 22.8 %collective-permute-done.28 = bf16[2,256,1408]{2,1,0:T(8,128)(2,1)} collective-permute-done((bf16[2,256,1408]{2,1,0:T(8,128)(2,1)}, bf16[2,256,1408]{2,1,0:T(8,128)(2,1)}, u32[]{:S(2)}, u32[]{:S(2)}) %collective-permute-start.28) | collective-permute-done | bytes 1441824 | tf_op jit(solution)/shard_map/ppermute | solution.py:82
  340.5 3.0 collective-permute-done.27
  353.9 3.1 collective-permute-start.31
  360.5 17.0 %collective-permute-done.31 = bf16[128,2048]{1,0:T(8,128)(2,1)S(1)} collective-permute-done((bf16[128,2048]{1,0:T(8,128)(2,1)S(1)}, bf16[128,2048]{1,0:T(8,128)(2,1)S(1)}, u32[]{:S(2)}, u32[]{:S(2)}) %collective-permute-start.31) | collective-permute-done | bytes 524320 | tf_op jit(solution)/shard_map/ppermute | solution.py:124
  377.5 3.7 collective-permute-done.33
  381.2 16.7 %collective-permute-done.32 = bf16[128,2048]{1,0:T(8,128)(2,1)S(1)} collective-permute-done((bf16[128,2048]{1,0:T(8,128)(2,1)S(1)}, bf16[128,2048]{1,0:T(8,128)(2,1)S(1)}, u32[]{:S(2)}, u32[]{:S(2)}) %collective-permute-start.32) | collective-permute-done | bytes 524320 | tf_op jit(solution)/shard_map/ppermute | solution.py:124
  400.8 4.6 all-to-all-start.1
  406.7 4.6 fusion.14.d_mixed_ref
  411.3 7.0 %shard_map.275 = (bf16[1024,768]{1,0:T(8,128)(2,1)S(1)}, bf16[1024,256]{1,0:T(8,128)(2,1)S(1)}) custom-call(f32[1024,768]{1,0:T(8,128)} %copy-done.3, f32[1024,256]{1,0:T(8,128)S(1)} %get-tuple-element.93.state_ref, f32[1024,256]{1,0:T(8,128)S(1)} %fusion.14.d_mixed_ref, bf16[1024,128]{1,0:T(8,128)(2,1)S(1)} %slice.104.riders_ref, ...), custom_call_target="tpu_custom_call" | custom-call | tf_op jit(solution)/shard_map/pallas_call | solution.py:371
  421.7 5.9 convolution_convert_fusion.5
  430.2 10.3 %all-to-all-done.1 = bf16[8,64,1408]{2,1,0:T(8,128)(2,1)} async-done(((bf16[8,64,1408]{2,1,0:T(8,128)(2,1)}), bf16[8,64,1408]{2,1,0:T(8,128)(2,1)}, u32[]{:S(2)}, u32[]{:S(2)}) %all-to-all-start.1) | async-done | bytes 1441824 | tf_op jit(solution)/shard_map/all_to_all | solution.py:41
  440.6 5.6 convolution_convert_fusion.4
  447.2 4.0 collective-permute-done.34
  455.5 7.8 %reshape.231 = bf16[4,2,64,2,4,176]{5,4,3,2,1,0:T(4,128)(2,1)S(1)} reshape(bf16[8,64,1408]{2,1,0:T(8,128)(2,1)} %all-to-all-done.1) | data formatting | bytes 2883584 | tf_op jit(solution)/shard_map/reshape | solution.py:719
  468.7 4.6 copy.73
  473.3 6.6 %reshape.232.grad_ref = bf16[2,64,5632]{2,1,0:T(8,128)(2,1)} reshape(bf16[2,64,4,4,2,176]{5,4,3,2,1,0:T(2,128)(2,1)} %copy.73) | data formatting | bytes 2883584 | tf_op jit(solution)/shard_map/reshape | solution.py:720
  499.3 22.8 %reduce-scatter.9.cloned.1.call-done = bf16[512,1024]{1,0:T(8,128)(2,1)} async-done(((bf16[2048,1024]{1,0:T(8,128)(2,1)}), bf16[512,1024]{1,0:T(8,128)(2,1)}) %reduce-scatter.9.cloned.1.call-update) | async-done | bytes 1048592 | tf_op jit(solution)/shard_map/reduce_scatter | solution.py:37
  524.2 4.6 all-to-all-start.2
  531.4 10.0 %all-to-all-done.2.got_ref = bf16[8,64,768]{2,1,0:T(8,128)(2,1)} async-done(((bf16[8,64,768]{2,1,0:T(8,128)(2,1)}), bf16[8,64,768]{2,1,0:T(8,128)(2,1)}, u32[]{:S(2)}, u32[]{:S(2)}) %all-to-all-start.2) | async-done | bytes 786464 | tf_op jit(solution)/shard_map/all_to_all | solution.py:41
  562.9 4.3 collective-permute-start.43
  568.8 5.7 multiply_subtract_fusion
  574.5 7.4 %shard_map.277 = (f32[64,4,2048]{2,1,0:T(4,128)}, f32[64,4,2048]{2,1,0:T(4,128)}, f32[64,4,2048]{2,1,0:T(4,128)}) custom-call(f32[1,1]{1,0:T(1,128)} %bitcast.104.clip_ref, f32[64,4,2048]{2,1,0:T(4,128)S(1)} %copy-done.6, f32[64,4,2048]{2,1,0:T(4,128)S(1)} %copy-done.11, f32[64,4,2048]{2,1,0:T(4,128)} %second_ref.2, f32[4,64,2048]{2,1,0:T(8,128)} %copy-done.12), custom_call_target="tpu_custom_call" | custom-call | tf_op jit(solution)/shard_map/pallas_call | solution.py:400
  581.9 9.0 %shard_map.278 = (f32[64,2,5632]{2,1,0:T(2,128)}, f32[64,2,5632]{2,1,0:T(2,128)}, f32[64,2,5632]{2,1,0:T(2,128)}) custom-call(f32[1,1]{1,0:T(1,128)} %bitcast.104.clip_ref, f32[64,2,5632]{2,1,0:T(2,128)S(1)} %copy-done.1, f32[64,2,5632]{2,1,0:T(2,128)} %first_ref.3, f32[64,2,5632]{2,1,0:T(2,128)} %second_ref.3, bf16[2,64,5632]{2,1,0:T(8,128)(2,1)S(1)} %copy-done.4), custom_call_target="tpu_custom_call" | custom-call | tf_op jit(solution)/shard_map/pallas_call | solution.py:400
  (327 shorter events, 176.6 us)
Async XLA Ops:
  7.2 36.9 %all-gather.12.cloned.1.call-start = ((), (), s32[]{:S(2)}) async-start(), calls=%async_computation.14 | async-start | bytes 1310720 | tf_op jit(solution)/shard_map/all_gather | solution.py:33
  19.3 24.8 %all-to-all-start = ((bf16[8,64,768]{2,1,0:T(8,128)(2,1)}), bf16[8,64,768]{2,1,0:T(8,128)(2,1)}, u32[]{:S(2)}, u32[]{:S(2)}) async-start(bf16[8,64,768]{2,1,0:T(8,128)(2,1)} %copy-done.17), calls=%async_computation | async-start | bytes 1572864 | tf_op jit(solution)/shard_map/all_to_all | solution.py:41
  24.4 88.9 %all-gather.6.cloned.1.call-start = ((), (), s32[]{:S(2)}) async-start(), calls=%async_computation.7 | async-start | bytes 3932160 | tf_op jit(solution)/shard_map/all_gather | solution.py:33
  47.7 149.3 %reduce-scatter.5.cloned.1.call-start = ((), (), s32[]{:S(2)}) async-start(), calls=%async_computation.8 | async-start | bytes 5013504 | tf_op jit(solution)/shard_map/reduce_scatter | solution.py:37
  49.1 5.5 collective-permute-start.11
  51.1 15.0 %collective-permute-start.4 = (bf16[128,1024]{1,0:T(8,128)(2,1)S(1)}, bf16[128,1024]{1,0:T(8,128)(2,1)S(1)}, u32[]{:S(2)}, u32[]{:S(2)}) collective-permute-start(bf16[128,1024]{1,0:T(8,128)(2,1)S(1)} %get-tuple-element.230), channel_id=1, source_target_pairs={{0,2},{2,0},{1,3},{3,1},{4,6},{6,4},{5,7},{7,5},{8,10},{10,8},{9,1... | collective-permute-start | bytes 786440 | tf_op jit(solution)/shard_map/ppermute | solution.py:47
  52.7 14.1 %collective-permute-start.6 = (bf16[128,1024]{1,0:T(8,128)(2,1)S(1)}, bf16[128,1024]{1,0:T(8,128)(2,1)}, u32[]{:S(2)}, u32[]{:S(2)}) collective-permute-start(bf16[128,1024]{1,0:T(8,128)(2,1)S(1)} %get-tuple-element.231), channel_id=1, source_target_pairs={{0,4},{4,0},{1,5},{5,1},{2,6},{6,2},{3,7},{7,3},{8,12},{12,8},{9,1... | collective-permute-start | bytes 786440 | tf_op jit(solution)/shard_map/ppermute | solution.py:47
  54.7 5.0 collective-permute-start.12
  57.6 12.6 %collective-permute-start = (bf16[88,2048]{1,0:T(8,128)(2,1)}, bf16[88,2048]{1,0:T(8,128)(2,1)}, u32[]{:S(2)}, u32[]{:S(2)}) collective-permute-start(bf16[88,2048]{1,0:T(8,128)(2,1)} %get-tuple-element.226), channel_id=1, source_target_pairs={{0,2},{2,0},{1,3},{3,1},{4,6},{6,4},{5,7},{7,5},{8,10},{10,8},{9,1... | collective-permute-start | bytes 1081352 | tf_op jit(solution)/shard_map/ppermute | solution.py:47
  57.8 12.4 %collective-permute-start.2 = (bf16[88,2048]{1,0:T(8,128)(2,1)}, bf16[88,2048]{1,0:T(8,128)(2,1)}, u32[]{:S(2)}, u32[]{:S(2)}) collective-permute-start(bf16[88,2048]{1,0:T(8,128)(2,1)} %get-tuple-element.227), channel_id=1, source_target_pairs={{0,4},{4,0},{1,5},{5,1},{2,6},{6,2},{3,7},{7,3},{8,12},{12,8},{9,1... | collective-permute-start | bytes 1081352 | tf_op jit(solution)/shard_map/ppermute | solution.py:47
  59.7 5.9 collective-permute-start.13
  65.7 18.9 %collective-permute-start.14 = (bf16[4,64,1408]{2,1,0:T(8,128)(2,1)}, bf16[4,64,1408]{2,1,0:T(8,128)(2,1)}, u32[]{:S(2)}, u32[]{:S(2)}) collective-permute-start(bf16[4,64,1408]{2,1,0:T(8,128)(2,1)} %dynamic-slice_bitcast_fusion.8), channel_id=1, source_target_pairs={{0,1},{1,0},{2,3},{3,2},{4,5},{5,4},{6,7},{7,6},{8,9},{9,8},{10,11... | collective-permute-start | bytes 2162696 | tf_op jit(solution)/shard_map/ppermute | solution.py:200
  68.0 14.8 %collective-permute-start.7 = (bf16[2,128,1024]{2,1,0:T(8,128)(2,1)S(1)}, bf16[2,128,1024]{2,1,0:T(8,128)(2,1)S(1)}, u32[]{:S(2)}, u32[]{:S(2)}) collective-permute-start(bf16[2,128,1024]{2,1,0:T(8,128)(2,1)S(1)} %pad_maximum_fusion.16), channel_id=1, source_target_pairs={{0,2},{2,0},{1,3},{3,1},{4,6},{6,4},{5,7},{7,5},{8,10},{10,8},{9,1... | collective-permute-start | bytes 1572872 | tf_op jit(solution)/shard_map/ppermute | solution.py:47
  69.4 14.8 %collective-permute-start.5 = (bf16[2,128,1024]{2,1,0:T(8,128)(2,1)S(1)}, bf16[2,128,1024]{2,1,0:T(8,128)(2,1)S(1)}, u32[]{:S(2)}, u32[]{:S(2)}) collective-permute-start(bf16[2,128,1024]{2,1,0:T(8,128)(2,1)S(1)} %pad_maximum_fusion.15), channel_id=1, source_target_pairs={{0,4},{4,0},{1,5},{5,1},{2,6},{6,2},{3,7},{7,3},{8,12},{12,8},{9,1... | collective-permute-start | bytes 1572872 | tf_op jit(solution)/shard_map/ppermute | solution.py:47
  71.5 26.3 %collective-permute-start.3 = (bf16[2,88,2048]{2,1,0:T(8,128)(2,1)S(1)}, bf16[2,88,2048]{2,1,0:T(8,128)(2,1)S(1)}, u32[]{:S(2)}, u32[]{:S(2)}) collective-permute-start(bf16[2,88,2048]{2,1,0:T(8,128)(2,1)S(1)} %pad_maximum_fusion.14), channel_id=1, source_target_pairs={{0,2},{2,0},{1,3},{3,1},{4,6},{6,4},{5,7},{7,5},{8,10},{10,8},{9,1... | collective-permute-start | bytes 2162696 | tf_op jit(solution)/shard_map/ppermute | solution.py:47
  71.9 27.1 %collective-permute-start.1 = (bf16[2,88,2048]{2,1,0:T(8,128)(2,1)S(1)}, bf16[2,88,2048]{2,1,0:T(8,128)(2,1)S(1)}, u32[]{:S(2)}, u32[]{:S(2)}) collective-permute-start(bf16[2,88,2048]{2,1,0:T(8,128)(2,1)S(1)} %pad_maximum_fusion.13), channel_id=1, source_target_pairs={{0,4},{4,0},{1,5},{5,1},{2,6},{6,2},{3,7},{7,3},{8,12},{12,8},{9,1... | collective-permute-start | bytes 2162696 | tf_op jit(solution)/shard_map/ppermute | solution.py:47
  84.5 16.4 %collective-permute-start.8 = (bf16[2,2,128,2048]{3,2,1,0:T(8,128)(2,1)S(1)}, bf16[2,2,128,2048]{3,2,1,0:T(8,128)(2,1)S(1)}, u32[]{:S(2)}, u32[]{:S(2)}) collective-permute-start(bf16[2,2,128,2048]{3,2,1,0:T(8,128)(2,1)S(1)} %pad_maximum_fusion.4), channel_id=1, source_target_pairs={{0,1},{1,0},{2,3},{3,2},{4,5},{5,4},{6,7},{7,6},{8,9},{9,8},{10,11... | collective-permute-start | bytes 6291464 | tf_op jit(solution)/shard_map/ppermute | solution.py:47
  113.4 25.1 %collective-permute-start.16 = (bf16[128,2048]{1,0:T(8,128)(2,1)S(1)}, bf16[128,2048]{1,0:T(8,128)(2,1)S(1)}, u32[]{:S(2)}, u32[]{:S(2)}) collective-permute-start(bf16[128,2048]{1,0:T(8,128)(2,1)S(1)} %multiply_convert_fusion.4.cot_ref), channel_id=1, source_target_pairs={{0,24},{8,0},{16,8},{24,16},{1,25},{9,1},{17,9},{25,17},{2,26},{10... | collective-permute-start | bytes 1572872 | tf_op jit(solution)/shard_map/ppermute | solution.py:181
  114.1 24.4 %collective-permute-start.15 = (bf16[128,2048]{1,0:T(8,128)(2,1)S(1)}, bf16[128,2048]{1,0:T(8,128)(2,1)}, u32[]{:S(2)}, u32[]{:S(2)}) collective-permute-start(bf16[128,2048]{1,0:T(8,128)(2,1)S(1)} %multiply_convert_fusion.4.cot_ref), channel_id=1, source_target_pairs={{0,8},{8,16},{16,24},{24,0},{1,9},{9,17},{17,25},{25,1},{2,10},{10... | collective-permute-start | bytes 1572872 | tf_op jit(solution)/shard_map/ppermute | solution.py:181
  139.3 123.2 %all-gather.8.cloned.1.call-start = ((), (), s32[]{:S(2)}) async-start(), calls=%async_computation.9 | async-start | bytes 4718592 | tf_op jit(solution)/shard_map/all_gather | solution.py:33
  141.4 10.7 %collective-permute-start.19 = (bf16[2,64,1408]{2,1,0:T(8,128)(2,1)}, bf16[2,64,1408]{2,1,0:T(8,128)(2,1)}, u32[]{:S(2)}, u32[]{:S(2)}) collective-permute-start(bf16[2,64,1408]{2,1,0:T(8,128)(2,1)} %get-tuple-element.205), channel_id=1, source_target_pairs={{0,24},{8,0},{16,8},{24,16},{1,25},{9,1},{17,9},{25,17},{2,26},{10... | collective-permute-start | bytes 1081352 | tf_op jit(solution)/shard_map/ppermute | solution.py:210
  142.8 44.4 %collective-permute-start.18 = (bf16[2,64,1408]{2,1,0:T(8,128)(2,1)}, bf16[2,64,1408]{2,1,0:T(8,128)(2,1)}, u32[]{:S(2)}, u32[]{:S(2)}) collective-permute-start(bf16[2,64,1408]{2,1,0:T(8,128)(2,1)} %get-tuple-element.206), channel_id=1, source_target_pairs={{0,16},{8,24},{16,0},{24,8},{1,17},{9,25},{17,1},{25,9},{2,18},{10... | collective-permute-start | bytes 1081352 | tf_op jit(solution)/shard_map/ppermute | solution.py:210
  143.1 44.0 %collective-permute-start.17 = (bf16[2,64,1408]{2,1,0:T(8,128)(2,1)S(1)}, bf16[2,64,1408]{2,1,0:T(8,128)(2,1)}, u32[]{:S(2)}, u32[]{:S(2)}) collective-permute-start(bf16[2,64,1408]{2,1,0:T(8,128)(2,1)S(1)} %get-tuple-element.207), channel_id=1, source_target_pairs={{0,8},{8,16},{16,24},{24,0},{1,9},{9,17},{17,25},{25,1},{2,10},{10... | collective-permute-start | bytes 1081352 | tf_op jit(solution)/shard_map/ppermute | solution.py:210
  144.6 52.4 %collective-permute-start.20 = (bf16[128,2048]{1,0:T(8,128)(2,1)S(1)}, bf16[128,2048]{1,0:T(8,128)(2,1)}, u32[]{:S(2)}, u32[]{:S(2)}) collective-permute-start(bf16[128,2048]{1,0:T(8,128)(2,1)S(1)} %multiply_convert_fusion.4.cot_ref), channel_id=1, source_target_pairs={{0,16},{8,24},{16,0},{24,8},{1,17},{9,25},{17,1},{25,9},{2,18},{10... | collective-permute-start | bytes 1572872 | tf_op jit(solution)/shard_map/ppermute | solution.py:181
  200.3 143.2 %reduce-scatter.7.cloned.1.call-start = ((), (), s32[]{:S(2)}) async-start(), calls=%async_computation.10 | async-start | bytes 4718592 | tf_op jit(solution)/shard_map/reduce_scatter | solution.py:37
  201.9 16.9 %collective-permute-start.24 = (bf16[256,1408]{1,0:T(8,128)(2,1)S(1)}, bf16[256,1408]{1,0:T(8,128)(2,1)S(1)}, u32[]{:S(2)}, u32[]{:S(2)}) collective-permute-start(bf16[256,1408]{1,0:T(8,128)(2,1)S(1)} %bitcast.283), channel_id=1, source_target_pairs={{0,4},{4,0},{1,5},{5,1},{2,6},{6,2},{3,7},{7,3},{8,12},{12,8},{9,1... | collective-permute-start | bytes 2162696 | tf_op jit(solution)/shard_map/ppermute | solution.py:47
  205.1 20.2 %collective-permute-start.21 = (bf16[4,128,2048]{2,1,0:T(8,128)(2,1)S(1)}, bf16[4,128,2048]{2,1,0:T(8,128)(2,1)S(1)}, u32[]{:S(2)}, u32[]{:S(2)}) collective-permute-start(bf16[4,128,2048]{2,1,0:T(8,128)(2,1)S(1)} %pad_maximum_fusion.5), channel_id=1, source_target_pairs={{0,1},{1,0},{2,3},{3,2},{4,5},{5,4},{6,7},{7,6},{8,9},{9,8},{10,11... | collective-permute-start | bytes 6291464 | tf_op jit(solution)/shard_map/ppermute | solution.py:47
  205.2 19.0 %collective-permute-start.22 = (bf16[256,1408]{1,0:T(8,128)(2,1)S(1)}, bf16[256,1408]{1,0:T(8,128)(2,1)S(1)}, u32[]{:S(2)}, u32[]{:S(2)}) collective-permute-start(bf16[256,1408]{1,0:T(8,128)(2,1)S(1)} %bitcast.282), channel_id=1, source_target_pairs={{0,2},{2,0},{1,3},{3,1},{4,6},{6,4},{5,7},{7,5},{8,10},{10,8},{9,1... | collective-permute-start | bytes 2162696 | tf_op jit(solution)/shard_map/ppermute | solution.py:47
  219.1 35.5 %collective-permute-start.25 = (bf16[2,256,1408]{2,1,0:T(8,128)(2,1)S(1)}, bf16[2,256,1408]{2,1,0:T(8,128)(2,1)S(1)}, u32[]{:S(2)}, u32[]{:S(2)}) collective-permute-start(bf16[2,256,1408]{2,1,0:T(8,128)(2,1)S(1)} %pad_maximum_fusion.11), channel_id=1, source_target_pairs={{0,2},{2,0},{1,3},{3,1},{4,6},{6,4},{5,7},{7,5},{8,10},{10,8},{9,1... | collective-permute-start | bytes 4325384 | tf_op jit(solution)/shard_map/ppermute | solution.py:47
  224.6 32.9 %collective-permute-start.23 = (bf16[2,256,1408]{2,1,0:T(8,128)(2,1)S(1)}, bf16[2,256,1408]{2,1,0:T(8,128)(2,1)S(1)}, u32[]{:S(2)}, u32[]{:S(2)}) collective-permute-start(bf16[2,256,1408]{2,1,0:T(8,128)(2,1)S(1)} %pad_maximum_fusion.10), channel_id=1, source_target_pairs={{0,4},{4,0},{1,5},{5,1},{2,6},{6,2},{3,7},{7,3},{8,12},{12,8},{9,1... | collective-permute-start | bytes 4325384 | tf_op jit(solution)/shard_map/ppermute | solution.py:47
  287.9 112.9 %all-gather.10.cloned.1.call-start = ((), (), s32[]{:S(2)}) async-start(), calls=%async_computation.11 | async-start | bytes 5013504 | tf_op jit(solution)/shard_map/all_gather | solution.py:33
  296.9 46.6 %collective-permute-start.26 = (bf16[4,128,2048]{2,1,0:T(8,128)(2,1)}, bf16[4,128,2048]{2,1,0:T(8,128)(2,1)}, u32[]{:S(2)}, u32[]{:S(2)}) collective-permute-start(bf16[4,128,2048]{2,1,0:T(8,128)(2,1)} %get-tuple-element.170), channel_id=1, source_target_pairs={{0,1},{1,0},{2,3},{3,2},{4,5},{5,4},{6,7},{7,6},{8,9},{9,8},{10,11... | collective-permute-start | bytes 6291464 | tf_op jit(solution)/shard_map/ppermute | solution.py:82
  308.1 32.5 %collective-permute-start.28 = (bf16[2,256,1408]{2,1,0:T(8,128)(2,1)}, bf16[2,256,1408]{2,1,0:T(8,128)(2,1)}, u32[]{:S(2)}, u32[]{:S(2)}) collective-permute-start(bf16[2,256,1408]{2,1,0:T(8,128)(2,1)} %get-tuple-element.176), channel_id=1, source_target_pairs={{0,2},{2,0},{1,3},{3,1},{4,6},{6,4},{5,7},{7,5},{8,10},{10,8},{9,1... | collective-permute-start | bytes 4325384 | tf_op jit(solution)/shard_map/ppermute | solution.py:82
  311.3 32.2 %collective-permute-start.27 = (bf16[2,256,1408]{2,1,0:T(8,128)(2,1)}, bf16[2,256,1408]{2,1,0:T(8,128)(2,1)}, u32[]{:S(2)}, u32[]{:S(2)}) collective-permute-start(bf16[2,256,1408]{2,1,0:T(8,128)(2,1)} %get-tuple-element.178), channel_id=1, source_target_pairs={{0,4},{4,0},{1,5},{5,1},{2,6},{6,2},{3,7},{7,3},{8,12},{12,8},{9,1... | collective-permute-start | bytes 4325384 | tf_op jit(solution)/shard_map/ppermute | solution.py:82
  348.4 145.2 %reduce-scatter.11.cloned.1.call-start = ((), (), s32[]{:S(2)}) async-start(), calls=%async_computation.13 | async-start | bytes 3604480 | tf_op jit(solution)/shard_map/reduce_scatter | solution.py:37
  350.8 48.4 %collective-permute-start.29 = (bf16[256,1408]{1,0:T(8,128)(2,1)S(1)}, bf16[256,1408]{1,0:T(8,128)(2,1)S(1)}, u32[]{:S(2)}, u32[]{:S(2)}) collective-permute-start(bf16[256,1408]{1,0:T(8,128)(2,1)S(1)} %dynamic-slice_bitcast_fusion.7), channel_id=1, source_target_pairs={{0,2},{2,0},{1,3},{3,1},{4,6},{6,4},{5,7},{7,5},{8,10},{10,8},{9,1... | collective-permute-start | bytes 2162696 | tf_op jit(solution)/shard_map/ppermute | solution.py:82
  353.9 23.6 %collective-permute-start.31 = (bf16[128,2048]{1,0:T(8,128)(2,1)S(1)}, bf16[128,2048]{1,0:T(8,128)(2,1)S(1)}, u32[]{:S(2)}, u32[]{:S(2)}) collective-permute-start(bf16[128,2048]{1,0:T(8,128)(2,1)S(1)} %get-tuple-element.192), channel_id=1, source_target_pairs={{0,24},{8,0},{16,8},{24,16},{1,25},{9,1},{17,9},{25,17},{2,26},{10... | collective-permute-start | bytes 1572872 | tf_op jit(solution)/shard_map/ppermute | solution.py:124
  357.0 24.2 %collective-permute-start.33 = (bf16[128,2048]{1,0:T(8,128)(2,1)S(1)}, bf16[128,2048]{1,0:T(8,128)(2,1)S(1)}, u32[]{:S(2)}, u32[]{:S(2)}) collective-permute-start(bf16[128,2048]{1,0:T(8,128)(2,1)S(1)} %get-tuple-element.193), channel_id=1, source_target_pairs={{0,8},{8,16},{16,24},{24,0},{1,9},{9,17},{17,25},{25,1},{2,10},{10... | collective-permute-start | bytes 1572872 | tf_op jit(solution)/shard_map/ppermute | solution.py:124
  357.2 40.7 %collective-permute-start.32 = (bf16[128,2048]{1,0:T(8,128)(2,1)S(1)}, bf16[128,2048]{1,0:T(8,128)(2,1)S(1)}, u32[]{:S(2)}, u32[]{:S(2)}) collective-permute-start(bf16[128,2048]{1,0:T(8,128)(2,1)S(1)} %get-tuple-element.194), channel_id=1, source_target_pairs={{0,16},{8,24},{16,0},{24,8},{1,17},{9,25},{17,1},{25,9},{2,18},{10... | collective-permute-start | bytes 1572872 | tf_op jit(solution)/shard_map/ppermute | solution.py:124
  359.6 39.8 %collective-permute-start.30 = (bf16[256,1408]{1,0:T(8,128)(2,1)S(1)}, bf16[256,1408]{1,0:T(8,128)(2,1)S(1)}, u32[]{:S(2)}, u32[]{:S(2)}) collective-permute-start(bf16[256,1408]{1,0:T(8,128)(2,1)S(1)} %dynamic-slice_bitcast_fusion.6), channel_id=1, source_target_pairs={{0,4},{4,0},{1,5},{5,1},{2,6},{6,2},{3,7},{7,3},{8,12},{12,8},{9,1... | collective-permute-start | bytes 2162696 | tf_op jit(solution)/shard_map/ppermute | solution.py:82
  400.8 39.7 %all-to-all-start.1 = ((bf16[8,64,1408]{2,1,0:T(8,128)(2,1)}), bf16[8,64,1408]{2,1,0:T(8,128)(2,1)}, u32[]{:S(2)}, u32[]{:S(2)}) async-start(bf16[8,64,1408]{2,1,0:T(8,128)(2,1)} %bitcast.273), calls=%async_computation.3 | async-start | bytes 2883584 | tf_op jit(solution)/shard_map/all_to_all | solution.py:41
  405.4 116.7 %reduce-scatter.9.cloned.1.call-start = ((), (), s32[]{:S(2)}) async-start(), calls=%async_computation.12 | async-start | bytes 5242880 | tf_op jit(solution)/shard_map/reduce_scatter | solution.py:37
  454.0 25.9 %collective-permute-start.37 = (bf16[2,128,1024]{2,1,0:T(8,128)(2,1)}, bf16[2,128,1024]{2,1,0:T(8,128)(2,1)}, u32[]{:S(2)}, u32[]{:S(2)}) collective-permute-start(bf16[2,128,1024]{2,1,0:T(8,128)(2,1)} %dynamic-slice_bitcast_fusion.9), channel_id=1, source_target_pairs={{0,2},{2,0},{1,3},{3,1},{4,6},{6,4},{5,7},{7,5},{8,10},{10,8},{9,1... | collective-permute-start | bytes 1572872 | tf_op jit(solution)/shard_map/ppermute | solution.py:82
  465.2 17.6 %collective-permute-start.35 = (bf16[2,128,1024]{2,1,0:T(8,128)(2,1)}, bf16[2,128,1024]{2,1,0:T(8,128)(2,1)}, u32[]{:S(2)}, u32[]{:S(2)}) collective-permute-start(bf16[2,128,1024]{2,1,0:T(8,128)(2,1)} %dynamic-slice_bitcast_fusion.10), channel_id=1, source_target_pairs={{0,4},{4,0},{1,5},{5,1},{2,6},{6,2},{3,7},{7,3},{8,12},{12,8},{9,1... | collective-permute-start | bytes 1572872 | tf_op jit(solution)/shard_map/ppermute | solution.py:82
  481.5 7.9 %collective-permute-start.38 = (bf16[128,1024]{1,0:T(8,128)(2,1)S(1)}, bf16[128,1024]{1,0:T(8,128)(2,1)S(1)}, u32[]{:S(2)}, u32[]{:S(2)}) collective-permute-start(bf16[128,1024]{1,0:T(8,128)(2,1)S(1)} %dynamic-slice_bitcast_fusion.17), channel_id=1, source_target_pairs={{0,4},{4,0},{1,5},{5,1},{2,6},{6,2},{3,7},{7,3},{8,12},{12,8},{9,1... | collective-permute-start | bytes 786440 | tf_op jit(solution)/shard_map/ppermute | solution.py:82
  484.2 7.6 %collective-permute-start.36 = (bf16[128,1024]{1,0:T(8,128)(2,1)S(1)}, bf16[128,1024]{1,0:T(8,128)(2,1)S(1)}, u32[]{:S(2)}, u32[]{:S(2)}) collective-permute-start(bf16[128,1024]{1,0:T(8,128)(2,1)S(1)} %dynamic-slice_bitcast_fusion.18), channel_id=1, source_target_pairs={{0,2},{2,0},{1,3},{3,1},{4,6},{6,4},{5,7},{7,5},{8,10},{10,8},{9,1... | collective-permute-start | bytes 786440 | tf_op jit(solution)/shard_map/ppermute | solution.py:82
  524.2 17.2 %all-to-all-start.2 = ((bf16[8,64,768]{2,1,0:T(8,128)(2,1)}), bf16[8,64,768]{2,1,0:T(8,128)(2,1)}, u32[]{:S(2)}, u32[]{:S(2)}) async-start(bf16[8,64,768]{2,1,0:T(8,128)(2,1)} %bitcast.278), calls=%async_computation.6 | async-start | bytes 1572864 | tf_op jit(solution)/shard_map/all_to_all | solution.py:41
  562.9 4.5 collective-permute-start.43
  (60 other events, 410.0 us)
Sparse Core Ops, SparseCore 0:
  10.4 30.6 all-gather.11
  47.8 65.4 all-gather.5
  138.6 51.9 reduce-scatter.4
  200.5 46.8 all-gather.7
  288.0 49.0 reduce-scatter.6
  348.5 44.7 all-gather.9
  400.9 41.9 reduce-scatter.10
  445.4 76.7 reduce-scatter.8

commit v5 on v4

--- a/solution.py
+++ b/solution.py
@@ -222,8 +222,8 @@
     return ring_terms(value, "c")
 
 
-def total_of(value):
-    for axis in ("c", "x", "y", "z"):
+def total_of(value, axes):
+    for axis in axes:
         count = lax.axis_size(axis)
         hop = 1
         while hop < count:
@@ -443,13 +443,34 @@
     )(weight)
 
 
-def settle(got_ref, out_ref, low_ref, grad_ref, first_ref, inner_ref, total_ref):
+def row_sums(shard_ref, first_ref, inner_ref, sums_ref):
+    split = first_ref.shape[1]
+    grad = shard_ref[...].astype(F32)
+    first = jnp.sum(grad[:, :split] * first_ref[...].astype(F32), axis=1, keepdims=True)
+    inner = jnp.sum(grad[:, split:] * inner_ref[...].astype(F32), axis=1, keepdims=True)
+    squares = jnp.sum(grad * grad, axis=1, keepdims=True)
+    lane = lax.broadcasted_iota(jnp.int32, sums_ref.shape, 1)
+    sums_ref[...] = jnp.where(lane == 0, first, jnp.where(lane == 1, inner, squares))
+
+
+def run_row_sums(shard, first, inner):
+    if first.shape[1] % 128 != 0 or inner.shape[1] % 128 != 0:
+        grad = shard.astype(F32)
+        split = first.shape[1]
+        parts = [grad[:, :split] * first.astype(F32), grad[:, split:] * inner.astype(F32), grad * grad]
+        return [jnp.sum(part, axis=1) for part in parts]
+    sums = pl.pallas_call(
+        row_sums,
+        out_shape=jax.ShapeDtypeStruct((shard.shape[0], 128), F32),
+        compiler_params=pltpu.CompilerParams(vmem_limit_bytes=48 * 2**20),
+    )(shard, first, inner)
+    return [sums[:, column] for column in range(3)]
+
+
+def settle(got_ref, out_ref, grad_ref):
     spots, own, packed = got_ref.shape
-    width = out_ref.shape[1]
     planes = packed // (3 * own)
     low_half = lax.broadcasted_iota(jnp.int32, (own, 2 * own), 1) < own
-    total = jnp.zeros((own, 2 * own), F32)
-    first, inner = total, total
     for pair in range(0, spots, 2):
         for kind in range(3):
             for plane in range(0, planes, 2):
@@ -459,39 +480,22 @@
                 near = jnp.where(low_half, even, pltpu.roll(odd, own, 1))
                 far = jnp.where(low_half, pltpu.roll(even, own, 1), odd)
                 for step, grad in enumerate((near, far)):
-                    place = pl.ds(((plane + step) * spots + pair) * own, 2 * own)
-                    grad_ref[kind, :, place] = grad
-                    total += grad * grad
-                    first += grad * low_ref[kind, :, place].astype(F32)
-    for start in range(0, width, 2 * own):
-        place = pl.ds(start, 2 * own)
-        grad = out_ref[:, place].astype(F32)
-        grad_ref[3, :, place] = grad
-        total += grad * grad
-        inner += grad * low_ref[3, :, place].astype(F32)
-    first_ref[...] = jnp.sum(first, axis=1, keepdims=True)
-    inner_ref[...] = jnp.sum(inner, axis=1, keepdims=True)
-    total_ref[...] = jnp.sum(total, axis=1, keepdims=True)
-
-
-def run_settle(got, shard_out, low_mixer):
+                    grad_ref[kind, :, pl.ds(((plane + step) * spots + pair) * own, 2 * own)] = grad
+    grad_ref[3, :, :] = out_ref[...].astype(F32)
+
+
+def run_settle(got, shard_out):
     spots, own, packed = got.shape
     width = shard_out.shape[1]
     planes = packed // (3 * own)
     if 2 * own != 128 or planes % 2 != 0:
-        grad = got.reshape(spots, own, 3, planes, own).transpose(1, 2, 3, 0, 4)
-        grad = jnp.concatenate([grad.reshape(own, 3, width), shard_out[:, None, :]], axis=1)
-        grad = grad.astype(F32)
-        product = jnp.sum(grad * low_mixer.swapaxes(0, 1).astype(F32), axis=2)
-        squares = jnp.sum(grad * grad, axis=(1, 2))
-        return grad.swapaxes(0, 1), jnp.sum(product[:, :3], axis=1), product[:, 3], squares
-    column = jax.ShapeDtypeStruct((own, 1), F32)
-    grad, *sums = pl.pallas_call(
+        grad = got.reshape(spots, own, 3, planes, own).transpose(2, 1, 3, 0, 4).reshape(3, own, width)
+        return jnp.concatenate([grad, shard_out[None]], axis=0).astype(F32)
+    return pl.pallas_call(
         settle,
-        out_shape=[jax.ShapeDtypeStruct((4, own, width), F32)] + [column] * 3,
+        out_shape=jax.ShapeDtypeStruct((4, own, width), F32),
         compiler_params=pltpu.CompilerParams(vmem_limit_bytes=48 * 2**20),
-    )(got, shard_out, low_mixer)
-    return [grad] + [column[:, 0] for column in sums]
+    )(got, shard_out)
 
 
 def column_blocks(width, first, second):
@@ -677,8 +681,6 @@
     silu_gate = silu(gate)
     hidden = (silu_gate * up_value).astype(BF)
 
-    grad_down = lax.dot_general(hidden, cot_all, (((0,), (0,)), ((), ())), preferred_element_type=F32)
-    grad_down = grad_down.astype(BF)
     d_hidden = lax.dot_general(cot_all, w_down, (((1,), (1,)), ((), ())), preferred_element_type=F32)
     d_gate = d_hidden * up_value * silu_grad(gate)
     d_up = d_hidden * silu_gate
@@ -689,14 +691,15 @@
     grad_in = grad_in.astype(BF)
     down = jnp.dot(hidden, w_down, preferred_element_type=F32).astype(BF)
     sums_in = quad_sums(grad_in)
-    downs = core_terms(down)
-    d_n2, grad_down, *held_terms = tied(d_n2, grad_down, *downs, *sums_in)
-    downs, sums_in = held_terms[: len(downs)], held_terms[len(downs) :]
+    down, held_hidden = tied(added(core_terms(down)).astype(BF), hidden)
+    grad_down = lax.dot_general(
+        held_hidden, cot_all, (((0,), (0,)), ((), ())), preferred_element_type=F32
+    ).astype(BF)
+    d_n2, grad_down, down, *sums_in = tied(d_n2, grad_down, down, *sums_in)
     d_mid, d_mix_home = run_leave(
         d_n2, cot_low, after_mix, mid_factor, mix_raw, home_factor, gain_glu, order
     )
-    *downs, d_mix_home = tied(*downs, d_mix_home)
-    down = direct_scatter(added(downs).astype(BF), "z")
+    down = direct_scatter(down, "z")
     shard_in = quad_rest(*sums_in).astype(BF)
     d_mix = gather(d_mix_home, PLANE)
     d_mix, shard_in, grad_down, down = tied(d_mix, shard_in, grad_down, down)
@@ -724,17 +727,34 @@
     d_n1 = lax.dot_general(held_proj, w_proj, (((1,), (1,)), ((), ())), preferred_element_type=F32)
     d_n1 = plane_scatter(d_n1.astype(BF))
     input_grad = d_mid + norm_back(d_n1 * full_gains[0], x_normed, x_factor)
-    shard_all, shard_in, shard_down, gain_in, total_early, input_grad = tied(
-        shard_all, shard_in, shard_down, gain_in, total_early, input_grad
-    )
-    got_proj = exchange(shard_all[:, : 3 * chans].reshape(spots, own, 3 * chans), PLANE)
+    plane_rows = spots * own
+    first_row = lax.axis_index("z") * plane_rows
+    rows_first = lax.dynamic_slice_in_dim(w_proj, first_row, plane_rows)
+    rows_inner = low_mixer[3].reshape(plane_rows, chans)
+    shard_all, shard_in, shard_down, gain_in, total_early, input_grad, rows_first, rows_inner = tied(
+        shard_all, shard_in, shard_down, gain_in, total_early, input_grad, rows_first, rows_inner
+    )
+    shard_proj = shard_all[:, : 3 * chans]
+    got_proj = exchange(shard_proj.reshape(spots, own, 3 * chans), PLANE)
     shard_out = shard_all[:, 3 * chans :].reshape(own, width)
 
-    shard_mixer, gain_first, gain_inner, total_mixer = run_settle(got_proj, shard_out, low_mixer)
-    shard_gains = jnp.stack([gain_first, gain_inner, gain_in]) / gains
-    local_total = jnp.sum(total_mixer) + total_early + jnp.sum(shard_gains * shard_gains)
-    grad_norm = jnp.sqrt(total_of(local_total.reshape(1, 1))[0, 0])
+    row_first, row_inner, row_squares = run_row_sums(shard_all, rows_first, rows_inner)
+    gain_inner = jnp.sum(row_inner.reshape(own, spots), axis=1) / gains[1]
+    gain_in = gain_in / gains[2]
+    local_total = jnp.sum(row_squares) + total_early
+    local_total += jnp.sum(gain_inner * gain_inner) + jnp.sum(gain_in * gain_in)
+    sums = jnp.concatenate(
+        [row_first.reshape(spots, own), jnp.full((1, own), local_total)], axis=0
+    )
+    sums = total_of(sums, ("c", "x", "y"))
+    gain_rows = lax.dynamic_slice_in_dim(full_gains[0], first_row, plane_rows).reshape(spots, own)
+    gain_first = sums[:spots] / gain_rows
+    total = sums[spots:, :1] + jnp.sum(gain_first * gain_first)
+    grad_norm = jnp.sqrt(total_of(total, ("z",))[0, 0])
+    gain_first = lax.dynamic_index_in_dim(gain_first, spot, 0, False)
+    shard_gains = jnp.stack([gain_first, gain_inner, gain_in])
     clip = jnp.minimum(1.0, CLIP_NORM / (grad_norm + 1e-06))
+    shard_mixer = run_settle(got_proj, shard_out)
     new_mixer, new_mixer_m, new_mixer_v = run_adam(mixer_w, mixer_m, mixer_v, shard_mixer, clip)
     new_in, new_in_m, new_in_v = run_adam(mlp_in, in_m, in_v, shard_in, clip)
     new_down, new_down_m, new_down_v = adam_step(

time: 606 us -> 592 us (0.977)
  waiting for transfers between devices: 250 us -> 217 us
  starting transfers between devices: 69.4 us -> 78.5 us
  local copies, waits for them, and re-layouts: 85 us -> 92.1 us
    ppermute x3, waiting for transfers between devices: 40.7 us -> 23.1 us  [line_exchange(): lax.ppermute(blocks[back], 'z', [(i, (i - back) % count) for i in range(c...]
    ppermute x3, waiting for transfers between devices: 13 us -> 29.5 us  [direct_gather(): return [value] + [lax.ppermute(value, axis, hop) for hop in hops]]
    all_to_all x3, waiting for transfers between devices: 20.3 us -> 10.3 us  [exchange(): return lax.all_to_all(value, axes, 0, 0, tiled=True)]
    ppermute x3, waiting for transfers between devices: 37.3 us -> 28.7 us  [direct_scatter(): lax.ppermute(block, axis, [(i, (i - back) % count) for i in range(count)])]
    all_to_all x3, starting transfers between devices: 14.4 us -> 20.8 us  [exchange(): return lax.all_to_all(value, axes, 0, 0, tiled=True)]
    unnamed x106 -> x122, local copies, waits for them, and re-layouts: 22.5 us -> 25.8 us
  transfers between devices with their start and end apart: 55 -> 55, of which waited for: 32 -> 29; matrix products, arithmetic and copies ran while one was open for 27% -> 30% of each run, Pallas kernels for 3% -> 5%
where the time goes in v5:
time: 592 us; the launch traced here: 585 us
  waiting for transfers between devices  217 us (37%)
  local copies, waits for them, and re-layouts  92.1 us (16%)
  starting transfers between devices  78.5 us (13%)
  matrix products  68.2 us (12%)
  other arithmetic  68.1 us (12%)
  Pallas kernels  38.6 us (7%)
  between operations  22.8 us (4%)
    ppermute x14, waiting for transfers between devices, ring_gather(): other = lax.ppermute(value, axis, [(0, 1), (1, 0)])  65.2 us
    ppermute x3, waiting for transfers between devices, direct_gather(): return [value] + [lax.ppermute(value, axis, hop) for hop in hops]  29.5 us
    ppermute x10, waiting for transfers between devices, ring_terms(): return [block(0), lax.ppermute(block(1), axis, [(0, 1), (1, 0)])]  29.5 us
    ppermute x3, waiting for transfers between devices, direct_scatter(): lax.ppermute(block, axis, [(i, (i - back) % count) for i in range(count)])  28.7 us
    unnamed x122, local copies, waits for them, and re-layouts  25.8 us
    ppermute x3, waiting for transfers between devices, line_exchange(): lax.ppermute(blocks[back], 'z', [(i, (i - back) % count) for i in range(c...  23.1 us
    all_to_all x3, starting transfers between devices, exchange(): return lax.all_to_all(value, axes, 0, 0, tiled=True)  20.8 us
    reduce_scatter x4, waiting for transfers between devices, scatter(): return lax.psum_scatter(value, axes, scatter_dimension=0, tiled=True)  17.4 us
  transfers between devices with their start and end apart: 55, of which 29 were waited for; matrix products, arithmetic and copies ran while one was open for 30% of the time, Pallas kernels for 5%

profile of v5, /device:TPU:0, one launch (start us, length us, event | category | flops | bytes accessed | tf_op | source)
XLA Modules:
  0.0 585.5 jit_solution(11669803164525788903)
XLA Ops:
  12.0 5.4 shard_map.271
  19.2 5.2 all-to-all-start
  26.2 8.3 %reshape.219 = bf16[64,2,4,4,2,176]{5,4,3,2,0,1:T(2,128)(2,1)S(1)} reshape(bf16[64,2,5632]{2,0,1:T(8,128)(2,1)} %copy.84) | data formatting | bytes 2883584 | tf_op jit(solution)/shard_map/reshape | solution.py:634
  36.7 5.4 reshape.220
  64.7 2.8 collective-permute-done.4
  75.0 9.2 %collective-permute-done.7 = bf16[2,128,1024]{2,1,0:T(8,128)(2,1)S(1)} collective-permute-done((bf16[2,128,1024]{2,1,0:T(8,128)(2,1)S(1)}, bf16[2,128,1024]{2,1,0:T(8,128)(2,1)S(1)}, u32[]{:S(2)}, u32[]{:S(2)}) %collective-permute-start.7) | collective-permute-done | bytes 524320 | tf_op jit(solution)/shard_map/ppermute | solution.py:47
  89.5 7.9 %collective-permute-done.3 = bf16[2,88,2048]{2,1,0:T(8,128)(2,1)S(1)} collective-permute-done((bf16[2,88,2048]{2,1,0:T(8,128)(2,1)S(1)}, bf16[2,88,2048]{2,1,0:T(8,128)(2,1)S(1)}, u32[]{:S(2)}, u32[]{:S(2)}) %collective-permute-start.3) | collective-permute-done | bytes 720928 | tf_op jit(solution)/shard_map/ppermute | solution.py:47
  102.8 2.8 fusion.1
  105.6 7.0 %all-gather.6.cloned.1.call-done = bf16[2048,768]{1,0:T(8,128)(2,1)} async-done(((bf16[512,768]{1,0:T(8,128)(2,1)}), bf16[2048,768]{1,0:T(8,128)(2,1)}) %all-gather.6.cloned.1.call-update) | async-done | bytes 3145744 | tf_op jit(solution)/shard_map/all_gather | solution.py:33
  112.5 4.2 collective-permute-start.16
  116.8 6.1 %fusion.60.proj_ref = f32[1024,768]{1,0:T(8,128)S(1)} fusion(bf16[1024,2048]{1,0:T(8,128)(2,1)} %fusion.1, bf16[2048,768]{1,0:T(8,128)(2,1)} %all-gather.6.cloned.1.call-done), kind=kOutput, calls=%fused_computation.225 | convolution fusion | flops 3221225472 | bytes 10485760 | tf_op jit(solution)/shard_map/dot_general | solution.py:656
  122.9 5.7 shard_map.272
  129.8 3.5 convolution_convert_fusion.1
  133.3 4.6 collective-permute-done.16
  142.5 2.7 collective-permute-start.19
  146.2 7.6 %collective-permute-done.17 = bf16[2,64,1408]{2,1,0:T(8,128)(2,1)} collective-permute-done((bf16[2,64,1408]{2,1,0:T(8,128)(2,1)}, bf16[2,64,1408]{2,1,0:T(8,128)(2,1)}, u32[]{:S(2)}, u32[]{:S(2)}) %collective-permute-start.17) | collective-permute-done | bytes 360480 | tf_op jit(solution)/shard_map/ppermute | solution.py:210
  153.8 15.5 %collective-permute-done.18 = bf16[2,64,1408]{2,1,0:T(8,128)(2,1)} collective-permute-done((bf16[2,64,1408]{2,1,0:T(8,128)(2,1)}, bf16[2,64,1408]{2,1,0:T(8,128)(2,1)}, u32[]{:S(2)}, u32[]{:S(2)}) %collective-permute-start.18) | collective-permute-done | bytes 360480 | tf_op jit(solution)/shard_map/ppermute | solution.py:210
  172.2 24.9 %collective-permute-done.20 = bf16[128,2048]{1,0:T(8,128)(2,1)} collective-permute-done((bf16[128,2048]{1,0:T(8,128)(2,1)S(1)}, bf16[128,2048]{1,0:T(8,128)(2,1)}, u32[]{:S(2)}, u32[]{:S(2)}) %collective-permute-start.20) | collective-permute-done | bytes 524320 | tf_op jit(solution)/shard_map/ppermute | solution.py:181
  207.1 12.7 %collective-permute-done.24 = bf16[256,1408]{1,0:T(8,128)(2,1)S(1)} collective-permute-done((bf16[256,1408]{1,0:T(8,128)(2,1)S(1)}, bf16[256,1408]{1,0:T(8,128)(2,1)S(1)}, u32[]{:S(2)}, u32[]{:S(2)}) %collective-permute-start.24) | collective-permute-done | bytes 720928 | tf_op jit(solution)/shard_map/ppermute | solution.py:47
  228.6 26.3 %collective-permute-done.25 = bf16[2,256,1408]{2,1,0:T(8,128)(2,1)S(1)} collective-permute-done((bf16[2,256,1408]{2,1,0:T(8,128)(2,1)S(1)}, bf16[2,256,1408]{2,1,0:T(8,128)(2,1)S(1)}, u32[]{:S(2)}, u32[]{:S(2)}) %collective-permute-start.25) | collective-permute-done | bytes 1441824 | tf_op jit(solution)/shard_map/ppermute | solution.py:47
  258.1 4.8 pad_maximum_fusion
  262.9 10.3 %fusion.61 = f32[1024,1408]{0,1:T(8,128)S(1)} fusion(bf16[1024,2048]{1,0:T(8,128)(2,1)} %all-gather.8.cloned.1.call-done, bf16[2048,1408]{1,0:T(8,128)(2,1)} %bitcast.276), kind=kOutput, calls=%fused_computation.226 | convolution fusion | flops 5905580032 | bytes 15728640 | tf_op jit(solution)/shard_map/dot_general | solution.py:679
  273.3 5.2 multiply_convert_fusion.2
  280.0 8.3 %convolution_convert_fusion.3 = bf16[1024,2048]{1,0:T(8,128)(2,1)} fusion(bf16[2048,1408]{1,0:T(8,128)(2,1)S(1)} %bitcast.277, bf16[1024,704]{0,1:T(8,128)(2,1)S(1)} %get-tuple-element.161, bf16[1024,704]{0,1:T(8,128)(2,1)S(1)} %get-tuple-element.160), kind=kOutput, calls=%fused_computation.16 | convolution fusion | flops 5913444352 | bytes 12845056 | tf_op jit(solution)/shard_map/dot_general | solution.py:688
  288.9 5.9 %convolution_convert_fusion.2 = bf16[1024,2048]{1,0:T(8,128)(2,1)S(1)} fusion(bf16[1024,704]{0,1:T(8,128)(2,1)} %get-tuple-element.106, bf16[704,2048]{1,0:T(8,128)(2,1)} %bitcast.289), kind=kOutput, calls=%fused_computation.15 | convolution fusion | flops 2954887168 | bytes 8519680 | tf_op jit(solution)/shard_map/dot_general | solution.py:692
  299.2 7.0 %convolution_convert_fusion = bf16[2048,1408]{1,0:T(8,128)(2,1)S(1)} fusion(bf16[1024,2048]{1,0:T(8,128)(2,1)S(1)} %copy-done.50, bf16[1024,704]{0,1:T(8,128)(2,1)S(1)} %copy-done.57, bf16[1024,704]{0,1:T(8,128)(2,1)S(1)} %copy-done.55), kind=kOutput, calls=%fused_computation.4 | convolution fusion | flops 5914230784 | bytes 12845056 | tf_op jit(solution)/shard_map/dot_general | solution.py:690
  312.3 4.6 fusion.3
  316.9 4.4 convolution_convert_fusion.6
  321.4 20.2 %collective-permute-done.27 = bf16[2,256,1408]{2,1,0:T(8,128)(2,1)} collective-permute-done((bf16[2,256,1408]{2,1,0:T(8,128)(2,1)}, bf16[2,256,1408]{2,1,0:T(8,128)(2,1)}, u32[]{:S(2)}, u32[]{:S(2)}) %collective-permute-start.27) | collective-permute-done | bytes 1441824 | tf_op jit(solution)/shard_map/ppermute | solution.py:82
  359.9 9.4 %collective-permute-done.33 = bf16[128,2048]{1,0:T(8,128)(2,1)S(1)} collective-permute-done((bf16[128,2048]{1,0:T(8,128)(2,1)S(1)}, bf16[128,2048]{1,0:T(8,128)(2,1)S(1)}, u32[]{:S(2)}, u32[]{:S(2)}) %collective-permute-start.33) | collective-permute-done | bytes 524320 | tf_op jit(solution)/shard_map/ppermute | solution.py:124
  369.3 19.3 %collective-permute-done.32 = bf16[128,2048]{1,0:T(8,128)(2,1)S(1)} collective-permute-done((bf16[128,2048]{1,0:T(8,128)(2,1)S(1)}, bf16[128,2048]{1,0:T(8,128)(2,1)S(1)}, u32[]{:S(2)}, u32[]{:S(2)}) %collective-permute-start.32) | collective-permute-done | bytes 524320 | tf_op jit(solution)/shard_map/ppermute | solution.py:124
  392.5 11.2 %all-to-all-start.1 = ((bf16[8,64,1408]{2,1,0:T(8,128)(2,1)}), bf16[8,64,1408]{2,1,0:T(8,128)(2,1)}, u32[]{:S(2)}, u32[]{:S(2)}) async-start(bf16[8,64,1408]{2,1,0:T(8,128)(2,1)} %bitcast.281), calls=%async_computation.3 | async-start | bytes 2883584 | tf_op jit(solution)/shard_map/all_to_all | solution.py:41
  404.9 4.6 fusion.15.d_mixed_ref
  409.6 7.0 %shard_map.275 = (bf16[1024,768]{1,0:T(8,128)(2,1)S(1)}, bf16[1024,256]{1,0:T(8,128)(2,1)S(1)}) custom-call(f32[1024,768]{1,0:T(8,128)} %copy-done.3, f32[1024,256]{1,0:T(8,128)S(1)} %get-tuple-element.89.state_ref, f32[1024,256]{1,0:T(8,128)S(1)} %fusion.15.d_mixed_ref, bf16[1024,128]{1,0:T(8,128)(2,1)S(1)} %slice.129.riders_ref, ...), custom_call_target="tpu_custom_call" | custom-call | tf_op jit(solution)/shard_map/pallas_call | solution.py:371
  420.0 5.9 %convolution_convert_fusion.5 = bf16[2048,768]{1,0:T(8,128)(2,1)S(1)} fusion(bf16[1024,2048]{1,0:T(8,128)(2,1)} %fusion.1, bf16[1024,768]{1,0:T(8,128)(2,1)S(1)} %copy-done.24), kind=kOutput, calls=%fused_computation.18 | convolution fusion | flops 3222798336 | bytes 8912896 | tf_op jit(solution)/shard_map/dot_general | solution.py:715
  428.5 10.3 %all-to-all-done.1 = bf16[8,64,1408]{2,1,0:T(8,128)(2,1)} async-done(((bf16[8,64,1408]{2,1,0:T(8,128)(2,1)}), bf16[8,64,1408]{2,1,0:T(8,128)(2,1)}, u32[]{:S(2)}, u32[]{:S(2)}) %all-to-all-start.1) | async-done | bytes 1441824 | tf_op jit(solution)/shard_map/all_to_all | solution.py:41
  438.8 5.6 convolution_convert_fusion.4
  458.9 7.8 %reshape.235 = bf16[4,2,64,2,4,176]{5,4,3,2,1,0:T(4,128)(2,1)S(1)} reshape(bf16[8,64,1408]{2,1,0:T(8,128)(2,1)} %all-to-all-done.1) | data formatting | bytes 2883584 | tf_op jit(solution)/shard_map/reshape | solution.py:722
  469.3 2.8 multiply_reduce_fusion.1
  472.1 4.6 copy.69
  476.6 6.6 %reshape.236.grad_ref = bf16[2,64,5632]{2,1,0:T(8,128)(2,1)} reshape(bf16[2,64,4,4,2,176]{5,4,3,2,1,0:T(2,128)(2,1)} %copy.69) | data formatting | bytes 2883584 | tf_op jit(solution)/shard_map/reshape | solution.py:723
  502.8 17.4 %reduce-scatter.9.cloned.1.call-done.shard_ref = bf16[512,1024]{1,0:T(8,128)(2,1)} async-done(((bf16[2048,1024]{1,0:T(8,128)(2,1)}), bf16[512,1024]{1,0:T(8,128)(2,1)}) %reduce-scatter.9.cloned.1.call-update) | async-done | bytes 1048592 | tf_op jit(solution)/shard_map/reduce_scatter | solution.py:37
  534.5 4.5 all-to-all-start.2
  541.5 2.9 collective-permute-start.42
  545.8 4.3 collective-permute-start.43
  552.5 9.1 %shard_map.279 = (f32[64,2,5632]{2,1,0:T(2,128)}, f32[64,2,5632]{2,1,0:T(2,128)}, f32[64,2,5632]{2,1,0:T(2,128)}) custom-call(f32[1,1]{1,0:T(1,128)} %bitcast.104.clip_ref, f32[64,2,5632]{2,1,0:T(2,128)S(1)} %copy-done.1, f32[64,2,5632]{2,1,0:T(2,128)} %first_ref.3, f32[64,2,5632]{2,1,0:T(2,128)} %second_ref.3, bf16[2,64,5632]{2,1,0:T(8,128)(2,1)S(1)} %copy-done.4), custom_call_target="tpu_custom_call" | custom-call | tf_op jit(solution)/shard_map/pallas_call | solution.py:400
  562.3 2.9 multiply_subtract_fusion
  569.8 7.3 %shard_map.278 = (f32[64,4,2048]{2,1,0:T(4,128)}, f32[64,4,2048]{2,1,0:T(4,128)}, f32[64,4,2048]{2,1,0:T(4,128)}) custom-call(f32[1,1]{1,0:T(1,128)} %bitcast.104.clip_ref, f32[64,4,2048]{2,1,0:T(4,128)S(1)} %copy-done.6, f32[64,4,2048]{2,1,0:T(4,128)S(1)} %copy-done.15, f32[64,4,2048]{2,1,0:T(4,128)} %second_ref.2, f32[4,64,2048]{2,1,0:T(8,128)} %copy-done.7), custom_call_target="tpu_custom_call" | custom-call | tf_op jit(solution)/shard_map/pallas_call | solution.py:400
  (358 shorter events, 180.8 us)
Async XLA Ops:
  7.2 36.7 %all-gather.12.cloned.1.call-start = ((), (), s32[]{:S(2)}) async-start(), calls=%async_computation.14 | async-start | bytes 1310720 | tf_op jit(solution)/shard_map/all_gather | solution.py:33
  19.2 24.6 %all-to-all-start = ((bf16[8,64,768]{2,1,0:T(8,128)(2,1)}), bf16[8,64,768]{2,1,0:T(8,128)(2,1)}, u32[]{:S(2)}, u32[]{:S(2)}) async-start(bf16[8,64,768]{2,1,0:T(8,128)(2,1)} %copy-done.19), calls=%async_computation | async-start | bytes 1572864 | tf_op jit(solution)/shard_map/all_to_all | solution.py:41
  24.4 88.1 %all-gather.6.cloned.1.call-start = ((), (), s32[]{:S(2)}) async-start(), calls=%async_computation.7 | async-start | bytes 3932160 | tf_op jit(solution)/shard_map/all_gather | solution.py:33
  47.5 149.5 %reduce-scatter.5.cloned.1.call-start = ((), (), s32[]{:S(2)}) async-start(), calls=%async_computation.8 | async-start | bytes 5013504 | tf_op jit(solution)/shard_map/reduce_scatter | solution.py:37
  49.2 4.6 collective-permute-start.11
  51.8 19.4 %collective-permute-start = (bf16[88,2048]{1,0:T(8,128)(2,1)}, bf16[88,2048]{1,0:T(8,128)(2,1)}, u32[]{:S(2)}, u32[]{:S(2)}) collective-permute-start(bf16[88,2048]{1,0:T(8,128)(2,1)} %get-tuple-element.221), channel_id=1, source_target_pairs={{0,2},{2,0},{1,3},{3,1},{4,6},{6,4},{5,7},{7,5},{8,10},{10,8},{9,1... | collective-permute-start | bytes 1081352 | tf_op jit(solution)/shard_map/ppermute | solution.py:47
  53.3 17.9 %collective-permute-start.2 = (bf16[88,2048]{1,0:T(8,128)(2,1)}, bf16[88,2048]{1,0:T(8,128)(2,1)}, u32[]{:S(2)}, u32[]{:S(2)}) collective-permute-start(bf16[88,2048]{1,0:T(8,128)(2,1)} %get-tuple-element.222), channel_id=1, source_target_pairs={{0,4},{4,0},{1,5},{5,1},{2,6},{6,2},{3,7},{7,3},{8,12},{12,8},{9,1... | collective-permute-start | bytes 1081352 | tf_op jit(solution)/shard_map/ppermute | solution.py:47
  55.9 11.5 %collective-permute-start.4 = (bf16[128,1024]{1,0:T(8,128)(2,1)S(1)}, bf16[128,1024]{1,0:T(8,128)(2,1)S(1)}, u32[]{:S(2)}, u32[]{:S(2)}) collective-permute-start(bf16[128,1024]{1,0:T(8,128)(2,1)S(1)} %get-tuple-element.225), channel_id=1, source_target_pairs={{0,2},{2,0},{1,3},{3,1},{4,6},{6,4},{5,7},{7,5},{8,10},{10,8},{9,1... | collective-permute-start | bytes 786440 | tf_op jit(solution)/shard_map/ppermute | solution.py:47
  56.7 11.4 %collective-permute-start.6 = (bf16[128,1024]{1,0:T(8,128)(2,1)S(1)}, bf16[128,1024]{1,0:T(8,128)(2,1)}, u32[]{:S(2)}, u32[]{:S(2)}) collective-permute-start(bf16[128,1024]{1,0:T(8,128)(2,1)S(1)} %get-tuple-element.226), channel_id=1, source_target_pairs={{0,4},{4,0},{1,5},{5,1},{2,6},{6,2},{3,7},{7,3},{8,12},{12,8},{9,1... | collective-permute-start | bytes 786440 | tf_op jit(solution)/shard_map/ppermute | solution.py:47
  58.2 6.0 %collective-permute-start.13 = (f32[16,3,64]{2,1,0:T(4,128)S(1)}, f32[16,3,64]{2,1,0:T(4,128)S(1)}, u32[]{:S(2)}, u32[]{:S(2)}) collective-permute-start(f32[16,3,64]{2,1,0:T(4,128)S(1)} %pad_maximum_fusion.17), channel_id=1, source_target_pairs={{0,16},{8,24},{16,0},{24,8},{1,17},{9,25},{17,1},{25,9},{2,18},{10... | collective-permute-start | bytes 36872 | tf_op jit(solution)/shard_map/ppermute | solution.py:100
  64.3 21.6 %collective-permute-start.14 = (bf16[4,64,1408]{2,1,0:T(8,128)(2,1)}, bf16[4,64,1408]{2,1,0:T(8,128)(2,1)}, u32[]{:S(2)}, u32[]{:S(2)}) collective-permute-start(bf16[4,64,1408]{2,1,0:T(8,128)(2,1)} %dynamic-slice_bitcast_fusion.7), channel_id=1, source_target_pairs={{0,1},{1,0},{2,3},{3,2},{4,5},{5,4},{6,7},{7,6},{8,9},{9,8},{10,11... | collective-permute-start | bytes 2162696 | tf_op jit(solution)/shard_map/ppermute | solution.py:200
  69.3 14.9 %collective-permute-start.7 = (bf16[2,128,1024]{2,1,0:T(8,128)(2,1)S(1)}, bf16[2,128,1024]{2,1,0:T(8,128)(2,1)S(1)}, u32[]{:S(2)}, u32[]{:S(2)}) collective-permute-start(bf16[2,128,1024]{2,1,0:T(8,128)(2,1)S(1)} %pad_maximum_fusion.16), channel_id=1, source_target_pairs={{0,2},{2,0},{1,3},{3,1},{4,6},{6,4},{5,7},{7,5},{8,10},{10,8},{9,1... | collective-permute-start | bytes 1572872 | tf_op jit(solution)/shard_map/ppermute | solution.py:47
  70.6 14.9 %collective-permute-start.5 = (bf16[2,128,1024]{2,1,0:T(8,128)(2,1)S(1)}, bf16[2,128,1024]{2,1,0:T(8,128)(2,1)S(1)}, u32[]{:S(2)}, u32[]{:S(2)}) collective-permute-start(bf16[2,128,1024]{2,1,0:T(8,128)(2,1)S(1)} %pad_maximum_fusion.15), channel_id=1, source_target_pairs={{0,4},{4,0},{1,5},{5,1},{2,6},{6,2},{3,7},{7,3},{8,12},{12,8},{9,1... | collective-permute-start | bytes 1572872 | tf_op jit(solution)/shard_map/ppermute | solution.py:47
  72.5 24.9 %collective-permute-start.3 = (bf16[2,88,2048]{2,1,0:T(8,128)(2,1)S(1)}, bf16[2,88,2048]{2,1,0:T(8,128)(2,1)S(1)}, u32[]{:S(2)}, u32[]{:S(2)}) collective-permute-start(bf16[2,88,2048]{2,1,0:T(8,128)(2,1)S(1)} %pad_maximum_fusion.14), channel_id=1, source_target_pairs={{0,2},{2,0},{1,3},{3,1},{4,6},{6,4},{5,7},{7,5},{8,10},{10,8},{9,1... | collective-permute-start | bytes 2162696 | tf_op jit(solution)/shard_map/ppermute | solution.py:47
  73.5 24.5 %collective-permute-start.1 = (bf16[2,88,2048]{2,1,0:T(8,128)(2,1)S(1)}, bf16[2,88,2048]{2,1,0:T(8,128)(2,1)S(1)}, u32[]{:S(2)}, u32[]{:S(2)}) collective-permute-start(bf16[2,88,2048]{2,1,0:T(8,128)(2,1)S(1)} %pad_maximum_fusion.13), channel_id=1, source_target_pairs={{0,4},{4,0},{1,5},{5,1},{2,6},{6,2},{3,7},{7,3},{8,12},{12,8},{9,1... | collective-permute-start | bytes 2162696 | tf_op jit(solution)/shard_map/ppermute | solution.py:47
  85.8 14.2 %collective-permute-start.8 = (bf16[2,2,128,2048]{3,2,1,0:T(8,128)(2,1)S(1)}, bf16[2,2,128,2048]{3,2,1,0:T(8,128)(2,1)S(1)}, u32[]{:S(2)}, u32[]{:S(2)}) collective-permute-start(bf16[2,2,128,2048]{3,2,1,0:T(8,128)(2,1)S(1)} %pad_maximum_fusion.4), channel_id=1, source_target_pairs={{0,1},{1,0},{2,3},{3,2},{4,5},{5,4},{6,7},{7,6},{8,9},{9,8},{10,11... | collective-permute-start | bytes 6291464 | tf_op jit(solution)/shard_map/ppermute | solution.py:47
  112.5 20.8 %collective-permute-start.15 = (bf16[128,2048]{1,0:T(8,128)(2,1)S(1)}, bf16[128,2048]{1,0:T(8,128)(2,1)S(1)}, u32[]{:S(2)}, u32[]{:S(2)}) collective-permute-start(bf16[128,2048]{1,0:T(8,128)(2,1)S(1)} %multiply_convert_fusion.4.cot_ref), channel_id=1, source_target_pairs={{0,8},{8,16},{16,24},{24,0},{1,9},{9,17},{17,25},{25,1},{2,10},{10... | collective-permute-start | bytes 1572872 | tf_op jit(solution)/shard_map/ppermute | solution.py:181
  112.5 25.4 %collective-permute-start.16 = (bf16[128,2048]{1,0:T(8,128)(2,1)S(1)}, bf16[128,2048]{1,0:T(8,128)(2,1)}, u32[]{:S(2)}, u32[]{:S(2)}) collective-permute-start(bf16[128,2048]{1,0:T(8,128)(2,1)S(1)} %multiply_convert_fusion.4.cot_ref), channel_id=1, source_target_pairs={{0,24},{8,0},{16,8},{24,16},{1,25},{9,1},{17,9},{25,17},{2,26},{10... | collective-permute-start | bytes 1572872 | tf_op jit(solution)/shard_map/ppermute | solution.py:181
  138.0 124.9 %all-gather.8.cloned.1.call-start = ((), (), s32[]{:S(2)}) async-start(), calls=%async_computation.9 | async-start | bytes 4718592 | tf_op jit(solution)/shard_map/all_gather | solution.py:33
  140.2 13.6 %collective-permute-start.17 = (bf16[2,64,1408]{2,1,0:T(8,128)(2,1)}, bf16[2,64,1408]{2,1,0:T(8,128)(2,1)}, u32[]{:S(2)}, u32[]{:S(2)}) collective-permute-start(bf16[2,64,1408]{2,1,0:T(8,128)(2,1)} %get-tuple-element.202), channel_id=1, source_target_pairs={{0,8},{8,16},{16,24},{24,0},{1,9},{9,17},{17,25},{25,1},{2,10},{10... | collective-permute-start | bytes 1081352 | tf_op jit(solution)/shard_map/ppermute | solution.py:210
  141.2 28.1 %collective-permute-start.18 = (bf16[2,64,1408]{2,1,0:T(8,128)(2,1)}, bf16[2,64,1408]{2,1,0:T(8,128)(2,1)}, u32[]{:S(2)}, u32[]{:S(2)}) collective-permute-start(bf16[2,64,1408]{2,1,0:T(8,128)(2,1)} %get-tuple-element.201), channel_id=1, source_target_pairs={{0,16},{8,24},{16,0},{24,8},{1,17},{9,25},{17,1},{25,9},{2,18},{10... | collective-permute-start | bytes 1081352 | tf_op jit(solution)/shard_map/ppermute | solution.py:210
  142.5 26.8 %collective-permute-start.19 = (bf16[2,64,1408]{2,1,0:T(8,128)(2,1)S(1)}, bf16[2,64,1408]{2,1,0:T(8,128)(2,1)}, u32[]{:S(2)}, u32[]{:S(2)}) collective-permute-start(bf16[2,64,1408]{2,1,0:T(8,128)(2,1)S(1)} %get-tuple-element.200), channel_id=1, source_target_pairs={{0,24},{8,0},{16,8},{24,16},{1,25},{9,1},{17,9},{25,17},{2,26},{10... | collective-permute-start | bytes 1081352 | tf_op jit(solution)/shard_map/ppermute | solution.py:210
  145.3 51.8 %collective-permute-start.20 = (bf16[128,2048]{1,0:T(8,128)(2,1)S(1)}, bf16[128,2048]{1,0:T(8,128)(2,1)}, u32[]{:S(2)}, u32[]{:S(2)}) collective-permute-start(bf16[128,2048]{1,0:T(8,128)(2,1)S(1)} %multiply_convert_fusion.4.cot_ref), channel_id=1, source_target_pairs={{0,16},{8,24},{16,0},{24,8},{1,17},{9,25},{17,1},{25,9},{2,18},{10... | collective-permute-start | bytes 1572872 | tf_op jit(solution)/shard_map/ppermute | solution.py:181
  200.3 143.1 %reduce-scatter.7.cloned.1.call-start = ((), (), s32[]{:S(2)}) async-start(), calls=%async_computation.10 | async-start | bytes 4718592 | tf_op jit(solution)/shard_map/reduce_scatter | solution.py:37
  201.9 17.9 %collective-permute-start.24 = (bf16[256,1408]{1,0:T(8,128)(2,1)S(1)}, bf16[256,1408]{1,0:T(8,128)(2,1)S(1)}, u32[]{:S(2)}, u32[]{:S(2)}) collective-permute-start(bf16[256,1408]{1,0:T(8,128)(2,1)S(1)} %bitcast.292), channel_id=1, source_target_pairs={{0,4},{4,0},{1,5},{5,1},{2,6},{6,2},{3,7},{7,3},{8,12},{12,8},{9,1... | collective-permute-start | bytes 2162696 | tf_op jit(solution)/shard_map/ppermute | solution.py:47
  205.4 19.9 %collective-permute-start.21 = (bf16[4,128,2048]{2,1,0:T(8,128)(2,1)S(1)}, bf16[4,128,2048]{2,1,0:T(8,128)(2,1)S(1)}, u32[]{:S(2)}, u32[]{:S(2)}) collective-permute-start(bf16[4,128,2048]{2,1,0:T(8,128)(2,1)S(1)} %pad_maximum_fusion.5), channel_id=1, source_target_pairs={{0,1},{1,0},{2,3},{3,2},{4,5},{5,4},{6,7},{7,6},{8,9},{9,8},{10,11... | collective-permute-start | bytes 6291464 | tf_op jit(solution)/shard_map/ppermute | solution.py:47
  205.5 19.0 %collective-permute-start.22 = (bf16[256,1408]{1,0:T(8,128)(2,1)S(1)}, bf16[256,1408]{1,0:T(8,128)(2,1)S(1)}, u32[]{:S(2)}, u32[]{:S(2)}) collective-permute-start(bf16[256,1408]{1,0:T(8,128)(2,1)S(1)} %bitcast.291), channel_id=1, source_target_pairs={{0,2},{2,0},{1,3},{3,1},{4,6},{6,4},{5,7},{7,5},{8,10},{10,8},{9,1... | collective-permute-start | bytes 2162696 | tf_op jit(solution)/shard_map/ppermute | solution.py:47
  220.1 34.8 %collective-permute-start.25 = (bf16[2,256,1408]{2,1,0:T(8,128)(2,1)S(1)}, bf16[2,256,1408]{2,1,0:T(8,128)(2,1)S(1)}, u32[]{:S(2)}, u32[]{:S(2)}) collective-permute-start(bf16[2,256,1408]{2,1,0:T(8,128)(2,1)S(1)} %pad_maximum_fusion.11), channel_id=1, source_target_pairs={{0,2},{2,0},{1,3},{3,1},{4,6},{6,4},{5,7},{7,5},{8,10},{10,8},{9,1... | collective-permute-start | bytes 4325384 | tf_op jit(solution)/shard_map/ppermute | solution.py:47
  224.9 32.9 %collective-permute-start.23 = (bf16[2,256,1408]{2,1,0:T(8,128)(2,1)S(1)}, bf16[2,256,1408]{2,1,0:T(8,128)(2,1)S(1)}, u32[]{:S(2)}, u32[]{:S(2)}) collective-permute-start(bf16[2,256,1408]{2,1,0:T(8,128)(2,1)S(1)} %pad_maximum_fusion.10), channel_id=1, source_target_pairs={{0,4},{4,0},{1,5},{5,1},{2,6},{6,2},{3,7},{7,3},{8,12},{12,8},{9,1... | collective-permute-start | bytes 4325384 | tf_op jit(solution)/shard_map/ppermute | solution.py:47
  288.3 104.2 %all-gather.10.cloned.1.call-start = ((), (), s32[]{:S(2)}) async-start(), calls=%async_computation.11 | async-start | bytes 5013504 | tf_op jit(solution)/shard_map/all_gather | solution.py:33
  297.9 14.4 %collective-permute-start.26 = (bf16[4,128,2048]{2,1,0:T(8,128)(2,1)}, bf16[4,128,2048]{2,1,0:T(8,128)(2,1)}, u32[]{:S(2)}, u32[]{:S(2)}) collective-permute-start(bf16[4,128,2048]{2,1,0:T(8,128)(2,1)} %dynamic-slice_bitcast_fusion), channel_id=1, source_target_pairs={{0,1},{1,0},{2,3},{3,2},{4,5},{5,4},{6,7},{7,6},{8,9},{9,8},{10,11... | collective-permute-start | bytes 6291464 | tf_op jit(solution)/shard_map/ppermute | solution.py:82
  308.5 33.0 %collective-permute-start.27 = (bf16[2,256,1408]{2,1,0:T(8,128)(2,1)}, bf16[2,256,1408]{2,1,0:T(8,128)(2,1)}, u32[]{:S(2)}, u32[]{:S(2)}) collective-permute-start(bf16[2,256,1408]{2,1,0:T(8,128)(2,1)} %get-tuple-element.173), channel_id=1, source_target_pairs={{0,4},{4,0},{1,5},{5,1},{2,6},{6,2},{3,7},{7,3},{8,12},{12,8},{9,1... | collective-permute-start | bytes 4325384 | tf_op jit(solution)/shard_map/ppermute | solution.py:82
  310.7 32.8 %collective-permute-start.28 = (bf16[2,256,1408]{2,1,0:T(8,128)(2,1)}, bf16[2,256,1408]{2,1,0:T(8,128)(2,1)}, u32[]{:S(2)}, u32[]{:S(2)}) collective-permute-start(bf16[2,256,1408]{2,1,0:T(8,128)(2,1)} %get-tuple-element.171), channel_id=1, source_target_pairs={{0,2},{2,0},{1,3},{3,1},{4,6},{6,4},{5,7},{7,5},{8,10},{10,8},{9,1... | collective-permute-start | bytes 4325384 | tf_op jit(solution)/shard_map/ppermute | solution.py:82
  348.3 148.7 %reduce-scatter.11.cloned.1.call-start = ((), (), s32[]{:S(2)}) async-start(), calls=%async_computation.13 | async-start | bytes 3604480 | tf_op jit(solution)/shard_map/reduce_scatter | solution.py:37
  350.7 39.3 %collective-permute-start.30 = (bf16[256,1408]{1,0:T(8,128)(2,1)S(1)}, bf16[256,1408]{1,0:T(8,128)(2,1)S(1)}, u32[]{:S(2)}, u32[]{:S(2)}) collective-permute-start(bf16[256,1408]{1,0:T(8,128)(2,1)S(1)} %dynamic-slice_bitcast_fusion.5), channel_id=1, source_target_pairs={{0,4},{4,0},{1,5},{5,1},{2,6},{6,2},{3,7},{7,3},{8,12},{12,8},{9,1... | collective-permute-start | bytes 2162696 | tf_op jit(solution)/shard_map/ppermute | solution.py:82
  352.5 16.8 %collective-permute-start.33 = (bf16[128,2048]{1,0:T(8,128)(2,1)S(1)}, bf16[128,2048]{1,0:T(8,128)(2,1)S(1)}, u32[]{:S(2)}, u32[]{:S(2)}) collective-permute-start(bf16[128,2048]{1,0:T(8,128)(2,1)S(1)} %get-tuple-element.188), channel_id=1, source_target_pairs={{0,8},{8,16},{16,24},{24,0},{1,9},{9,17},{17,25},{25,1},{2,10},{10... | collective-permute-start | bytes 1572872 | tf_op jit(solution)/shard_map/ppermute | solution.py:124
  352.6 36.0 %collective-permute-start.32 = (bf16[128,2048]{1,0:T(8,128)(2,1)S(1)}, bf16[128,2048]{1,0:T(8,128)(2,1)S(1)}, u32[]{:S(2)}, u32[]{:S(2)}) collective-permute-start(bf16[128,2048]{1,0:T(8,128)(2,1)S(1)} %get-tuple-element.189), channel_id=1, source_target_pairs={{0,16},{8,24},{16,0},{24,8},{1,17},{9,25},{17,1},{25,9},{2,18},{10... | collective-permute-start | bytes 1572872 | tf_op jit(solution)/shard_map/ppermute | solution.py:124
  354.4 34.3 %collective-permute-start.31 = (bf16[128,2048]{1,0:T(8,128)(2,1)S(1)}, bf16[128,2048]{1,0:T(8,128)(2,1)S(1)}, u32[]{:S(2)}, u32[]{:S(2)}) collective-permute-start(bf16[128,2048]{1,0:T(8,128)(2,1)S(1)} %get-tuple-element.187), channel_id=1, source_target_pairs={{0,24},{8,0},{16,8},{24,16},{1,25},{9,1},{17,9},{25,17},{2,26},{10... | collective-permute-start | bytes 1572872 | tf_op jit(solution)/shard_map/ppermute | solution.py:124
  358.4 31.8 %collective-permute-start.29 = (bf16[256,1408]{1,0:T(8,128)(2,1)S(1)}, bf16[256,1408]{1,0:T(8,128)(2,1)S(1)}, u32[]{:S(2)}, u32[]{:S(2)}) collective-permute-start(bf16[256,1408]{1,0:T(8,128)(2,1)S(1)} %dynamic-slice_bitcast_fusion.6), channel_id=1, source_target_pairs={{0,2},{2,0},{1,3},{3,1},{4,6},{6,4},{5,7},{7,5},{8,10},{10,8},{9,1... | collective-permute-start | bytes 2162696 | tf_op jit(solution)/shard_map/ppermute | solution.py:82
  392.5 46.3 %all-to-all-start.1 = ((bf16[8,64,1408]{2,1,0:T(8,128)(2,1)}), bf16[8,64,1408]{2,1,0:T(8,128)(2,1)}, u32[]{:S(2)}, u32[]{:S(2)}) async-start(bf16[8,64,1408]{2,1,0:T(8,128)(2,1)} %bitcast.281), calls=%async_computation.3 | async-start | bytes 2883584 | tf_op jit(solution)/shard_map/all_to_all | solution.py:41
  403.7 116.5 %reduce-scatter.9.cloned.1.call-start = ((), (), s32[]{:S(2)}) async-start(), calls=%async_computation.12 | async-start | bytes 5242880 | tf_op jit(solution)/shard_map/reduce_scatter | solution.py:37
  455.4 27.9 %collective-permute-start.37 = (bf16[2,128,1024]{2,1,0:T(8,128)(2,1)}, bf16[2,128,1024]{2,1,0:T(8,128)(2,1)}, u32[]{:S(2)}, u32[]{:S(2)}) collective-permute-start(bf16[2,128,1024]{2,1,0:T(8,128)(2,1)} %dynamic-slice_bitcast_fusion.8), channel_id=1, source_target_pairs={{0,2},{2,0},{1,3},{3,1},{4,6},{6,4},{5,7},{7,5},{8,10},{10,8},{9,1... | collective-permute-start | bytes 1572872 | tf_op jit(solution)/shard_map/ppermute | solution.py:82
  468.6 17.6 %collective-permute-start.35 = (bf16[2,128,1024]{2,1,0:T(8,128)(2,1)}, bf16[2,128,1024]{2,1,0:T(8,128)(2,1)}, u32[]{:S(2)}, u32[]{:S(2)}) collective-permute-start(bf16[2,128,1024]{2,1,0:T(8,128)(2,1)} %dynamic-slice_bitcast_fusion.9), channel_id=1, source_target_pairs={{0,4},{4,0},{1,5},{5,1},{2,6},{6,2},{3,7},{7,3},{8,12},{12,8},{9,1... | collective-permute-start | bytes 1572872 | tf_op jit(solution)/shard_map/ppermute | solution.py:82
  484.9 7.8 %collective-permute-start.38 = (bf16[128,1024]{1,0:T(8,128)(2,1)S(1)}, bf16[128,1024]{1,0:T(8,128)(2,1)S(1)}, u32[]{:S(2)}, u32[]{:S(2)}) collective-permute-start(bf16[128,1024]{1,0:T(8,128)(2,1)S(1)} %dynamic-slice_bitcast_fusion.16), channel_id=1, source_target_pairs={{0,4},{4,0},{1,5},{5,1},{2,6},{6,2},{3,7},{7,3},{8,12},{12,8},{9,1... | collective-permute-start | bytes 786440 | tf_op jit(solution)/shard_map/ppermute | solution.py:82
  487.6 7.6 %collective-permute-start.36 = (bf16[128,1024]{1,0:T(8,128)(2,1)S(1)}, bf16[128,1024]{1,0:T(8,128)(2,1)S(1)}, u32[]{:S(2)}, u32[]{:S(2)}) collective-permute-start(bf16[128,1024]{1,0:T(8,128)(2,1)S(1)} %dynamic-slice_bitcast_fusion.17), channel_id=1, source_target_pairs={{0,2},{2,0},{1,3},{3,1},{4,6},{6,4},{5,7},{7,5},{8,10},{10,8},{9,1... | collective-permute-start | bytes 786440 | tf_op jit(solution)/shard_map/ppermute | solution.py:82
  532.0 7.1 %collective-permute-start.41 = (f32[9,64]{1,0:T(8,128)S(1)}, f32[9,64]{1,0:T(8,128)S(1)}, u32[]{:S(2)}, u32[]{:S(2)}) collective-permute-start(f32[9,64]{1,0:T(8,128)S(1)} %add.434), channel_id=1, source_target_pairs={{0,4},{4,0},{1,5},{5,1},{2,6},{6,2},{3,7},{7,3},{8,12},{12,8},{9,1... | collective-permute-start | bytes 6920 | tf_op jit(solution)/shard_map/ppermute | solution.py:230
  534.5 30.7 %all-to-all-start.2 = ((bf16[8,64,768]{2,1,0:T(8,128)(2,1)}), bf16[8,64,768]{2,1,0:T(8,128)(2,1)}, u32[]{:S(2)}, u32[]{:S(2)}) async-start(bf16[8,64,768]{2,1,0:T(8,128)(2,1)} %bitcast.287), calls=%async_computation.6 | async-start | bytes 1572864 | tf_op jit(solution)/shard_map/all_to_all | solution.py:41
  545.8 4.7 collective-permute-start.43
  (68 other events, 411.1 us)
Sparse Core Ops, SparseCore 0:
  10.4 30.6 all-gather.11
  47.7 64.8 all-gather.5
  138.1 52.2 reduce-scatter.4
  200.5 46.0 all-gather.7
  288.4 47.8 reduce-scatter.6
  348.4 44.0 all-gather.9
  396.4 44.5 reduce-scatter.10
  443.4 76.7 reduce-scatter.8

commit v6 on v5

--- a/solution.py
+++ b/solution.py
@@ -296,7 +296,7 @@
         squares_ref[place, :] = jnp.sum(state * state, axis=-1, keepdims=True)
         return state[TILE - 1 :, :]
 
-    lax.fori_loop(0, rows // TILE, step, jnp.zeros((1, width), F32), unroll=4)
+    lax.fori_loop(0, rows // TILE, step, jnp.zeros((1, width), F32), unroll=8)
 
 
 def scan_backward(
@@ -351,7 +351,7 @@
         mixed_ref[place, :] = both[3]
         return carry
 
-    lax.fori_loop(0, rows // (2 * TILE), step, jnp.zeros((1, width), F32), unroll=2)
+    lax.fori_loop(0, rows // (2 * TILE), step, jnp.zeros((1, width), F32), unroll=4)
 
 
 def run_forward(proj, started, gap):
@@ -480,8 +480,8 @@
                 near = jnp.where(low_half, even, pltpu.roll(odd, own, 1))
                 far = jnp.where(low_half, pltpu.roll(even, own, 1), odd)
                 for step, grad in enumerate((near, far)):
-                    grad_ref[kind, :, pl.ds(((plane + step) * spots + pair) * own, 2 * own)] = grad
-    grad_ref[3, :, :] = out_ref[...].astype(F32)
+                    grad_ref[kind, :, pl.ds(((plane + step) * spots + pair) * own, 2 * own)] = grad.astype(BF)
+    grad_ref[3, :, :] = out_ref[...]
 
 
 def run_settle(got, shard_out):
@@ -490,10 +490,10 @@
     planes = packed // (3 * own)
     if 2 * own != 128 or planes % 2 != 0:
         grad = got.reshape(spots, own, 3, planes, own).transpose(2, 1, 3, 0, 4).reshape(3, own, width)
-        return jnp.concatenate([grad, shard_out[None]], axis=0).astype(F32)
+        return jnp.concatenate([grad, shard_out[None]], axis=0)
     return pl.pallas_call(
         settle,
-        out_shape=jax.ShapeDtypeStruct((4, own, width), F32),
+        out_shape=jax.ShapeDtypeStruct((4, own, width), BF),
         compiler_params=pltpu.CompilerParams(vmem_limit_bytes=48 * 2**20),
     )(got, shard_out)
 
@@ -668,14 +668,16 @@
     w_ride = ride + jnp.pad(w_out, ((0, 128), (0, 128)))
     mix_part = jnp.dot(raw, w_ride, preferred_element_type=F32).astype(BF)
     mix_part, cots[1], cots[-1] = tied(mix_part, cots[1], cots[-1])
-    mix_raw, part_in, *cots = tied(scatter(mix_part, PLANE), part_in, *cots)
+    in_halves = quad_halves(part_in.reshape(planes * pairs * own, 2 * inner), 0)
+    mix_raw, *cots = tied(scatter(mix_part, PLANE), *cots)
     cot_all = ring_gather(in_order(cots, "z"), "c").swapaxes(0, 1)
     cot_all = cot_all.reshape(planes * pairs * rows, width)
-    w_in = quad_whole(quad_parts(part_in.reshape(planes * pairs * own, 2 * inner), 0))
 
     order, gain_glu = (planes, quads), full_gains[2].reshape(1, width)
     after_mix, n2_home, mid_factor, home_factor = run_enter(mix_raw, tokens, gain_glu, order)
+    n2_home, *in_halves = tied(n2_home, *in_halves)
     n2 = gather(n2_home, LINE)
+    w_in = quad_whole(quad_others(*in_halves))
     gate_up = jnp.dot(n2, w_in, preferred_element_type=F32)
     gate, up_value = gate_up[:, :inner], gate_up[:, inner:]
     silu_gate = silu(gate)

time: 592 us -> 589 us (level)
  waiting for transfers between devices: 217 us -> 203 us
  other arithmetic: 68.1 us -> 75.3 us
    ppermute x3, waiting for transfers between devices: 29.5 us -> 9.78 us  [direct_gather(): return [value] + [lax.ppermute(value, axis, hop) for hop in hops]]
    another operation x18 -> x17, other arithmetic: 6.06 us -> 12.6 us  [ring_gather(): jnp.stack([jnp.where(mine == 0, value, other), jnp.where(mine == 0, other...]
    ppermute x3, starting transfers between devices: 5.12 us -> 11.3 us  [direct_gather(): return [value] + [lax.ppermute(value, axis, hop) for hop in hops]]
    unnamed x122 -> x124, local copies, waits for them, and re-layouts: 25.8 us -> 25.6 us
  transfers between devices with their start and end apart: 55 -> 55, of which waited for: 29 -> 27; matrix products, arithmetic and copies ran while one was open for 30% -> 31% of each run, Pallas kernels for 5% -> 4%
where the time goes in v6:
time: 589 us; the launch traced here: 582 us
  waiting for transfers between devices  203 us (34%)
  local copies, waits for them, and re-layouts  90.6 us (15%)
  starting transfers between devices  84.3 us (14%)
  other arithmetic  75.3 us (13%)
  matrix products  70.9 us (12%)
  Pallas kernels  34.5 us (6%)
  between operations  22.8 us (4%)
    ppermute x14, waiting for transfers between devices, ring_gather(): other = lax.ppermute(value, axis, [(0, 1), (1, 0)])  66.2 us
    ppermute x10, waiting for transfers between devices, ring_terms(): return [block(0), lax.ppermute(block(1), axis, [(0, 1), (1, 0)])]  30.8 us
    ppermute x3, waiting for transfers between devices, direct_scatter(): lax.ppermute(block, axis, [(i, (i - back) % count) for i in range(count)])  29.5 us
    unnamed x124, local copies, waits for them, and re-layouts  25.6 us
    ppermute x3, waiting for transfers between devices, line_exchange(): lax.ppermute(blocks[back], 'z', [(i, (i - back) % count) for i in range(c...  22.1 us
    all_to_all x3, starting transfers between devices, exchange(): return lax.all_to_all(value, axes, 0, 0, tiled=True)  21.9 us
    reduce_scatter x4, waiting for transfers between devices, scatter(): return lax.psum_scatter(value, axes, scatter_dimension=0, tiled=True)  18.1 us
    pallas_call x2, Pallas kernels, run_adam(): pl.pallas_call(adam_rows, grid=(own // rows,), in_specs=[pl.BlockSpec(mem...  16.1 us
  transfers between devices with their start and end apart: 55, of which 27 were waited for; matrix products, arithmetic and copies ran while one was open for 31% of the time, Pallas kernels for 4%

profile of v6, /device:TPU:0, one launch (start us, length us, event | category | flops | bytes accessed | tf_op | source)
XLA Modules:
  0.0 581.8 jit_solution(13566126501663300054)
XLA Ops:
  12.0 5.4 shard_map.271
  19.2 5.2 all-to-all-start
  26.2 8.3 %reshape.219 = bf16[64,2,4,4,2,176]{5,4,3,2,0,1:T(2,128)(2,1)S(1)} reshape(bf16[64,2,5632]{2,0,1:T(8,128)(2,1)} %copy.84) | data formatting | bytes 2883584 | tf_op jit(solution)/shard_map/reshape | solution.py:634
  36.7 5.4 reshape.220
  75.0 9.2 %collective-permute-done.7 = bf16[2,128,1024]{2,1,0:T(8,128)(2,1)S(1)} collective-permute-done((bf16[2,128,1024]{2,1,0:T(8,128)(2,1)S(1)}, bf16[2,128,1024]{2,1,0:T(8,128)(2,1)S(1)}, u32[]{:S(2)}, u32[]{:S(2)}) %collective-permute-start.7) | collective-permute-done | bytes 524320 | tf_op jit(solution)/shard_map/ppermute | solution.py:47
  89.5 7.9 %collective-permute-done.3 = bf16[2,88,2048]{2,1,0:T(8,128)(2,1)S(1)} collective-permute-done((bf16[2,88,2048]{2,1,0:T(8,128)(2,1)S(1)}, bf16[2,88,2048]{2,1,0:T(8,128)(2,1)S(1)}, u32[]{:S(2)}, u32[]{:S(2)}) %collective-permute-start.3) | collective-permute-done | bytes 720928 | tf_op jit(solution)/shard_map/ppermute | solution.py:47
  105.6 7.0 %all-gather.6.cloned.1.call-done = bf16[2048,768]{1,0:T(8,128)(2,1)} async-done(((bf16[512,768]{1,0:T(8,128)(2,1)}), bf16[2048,768]{1,0:T(8,128)(2,1)}) %all-gather.6.cloned.1.call-update) | async-done | bytes 3145744 | tf_op jit(solution)/shard_map/all_gather | solution.py:33
  112.5 4.2 collective-permute-start.16
  116.8 6.1 %fusion.59.proj_ref = f32[1024,768]{1,0:T(8,128)S(1)} fusion(bf16[1024,2048]{1,0:T(8,128)(2,1)} %fusion.1, bf16[2048,768]{1,0:T(8,128)(2,1)} %all-gather.6.cloned.1.call-done), kind=kOutput, calls=%fused_computation.225 | convolution fusion | flops 3221225472 | bytes 10485760 | tf_op jit(solution)/shard_map/dot_general | solution.py:656
  122.9 3.3 shard_map.272
  127.5 3.5 convolution_convert_fusion.1
  131.0 7.0 %collective-permute-done.16 = bf16[128,2048]{1,0:T(8,128)(2,1)} collective-permute-done((bf16[128,2048]{1,0:T(8,128)(2,1)S(1)}, bf16[128,2048]{1,0:T(8,128)(2,1)}, u32[]{:S(2)}, u32[]{:S(2)}) %collective-permute-start.16) | collective-permute-done | bytes 524320 | tf_op jit(solution)/shard_map/ppermute | solution.py:181
  145.2 8.6 %collective-permute-done.19 = bf16[2,64,1408]{2,1,0:T(8,128)(2,1)} collective-permute-done((bf16[2,64,1408]{2,1,0:T(8,128)(2,1)}, bf16[2,64,1408]{2,1,0:T(8,128)(2,1)}, u32[]{:S(2)}, u32[]{:S(2)}) %collective-permute-start.19) | collective-permute-done | bytes 360480 | tf_op jit(solution)/shard_map/ppermute | solution.py:210
  153.8 13.5 %collective-permute-done.20 = bf16[2,64,1408]{2,1,0:T(8,128)(2,1)} collective-permute-done((bf16[2,64,1408]{2,1,0:T(8,128)(2,1)}, bf16[2,64,1408]{2,1,0:T(8,128)(2,1)}, u32[]{:S(2)}, u32[]{:S(2)}) %collective-permute-start.20) | collective-permute-done | bytes 360480 | tf_op jit(solution)/shard_map/ppermute | solution.py:210
  173.6 7.1 %collective-permute-start.17 = (bf16[128,2048]{1,0:T(8,128)(2,1)S(1)}, bf16[128,2048]{1,0:T(8,128)(2,1)S(1)}, u32[]{:S(2)}, u32[]{:S(2)}) collective-permute-start(bf16[128,2048]{1,0:T(8,128)(2,1)S(1)} %multiply_convert_fusion.4.cot_ref), channel_id=1, source_target_pairs={{0,16},{8,24},{16,0},{24,8},{1,17},{9,25},{17,1},{25,9},{2,18},{10... | collective-permute-start | bytes 1572872 | tf_op jit(solution)/shard_map/ppermute | solution.py:181
  180.7 15.1 %collective-permute-done.22 = bf16[256,1408]{1,0:T(8,128)(2,1)} collective-permute-done((bf16[256,1408]{1,0:T(8,128)(2,1)}, bf16[256,1408]{1,0:T(8,128)(2,1)}, u32[]{:S(2)}, u32[]{:S(2)}) %collective-permute-start.22) | collective-permute-done | bytes 720928 | tf_op jit(solution)/shard_map/ppermute | solution.py:47
  200.6 2.8 collective-permute-done.17
  209.8 29.8 %collective-permute-done.25 = bf16[2,256,1408]{2,1,0:T(8,128)(2,1)} collective-permute-done((bf16[2,256,1408]{2,1,0:T(8,128)(2,1)}, bf16[2,256,1408]{2,1,0:T(8,128)(2,1)}, u32[]{:S(2)}, u32[]{:S(2)}) %collective-permute-start.25) | collective-permute-done | bytes 1441824 | tf_op jit(solution)/shard_map/ppermute | solution.py:47
  242.9 4.9 pad_maximum_fusion
  252.3 3.0 all-gather.8.cloned.1.call-done
  255.3 10.3 %fusion.60 = f32[1024,1408]{0,1:T(8,128)S(1)} fusion(bf16[1024,2048]{1,0:T(8,128)(2,1)} %all-gather.8.cloned.1.call-done, bf16[2048,1408]{1,0:T(8,128)(2,1)} %bitcast.276), kind=kOutput, calls=%fused_computation.226 | convolution fusion | flops 5905580032 | bytes 15728640 | tf_op jit(solution)/shard_map/dot_general | solution.py:681
  265.7 5.2 multiply_convert_fusion.2
  272.4 11.0 %convolution_convert_fusion.3 = bf16[1024,2048]{1,0:T(8,128)(2,1)} fusion(bf16[2048,1408]{1,0:T(8,128)(2,1)} %bitcast.277, bf16[1024,704]{0,1:T(8,128)(2,1)S(1)} %get-tuple-element.165, bf16[1024,704]{0,1:T(8,128)(2,1)S(1)} %get-tuple-element.164), kind=kOutput, calls=%fused_computation.16 | convolution fusion | flops 5913444352 | bytes 12845056 | tf_op jit(solution)/shard_map/dot_general | solution.py:690
  283.8 5.9 %convolution_convert_fusion.2 = bf16[1024,2048]{1,0:T(8,128)(2,1)S(1)} fusion(bf16[1024,704]{0,1:T(8,128)(2,1)} %get-tuple-element.110, bf16[704,2048]{1,0:T(8,128)(2,1)} %bitcast.289), kind=kOutput, calls=%fused_computation.15 | convolution fusion | flops 2954887168 | bytes 8519680 | tf_op jit(solution)/shard_map/dot_general | solution.py:694
  294.1 7.0 %convolution_convert_fusion = bf16[2048,1408]{1,0:T(8,128)(2,1)S(1)} fusion(bf16[1024,2048]{1,0:T(8,128)(2,1)S(1)} %copy-done.51, bf16[1024,704]{0,1:T(8,128)(2,1)S(1)} %copy-done.58, bf16[1024,704]{0,1:T(8,128)(2,1)S(1)} %copy-done.56), kind=kOutput, calls=%fused_computation.4 | convolution fusion | flops 5914230784 | bytes 12845056 | tf_op jit(solution)/shard_map/dot_general | solution.py:692
  308.1 4.6 fusion.3
  312.8 4.4 convolution_convert_fusion.6
  317.2 20.2 %collective-permute-done.27 = bf16[2,256,1408]{2,1,0:T(8,128)(2,1)} collective-permute-done((bf16[2,256,1408]{2,1,0:T(8,128)(2,1)}, bf16[2,256,1408]{2,1,0:T(8,128)(2,1)}, u32[]{:S(2)}, u32[]{:S(2)}) %collective-permute-start.27) | collective-permute-done | bytes 1441824 | tf_op jit(solution)/shard_map/ppermute | solution.py:82
  337.5 3.0 collective-permute-done.28
  356.2 9.1 %collective-permute-done.33 = bf16[128,2048]{1,0:T(8,128)(2,1)S(1)} collective-permute-done((bf16[128,2048]{1,0:T(8,128)(2,1)S(1)}, bf16[128,2048]{1,0:T(8,128)(2,1)S(1)}, u32[]{:S(2)}, u32[]{:S(2)}) %collective-permute-start.33) | collective-permute-done | bytes 524320 | tf_op jit(solution)/shard_map/ppermute | solution.py:124
  365.3 20.4 %collective-permute-done.32 = bf16[128,2048]{1,0:T(8,128)(2,1)S(1)} collective-permute-done((bf16[128,2048]{1,0:T(8,128)(2,1)S(1)}, bf16[128,2048]{1,0:T(8,128)(2,1)S(1)}, u32[]{:S(2)}, u32[]{:S(2)}) %collective-permute-start.32) | collective-permute-done | bytes 524320 | tf_op jit(solution)/shard_map/ppermute | solution.py:124
  388.6 12.3 %all-to-all-start.1 = ((bf16[8,64,1408]{2,1,0:T(8,128)(2,1)}), bf16[8,64,1408]{2,1,0:T(8,128)(2,1)}, u32[]{:S(2)}, u32[]{:S(2)}) async-start(bf16[8,64,1408]{2,1,0:T(8,128)(2,1)} %bitcast.281), calls=%async_computation.3 | async-start | bytes 2883584 | tf_op jit(solution)/shard_map/all_to_all | solution.py:41
  402.2 4.6 fusion.15.d_mixed_ref
  406.9 5.6 shard_map.275
  416.0 5.9 %convolution_convert_fusion.5 = bf16[2048,768]{1,0:T(8,128)(2,1)S(1)} fusion(bf16[1024,2048]{1,0:T(8,128)(2,1)} %fusion.1, bf16[1024,768]{1,0:T(8,128)(2,1)S(1)} %copy-done.23), kind=kOutput, calls=%fused_computation.18 | convolution fusion | flops 3222798336 | bytes 8912896 | tf_op jit(solution)/shard_map/dot_general | solution.py:717
  424.5 11.6 %all-to-all-done.1 = bf16[8,64,1408]{2,1,0:T(8,128)(2,1)} async-done(((bf16[8,64,1408]{2,1,0:T(8,128)(2,1)}), bf16[8,64,1408]{2,1,0:T(8,128)(2,1)}, u32[]{:S(2)}, u32[]{:S(2)}) %all-to-all-start.1) | async-done | bytes 1441824 | tf_op jit(solution)/shard_map/all_to_all | solution.py:41
  436.1 5.6 convolution_convert_fusion.4
  456.4 7.8 %reshape.235 = bf16[4,2,64,2,4,176]{5,4,3,2,1,0:T(4,128)(2,1)S(1)} reshape(bf16[8,64,1408]{2,1,0:T(8,128)(2,1)} %all-to-all-done.1) | data formatting | bytes 2883584 | tf_op jit(solution)/shard_map/reshape | solution.py:724
  470.3 4.6 copy.69
  474.8 6.6 %reshape.236.grad_ref = bf16[2,64,5632]{2,1,0:T(8,128)(2,1)} reshape(bf16[2,64,4,4,2,176]{5,4,3,2,1,0:T(2,128)(2,1)} %copy.69) | data formatting | bytes 2883584 | tf_op jit(solution)/shard_map/reshape | solution.py:725
  487.5 3.3 collective-permute-done.38
  500.3 18.1 %reduce-scatter.9.cloned.1.call-done.shard_ref = bf16[512,1024]{1,0:T(8,128)(2,1)} async-done(((bf16[2048,1024]{1,0:T(8,128)(2,1)}), bf16[512,1024]{1,0:T(8,128)(2,1)}) %reduce-scatter.9.cloned.1.call-update) | async-done | bytes 1048592 | tf_op jit(solution)/shard_map/reduce_scatter | solution.py:37
  532.7 4.4 all-to-all-start.2
  539.7 2.9 collective-permute-start.42
  543.9 4.3 collective-permute-start.43
  550.6 9.1 %shard_map.279 = (f32[64,2,5632]{2,1,0:T(2,128)}, f32[64,2,5632]{2,1,0:T(2,128)}, f32[64,2,5632]{2,1,0:T(2,128)}) custom-call(f32[1,1]{1,0:T(1,128)} %bitcast.104.clip_ref, f32[64,2,5632]{2,1,0:T(2,128)S(1)} %copy-done.1, f32[64,2,5632]{2,1,0:T(2,128)} %first_ref.3, f32[64,2,5632]{2,1,0:T(2,128)} %second_ref.3, bf16[2,64,5632]{2,1,0:T(8,128)(2,1)S(1)} %copy-done.4), custom_call_target="tpu_custom_call" | custom-call | tf_op jit(solution)/shard_map/pallas_call | solution.py:400
  560.3 2.9 multiply_subtract_fusion
  566.7 6.9 %shard_map.278 = (f32[64,4,2048]{2,1,0:T(4,128)}, f32[64,4,2048]{2,1,0:T(4,128)}, f32[64,4,2048]{2,1,0:T(4,128)}) custom-call(f32[1,1]{1,0:T(1,128)} %bitcast.104.clip_ref, f32[64,4,2048]{2,1,0:T(4,128)S(1)} %copy-done.6, f32[64,4,2048]{2,1,0:T(4,128)S(1)} %copy-done.14, f32[64,4,2048]{2,1,0:T(4,128)} %second_ref.2, bf16[4,64,2048]{2,1,0:T(8,128)(2,1)S(1)} %shard_map.277.grad_ref), custom_call_target="tpu_custom_call" | custom-call | tf_op jit(solution)/shard_map/pallas_call | solution.py:400
  (359 shorter events, 183.9 us)
Async XLA Ops:
  7.2 36.7 %all-gather.12.cloned.1.call-start = ((), (), s32[]{:S(2)}) async-start(), calls=%async_computation.14 | async-start | bytes 1310720 | tf_op jit(solution)/shard_map/all_gather | solution.py:33
  19.2 24.6 %all-to-all-start = ((bf16[8,64,768]{2,1,0:T(8,128)(2,1)}), bf16[8,64,768]{2,1,0:T(8,128)(2,1)}, u32[]{:S(2)}, u32[]{:S(2)}) async-start(bf16[8,64,768]{2,1,0:T(8,128)(2,1)} %copy-done.18), calls=%async_computation | async-start | bytes 1572864 | tf_op jit(solution)/shard_map/all_to_all | solution.py:41
  24.4 88.1 %all-gather.6.cloned.1.call-start = ((), (), s32[]{:S(2)}) async-start(), calls=%async_computation.7 | async-start | bytes 3932160 | tf_op jit(solution)/shard_map/all_gather | solution.py:33
  47.5 155.9 %reduce-scatter.5.cloned.1.call-start = ((), (), s32[]{:S(2)}) async-start(), calls=%async_computation.8 | async-start | bytes 5013504 | tf_op jit(solution)/shard_map/reduce_scatter | solution.py:37
  49.2 4.6 collective-permute-start.11
  51.8 19.4 %collective-permute-start = (bf16[88,2048]{1,0:T(8,128)(2,1)}, bf16[88,2048]{1,0:T(8,128)(2,1)}, u32[]{:S(2)}, u32[]{:S(2)}) collective-permute-start(bf16[88,2048]{1,0:T(8,128)(2,1)} %get-tuple-element.223), channel_id=1, source_target_pairs={{0,2},{2,0},{1,3},{3,1},{4,6},{6,4},{5,7},{7,5},{8,10},{10,8},{9,1... | collective-permute-start | bytes 1081352 | tf_op jit(solution)/shard_map/ppermute | solution.py:47
  53.3 17.9 %collective-permute-start.2 = (bf16[88,2048]{1,0:T(8,128)(2,1)}, bf16[88,2048]{1,0:T(8,128)(2,1)}, u32[]{:S(2)}, u32[]{:S(2)}) collective-permute-start(bf16[88,2048]{1,0:T(8,128)(2,1)} %get-tuple-element.224), channel_id=1, source_target_pairs={{0,4},{4,0},{1,5},{5,1},{2,6},{6,2},{3,7},{7,3},{8,12},{12,8},{9,1... | collective-permute-start | bytes 1081352 | tf_op jit(solution)/shard_map/ppermute | solution.py:47
  55.9 11.5 %collective-permute-start.4 = (bf16[128,1024]{1,0:T(8,128)(2,1)S(1)}, bf16[128,1024]{1,0:T(8,128)(2,1)S(1)}, u32[]{:S(2)}, u32[]{:S(2)}) collective-permute-start(bf16[128,1024]{1,0:T(8,128)(2,1)S(1)} %get-tuple-element.227), channel_id=1, source_target_pairs={{0,2},{2,0},{1,3},{3,1},{4,6},{6,4},{5,7},{7,5},{8,10},{10,8},{9,1... | collective-permute-start | bytes 786440 | tf_op jit(solution)/shard_map/ppermute | solution.py:47
  56.7 11.4 %collective-permute-start.6 = (bf16[128,1024]{1,0:T(8,128)(2,1)S(1)}, bf16[128,1024]{1,0:T(8,128)(2,1)}, u32[]{:S(2)}, u32[]{:S(2)}) collective-permute-start(bf16[128,1024]{1,0:T(8,128)(2,1)S(1)} %get-tuple-element.228), channel_id=1, source_target_pairs={{0,4},{4,0},{1,5},{5,1},{2,6},{6,2},{3,7},{7,3},{8,12},{12,8},{9,1... | collective-permute-start | bytes 786440 | tf_op jit(solution)/shard_map/ppermute | solution.py:47
  58.2 6.0 %collective-permute-start.13 = (f32[16,3,64]{2,1,0:T(4,128)S(1)}, f32[16,3,64]{2,1,0:T(4,128)S(1)}, u32[]{:S(2)}, u32[]{:S(2)}) collective-permute-start(f32[16,3,64]{2,1,0:T(4,128)S(1)} %pad_maximum_fusion.18), channel_id=1, source_target_pairs={{0,16},{8,24},{16,0},{24,8},{1,17},{9,25},{17,1},{25,9},{2,18},{10... | collective-permute-start | bytes 36872 | tf_op jit(solution)/shard_map/ppermute | solution.py:100
  64.2 21.6 %collective-permute-start.14 = (bf16[4,64,1408]{2,1,0:T(8,128)(2,1)}, bf16[4,64,1408]{2,1,0:T(8,128)(2,1)}, u32[]{:S(2)}, u32[]{:S(2)}) collective-permute-start(bf16[4,64,1408]{2,1,0:T(8,128)(2,1)} %dynamic-slice_bitcast_fusion.7), channel_id=1, source_target_pairs={{0,1},{1,0},{2,3},{3,2},{4,5},{5,4},{6,7},{7,6},{8,9},{9,8},{10,11... | collective-permute-start | bytes 2162696 | tf_op jit(solution)/shard_map/ppermute | solution.py:200
  69.3 14.9 %collective-permute-start.7 = (bf16[2,128,1024]{2,1,0:T(8,128)(2,1)S(1)}, bf16[2,128,1024]{2,1,0:T(8,128)(2,1)S(1)}, u32[]{:S(2)}, u32[]{:S(2)}) collective-permute-start(bf16[2,128,1024]{2,1,0:T(8,128)(2,1)S(1)} %pad_maximum_fusion.17), channel_id=1, source_target_pairs={{0,2},{2,0},{1,3},{3,1},{4,6},{6,4},{5,7},{7,5},{8,10},{10,8},{9,1... | collective-permute-start | bytes 1572872 | tf_op jit(solution)/shard_map/ppermute | solution.py:47
  70.6 14.9 %collective-permute-start.5 = (bf16[2,128,1024]{2,1,0:T(8,128)(2,1)S(1)}, bf16[2,128,1024]{2,1,0:T(8,128)(2,1)S(1)}, u32[]{:S(2)}, u32[]{:S(2)}) collective-permute-start(bf16[2,128,1024]{2,1,0:T(8,128)(2,1)S(1)} %pad_maximum_fusion.16), channel_id=1, source_target_pairs={{0,4},{4,0},{1,5},{5,1},{2,6},{6,2},{3,7},{7,3},{8,12},{12,8},{9,1... | collective-permute-start | bytes 1572872 | tf_op jit(solution)/shard_map/ppermute | solution.py:47
  72.5 24.9 %collective-permute-start.3 = (bf16[2,88,2048]{2,1,0:T(8,128)(2,1)S(1)}, bf16[2,88,2048]{2,1,0:T(8,128)(2,1)S(1)}, u32[]{:S(2)}, u32[]{:S(2)}) collective-permute-start(bf16[2,88,2048]{2,1,0:T(8,128)(2,1)S(1)} %pad_maximum_fusion.13), channel_id=1, source_target_pairs={{0,2},{2,0},{1,3},{3,1},{4,6},{6,4},{5,7},{7,5},{8,10},{10,8},{9,1... | collective-permute-start | bytes 2162696 | tf_op jit(solution)/shard_map/ppermute | solution.py:47
  73.5 24.5 %collective-permute-start.1 = (bf16[2,88,2048]{2,1,0:T(8,128)(2,1)S(1)}, bf16[2,88,2048]{2,1,0:T(8,128)(2,1)S(1)}, u32[]{:S(2)}, u32[]{:S(2)}) collective-permute-start(bf16[2,88,2048]{2,1,0:T(8,128)(2,1)S(1)} %pad_maximum_fusion.12), channel_id=1, source_target_pairs={{0,4},{4,0},{1,5},{5,1},{2,6},{6,2},{3,7},{7,3},{8,12},{12,8},{9,1... | collective-permute-start | bytes 2162696 | tf_op jit(solution)/shard_map/ppermute | solution.py:47
  85.8 14.2 %collective-permute-start.8 = (bf16[2,2,128,2048]{3,2,1,0:T(8,128)(2,1)S(1)}, bf16[2,2,128,2048]{3,2,1,0:T(8,128)(2,1)S(1)}, u32[]{:S(2)}, u32[]{:S(2)}) collective-permute-start(bf16[2,2,128,2048]{3,2,1,0:T(8,128)(2,1)S(1)} %pad_maximum_fusion.4), channel_id=1, source_target_pairs={{0,1},{1,0},{2,3},{3,2},{4,5},{5,4},{6,7},{7,6},{8,9},{9,8},{10,11... | collective-permute-start | bytes 6291464 | tf_op jit(solution)/shard_map/ppermute | solution.py:47
  112.5 18.4 %collective-permute-start.15 = (bf16[128,2048]{1,0:T(8,128)(2,1)S(1)}, bf16[128,2048]{1,0:T(8,128)(2,1)S(1)}, u32[]{:S(2)}, u32[]{:S(2)}) collective-permute-start(bf16[128,2048]{1,0:T(8,128)(2,1)S(1)} %multiply_convert_fusion.4.cot_ref), channel_id=1, source_target_pairs={{0,8},{8,16},{16,24},{24,0},{1,9},{9,17},{17,25},{25,1},{2,10},{10... | collective-permute-start | bytes 1572872 | tf_op jit(solution)/shard_map/ppermute | solution.py:181
  112.5 25.4 %collective-permute-start.16 = (bf16[128,2048]{1,0:T(8,128)(2,1)S(1)}, bf16[128,2048]{1,0:T(8,128)(2,1)}, u32[]{:S(2)}, u32[]{:S(2)}) collective-permute-start(bf16[128,2048]{1,0:T(8,128)(2,1)S(1)} %multiply_convert_fusion.4.cot_ref), channel_id=1, source_target_pairs={{0,24},{8,0},{16,8},{24,16},{1,25},{9,1},{17,9},{25,17},{2,26},{10... | collective-permute-start | bytes 1572872 | tf_op jit(solution)/shard_map/ppermute | solution.py:181
  138.0 117.4 %all-gather.8.cloned.1.call-start = ((), (), s32[]{:S(2)}) async-start(), calls=%async_computation.9 | async-start | bytes 4718592 | tf_op jit(solution)/shard_map/all_gather | solution.py:33
  140.2 13.6 %collective-permute-start.19 = (bf16[2,64,1408]{2,1,0:T(8,128)(2,1)}, bf16[2,64,1408]{2,1,0:T(8,128)(2,1)}, u32[]{:S(2)}, u32[]{:S(2)}) collective-permute-start(bf16[2,64,1408]{2,1,0:T(8,128)(2,1)} %get-tuple-element.204), channel_id=1, source_target_pairs={{0,8},{8,16},{16,24},{24,0},{1,9},{9,17},{17,25},{25,1},{2,10},{10... | collective-permute-start | bytes 1081352 | tf_op jit(solution)/shard_map/ppermute | solution.py:210
  141.2 26.1 %collective-permute-start.20 = (bf16[2,64,1408]{2,1,0:T(8,128)(2,1)}, bf16[2,64,1408]{2,1,0:T(8,128)(2,1)}, u32[]{:S(2)}, u32[]{:S(2)}) collective-permute-start(bf16[2,64,1408]{2,1,0:T(8,128)(2,1)} %get-tuple-element.203), channel_id=1, source_target_pairs={{0,16},{8,24},{16,0},{24,8},{1,17},{9,25},{17,1},{25,9},{2,18},{10... | collective-permute-start | bytes 1081352 | tf_op jit(solution)/shard_map/ppermute | solution.py:210
  142.5 24.8 %collective-permute-start.21 = (bf16[2,64,1408]{2,1,0:T(8,128)(2,1)S(1)}, bf16[2,64,1408]{2,1,0:T(8,128)(2,1)}, u32[]{:S(2)}, u32[]{:S(2)}) collective-permute-start(bf16[2,64,1408]{2,1,0:T(8,128)(2,1)S(1)} %get-tuple-element.202), channel_id=1, source_target_pairs={{0,24},{8,0},{16,8},{24,16},{1,25},{9,1},{17,9},{25,17},{2,26},{10... | collective-permute-start | bytes 1081352 | tf_op jit(solution)/shard_map/ppermute | solution.py:210
  169.8 26.0 %collective-permute-start.22 = (bf16[256,1408]{1,0:T(8,128)(2,1)}, bf16[256,1408]{1,0:T(8,128)(2,1)}, u32[]{:S(2)}, u32[]{:S(2)}) collective-permute-start(bf16[256,1408]{1,0:T(8,128)(2,1)} %bitcast.55), channel_id=1, source_target_pairs={{0,2},{2,0},{1,3},{3,1},{4,6},{6,4},{5,7},{7,5},{8,10},{10,8},{9,1... | collective-permute-start | bytes 2162696 | tf_op jit(solution)/shard_map/ppermute | solution.py:47
  172.1 25.1 %collective-permute-start.23 = (bf16[256,1408]{1,0:T(8,128)(2,1)}, bf16[256,1408]{1,0:T(8,128)(2,1)}, u32[]{:S(2)}, u32[]{:S(2)}) collective-permute-start(bf16[256,1408]{1,0:T(8,128)(2,1)} %bitcast.58), channel_id=1, source_target_pairs={{0,4},{4,0},{1,5},{5,1},{2,6},{6,2},{3,7},{7,3},{8,12},{12,8},{9,1... | collective-permute-start | bytes 2162696 | tf_op jit(solution)/shard_map/ppermute | solution.py:47
  173.6 29.8 %collective-permute-start.17 = (bf16[128,2048]{1,0:T(8,128)(2,1)S(1)}, bf16[128,2048]{1,0:T(8,128)(2,1)S(1)}, u32[]{:S(2)}, u32[]{:S(2)}) collective-permute-start(bf16[128,2048]{1,0:T(8,128)(2,1)S(1)} %multiply_convert_fusion.4.cot_ref), channel_id=1, source_target_pairs={{0,16},{8,24},{16,0},{24,8},{1,17},{9,25},{17,1},{25,9},{2,18},{10... | collective-permute-start | bytes 1572872 | tf_op jit(solution)/shard_map/ppermute | solution.py:181
  206.9 133.6 %reduce-scatter.7.cloned.1.call-start = ((), (), s32[]{:S(2)}) async-start(), calls=%async_computation.10 | async-start | bytes 4718592 | tf_op jit(solution)/shard_map/reduce_scatter | solution.py:37
  206.9 32.7 %collective-permute-start.25 = (bf16[2,256,1408]{2,1,0:T(8,128)(2,1)}, bf16[2,256,1408]{2,1,0:T(8,128)(2,1)}, u32[]{:S(2)}, u32[]{:S(2)}) collective-permute-start(bf16[2,256,1408]{2,1,0:T(8,128)(2,1)} %get-tuple-element.109), channel_id=1, source_target_pairs={{0,2},{2,0},{1,3},{3,1},{4,6},{6,4},{5,7},{7,5},{8,10},{10,8},{9,1... | collective-permute-start | bytes 4325384 | tf_op jit(solution)/shard_map/ppermute | solution.py:47
  207.5 34.0 %collective-permute-start.24 = (bf16[2,256,1408]{2,1,0:T(8,128)(2,1)}, bf16[2,256,1408]{2,1,0:T(8,128)(2,1)S(1)}, u32[]{:S(2)}, u32[]{:S(2)}) collective-permute-start(bf16[2,256,1408]{2,1,0:T(8,128)(2,1)} %get-tuple-element.108), channel_id=1, source_target_pairs={{0,4},{4,0},{1,5},{5,1},{2,6},{6,2},{3,7},{7,3},{8,12},{12,8},{9,1... | collective-permute-start | bytes 4325384 | tf_op jit(solution)/shard_map/ppermute | solution.py:47
  209.7 38.1 %collective-permute-start.18 = (bf16[4,128,2048]{2,1,0:T(8,128)(2,1)S(1)}, bf16[4,128,2048]{2,1,0:T(8,128)(2,1)}, u32[]{:S(2)}, u32[]{:S(2)}) collective-permute-start(bf16[4,128,2048]{2,1,0:T(8,128)(2,1)S(1)} %pad_maximum_fusion.5), channel_id=1, source_target_pairs={{0,1},{1,0},{2,3},{3,2},{4,5},{5,4},{6,7},{7,6},{8,9},{9,8},{10,11... | collective-permute-start | bytes 6291464 | tf_op jit(solution)/shard_map/ppermute | solution.py:47
  283.4 105.2 %all-gather.10.cloned.1.call-start = ((), (), s32[]{:S(2)}) async-start(), calls=%async_computation.11 | async-start | bytes 5013504 | tf_op jit(solution)/shard_map/all_gather | solution.py:33
  292.8 15.3 %collective-permute-start.26 = (bf16[4,128,2048]{2,1,0:T(8,128)(2,1)}, bf16[4,128,2048]{2,1,0:T(8,128)(2,1)}, u32[]{:S(2)}, u32[]{:S(2)}) collective-permute-start(bf16[4,128,2048]{2,1,0:T(8,128)(2,1)} %dynamic-slice_bitcast_fusion), channel_id=1, source_target_pairs={{0,1},{1,0},{2,3},{3,2},{4,5},{5,4},{6,7},{7,6},{8,9},{9,8},{10,11... | collective-permute-start | bytes 6291464 | tf_op jit(solution)/shard_map/ppermute | solution.py:82
  303.4 34.1 %collective-permute-start.27 = (bf16[2,256,1408]{2,1,0:T(8,128)(2,1)}, bf16[2,256,1408]{2,1,0:T(8,128)(2,1)}, u32[]{:S(2)}, u32[]{:S(2)}) collective-permute-start(bf16[2,256,1408]{2,1,0:T(8,128)(2,1)} %get-tuple-element.177), channel_id=1, source_target_pairs={{0,4},{4,0},{1,5},{5,1},{2,6},{6,2},{3,7},{7,3},{8,12},{12,8},{9,1... | collective-permute-start | bytes 4325384 | tf_op jit(solution)/shard_map/ppermute | solution.py:82
  306.7 33.8 %collective-permute-start.28 = (bf16[2,256,1408]{2,1,0:T(8,128)(2,1)}, bf16[2,256,1408]{2,1,0:T(8,128)(2,1)}, u32[]{:S(2)}, u32[]{:S(2)}) collective-permute-start(bf16[2,256,1408]{2,1,0:T(8,128)(2,1)} %get-tuple-element.175), channel_id=1, source_target_pairs={{0,2},{2,0},{1,3},{3,1},{4,6},{6,4},{5,7},{7,5},{8,10},{10,8},{9,1... | collective-permute-start | bytes 4325384 | tf_op jit(solution)/shard_map/ppermute | solution.py:82
  345.3 149.2 %reduce-scatter.11.cloned.1.call-start = ((), (), s32[]{:S(2)}) async-start(), calls=%async_computation.13 | async-start | bytes 3604480 | tf_op jit(solution)/shard_map/reduce_scatter | solution.py:37
  347.7 39.3 %collective-permute-start.30 = (bf16[256,1408]{1,0:T(8,128)(2,1)S(1)}, bf16[256,1408]{1,0:T(8,128)(2,1)S(1)}, u32[]{:S(2)}, u32[]{:S(2)}) collective-permute-start(bf16[256,1408]{1,0:T(8,128)(2,1)S(1)} %dynamic-slice_bitcast_fusion.5), channel_id=1, source_target_pairs={{0,4},{4,0},{1,5},{5,1},{2,6},{6,2},{3,7},{7,3},{8,12},{12,8},{9,1... | collective-permute-start | bytes 2162696 | tf_op jit(solution)/shard_map/ppermute | solution.py:82
  348.5 16.8 %collective-permute-start.33 = (bf16[128,2048]{1,0:T(8,128)(2,1)S(1)}, bf16[128,2048]{1,0:T(8,128)(2,1)S(1)}, u32[]{:S(2)}, u32[]{:S(2)}) collective-permute-start(bf16[128,2048]{1,0:T(8,128)(2,1)S(1)} %get-tuple-element.192), channel_id=1, source_target_pairs={{0,8},{8,16},{16,24},{24,0},{1,9},{9,17},{17,25},{25,1},{2,10},{10... | collective-permute-start | bytes 1572872 | tf_op jit(solution)/shard_map/ppermute | solution.py:124
  348.8 36.9 %collective-permute-start.32 = (bf16[128,2048]{1,0:T(8,128)(2,1)S(1)}, bf16[128,2048]{1,0:T(8,128)(2,1)S(1)}, u32[]{:S(2)}, u32[]{:S(2)}) collective-permute-start(bf16[128,2048]{1,0:T(8,128)(2,1)S(1)} %get-tuple-element.193), channel_id=1, source_target_pairs={{0,16},{8,24},{16,0},{24,8},{1,17},{9,25},{17,1},{25,9},{2,18},{10... | collective-permute-start | bytes 1572872 | tf_op jit(solution)/shard_map/ppermute | solution.py:124
  350.3 35.4 %collective-permute-start.31 = (bf16[128,2048]{1,0:T(8,128)(2,1)S(1)}, bf16[128,2048]{1,0:T(8,128)(2,1)S(1)}, u32[]{:S(2)}, u32[]{:S(2)}) collective-permute-start(bf16[128,2048]{1,0:T(8,128)(2,1)S(1)} %get-tuple-element.191), channel_id=1, source_target_pairs={{0,24},{8,0},{16,8},{24,16},{1,25},{9,1},{17,9},{25,17},{2,26},{10... | collective-permute-start | bytes 1572872 | tf_op jit(solution)/shard_map/ppermute | solution.py:124
  354.6 32.6 %collective-permute-start.29 = (bf16[256,1408]{1,0:T(8,128)(2,1)S(1)}, bf16[256,1408]{1,0:T(8,128)(2,1)S(1)}, u32[]{:S(2)}, u32[]{:S(2)}) collective-permute-start(bf16[256,1408]{1,0:T(8,128)(2,1)S(1)} %dynamic-slice_bitcast_fusion.6), channel_id=1, source_target_pairs={{0,2},{2,0},{1,3},{3,1},{4,6},{6,4},{5,7},{7,5},{8,10},{10,8},{9,1... | collective-permute-start | bytes 2162696 | tf_op jit(solution)/shard_map/ppermute | solution.py:82
  388.6 47.5 %all-to-all-start.1 = ((bf16[8,64,1408]{2,1,0:T(8,128)(2,1)}), bf16[8,64,1408]{2,1,0:T(8,128)(2,1)}, u32[]{:S(2)}, u32[]{:S(2)}) async-start(bf16[8,64,1408]{2,1,0:T(8,128)(2,1)} %bitcast.281), calls=%async_computation.3 | async-start | bytes 2883584 | tf_op jit(solution)/shard_map/all_to_all | solution.py:41
  401.0 117.4 %reduce-scatter.9.cloned.1.call-start = ((), (), s32[]{:S(2)}) async-start(), calls=%async_computation.12 | async-start | bytes 5242880 | tf_op jit(solution)/shard_map/reduce_scatter | solution.py:37
  443.8 4.5 collective-permute-start.34
  452.7 28.7 %collective-permute-start.37 = (bf16[2,128,1024]{2,1,0:T(8,128)(2,1)}, bf16[2,128,1024]{2,1,0:T(8,128)(2,1)}, u32[]{:S(2)}, u32[]{:S(2)}) collective-permute-start(bf16[2,128,1024]{2,1,0:T(8,128)(2,1)} %dynamic-slice_bitcast_fusion.8), channel_id=1, source_target_pairs={{0,2},{2,0},{1,3},{3,1},{4,6},{6,4},{5,7},{7,5},{8,10},{10,8},{9,1... | collective-permute-start | bytes 1572872 | tf_op jit(solution)/shard_map/ppermute | solution.py:82
  466.1 17.6 %collective-permute-start.35 = (bf16[2,128,1024]{2,1,0:T(8,128)(2,1)}, bf16[2,128,1024]{2,1,0:T(8,128)(2,1)}, u32[]{:S(2)}, u32[]{:S(2)}) collective-permute-start(bf16[2,128,1024]{2,1,0:T(8,128)(2,1)} %dynamic-slice_bitcast_fusion.9), channel_id=1, source_target_pairs={{0,4},{4,0},{1,5},{5,1},{2,6},{6,2},{3,7},{7,3},{8,12},{12,8},{9,1... | collective-permute-start | bytes 1572872 | tf_op jit(solution)/shard_map/ppermute | solution.py:82
  483.1 7.8 %collective-permute-start.38 = (bf16[128,1024]{1,0:T(8,128)(2,1)S(1)}, bf16[128,1024]{1,0:T(8,128)(2,1)S(1)}, u32[]{:S(2)}, u32[]{:S(2)}) collective-permute-start(bf16[128,1024]{1,0:T(8,128)(2,1)S(1)} %dynamic-slice_bitcast_fusion.16), channel_id=1, source_target_pairs={{0,4},{4,0},{1,5},{5,1},{2,6},{6,2},{3,7},{7,3},{8,12},{12,8},{9,1... | collective-permute-start | bytes 786440 | tf_op jit(solution)/shard_map/ppermute | solution.py:82
  485.1 7.6 %collective-permute-start.36 = (bf16[128,1024]{1,0:T(8,128)(2,1)S(1)}, bf16[128,1024]{1,0:T(8,128)(2,1)S(1)}, u32[]{:S(2)}, u32[]{:S(2)}) collective-permute-start(bf16[128,1024]{1,0:T(8,128)(2,1)S(1)} %dynamic-slice_bitcast_fusion.17), channel_id=1, source_target_pairs={{0,2},{2,0},{1,3},{3,1},{4,6},{6,4},{5,7},{7,5},{8,10},{10,8},{9,1... | collective-permute-start | bytes 786440 | tf_op jit(solution)/shard_map/ppermute | solution.py:82
  530.2 7.1 %collective-permute-start.41 = (f32[9,64]{1,0:T(8,128)S(1)}, f32[9,64]{1,0:T(8,128)S(1)}, u32[]{:S(2)}, u32[]{:S(2)}) collective-permute-start(f32[9,64]{1,0:T(8,128)S(1)} %add.434), channel_id=1, source_target_pairs={{0,4},{4,0},{1,5},{5,1},{2,6},{6,2},{3,7},{7,3},{8,12},{12,8},{9,1... | collective-permute-start | bytes 6920 | tf_op jit(solution)/shard_map/ppermute | solution.py:230
  532.7 30.6 %all-to-all-start.2 = ((bf16[8,64,768]{2,1,0:T(8,128)(2,1)}), bf16[8,64,768]{2,1,0:T(8,128)(2,1)}, u32[]{:S(2)}, u32[]{:S(2)}) async-start(bf16[8,64,768]{2,1,0:T(8,128)(2,1)} %bitcast.287), calls=%async_computation.6 | async-start | bytes 1572864 | tf_op jit(solution)/shard_map/all_to_all | solution.py:41
  (69 other events, 434.9 us)
Sparse Core Ops, SparseCore 0:
  10.4 30.6 all-gather.11
  47.7 64.8 all-gather.5
  138.1 58.2 reduce-scatter.4
  207.0 48.3 all-gather.7
  283.6 48.7 reduce-scatter.6
  345.4 42.9 all-gather.9
  392.3 46.8 reduce-scatter.10
  441.6 76.7 reduce-scatter.8

commit v7 on v6

--- a/solution.py
+++ b/solution.py
@@ -733,8 +733,8 @@
     first_row = lax.axis_index("z") * plane_rows
     rows_first = lax.dynamic_slice_in_dim(w_proj, first_row, plane_rows)
     rows_inner = low_mixer[3].reshape(plane_rows, chans)
-    shard_all, shard_in, shard_down, gain_in, total_early, input_grad, rows_first, rows_inner = tied(
-        shard_all, shard_in, shard_down, gain_in, total_early, input_grad, rows_first, rows_inner
+    shard_all, shard_in, shard_down, gain_in, total_early, input_grad, rows_first, rows_inner, block_out = tied(
+        shard_all, shard_in, shard_down, gain_in, total_early, input_grad, rows_first, rows_inner, block_out
     )
     shard_proj = shard_all[:, : 3 * chans]
     got_proj = exchange(shard_proj.reshape(spots, own, 3 * chans), PLANE)

time: 589 us -> 589 us (level)
    unnamed x124 -> x126, local copies, waits for them, and re-layouts: 25.6 us -> 25.7 us
  transfers between devices with their start and end apart: 55 -> 55, of which waited for: 27 -> 28; matrix products, arithmetic and copies ran while one was open for 31% -> 31% of each run, Pallas kernels for 4% -> 4%
where the time goes in v7:
time: 589 us; the launch traced here: 582 us
  waiting for transfers between devices  204 us (35%)
  local copies, waits for them, and re-layouts  91.9 us (16%)
  starting transfers between devices  83.6 us (14%)
  other arithmetic  74 us (13%)
  matrix products  71 us (12%)
  Pallas kernels  34.5 us (6%)
  between operations  22.8 us (4%)
    ppermute x14, waiting for transfers between devices, ring_gather(): other = lax.ppermute(value, axis, [(0, 1), (1, 0)])  66.4 us
    ppermute x3, waiting for transfers between devices, direct_scatter(): lax.ppermute(block, axis, [(i, (i - back) % count) for i in range(count)])  29.9 us
    ppermute x10, waiting for transfers between devices, ring_terms(): return [block(0), lax.ppermute(block(1), axis, [(0, 1), (1, 0)])]  28.7 us
    unnamed x126, local copies, waits for them, and re-layouts  25.7 us
    ppermute x3, waiting for transfers between devices, line_exchange(): lax.ppermute(blocks[back], 'z', [(i, (i - back) % count) for i in range(c...  21.9 us
    all_to_all x3, starting transfers between devices, exchange(): return lax.all_to_all(value, axes, 0, 0, tiled=True)  21.9 us
    reduce_scatter x4, waiting for transfers between devices, scatter(): return lax.psum_scatter(value, axes, scatter_dimension=0, tiled=True)  19 us
    pallas_call x2, Pallas kernels, run_adam(): pl.pallas_call(adam_rows, grid=(own // rows,), in_specs=[pl.BlockSpec(mem...  16.1 us
  transfers between devices with their start and end apart: 55, of which 28 were waited for; matrix products, arithmetic and copies ran while one was open for 31% of the time, Pallas kernels for 4%

profile of v7, /device:TPU:0, one launch (start us, length us, event | category | flops | bytes accessed | tf_op | source)
XLA Modules:
  0.0 581.8 jit_solution(11711269191252403000)
XLA Ops:
  12.0 5.4 shard_map.271
  19.2 5.2 all-to-all-start
  26.2 8.3 %reshape.219 = bf16[64,2,4,4,2,176]{5,4,3,2,0,1:T(2,128)(2,1)S(1)} reshape(bf16[64,2,5632]{2,0,1:T(8,128)(2,1)} %copy.84) | data formatting | bytes 2883584 | tf_op jit(solution)/shard_map/reshape | solution.py:634
  36.7 5.4 reshape.220
  75.0 9.2 %collective-permute-done.7 = bf16[2,128,1024]{2,1,0:T(8,128)(2,1)S(1)} collective-permute-done((bf16[2,128,1024]{2,1,0:T(8,128)(2,1)S(1)}, bf16[2,128,1024]{2,1,0:T(8,128)(2,1)S(1)}, u32[]{:S(2)}, u32[]{:S(2)}) %collective-permute-start.7) | collective-permute-done | bytes 524320 | tf_op jit(solution)/shard_map/ppermute | solution.py:47
  89.4 7.9 %collective-permute-done.3 = bf16[2,88,2048]{2,1,0:T(8,128)(2,1)S(1)} collective-permute-done((bf16[2,88,2048]{2,1,0:T(8,128)(2,1)S(1)}, bf16[2,88,2048]{2,1,0:T(8,128)(2,1)S(1)}, u32[]{:S(2)}, u32[]{:S(2)}) %collective-permute-start.3) | collective-permute-done | bytes 720928 | tf_op jit(solution)/shard_map/ppermute | solution.py:47
  102.7 2.8 fusion.1
  105.5 7.0 %all-gather.6.cloned.1.call-done = bf16[2048,768]{1,0:T(8,128)(2,1)} async-done(((bf16[512,768]{1,0:T(8,128)(2,1)}), bf16[2048,768]{1,0:T(8,128)(2,1)}) %all-gather.6.cloned.1.call-update) | async-done | bytes 3145744 | tf_op jit(solution)/shard_map/all_gather | solution.py:33
  112.5 4.0 collective-permute-start.16
  116.5 6.1 %fusion.59.proj_ref = f32[1024,768]{1,0:T(8,128)S(1)} fusion(bf16[1024,2048]{1,0:T(8,128)(2,1)} %fusion.1, bf16[2048,768]{1,0:T(8,128)(2,1)} %all-gather.6.cloned.1.call-done), kind=kOutput, calls=%fused_computation.225 | convolution fusion | flops 3221225472 | bytes 10485760 | tf_op jit(solution)/shard_map/dot_general | solution.py:656
  122.7 3.3 shard_map.272
  127.2 3.5 convolution_convert_fusion.1
  130.8 6.9 %collective-permute-done.16 = bf16[128,2048]{1,0:T(8,128)(2,1)} collective-permute-done((bf16[128,2048]{1,0:T(8,128)(2,1)S(1)}, bf16[128,2048]{1,0:T(8,128)(2,1)}, u32[]{:S(2)}, u32[]{:S(2)}) %collective-permute-start.16) | collective-permute-done | bytes 524320 | tf_op jit(solution)/shard_map/ppermute | solution.py:181
  145.1 8.4 %collective-permute-done.19 = bf16[2,64,1408]{2,1,0:T(8,128)(2,1)} collective-permute-done((bf16[2,64,1408]{2,1,0:T(8,128)(2,1)}, bf16[2,64,1408]{2,1,0:T(8,128)(2,1)}, u32[]{:S(2)}, u32[]{:S(2)}) %collective-permute-start.19) | collective-permute-done | bytes 360480 | tf_op jit(solution)/shard_map/ppermute | solution.py:210
  153.6 13.5 %collective-permute-done.20 = bf16[2,64,1408]{2,1,0:T(8,128)(2,1)} collective-permute-done((bf16[2,64,1408]{2,1,0:T(8,128)(2,1)}, bf16[2,64,1408]{2,1,0:T(8,128)(2,1)}, u32[]{:S(2)}, u32[]{:S(2)}) %collective-permute-start.20) | collective-permute-done | bytes 360480 | tf_op jit(solution)/shard_map/ppermute | solution.py:210
  173.4 6.9 %collective-permute-start.17 = (bf16[128,2048]{1,0:T(8,128)(2,1)S(1)}, bf16[128,2048]{1,0:T(8,128)(2,1)S(1)}, u32[]{:S(2)}, u32[]{:S(2)}) collective-permute-start(bf16[128,2048]{1,0:T(8,128)(2,1)S(1)} %multiply_convert_fusion.4.cot_ref), channel_id=1, source_target_pairs={{0,16},{8,24},{16,0},{24,8},{1,17},{9,25},{17,1},{25,9},{2,18},{10... | collective-permute-start | bytes 1572872 | tf_op jit(solution)/shard_map/ppermute | solution.py:181
  180.3 15.4 %collective-permute-done.22 = bf16[256,1408]{1,0:T(8,128)(2,1)} collective-permute-done((bf16[256,1408]{1,0:T(8,128)(2,1)}, bf16[256,1408]{1,0:T(8,128)(2,1)}, u32[]{:S(2)}, u32[]{:S(2)}) %collective-permute-start.22) | collective-permute-done | bytes 720928 | tf_op jit(solution)/shard_map/ppermute | solution.py:47
  209.1 29.7 %collective-permute-done.25 = bf16[2,256,1408]{2,1,0:T(8,128)(2,1)} collective-permute-done((bf16[2,256,1408]{2,1,0:T(8,128)(2,1)}, bf16[2,256,1408]{2,1,0:T(8,128)(2,1)}, u32[]{:S(2)}, u32[]{:S(2)}) %collective-permute-start.25) | collective-permute-done | bytes 1441824 | tf_op jit(solution)/shard_map/ppermute | solution.py:47
  242.1 5.2 pad_maximum_fusion
  251.8 2.9 all-gather.8.cloned.1.call-done
  254.7 10.3 %fusion.60 = f32[1024,1408]{0,1:T(8,128)S(1)} fusion(bf16[1024,2048]{1,0:T(8,128)(2,1)} %all-gather.8.cloned.1.call-done, bf16[2048,1408]{1,0:T(8,128)(2,1)} %bitcast.276), kind=kOutput, calls=%fused_computation.226 | convolution fusion | flops 5905580032 | bytes 15728640 | tf_op jit(solution)/shard_map/dot_general | solution.py:681
  265.0 5.2 multiply_convert_fusion.2
  271.7 11.0 %convolution_convert_fusion.3 = bf16[1024,2048]{1,0:T(8,128)(2,1)} fusion(bf16[2048,1408]{1,0:T(8,128)(2,1)} %bitcast.277, bf16[1024,704]{0,1:T(8,128)(2,1)S(1)} %get-tuple-element.167, bf16[1024,704]{0,1:T(8,128)(2,1)S(1)} %get-tuple-element.166), kind=kOutput, calls=%fused_computation.16 | convolution fusion | flops 5913444352 | bytes 12845056 | tf_op jit(solution)/shard_map/dot_general | solution.py:690
  283.1 5.9 %convolution_convert_fusion.2 = bf16[1024,2048]{1,0:T(8,128)(2,1)S(1)} fusion(bf16[1024,704]{0,1:T(8,128)(2,1)} %get-tuple-element.110, bf16[704,2048]{1,0:T(8,128)(2,1)} %bitcast.289), kind=kOutput, calls=%fused_computation.15 | convolution fusion | flops 2954887168 | bytes 8519680 | tf_op jit(solution)/shard_map/dot_general | solution.py:694
  293.4 7.0 %convolution_convert_fusion = bf16[2048,1408]{1,0:T(8,128)(2,1)S(1)} fusion(bf16[1024,2048]{1,0:T(8,128)(2,1)S(1)} %copy-done.52, bf16[1024,704]{0,1:T(8,128)(2,1)S(1)} %copy-done.59, bf16[1024,704]{0,1:T(8,128)(2,1)S(1)} %copy-done.57), kind=kOutput, calls=%fused_computation.4 | convolution fusion | flops 5914230784 | bytes 12845056 | tf_op jit(solution)/shard_map/dot_general | solution.py:692
  307.4 4.6 fusion.3
  312.1 4.4 convolution_convert_fusion.6
  316.5 20.2 %collective-permute-done.27 = bf16[2,256,1408]{2,1,0:T(8,128)(2,1)} collective-permute-done((bf16[2,256,1408]{2,1,0:T(8,128)(2,1)}, bf16[2,256,1408]{2,1,0:T(8,128)(2,1)}, u32[]{:S(2)}, u32[]{:S(2)}) %collective-permute-start.27) | collective-permute-done | bytes 1441824 | tf_op jit(solution)/shard_map/ppermute | solution.py:82
  336.8 3.0 collective-permute-done.28
  355.1 9.5 %collective-permute-done.33 = bf16[128,2048]{1,0:T(8,128)(2,1)S(1)} collective-permute-done((bf16[128,2048]{1,0:T(8,128)(2,1)S(1)}, bf16[128,2048]{1,0:T(8,128)(2,1)S(1)}, u32[]{:S(2)}, u32[]{:S(2)}) %collective-permute-start.33) | collective-permute-done | bytes 524320 | tf_op jit(solution)/shard_map/ppermute | solution.py:124
  364.6 20.4 %collective-permute-done.32 = bf16[128,2048]{1,0:T(8,128)(2,1)S(1)} collective-permute-done((bf16[128,2048]{1,0:T(8,128)(2,1)S(1)}, bf16[128,2048]{1,0:T(8,128)(2,1)S(1)}, u32[]{:S(2)}, u32[]{:S(2)}) %collective-permute-start.32) | collective-permute-done | bytes 524320 | tf_op jit(solution)/shard_map/ppermute | solution.py:124
  387.9 12.3 %all-to-all-start.1 = ((bf16[8,64,1408]{2,1,0:T(8,128)(2,1)}), bf16[8,64,1408]{2,1,0:T(8,128)(2,1)}, u32[]{:S(2)}, u32[]{:S(2)}) async-start(bf16[8,64,1408]{2,1,0:T(8,128)(2,1)} %bitcast.281), calls=%async_computation.3 | async-start | bytes 2883584 | tf_op jit(solution)/shard_map/all_to_all | solution.py:41
  401.8 4.6 fusion.15.d_mixed_ref
  406.4 5.6 shard_map.275
  415.5 5.9 %convolution_convert_fusion.5 = bf16[2048,768]{1,0:T(8,128)(2,1)S(1)} fusion(bf16[1024,2048]{1,0:T(8,128)(2,1)} %fusion.1, bf16[1024,768]{1,0:T(8,128)(2,1)S(1)} %copy-done.23), kind=kOutput, calls=%fused_computation.18 | convolution fusion | flops 3222798336 | bytes 8912896 | tf_op jit(solution)/shard_map/dot_general | solution.py:717
  424.0 11.4 %all-to-all-done.1 = bf16[8,64,1408]{2,1,0:T(8,128)(2,1)} async-done(((bf16[8,64,1408]{2,1,0:T(8,128)(2,1)}), bf16[8,64,1408]{2,1,0:T(8,128)(2,1)}, u32[]{:S(2)}, u32[]{:S(2)}) %all-to-all-start.1) | async-done | bytes 1441824 | tf_op jit(solution)/shard_map/all_to_all | solution.py:41
  435.4 5.6 convolution_convert_fusion.4
  454.6 8.0 %reshape.235 = bf16[4,2,64,2,4,176]{5,4,3,2,1,0:T(4,128)(2,1)S(1)} reshape(bf16[8,64,1408]{2,1,0:T(8,128)(2,1)} %all-to-all-done.1) | data formatting | bytes 2883584 | tf_op jit(solution)/shard_map/reshape | solution.py:724
  468.7 4.6 copy.69
  473.2 6.6 %reshape.236.grad_ref = bf16[2,64,5632]{2,1,0:T(8,128)(2,1)} reshape(bf16[2,64,4,4,2,176]{5,4,3,2,1,0:T(2,128)(2,1)} %copy.69) | data formatting | bytes 2883584 | tf_op jit(solution)/shard_map/reshape | solution.py:725
  486.0 3.3 collective-permute-done.38
  498.7 19.0 %reduce-scatter.9.cloned.1.call-done.shard_ref = bf16[512,1024]{1,0:T(8,128)(2,1)} async-done(((bf16[2048,1024]{1,0:T(8,128)(2,1)}), bf16[512,1024]{1,0:T(8,128)(2,1)}) %reduce-scatter.9.cloned.1.call-update) | async-done | bytes 1048592 | tf_op jit(solution)/shard_map/reduce_scatter | solution.py:37
  532.8 4.4 all-to-all-start.2
  539.7 2.8 collective-permute-start.42
  544.0 4.3 collective-permute-start.43
  550.6 9.1 %shard_map.279 = (f32[64,2,5632]{2,1,0:T(2,128)}, f32[64,2,5632]{2,1,0:T(2,128)}, f32[64,2,5632]{2,1,0:T(2,128)}) custom-call(f32[1,1]{1,0:T(1,128)} %bitcast.104.clip_ref, f32[64,2,5632]{2,1,0:T(2,128)S(1)} %copy-done.1, f32[64,2,5632]{2,1,0:T(2,128)} %first_ref.3, f32[64,2,5632]{2,1,0:T(2,128)} %second_ref.3, bf16[2,64,5632]{2,1,0:T(8,128)(2,1)S(1)} %copy-done.4), custom_call_target="tpu_custom_call" | custom-call | tf_op jit(solution)/shard_map/pallas_call | solution.py:400
  560.4 2.9 multiply_subtract_fusion
  566.7 6.9 %shard_map.278 = (f32[64,4,2048]{2,1,0:T(4,128)}, f32[64,4,2048]{2,1,0:T(4,128)}, f32[64,4,2048]{2,1,0:T(4,128)}) custom-call(f32[1,1]{1,0:T(1,128)} %bitcast.104.clip_ref, f32[64,4,2048]{2,1,0:T(4,128)S(1)} %copy-done.6, f32[64,4,2048]{2,1,0:T(4,128)S(1)} %copy-done.14, f32[64,4,2048]{2,1,0:T(4,128)} %second_ref.2, bf16[4,64,2048]{2,1,0:T(8,128)(2,1)S(1)} %shard_map.277.grad_ref), custom_call_target="tpu_custom_call" | custom-call | tf_op jit(solution)/shard_map/pallas_call | solution.py:400
  (361 shorter events, 182.9 us)
Async XLA Ops:
  7.2 36.7 %all-gather.12.cloned.1.call-start = ((), (), s32[]{:S(2)}) async-start(), calls=%async_computation.14 | async-start | bytes 1310720 | tf_op jit(solution)/shard_map/all_gather | solution.py:33
  19.2 24.6 %all-to-all-start = ((bf16[8,64,768]{2,1,0:T(8,128)(2,1)}), bf16[8,64,768]{2,1,0:T(8,128)(2,1)}, u32[]{:S(2)}, u32[]{:S(2)}) async-start(bf16[8,64,768]{2,1,0:T(8,128)(2,1)} %copy-done.18), calls=%async_computation | async-start | bytes 1572864 | tf_op jit(solution)/shard_map/all_to_all | solution.py:41
  24.4 88.1 %all-gather.6.cloned.1.call-start = ((), (), s32[]{:S(2)}) async-start(), calls=%async_computation.7 | async-start | bytes 3932160 | tf_op jit(solution)/shard_map/all_gather | solution.py:33
  47.5 155.3 %reduce-scatter.5.cloned.1.call-start = ((), (), s32[]{:S(2)}) async-start(), calls=%async_computation.8 | async-start | bytes 5013504 | tf_op jit(solution)/shard_map/reduce_scatter | solution.py:37
  49.2 4.6 collective-permute-start.11
  51.7 19.4 %collective-permute-start = (bf16[88,2048]{1,0:T(8,128)(2,1)}, bf16[88,2048]{1,0:T(8,128)(2,1)}, u32[]{:S(2)}, u32[]{:S(2)}) collective-permute-start(bf16[88,2048]{1,0:T(8,128)(2,1)} %get-tuple-element.225), channel_id=1, source_target_pairs={{0,2},{2,0},{1,3},{3,1},{4,6},{6,4},{5,7},{7,5},{8,10},{10,8},{9,1... | collective-permute-start | bytes 1081352 | tf_op jit(solution)/shard_map/ppermute | solution.py:47
  53.2 17.9 %collective-permute-start.2 = (bf16[88,2048]{1,0:T(8,128)(2,1)}, bf16[88,2048]{1,0:T(8,128)(2,1)}, u32[]{:S(2)}, u32[]{:S(2)}) collective-permute-start(bf16[88,2048]{1,0:T(8,128)(2,1)} %get-tuple-element.226), channel_id=1, source_target_pairs={{0,4},{4,0},{1,5},{5,1},{2,6},{6,2},{3,7},{7,3},{8,12},{12,8},{9,1... | collective-permute-start | bytes 1081352 | tf_op jit(solution)/shard_map/ppermute | solution.py:47
  55.9 11.5 %collective-permute-start.4 = (bf16[128,1024]{1,0:T(8,128)(2,1)S(1)}, bf16[128,1024]{1,0:T(8,128)(2,1)S(1)}, u32[]{:S(2)}, u32[]{:S(2)}) collective-permute-start(bf16[128,1024]{1,0:T(8,128)(2,1)S(1)} %get-tuple-element.229), channel_id=1, source_target_pairs={{0,2},{2,0},{1,3},{3,1},{4,6},{6,4},{5,7},{7,5},{8,10},{10,8},{9,1... | collective-permute-start | bytes 786440 | tf_op jit(solution)/shard_map/ppermute | solution.py:47
  56.7 11.5 %collective-permute-start.6 = (bf16[128,1024]{1,0:T(8,128)(2,1)S(1)}, bf16[128,1024]{1,0:T(8,128)(2,1)}, u32[]{:S(2)}, u32[]{:S(2)}) collective-permute-start(bf16[128,1024]{1,0:T(8,128)(2,1)S(1)} %get-tuple-element.230), channel_id=1, source_target_pairs={{0,4},{4,0},{1,5},{5,1},{2,6},{6,2},{3,7},{7,3},{8,12},{12,8},{9,1... | collective-permute-start | bytes 786440 | tf_op jit(solution)/shard_map/ppermute | solution.py:47
  58.2 6.0 %collective-permute-start.13 = (f32[16,3,64]{2,1,0:T(4,128)S(1)}, f32[16,3,64]{2,1,0:T(4,128)S(1)}, u32[]{:S(2)}, u32[]{:S(2)}) collective-permute-start(f32[16,3,64]{2,1,0:T(4,128)S(1)} %pad_maximum_fusion.18), channel_id=1, source_target_pairs={{0,16},{8,24},{16,0},{24,8},{1,17},{9,25},{17,1},{25,9},{2,18},{10... | collective-permute-start | bytes 36872 | tf_op jit(solution)/shard_map/ppermute | solution.py:100
  64.2 21.6 %collective-permute-start.14 = (bf16[4,64,1408]{2,1,0:T(8,128)(2,1)}, bf16[4,64,1408]{2,1,0:T(8,128)(2,1)}, u32[]{:S(2)}, u32[]{:S(2)}) collective-permute-start(bf16[4,64,1408]{2,1,0:T(8,128)(2,1)} %dynamic-slice_bitcast_fusion.7), channel_id=1, source_target_pairs={{0,1},{1,0},{2,3},{3,2},{4,5},{5,4},{6,7},{7,6},{8,9},{9,8},{10,11... | collective-permute-start | bytes 2162696 | tf_op jit(solution)/shard_map/ppermute | solution.py:200
  69.3 14.9 %collective-permute-start.7 = (bf16[2,128,1024]{2,1,0:T(8,128)(2,1)S(1)}, bf16[2,128,1024]{2,1,0:T(8,128)(2,1)S(1)}, u32[]{:S(2)}, u32[]{:S(2)}) collective-permute-start(bf16[2,128,1024]{2,1,0:T(8,128)(2,1)S(1)} %pad_maximum_fusion.17), channel_id=1, source_target_pairs={{0,2},{2,0},{1,3},{3,1},{4,6},{6,4},{5,7},{7,5},{8,10},{10,8},{9,1... | collective-permute-start | bytes 1572872 | tf_op jit(solution)/shard_map/ppermute | solution.py:47
  70.5 14.9 %collective-permute-start.5 = (bf16[2,128,1024]{2,1,0:T(8,128)(2,1)S(1)}, bf16[2,128,1024]{2,1,0:T(8,128)(2,1)S(1)}, u32[]{:S(2)}, u32[]{:S(2)}) collective-permute-start(bf16[2,128,1024]{2,1,0:T(8,128)(2,1)S(1)} %pad_maximum_fusion.16), channel_id=1, source_target_pairs={{0,4},{4,0},{1,5},{5,1},{2,6},{6,2},{3,7},{7,3},{8,12},{12,8},{9,1... | collective-permute-start | bytes 1572872 | tf_op jit(solution)/shard_map/ppermute | solution.py:47
  72.4 24.9 %collective-permute-start.3 = (bf16[2,88,2048]{2,1,0:T(8,128)(2,1)S(1)}, bf16[2,88,2048]{2,1,0:T(8,128)(2,1)S(1)}, u32[]{:S(2)}, u32[]{:S(2)}) collective-permute-start(bf16[2,88,2048]{2,1,0:T(8,128)(2,1)S(1)} %pad_maximum_fusion.13), channel_id=1, source_target_pairs={{0,2},{2,0},{1,3},{3,1},{4,6},{6,4},{5,7},{7,5},{8,10},{10,8},{9,1... | collective-permute-start | bytes 2162696 | tf_op jit(solution)/shard_map/ppermute | solution.py:47
  73.4 24.5 %collective-permute-start.1 = (bf16[2,88,2048]{2,1,0:T(8,128)(2,1)S(1)}, bf16[2,88,2048]{2,1,0:T(8,128)(2,1)S(1)}, u32[]{:S(2)}, u32[]{:S(2)}) collective-permute-start(bf16[2,88,2048]{2,1,0:T(8,128)(2,1)S(1)} %pad_maximum_fusion.12), channel_id=1, source_target_pairs={{0,4},{4,0},{1,5},{5,1},{2,6},{6,2},{3,7},{7,3},{8,12},{12,8},{9,1... | collective-permute-start | bytes 2162696 | tf_op jit(solution)/shard_map/ppermute | solution.py:47
  85.8 14.2 %collective-permute-start.8 = (bf16[2,2,128,2048]{3,2,1,0:T(8,128)(2,1)S(1)}, bf16[2,2,128,2048]{3,2,1,0:T(8,128)(2,1)S(1)}, u32[]{:S(2)}, u32[]{:S(2)}) collective-permute-start(bf16[2,2,128,2048]{3,2,1,0:T(8,128)(2,1)S(1)} %pad_maximum_fusion.4), channel_id=1, source_target_pairs={{0,1},{1,0},{2,3},{3,2},{4,5},{5,4},{6,7},{7,6},{8,9},{9,8},{10,11... | collective-permute-start | bytes 6291464 | tf_op jit(solution)/shard_map/ppermute | solution.py:47
  112.5 18.3 %collective-permute-start.15 = (bf16[128,2048]{1,0:T(8,128)(2,1)S(1)}, bf16[128,2048]{1,0:T(8,128)(2,1)S(1)}, u32[]{:S(2)}, u32[]{:S(2)}) collective-permute-start(bf16[128,2048]{1,0:T(8,128)(2,1)S(1)} %multiply_convert_fusion.4.cot_ref), channel_id=1, source_target_pairs={{0,8},{8,16},{16,24},{24,0},{1,9},{9,17},{17,25},{25,1},{2,10},{10... | collective-permute-start | bytes 1572872 | tf_op jit(solution)/shard_map/ppermute | solution.py:181
  112.5 25.2 %collective-permute-start.16 = (bf16[128,2048]{1,0:T(8,128)(2,1)S(1)}, bf16[128,2048]{1,0:T(8,128)(2,1)}, u32[]{:S(2)}, u32[]{:S(2)}) collective-permute-start(bf16[128,2048]{1,0:T(8,128)(2,1)S(1)} %multiply_convert_fusion.4.cot_ref), channel_id=1, source_target_pairs={{0,24},{8,0},{16,8},{24,16},{1,25},{9,1},{17,9},{25,17},{2,26},{10... | collective-permute-start | bytes 1572872 | tf_op jit(solution)/shard_map/ppermute | solution.py:181
  137.7 116.9 %all-gather.8.cloned.1.call-start = ((), (), s32[]{:S(2)}) async-start(), calls=%async_computation.9 | async-start | bytes 4718592 | tf_op jit(solution)/shard_map/all_gather | solution.py:33
  140.0 13.6 %collective-permute-start.19 = (bf16[2,64,1408]{2,1,0:T(8,128)(2,1)}, bf16[2,64,1408]{2,1,0:T(8,128)(2,1)}, u32[]{:S(2)}, u32[]{:S(2)}) collective-permute-start(bf16[2,64,1408]{2,1,0:T(8,128)(2,1)} %get-tuple-element.206), channel_id=1, source_target_pairs={{0,8},{8,16},{16,24},{24,0},{1,9},{9,17},{17,25},{25,1},{2,10},{10... | collective-permute-start | bytes 1081352 | tf_op jit(solution)/shard_map/ppermute | solution.py:210
  141.0 26.1 %collective-permute-start.20 = (bf16[2,64,1408]{2,1,0:T(8,128)(2,1)}, bf16[2,64,1408]{2,1,0:T(8,128)(2,1)}, u32[]{:S(2)}, u32[]{:S(2)}) collective-permute-start(bf16[2,64,1408]{2,1,0:T(8,128)(2,1)} %get-tuple-element.205), channel_id=1, source_target_pairs={{0,16},{8,24},{16,0},{24,8},{1,17},{9,25},{17,1},{25,9},{2,18},{10... | collective-permute-start | bytes 1081352 | tf_op jit(solution)/shard_map/ppermute | solution.py:210
  142.5 24.6 %collective-permute-start.21 = (bf16[2,64,1408]{2,1,0:T(8,128)(2,1)S(1)}, bf16[2,64,1408]{2,1,0:T(8,128)(2,1)}, u32[]{:S(2)}, u32[]{:S(2)}) collective-permute-start(bf16[2,64,1408]{2,1,0:T(8,128)(2,1)S(1)} %get-tuple-element.204), channel_id=1, source_target_pairs={{0,24},{8,0},{16,8},{24,16},{1,25},{9,1},{17,9},{25,17},{2,26},{10... | collective-permute-start | bytes 1081352 | tf_op jit(solution)/shard_map/ppermute | solution.py:210
  169.5 26.1 %collective-permute-start.22 = (bf16[256,1408]{1,0:T(8,128)(2,1)}, bf16[256,1408]{1,0:T(8,128)(2,1)}, u32[]{:S(2)}, u32[]{:S(2)}) collective-permute-start(bf16[256,1408]{1,0:T(8,128)(2,1)} %bitcast.55), channel_id=1, source_target_pairs={{0,2},{2,0},{1,3},{3,1},{4,6},{6,4},{5,7},{7,5},{8,10},{10,8},{9,1... | collective-permute-start | bytes 2162696 | tf_op jit(solution)/shard_map/ppermute | solution.py:47
  171.9 25.2 %collective-permute-start.23 = (bf16[256,1408]{1,0:T(8,128)(2,1)}, bf16[256,1408]{1,0:T(8,128)(2,1)}, u32[]{:S(2)}, u32[]{:S(2)}) collective-permute-start(bf16[256,1408]{1,0:T(8,128)(2,1)} %bitcast.58), channel_id=1, source_target_pairs={{0,4},{4,0},{1,5},{5,1},{2,6},{6,2},{3,7},{7,3},{8,12},{12,8},{9,1... | collective-permute-start | bytes 2162696 | tf_op jit(solution)/shard_map/ppermute | solution.py:47
  173.4 29.5 %collective-permute-start.17 = (bf16[128,2048]{1,0:T(8,128)(2,1)S(1)}, bf16[128,2048]{1,0:T(8,128)(2,1)S(1)}, u32[]{:S(2)}, u32[]{:S(2)}) collective-permute-start(bf16[128,2048]{1,0:T(8,128)(2,1)S(1)} %multiply_convert_fusion.4.cot_ref), channel_id=1, source_target_pairs={{0,16},{8,24},{16,0},{24,8},{1,17},{9,25},{17,1},{25,9},{2,18},{10... | collective-permute-start | bytes 1572872 | tf_op jit(solution)/shard_map/ppermute | solution.py:181
  206.3 133.5 %reduce-scatter.7.cloned.1.call-start = ((), (), s32[]{:S(2)}) async-start(), calls=%async_computation.10 | async-start | bytes 4718592 | tf_op jit(solution)/shard_map/reduce_scatter | solution.py:37
  206.3 32.5 %collective-permute-start.25 = (bf16[2,256,1408]{2,1,0:T(8,128)(2,1)}, bf16[2,256,1408]{2,1,0:T(8,128)(2,1)}, u32[]{:S(2)}, u32[]{:S(2)}) collective-permute-start(bf16[2,256,1408]{2,1,0:T(8,128)(2,1)} %get-tuple-element.109), channel_id=1, source_target_pairs={{0,2},{2,0},{1,3},{3,1},{4,6},{6,4},{5,7},{7,5},{8,10},{10,8},{9,1... | collective-permute-start | bytes 4325384 | tf_op jit(solution)/shard_map/ppermute | solution.py:47
  206.8 34.0 %collective-permute-start.24 = (bf16[2,256,1408]{2,1,0:T(8,128)(2,1)}, bf16[2,256,1408]{2,1,0:T(8,128)(2,1)S(1)}, u32[]{:S(2)}, u32[]{:S(2)}) collective-permute-start(bf16[2,256,1408]{2,1,0:T(8,128)(2,1)} %get-tuple-element.108), channel_id=1, source_target_pairs={{0,4},{4,0},{1,5},{5,1},{2,6},{6,2},{3,7},{7,3},{8,12},{12,8},{9,1... | collective-permute-start | bytes 4325384 | tf_op jit(solution)/shard_map/ppermute | solution.py:47
  209.0 38.3 %collective-permute-start.18 = (bf16[4,128,2048]{2,1,0:T(8,128)(2,1)S(1)}, bf16[4,128,2048]{2,1,0:T(8,128)(2,1)}, u32[]{:S(2)}, u32[]{:S(2)}) collective-permute-start(bf16[4,128,2048]{2,1,0:T(8,128)(2,1)S(1)} %pad_maximum_fusion.5), channel_id=1, source_target_pairs={{0,1},{1,0},{2,3},{3,2},{4,5},{5,4},{6,7},{7,6},{8,9},{9,8},{10,11... | collective-permute-start | bytes 6291464 | tf_op jit(solution)/shard_map/ppermute | solution.py:47
  282.8 105.1 %all-gather.10.cloned.1.call-start = ((), (), s32[]{:S(2)}) async-start(), calls=%async_computation.11 | async-start | bytes 5013504 | tf_op jit(solution)/shard_map/all_gather | solution.py:33
  292.1 15.3 %collective-permute-start.26 = (bf16[4,128,2048]{2,1,0:T(8,128)(2,1)}, bf16[4,128,2048]{2,1,0:T(8,128)(2,1)}, u32[]{:S(2)}, u32[]{:S(2)}) collective-permute-start(bf16[4,128,2048]{2,1,0:T(8,128)(2,1)} %dynamic-slice_bitcast_fusion), channel_id=1, source_target_pairs={{0,1},{1,0},{2,3},{3,2},{4,5},{5,4},{6,7},{7,6},{8,9},{9,8},{10,11... | collective-permute-start | bytes 6291464 | tf_op jit(solution)/shard_map/ppermute | solution.py:82
  302.7 34.1 %collective-permute-start.27 = (bf16[2,256,1408]{2,1,0:T(8,128)(2,1)}, bf16[2,256,1408]{2,1,0:T(8,128)(2,1)}, u32[]{:S(2)}, u32[]{:S(2)}) collective-permute-start(bf16[2,256,1408]{2,1,0:T(8,128)(2,1)} %get-tuple-element.179), channel_id=1, source_target_pairs={{0,4},{4,0},{1,5},{5,1},{2,6},{6,2},{3,7},{7,3},{8,12},{12,8},{9,1... | collective-permute-start | bytes 4325384 | tf_op jit(solution)/shard_map/ppermute | solution.py:82
  306.0 33.8 %collective-permute-start.28 = (bf16[2,256,1408]{2,1,0:T(8,128)(2,1)}, bf16[2,256,1408]{2,1,0:T(8,128)(2,1)}, u32[]{:S(2)}, u32[]{:S(2)}) collective-permute-start(bf16[2,256,1408]{2,1,0:T(8,128)(2,1)} %get-tuple-element.177), channel_id=1, source_target_pairs={{0,2},{2,0},{1,3},{3,1},{4,6},{6,4},{5,7},{7,5},{8,10},{10,8},{9,1... | collective-permute-start | bytes 4325384 | tf_op jit(solution)/shard_map/ppermute | solution.py:82
  344.6 148.3 %reduce-scatter.11.cloned.1.call-start = ((), (), s32[]{:S(2)}) async-start(), calls=%async_computation.13 | async-start | bytes 3604480 | tf_op jit(solution)/shard_map/reduce_scatter | solution.py:37
  347.0 39.3 %collective-permute-start.30 = (bf16[256,1408]{1,0:T(8,128)(2,1)S(1)}, bf16[256,1408]{1,0:T(8,128)(2,1)S(1)}, u32[]{:S(2)}, u32[]{:S(2)}) collective-permute-start(bf16[256,1408]{1,0:T(8,128)(2,1)S(1)} %dynamic-slice_bitcast_fusion.5), channel_id=1, source_target_pairs={{0,4},{4,0},{1,5},{5,1},{2,6},{6,2},{3,7},{7,3},{8,12},{12,8},{9,1... | collective-permute-start | bytes 2162696 | tf_op jit(solution)/shard_map/ppermute | solution.py:82
  347.8 16.8 %collective-permute-start.33 = (bf16[128,2048]{1,0:T(8,128)(2,1)S(1)}, bf16[128,2048]{1,0:T(8,128)(2,1)S(1)}, u32[]{:S(2)}, u32[]{:S(2)}) collective-permute-start(bf16[128,2048]{1,0:T(8,128)(2,1)S(1)} %get-tuple-element.194), channel_id=1, source_target_pairs={{0,8},{8,16},{16,24},{24,0},{1,9},{9,17},{17,25},{25,1},{2,10},{10... | collective-permute-start | bytes 1572872 | tf_op jit(solution)/shard_map/ppermute | solution.py:124
  347.9 37.2 %collective-permute-start.32 = (bf16[128,2048]{1,0:T(8,128)(2,1)S(1)}, bf16[128,2048]{1,0:T(8,128)(2,1)S(1)}, u32[]{:S(2)}, u32[]{:S(2)}) collective-permute-start(bf16[128,2048]{1,0:T(8,128)(2,1)S(1)} %get-tuple-element.195), channel_id=1, source_target_pairs={{0,16},{8,24},{16,0},{24,8},{1,17},{9,25},{17,1},{25,9},{2,18},{10... | collective-permute-start | bytes 1572872 | tf_op jit(solution)/shard_map/ppermute | solution.py:124
  349.6 35.4 %collective-permute-start.31 = (bf16[128,2048]{1,0:T(8,128)(2,1)S(1)}, bf16[128,2048]{1,0:T(8,128)(2,1)S(1)}, u32[]{:S(2)}, u32[]{:S(2)}) collective-permute-start(bf16[128,2048]{1,0:T(8,128)(2,1)S(1)} %get-tuple-element.193), channel_id=1, source_target_pairs={{0,24},{8,0},{16,8},{24,16},{1,25},{9,1},{17,9},{25,17},{2,26},{10... | collective-permute-start | bytes 1572872 | tf_op jit(solution)/shard_map/ppermute | solution.py:124
  353.6 32.9 %collective-permute-start.29 = (bf16[256,1408]{1,0:T(8,128)(2,1)S(1)}, bf16[256,1408]{1,0:T(8,128)(2,1)S(1)}, u32[]{:S(2)}, u32[]{:S(2)}) collective-permute-start(bf16[256,1408]{1,0:T(8,128)(2,1)S(1)} %dynamic-slice_bitcast_fusion.6), channel_id=1, source_target_pairs={{0,2},{2,0},{1,3},{3,1},{4,6},{6,4},{5,7},{7,5},{8,10},{10,8},{9,1... | collective-permute-start | bytes 2162696 | tf_op jit(solution)/shard_map/ppermute | solution.py:82
  387.9 47.5 %all-to-all-start.1 = ((bf16[8,64,1408]{2,1,0:T(8,128)(2,1)}), bf16[8,64,1408]{2,1,0:T(8,128)(2,1)}, u32[]{:S(2)}, u32[]{:S(2)}) async-start(bf16[8,64,1408]{2,1,0:T(8,128)(2,1)} %bitcast.281), calls=%async_computation.3 | async-start | bytes 2883584 | tf_op jit(solution)/shard_map/all_to_all | solution.py:41
  400.3 117.4 %reduce-scatter.9.cloned.1.call-start = ((), (), s32[]{:S(2)}) async-start(), calls=%async_computation.12 | async-start | bytes 5242880 | tf_op jit(solution)/shard_map/reduce_scatter | solution.py:37
  443.1 4.5 collective-permute-start.34
  452.0 27.8 %collective-permute-start.37 = (bf16[2,128,1024]{2,1,0:T(8,128)(2,1)}, bf16[2,128,1024]{2,1,0:T(8,128)(2,1)}, u32[]{:S(2)}, u32[]{:S(2)}) collective-permute-start(bf16[2,128,1024]{2,1,0:T(8,128)(2,1)} %dynamic-slice_bitcast_fusion.8), channel_id=1, source_target_pairs={{0,2},{2,0},{1,3},{3,1},{4,6},{6,4},{5,7},{7,5},{8,10},{10,8},{9,1... | collective-permute-start | bytes 1572872 | tf_op jit(solution)/shard_map/ppermute | solution.py:82
  464.5 17.6 %collective-permute-start.35 = (bf16[2,128,1024]{2,1,0:T(8,128)(2,1)}, bf16[2,128,1024]{2,1,0:T(8,128)(2,1)}, u32[]{:S(2)}, u32[]{:S(2)}) collective-permute-start(bf16[2,128,1024]{2,1,0:T(8,128)(2,1)} %dynamic-slice_bitcast_fusion.9), channel_id=1, source_target_pairs={{0,4},{4,0},{1,5},{5,1},{2,6},{6,2},{3,7},{7,3},{8,12},{12,8},{9,1... | collective-permute-start | bytes 1572872 | tf_op jit(solution)/shard_map/ppermute | solution.py:82
  481.4 7.9 %collective-permute-start.38 = (bf16[128,1024]{1,0:T(8,128)(2,1)S(1)}, bf16[128,1024]{1,0:T(8,128)(2,1)S(1)}, u32[]{:S(2)}, u32[]{:S(2)}) collective-permute-start(bf16[128,1024]{1,0:T(8,128)(2,1)S(1)} %dynamic-slice_bitcast_fusion.16), channel_id=1, source_target_pairs={{0,4},{4,0},{1,5},{5,1},{2,6},{6,2},{3,7},{7,3},{8,12},{12,8},{9,1... | collective-permute-start | bytes 786440 | tf_op jit(solution)/shard_map/ppermute | solution.py:82
  483.5 7.6 %collective-permute-start.36 = (bf16[128,1024]{1,0:T(8,128)(2,1)S(1)}, bf16[128,1024]{1,0:T(8,128)(2,1)S(1)}, u32[]{:S(2)}, u32[]{:S(2)}) collective-permute-start(bf16[128,1024]{1,0:T(8,128)(2,1)S(1)} %dynamic-slice_bitcast_fusion.17), channel_id=1, source_target_pairs={{0,2},{2,0},{1,3},{3,1},{4,6},{6,4},{5,7},{7,5},{8,10},{10,8},{9,1... | collective-permute-start | bytes 786440 | tf_op jit(solution)/shard_map/ppermute | solution.py:82
  529.2 8.1 %collective-permute-start.41 = (f32[9,64]{1,0:T(8,128)S(1)}, f32[9,64]{1,0:T(8,128)S(1)}, u32[]{:S(2)}, u32[]{:S(2)}) collective-permute-start(f32[9,64]{1,0:T(8,128)S(1)} %add.434), channel_id=1, source_target_pairs={{0,4},{4,0},{1,5},{5,1},{2,6},{6,2},{3,7},{7,3},{8,12},{12,8},{9,1... | collective-permute-start | bytes 6920 | tf_op jit(solution)/shard_map/ppermute | solution.py:230
  532.8 30.6 %all-to-all-start.2 = ((bf16[8,64,768]{2,1,0:T(8,128)(2,1)}), bf16[8,64,768]{2,1,0:T(8,128)(2,1)}, u32[]{:S(2)}, u32[]{:S(2)}) async-start(bf16[8,64,768]{2,1,0:T(8,128)(2,1)} %bitcast.287), calls=%async_computation.6 | async-start | bytes 1572864 | tf_op jit(solution)/shard_map/all_to_all | solution.py:41
  (70 other events, 444.5 us)
Sparse Core Ops, SparseCore 0:
  10.4 30.6 all-gather.11
  47.6 64.8 all-gather.5
  137.8 58.3 reduce-scatter.4
  206.4 48.2 all-gather.7
  282.9 48.7 reduce-scatter.6
  344.7 42.9 all-gather.9
  391.6 46.8 reduce-scatter.10
  440.9 76.7 reduce-scatter.8
